TPU v7x, 32 devices: a whole 2x2x4 slice. The times are simulated.
32 devices in a mesh: row: 8 (over y, x, core), col: 4 (over z).
Axes of the slice: x: 2, y: 2, z: 4, core: 2. Of those that a mesh axis runs over, the one named last changes fastest.
Arguments:
- batch: float32 [4096, 1024], P(('row', 'col')), may hold values from -5 to 5, as said below
- running: float32 [4096, 1000], P(('row', 'col')), may hold values from -6 to 6
- targets: float32 [4096, 1000], P(('row', 'col')), may hold values from -6 to 6
- centers: float32 [2048, 1024], P('row'), may hold values from -5 to 5, as said below
- weights: float32 [2048, 1000], P('row'), may hold values from -0.5 to 0.5
Outputs:
- gradient: float32 [2048, 1000], P('row')
- residual: float32 [4096, 1000], P(('row', 'col'))
Inputs may be any that keep to these rules, and one draw needn't show every extreme that they name: Each row of batch is an independent vector of 1024 features times its own positive row scale. Each row of centers is an independent vector of 1024 features times its own positive row scale.
All inputs are finite; a program needn't handle non-finite values.
Results may differ from a plain program's by a relative error of at most 0.0001.
Values sent between devices are 32-bit elements; how exact they have to be, the bound alone decides.
No kernel may reach another device: no remote copies, remote signals or barrier semaphores. Data moves between devices by JAX's collectives and lax.ppermute only.
A program may use at most 64 MiB of HBM per device.

v0:
```python
import math

import jax
import jax.numpy as jnp
from jax import lax
from jax.sharding import PartitionSpec as P


def per_device(batch, running, targets, centers, weights):
    rows_here = batch.shape[0]
    feature_count = batch.shape[1]
    owners = lax.axis_size("row")
    devices_all = owners * lax.axis_size("col")
    length_scale = math.sqrt(feature_count) / 4.0
    row_sq = jnp.sum(batch * batch, axis=1, keepdims=True)
    predicted = running
    cent_piece = lax.all_gather(centers, "row", axis=0, tiled=True)
    weight_piece = lax.all_gather(weights, "row", axis=0, tiled=True)
    crossed = lax.dot_general(
        batch,
        cent_piece,
        (((1,), (1,)), ((), ())),
        precision=lax.Precision.HIGHEST,
        preferred_element_type=jnp.float32,
    )
    dist_sq = row_sq + jnp.sum(cent_piece * cent_piece, axis=1)[None, :] - 2.0 * crossed
    kern_piece = jnp.exp(-jnp.sqrt(dist_sq + 1.0) / length_scale)
    predicted = predicted + jnp.dot(
        kern_piece,
        weight_piece,
        precision=lax.Precision.HIGHEST,
        preferred_element_type=jnp.float32,
    )
    predicted, kernel = (predicted, kern_piece)
    residual = predicted - targets
    partial_sum = lax.psum_scatter(
        lax.dot_general(
            kernel,
            residual,
            (((0,), (0,)), ((), ())),
            precision=lax.Precision.HIGHEST,
            preferred_element_type=jnp.float32,
        ),
        "row",
        scatter_dimension=0,
        tiled=True,
    )
    summed = lax.psum(partial_sum, "col")
    factor = 1.0 / jnp.sqrt(jnp.float32(rows_here * devices_all))
    return (summed * factor, residual)


def solution(mesh):
    return jax.shard_map(
        per_device,
        mesh=mesh,
        in_specs=(
            P(("row", "col"), None),
            P(("row", "col"), None),
            P(("row", "col"), None),
            P("row", None),
            P("row", None),
        ),
        out_specs=(P("row", None), P(("row", "col"), None)),
        check_vma=False,
    )
```

profile of v0, /device:TPU:0, one launch (start us, length us, event | category | flops | bytes accessed | tf_op | source)
XLA Modules:
  0.0 275.1 jit_solution(8173915598616701772)
XLA Ops:
  7.2 0.0 copy-start.1
  7.2 0.0 all-gather.3.cloned.1.call-start
  7.2 0.7 all-gather.3.cloned.1.call-update
  7.9 0.0 all-gather.5.cloned.1.call-start
  8.0 0.7 all-gather.5.cloned.1.call-update
  8.7 0.0 reduce-scatter.2.cloned.1.call-start
  8.7 1.2 multiply_reduce_fusion.1
  9.9 57.2 %all-gather.3.cloned.1.call-done = f32[2048,1024]{1,0:T(8,128)} async-done(((f32[256,1024]{1,0:T(8,128)}), f32[2048,1024]{1,0:T(8,128)}) %all-gather.3.cloned.1.call-update) | async-done | bytes 8388624 | tf_op jit(solution)/shard_map/all_gather | solution.py:17
  67.0 4.1 %multiply_reduce_fusion = f32[2048]{0:T(1024)S(1)} fusion(f32[2048,1024]{1,0:T(8,128)} %all-gather.3.cloned.1.call-done), kind=kLoop, calls=%fused_computation | loop fusion | flops 4192256 | bytes 8396800 | tf_op jit(solution)/shard_map/reduce_sum | solution.py:26
  71.2 0.0 copy-done.1
  71.2 1.6 copy-done
  72.8 8.9 %fusion.5 = f32[128,2048]{1,0:T(8,128)S(1)} fusion(f32[128,1024]{1,0:T(8,128)S(1)} %copy-done.1, f32[2048,1024]{1,0:T(8,128)S(1)} %copy-done, f32[2048]{0:T(1024)S(1)} %multiply_reduce_fusion, f32[128]{0:T(128)S(1)} %multiply_reduce_fusion.1), kind=kOutput, calls=%fused_computation.7 | convolution fusion | flops 3222798336 | bytes 9970176 | tf_op jit(solution)/shard_map/dot_general | solution.py:19
  81.7 42.3 %all-gather.5.cloned.1.call-done = f32[2048,1000]{0,1:T(8,128)} async-done(((f32[256,1000]{0,1:T(8,128)}), f32[2048,1000]{0,1:T(8,128)}) %all-gather.5.cloned.1.call-update) | async-done | bytes 8192016 | tf_op jit(solution)/shard_map/all_gather | solution.py:18
  124.0 0.0 copy-done.3
  124.0 0.0 copy-done.4
  124.0 9.2 %fusion.6 = f32[128,1000]{0,1:T(8,128)S(1)} fusion(f32[128,1000]{0,1:T(8,128)S(1)} %copy-done.3, f32[128,1000]{0,1:T(8,128)S(1)} %copy-done.4, f32[128,2048]{1,0:T(8,128)S(1)} %fusion.5, f32[2048,1000]{0,1:T(8,128)} %all-gather.5.cloned.1.call-done), kind=kOutput, calls=%fused_computation.9 | convolution fusion | flops 3145984000 | bytes 10776576 | tf_op jit(solution)/shard_map/dot_general | solution.py:28
  133.2 0.0 copy-start.2
  133.2 8.7 %fusion.7 = f32[2048,1000]{0,1:T(8,128)} fusion(f32[128,2048]{1,0:T(8,128)S(1)} %fusion.5, f32[128,1000]{0,1:T(8,128)S(1)} %fusion.6), kind=kOutput, calls=%fused_computation.12 | convolution fusion | flops 3145728000 | bytes 9752576 | tf_op jit(solution)/shard_map/dot_general | solution.py:37
  141.9 0.0 reduce-scatter.2.cloned.1.call-update
  142.0 0.0 all-reduce.2.cloned.1.call-start
  142.0 70.4 %reduce-scatter.2.cloned.1.call-done = f32[256,1000]{0,1:T(8,128)} async-done(((f32[2048,1000]{0,1:T(8,128)}), f32[256,1000]{0,1:T(8,128)}) %reduce-scatter.2.cloned.1.call-update) | async-done | bytes 1024016 | tf_op jit(solution)/shard_map/reduce_scatter | solution.py:36
  212.4 0.0 all-reduce.2.cloned.1.call-update
  212.4 53.9 %all-reduce.2.cloned.1.call-done = f32[256,1000]{0,1:T(8,128)} async-done(((f32[256,1000]{0,1:T(8,128)}), f32[256,1000]{0,1:T(8,128)}) %all-reduce.2.cloned.1.call-update) | async-done | bytes 1024016 | tf_op jit(solution)/shard_map/psum | solution.py:48
  266.3 2.2 broadcast_multiply_fusion
  (4 shorter events, 0.0 us)
Async XLA Ops:
  7.2 64.0 %copy-start.1 = (f32[128,1024]{1,0:T(8,128)S(1)}, f32[128,1024]{1,0:T(8,128)}, u32[]{:S(2)}) copy-start(f32[128,1024]{1,0:T(8,128)} %param.5) | copy-start | bytes 1572868
  7.2 59.8 %all-gather.3.cloned.1.call-start = ((), (), s32[]{:S(2)}) async-start(), calls=%async_computation.1 | async-start | bytes 9437184 | tf_op jit(solution)/shard_map/all_gather | solution.py:17
  7.9 116.1 %all-gather.5.cloned.1.call-start = ((), (), s32[]{:S(2)}) async-start(), calls=%async_computation.2 | async-start | bytes 9216000 | tf_op jit(solution)/shard_map/all_gather | solution.py:18
  8.7 203.8 %reduce-scatter.2.cloned.1.call-start = ((), (), s32[]{:S(2)}) async-start(), calls=%async_computation.3 | async-start | bytes 9216000 | tf_op jit(solution)/shard_map/reduce_scatter | solution.py:36
  67.0 5.8 %copy-start = (f32[2048,1024]{1,0:T(8,128)S(1)}, f32[2048,1024]{1,0:T(8,128)}, u32[]{:S(2)}) copy-start(f32[2048,1024]{1,0:T(8,128)} %all-gather.3.cloned.1.call-done) | copy-start | bytes 25165828
  67.0 57.0 %copy-start.3 = (f32[128,1000]{0,1:T(8,128)S(1)}, f32[128,1000]{0,1:T(8,128)}, u32[]{:S(2)}) copy-start(f32[128,1000]{0,1:T(8,128)} %param.7) | copy-start | bytes 1536004
  67.0 57.0 %copy-start.4 = (f32[128,1000]{0,1:T(8,128)S(1)}, f32[128,1000]{0,1:T(8,128)}, u32[]{:S(2)}) copy-start(f32[128,1000]{0,1:T(8,128)} %param.6) | copy-start | bytes 1536004
  133.2 8.8 %copy-start.2 = (f32[128,1000]{0,1:T(8,128)}, f32[128,1000]{0,1:T(8,128)S(1)}, u32[]{:S(2)}) copy-start(f32[128,1000]{0,1:T(8,128)S(1)} %fusion.6) | copy-start | bytes 1536004
  142.0 124.4 %all-reduce.2.cloned.1.call-start = ((), (), s32[]{:S(2)}) async-start(), calls=%async_computation.4 | async-start | bytes 2048000 | tf_op jit(solution)/shard_map/psum | solution.py:48
Sparse Core Ops, SparseCore 0:
  9.9 57.0 all-gather.2
  68.9 55.0 all-gather.4
  142.1 70.2 reduce-scatter.1
  214.8 51.5 all-reduce.1
where the time goes:
time: 275 us
  waiting for transfers between devices  225 us (82%)
  matrix products  26.7 us (10%)
  between operations  13.8 us (5%)
  other arithmetic  7.55 us (3%)
    reduce_scatter x1, waiting for transfers between devices, per_device(): lax.psum_scatter(lax.dot_general(kernel, residual, (((0,), (0,)), ((), ()...  70.4 us
    all_gather x1, waiting for transfers between devices, per_device(): cent_piece = lax.all_gather(centers, 'row', axis=0, tiled=True)  57.2 us
    psum x1, waiting for transfers between devices, per_device(): summed = lax.psum(partial_sum, 'col')  53.9 us
    all_gather x1, waiting for transfers between devices, per_device(): weight_piece = lax.all_gather(weights, 'row', axis=0, tiled=True)  42.3 us
    dot_general x1, matrix products, per_device(): jnp.dot(kern_piece, weight_piece, precision=lax.Precision.HIGHEST, prefer...  9.15 us
    dot_general x1, matrix products, per_device(): lax.dot_general(batch, cent_piece, (((1,), (1,)), ((), ())), precision=la...  8.87 us
    dot_general x1, matrix products, per_device(): lax.dot_general(kernel, residual, (((0,), (0,)), ((), ())), precision=lax...  8.73 us
  transfers between devices with their start and end apart: 4, of which 4 were waited for; matrix products, arithmetic and copies ran while one was open for 5% of the time, Pallas kernels for 0%

commit v1 on v0

v1 whole, which is shorter than its diff:
```python
import math

import jax
import jax.numpy as jnp
from jax import lax
from jax.sharding import PartitionSpec as P

HIGHEST = lax.Precision.HIGHEST
HIGH = lax.Precision.HIGH
PIECES = 2


def dot(a, b, dims, precision):
    return lax.dot_general(
        a, b, (dims, ((), ())), precision=precision, preferred_element_type=jnp.float32
    )


def swap_row(value, owners, flip):
    return lax.ppermute(value, "row", [(i, i ^ flip) for i in range(owners)])


def sum_col(value, depth):
    if depth != 4:
        return lax.psum(value, "col")
    inner = value + lax.ppermute(value, "col", [(0, 1), (3, 2)])
    total = inner + lax.ppermute(inner, "col", [(1, 2), (2, 1)])
    back = lax.ppermute(total, "col", [(1, 0), (2, 3)])
    place = lax.axis_index("col")
    return jnp.where((place == 0) | (place == 3), back, total)


def cuts(size, pieces):
    step = -(-size // pieces // 8) * 8
    edges = list(range(0, size, step)) + [size]
    return list(zip(edges[:-1], edges[1:]))


def per_device(batch, running, targets, centers, weights):
    rows_here, feature_count = batch.shape
    owners = lax.axis_size("row")
    depth = lax.axis_size("col")
    chips = owners // 2
    length_scale = math.sqrt(feature_count) / 4.0
    factor = 1.0 / math.sqrt(rows_here * owners * depth)

    blocks = [batch] + [swap_row(batch, owners, 2 * j) for j in range(1, chips)]
    cent = jnp.concatenate([centers, swap_row(centers, owners, 1)], axis=0)
    weights_t = weights.T
    weight = jnp.concatenate([weights_t, swap_row(weights_t, owners, 1)], axis=1)
    cent_sq = jnp.sum(cent * cent, axis=1)

    kernels = []
    for block in blocks:
        crossed = dot(block, cent, ((1,), (1,)), HIGHEST)
        row_sq = jnp.sum(block * block, axis=1, keepdims=True)
        dist_sq = row_sq + cent_sq[None, :] - 2.0 * crossed
        kernels.append(jnp.exp(-jnp.sqrt(dist_sq + 1.0) / length_scale))

    running_t, targets_t = running.T, targets.T
    residuals, gradients = [], []
    for low, high in cuts(weights.shape[1], PIECES):
        piece = weight[low:high]
        predicted = running_t[low:high] + dot(piece, kernels[0], ((1,), (1,)), HIGH)
        for j in range(1, chips):
            share = dot(piece, kernels[j], ((1,), (1,)), HIGH)
            predicted = predicted + swap_row(share, owners, 2 * j)
        residual = predicted - targets_t[low:high]
        residuals.append(residual)
        gradient = dot(residual, kernels[0], ((1,), (0,)), HIGH)
        for j in range(1, chips):
            moved = swap_row(residual, owners, 2 * j)
            gradient = gradient + dot(moved, kernels[j], ((1,), (0,)), HIGH)
        half = centers.shape[0]
        owned = gradient[:, :half] + swap_row(gradient[:, half:], owners, 1)
        gradients.append(sum_col(owned * factor, depth))
    return (
        jnp.concatenate(gradients, axis=0).T,
        jnp.concatenate(residuals, axis=0).T,
    )


def solution(mesh):
    return jax.shard_map(
        per_device,
        mesh=mesh,
        in_specs=(
            P(("row", "col"), None),
            P(("row", "col"), None),
            P(("row", "col"), None),
            P("row", None),
            P("row", None),
        ),
        out_specs=(P("row", None), P(("row", "col"), None)),
        check_vma=False,
    )
```

time: 275 us -> 142 us (0.52)
  waiting for transfers between devices: 225 us -> 87.9 us
  starting transfers between devices: 0.16 us -> 30.4 us
  between operations: 13.8 us -> 1.06 us
  matrix products: 26.7 us -> 16.8 us
  other arithmetic: 7.55 us -> 4.43 us
    all_gather x2 -> x0, waiting for transfers between devices: 99.5 us -> none  [the longest x1 57.2 us: per_device(): cent_piece = lax.all_gather(centers, 'row', axis=0, tiled=True)]
    ppermute x0 -> x25, waiting for transfers between devices: none -> 87.9 us  [the longest x19 42.6 us: swap_row(): return lax.ppermute(value, 'row', [(i, i ^ flip) for i in range(owners)])]
    reduce_scatter x1 -> x0, waiting for transfers between devices: 70.4 us -> none  [per_device(): lax.psum_scatter(lax.dot_general(kernel, residual, (((0,), (0,)), ((), ()...]
    psum x1 -> x0, waiting for transfers between devices: 53.9 us -> none  [per_device(): summed = lax.psum(partial_sum, 'col')]
    ppermute x0 -> x25, starting transfers between devices: none -> 30.4 us  [the longest x19 21.1 us: swap_row(): return lax.ppermute(value, 'row', [(i, i ^ flip) for i in range(owners)])]
    dot_general x3 -> x20, matrix products: 26.7 us -> 16.8 us  [dot(): lax.dot_general(a, b, (dims, ((), ())), precision=precision, preferred_el...]
    reduce_sum x2 -> x5, other arithmetic: 5.31 us -> 1.75 us  [the longest x4 1.54 us: per_device(): row_sq = jnp.sum(block * block, axis=1, keepdims=True)]
  transfers between devices with their start and end apart: 4 -> 25, of which waited for: 4 -> 12; matrix products, arithmetic and copies ran while one was open for 5% -> 11% of each run, Pallas kernels for 0% -> 0%
where the time goes in v1:
time: 142 us
  waiting for transfers between devices  87.9 us (62%)
  starting transfers between devices  30.4 us (21%)
  matrix products  16.8 us (12%)
  other arithmetic  4.43 us (3%)
  local copies, waits for them, and re-layouts  1.5 us (1%)
    ppermute x19, waiting for transfers between devices, swap_row(): return lax.ppermute(value, 'row', [(i, i ^ flip) for i in range(owners)])  42.6 us
    ppermute x2, waiting for transfers between devices, sum_col(): back = lax.ppermute(total, 'col', [(1, 0), (2, 3)])  25.4 us
    ppermute x19, starting transfers between devices, swap_row(): return lax.ppermute(value, 'row', [(i, i ^ flip) for i in range(owners)])  21.1 us
    ppermute x2, waiting for transfers between devices, sum_col(): inner = value + lax.ppermute(value, 'col', [(0, 1), (3, 2)])  19.8 us
    dot_general x20, matrix products, dot(): lax.dot_general(a, b, (dims, ((), ())), precision=precision, preferred_el...  16.8 us
    ppermute x2, starting transfers between devices, sum_col(): inner = value + lax.ppermute(value, 'col', [(0, 1), (3, 2)])  5.27 us
  transfers between devices with their start and end apart: 25, of which 12 were waited for; matrix products, arithmetic and copies ran while one was open for 11% of the time, Pallas kernels for 0%

profile of v1, /device:TPU:0, one launch (start us, length us, event | category | flops | bytes accessed | tf_op | source)
XLA Modules:
  0.0 142.1 jit_solution(4477460248579569268)
XLA Ops:
  1.2 2.6 %collective-permute-start.2 = (f32[128,1024]{1,0:T(8,128)}, f32[128,1024]{1,0:T(8,128)S(1)}, u32[]{:S(2)}, u32[]{:S(2)}) collective-permute-start(f32[128,1024]{1,0:T(8,128)} %param.5), channel_id=1, source_target_pairs={{0,8},{4,12},{8,0},{12,4},{16,24},{20,28},{24,16},{28,20},{1,9},{5... | collective-permute-start | bytes 1572872 | tf_op jit(solution)/shard_map/ppermute | solution.py:20
  7.9 8.8 %collective-permute-done.2 = f32[128,1024]{1,0:T(8,128)S(1)} collective-permute-done((f32[128,1024]{1,0:T(8,128)}, f32[128,1024]{1,0:T(8,128)S(1)}, u32[]{:S(2)}, u32[]{:S(2)}) %collective-permute-start.2) | collective-permute-done | bytes 524320 | tf_op jit(solution)/shard_map/ppermute | solution.py:20
  16.8 12.3 %collective-permute-done.4 = f32[128,1024]{1,0:T(8,128)S(1)} collective-permute-done((f32[128,1024]{1,0:T(8,128)}, f32[128,1024]{1,0:T(8,128)S(1)}, u32[]{:S(2)}, u32[]{:S(2)}) %collective-permute-start.4) | collective-permute-done | bytes 524320 | tf_op jit(solution)/shard_map/ppermute | solution.py:20
  30.0 1.8 %multiply_exponential_fusion.2 = f32[128,512]{0,1:T(8,128)S(1)} fusion(f32[128]{0:T(128)S(1)} %multiply_reduce_fusion.3, f32[512,1024]{1,0:T(8,128)S(1)} %constant_dynamic-update-slice_fusion, f32[128,1024]{1,0:T(8,128)S(1)} %collective-permute-done.2, f32[512]{0:T(512)S(1)} %multiply_reduce_fusion), kind=kOutput, calls=%fused_computation.41 | convolution fusion | flops 805699584 | bytes 2886144 | tf_op jit(solution)/shard_map/dot_general | solution.py:14
  32.4 1.8 %multiply_exponential_fusion.1 = f32[128,512]{0,1:T(8,128)S(1)} fusion(f32[128]{0:T(128)S(1)} %multiply_reduce_fusion.2, f32[512,1024]{1,0:T(8,128)S(1)} %constant_dynamic-update-slice_fusion, f32[128,1024]{1,0:T(8,128)S(1)} %collective-permute-done.4, f32[512]{0:T(512)S(1)} %multiply_reduce_fusion), kind=kOutput, calls=%fused_computation.40 | convolution fusion | flops 805699584 | bytes 2886144 | tf_op jit(solution)/shard_map/dot_general | solution.py:14
  38.1 1.8 %multiply_exponential_fusion.3 = f32[128,512]{0,1:T(8,128)S(1)} fusion(f32[512,1024]{1,0:T(8,128)S(1)} %constant_dynamic-update-slice_fusion, f32[128,1024]{1,0:T(8,128)S(1)} %copy-done.1, f32[512]{0:T(512)S(1)} %multiply_reduce_fusion, f32[128]{0:T(128)S(1)} %multiply_reduce_fusion.4), kind=kOutput, calls=%fused_computation.42 | convolution fusion | flops 805699584 | bytes 2886144 | tf_op jit(solution)/shard_map/dot_general | solution.py:14
  40.0 1.6 %collective-permute-start.15 = (f32[496,128]{1,0:T(8,128)S(1)}, f32[496,128]{1,0:T(8,128)S(1)}, u32[]{:S(2)}, u32[]{:S(2)}) collective-permute-start(f32[496,128]{1,0:T(8,128)S(1)} %fusion.25), channel_id=1, source_target_pairs={{0,8},{4,12},{8,0},{12,4},{16,24},{20,28},{24,16},{28,20},{1,9},{5... | collective-permute-start | bytes 761864 | tf_op jit(solution)/shard_map/ppermute | solution.py:20
  42.0 1.8 %multiply_exponential_fusion = f32[128,512]{0,1:T(8,128)S(1)} fusion(f32[128]{0:T(128)S(1)} %multiply_reduce_fusion.1, f32[512,1024]{1,0:T(8,128)S(1)} %constant_dynamic-update-slice_fusion, f32[128,1024]{1,0:T(8,128)S(1)} %collective-permute-done.6, f32[512]{0:T(512)S(1)} %multiply_reduce_fusion), kind=kOutput, calls=%fused_computation.39 | convolution fusion | flops 805699584 | bytes 2886144 | tf_op jit(solution)/shard_map/dot_general | solution.py:14
  44.5 1.6 %collective-permute-start.17 = (f32[496,128]{1,0:T(8,128)S(1)}, f32[496,128]{1,0:T(8,128)S(1)}, u32[]{:S(2)}, u32[]{:S(2)}) collective-permute-start(f32[496,128]{1,0:T(8,128)S(1)} %fusion.27), channel_id=1, source_target_pairs={{0,24},{4,28},{8,16},{12,20},{16,8},{20,12},{24,0},{28,4},{1,25},{... | collective-permute-start | bytes 761864 | tf_op jit(solution)/shard_map/ppermute | solution.py:20
  46.8 3.9 %collective-permute-done.15 = f32[496,128]{1,0:T(8,128)S(1)} collective-permute-done((f32[496,128]{1,0:T(8,128)S(1)}, f32[496,128]{1,0:T(8,128)S(1)}, u32[]{:S(2)}, u32[]{:S(2)}) %collective-permute-start.15) | collective-permute-done | bytes 253984 | tf_op jit(solution)/shard_map/ppermute | solution.py:20
  52.2 7.4 %collective-permute-done.16 = f32[496,128]{1,0:T(8,128)S(1)} collective-permute-done((f32[496,128]{1,0:T(8,128)S(1)}, f32[496,128]{1,0:T(8,128)S(1)}, u32[]{:S(2)}, u32[]{:S(2)}) %collective-permute-start.16) | collective-permute-done | bytes 253984 | tf_op jit(solution)/shard_map/ppermute | solution.py:20
  61.2 2.1 %collective-permute-start.19 = (f32[496,128]{1,0:T(8,128)S(1)}, f32[496,128]{1,0:T(8,128)S(1)}, u32[]{:S(2)}, u32[]{:S(2)}) collective-permute-start(f32[496,128]{1,0:T(8,128)S(1)} %fusion.15), channel_id=1, source_target_pairs={{0,16},{4,20},{8,24},{12,28},{16,0},{20,4},{24,8},{28,12},{1,17},{... | collective-permute-start | bytes 761864 | tf_op jit(solution)/shard_map/ppermute | solution.py:20
  65.4 2.0 %collective-permute-start.9 = (f32[504,128]{1,0:T(8,128)S(1)}, f32[504,128]{1,0:T(8,128)S(1)}, u32[]{:S(2)}, u32[]{:S(2)}) collective-permute-start(f32[504,128]{1,0:T(8,128)S(1)} %fusion.11), channel_id=1, source_target_pairs={{0,16},{4,20},{8,24},{12,28},{16,0},{20,4},{24,8},{28,12},{1,17},{... | collective-permute-start | bytes 774152 | tf_op jit(solution)/shard_map/ppermute | solution.py:20
  67.4 1.9 %collective-permute-done.18 = f32[496,128]{1,0:T(8,128)S(1)} collective-permute-done((f32[496,128]{1,0:T(8,128)S(1)}, f32[496,128]{1,0:T(8,128)S(1)}, u32[]{:S(2)}, u32[]{:S(2)}) %collective-permute-start.18) | collective-permute-done | bytes 253984 | tf_op jit(solution)/shard_map/ppermute | solution.py:20
  69.4 2.4 %collective-permute-start.10 = (f32[504,128]{1,0:T(8,128)S(1)}, f32[504,128]{1,0:T(8,128)S(1)}, u32[]{:S(2)}, u32[]{:S(2)}) collective-permute-start(f32[504,128]{1,0:T(8,128)S(1)} %fusion.11), channel_id=1, source_target_pairs={{0,24},{4,28},{8,16},{12,20},{16,8},{20,12},{24,0},{28,4},{1,25},{... | collective-permute-start | bytes 774152 | tf_op jit(solution)/shard_map/ppermute | solution.py:20
  72.4 3.1 %collective-permute-done.19 = f32[496,128]{1,0:T(8,128)S(1)} collective-permute-done((f32[496,128]{1,0:T(8,128)S(1)}, f32[496,128]{1,0:T(8,128)S(1)}, u32[]{:S(2)}, u32[]{:S(2)}) %collective-permute-start.19) | collective-permute-done | bytes 253984 | tf_op jit(solution)/shard_map/ppermute | solution.py:20
  77.4 1.9 %collective-permute-done.8 = f32[504,128]{1,0:T(8,128)S(1)} collective-permute-done((f32[504,128]{1,0:T(8,128)S(1)}, f32[504,128]{1,0:T(8,128)S(1)}, u32[]{:S(2)}, u32[]{:S(2)}) %collective-permute-start.8) | collective-permute-done | bytes 258080 | tf_op jit(solution)/shard_map/ppermute | solution.py:20
  79.8 3.2 %collective-permute-done.9 = f32[504,128]{1,0:T(8,128)S(1)} collective-permute-done((f32[504,128]{1,0:T(8,128)S(1)}, f32[504,128]{1,0:T(8,128)S(1)}, u32[]{:S(2)}, u32[]{:S(2)}) %collective-permute-start.9) | collective-permute-done | bytes 258080 | tf_op jit(solution)/shard_map/ppermute | solution.py:20
  85.1 3.5 %collective-permute-start.22 = (f32[496,256]{1,0:T(8,128)S(1)}, f32[496,256]{1,0:T(8,128)S(1)}, u32[]{:S(2)}, u32[]{:S(2)}) collective-permute-start(f32[496,256]{1,0:T(8,128)S(1)} %fusion.18), channel_id=1, source_target_pairs={{0,1},{3,2},{4,5},{7,6},{8,9},{11,10},{12,13},{15,14},{16,17},{19,... | collective-permute-start | bytes 1523720 | tf_op jit(solution)/shard_map/ppermute | solution.py:26
  88.7 1.8 %collective-permute-start.12 = (f32[504,256]{1,0:T(8,128)S(1)}, f32[504,256]{1,0:T(8,128)S(1)}, u32[]{:S(2)}, u32[]{:S(2)}) collective-permute-start(f32[504,256]{1,0:T(8,128)S(1)} %fusion.17), channel_id=1, source_target_pairs={{0,1},{3,2},{4,5},{7,6},{8,9},{11,10},{12,13},{15,14},{16,17},{19,... | collective-permute-start | bytes 1548296 | tf_op jit(solution)/shard_map/ppermute | solution.py:26
  90.5 10.0 %collective-permute-done.22 = f32[496,256]{1,0:T(8,128)S(1)} collective-permute-done((f32[496,256]{1,0:T(8,128)S(1)}, f32[496,256]{1,0:T(8,128)S(1)}, u32[]{:S(2)}, u32[]{:S(2)}) %collective-permute-start.22) | collective-permute-done | bytes 507936 | tf_op jit(solution)/shard_map/ppermute | solution.py:26
  101.2 9.9 %collective-permute-done.12 = f32[504,256]{1,0:T(8,128)S(1)} collective-permute-done((f32[504,256]{1,0:T(8,128)S(1)}, f32[504,256]{1,0:T(8,128)S(1)}, u32[]{:S(2)}, u32[]{:S(2)}) %collective-permute-start.12) | collective-permute-done | bytes 516128 | tf_op jit(solution)/shard_map/ppermute | solution.py:26
  115.5 14.2 %collective-permute-done.24 = f32[496,256]{1,0:T(8,128)S(1)} collective-permute-done((f32[496,256]{1,0:T(8,128)S(1)}, f32[496,256]{1,0:T(8,128)S(1)}, u32[]{:S(2)}, u32[]{:S(2)}) %collective-permute-start.24) | collective-permute-done | bytes 507936 | tf_op jit(solution)/shard_map/ppermute | solution.py:28
  129.7 11.2 %collective-permute-done.14 = f32[504,256]{1,0:T(8,128)S(1)} collective-permute-done((f32[504,256]{1,0:T(8,128)S(1)}, f32[504,256]{1,0:T(8,128)S(1)}, u32[]{:S(2)}, u32[]{:S(2)}) %collective-permute-start.14) | collective-permute-done | bytes 516128 | tf_op jit(solution)/shard_map/ppermute | solution.py:28
  (75 shorter events, 28.4 us)
Async XLA Ops:
  0.6 28.8 %collective-permute-start = (f32[1000,256]{1,0:T(8,128)}, f32[1000,256]{1,0:T(8,128)S(1)}, u32[]{:S(2)}, u32[]{:S(2)}) collective-permute-start(f32[1000,256]{1,0:T(8,128)} %bitcast.63), channel_id=1, source_target_pairs={{0,4},{4,0},{8,12},{12,8},{16,20},{20,16},{24,28},{28,24},{1,5},{5... | collective-permute-start | bytes 3072008 | tf_op jit(solution)/shard_map/ppermute | solution.py:20
  1.2 15.6 %collective-permute-start.2 = (f32[128,1024]{1,0:T(8,128)}, f32[128,1024]{1,0:T(8,128)S(1)}, u32[]{:S(2)}, u32[]{:S(2)}) collective-permute-start(f32[128,1024]{1,0:T(8,128)} %param.5), channel_id=1, source_target_pairs={{0,8},{4,12},{8,0},{12,4},{16,24},{20,28},{24,16},{28,20},{1,9},{5... | collective-permute-start | bytes 1572872 | tf_op jit(solution)/shard_map/ppermute | solution.py:20
  3.7 25.4 %collective-permute-start.4 = (f32[128,1024]{1,0:T(8,128)}, f32[128,1024]{1,0:T(8,128)S(1)}, u32[]{:S(2)}, u32[]{:S(2)}) collective-permute-start(f32[128,1024]{1,0:T(8,128)} %param.5), channel_id=1, source_target_pairs={{0,16},{4,20},{8,24},{12,28},{16,0},{20,4},{24,8},{28,12},{1,17},{... | collective-permute-start | bytes 1572872 | tf_op jit(solution)/shard_map/ppermute | solution.py:20
  5.2 24.5 %collective-permute-start.1 = (f32[256,1024]{1,0:T(8,128)}, f32[256,1024]{1,0:T(8,128)S(1)}, u32[]{:S(2)}, u32[]{:S(2)}) collective-permute-start(f32[256,1024]{1,0:T(8,128)} %param.8), channel_id=1, source_target_pairs={{0,4},{4,0},{8,12},{12,8},{16,20},{20,16},{24,28},{28,24},{1,5},{5... | collective-permute-start | bytes 3145736 | tf_op jit(solution)/shard_map/ppermute | solution.py:20
  5.2 24.0 %collective-permute-start.6 = (f32[128,1024]{1,0:T(8,128)}, f32[128,1024]{1,0:T(8,128)S(1)}, u32[]{:S(2)}, u32[]{:S(2)}) collective-permute-start(f32[128,1024]{1,0:T(8,128)} %param.5), channel_id=1, source_target_pairs={{0,24},{4,28},{8,16},{12,20},{16,8},{20,12},{24,0},{28,4},{1,25},{... | collective-permute-start | bytes 1572872 | tf_op jit(solution)/shard_map/ppermute | solution.py:20
  36.0 27.3 %collective-permute-start.3 = (f32[504,128]{1,0:T(8,128)S(1)}, f32[504,128]{1,0:T(8,128)S(1)}, u32[]{:S(2)}, u32[]{:S(2)}) collective-permute-start(f32[504,128]{1,0:T(8,128)S(1)} %fusion.19), channel_id=1, source_target_pairs={{0,8},{4,12},{8,0},{12,4},{16,24},{20,28},{24,16},{28,20},{1,9},{5... | collective-permute-start | bytes 774152 | tf_op jit(solution)/shard_map/ppermute | solution.py:20
  37.2 26.6 %collective-permute-start.5 = (f32[504,128]{1,0:T(8,128)S(1)}, f32[504,128]{1,0:T(8,128)S(1)}, u32[]{:S(2)}, u32[]{:S(2)}) collective-permute-start(f32[504,128]{1,0:T(8,128)S(1)} %fusion.20), channel_id=1, source_target_pairs={{0,16},{4,20},{8,24},{12,28},{16,0},{20,4},{24,8},{28,12},{1,17},{... | collective-permute-start | bytes 774152 | tf_op jit(solution)/shard_map/ppermute | solution.py:20
  40.0 10.7 %collective-permute-start.15 = (f32[496,128]{1,0:T(8,128)S(1)}, f32[496,128]{1,0:T(8,128)S(1)}, u32[]{:S(2)}, u32[]{:S(2)}) collective-permute-start(f32[496,128]{1,0:T(8,128)S(1)} %fusion.25), channel_id=1, source_target_pairs={{0,8},{4,12},{8,0},{12,4},{16,24},{20,28},{24,16},{28,20},{1,9},{5... | collective-permute-start | bytes 761864 | tf_op jit(solution)/shard_map/ppermute | solution.py:20
  41.5 18.1 %collective-permute-start.16 = (f32[496,128]{1,0:T(8,128)S(1)}, f32[496,128]{1,0:T(8,128)S(1)}, u32[]{:S(2)}, u32[]{:S(2)}) collective-permute-start(f32[496,128]{1,0:T(8,128)S(1)} %fusion.26), channel_id=1, source_target_pairs={{0,16},{4,20},{8,24},{12,28},{16,0},{20,4},{24,8},{28,12},{1,17},{... | collective-permute-start | bytes 761864 | tf_op jit(solution)/shard_map/ppermute | solution.py:20
  44.5 15.1 %collective-permute-start.17 = (f32[496,128]{1,0:T(8,128)S(1)}, f32[496,128]{1,0:T(8,128)S(1)}, u32[]{:S(2)}, u32[]{:S(2)}) collective-permute-start(f32[496,128]{1,0:T(8,128)S(1)} %fusion.27), channel_id=1, source_target_pairs={{0,24},{4,28},{8,16},{12,20},{16,8},{20,12},{24,0},{28,4},{1,25},{... | collective-permute-start | bytes 761864 | tf_op jit(solution)/shard_map/ppermute | solution.py:20
  50.7 13.1 %collective-permute-start.7 = (f32[504,128]{1,0:T(8,128)S(1)}, f32[504,128]{1,0:T(8,128)S(1)}, u32[]{:S(2)}, u32[]{:S(2)}) collective-permute-start(f32[504,128]{1,0:T(8,128)S(1)} %fusion.21), channel_id=1, source_target_pairs={{0,24},{4,28},{8,16},{12,20},{16,8},{20,12},{24,0},{28,4},{1,25},{... | collective-permute-start | bytes 774152 | tf_op jit(solution)/shard_map/ppermute | solution.py:20
  60.3 9.1 %collective-permute-start.18 = (f32[496,128]{1,0:T(8,128)S(1)}, f32[496,128]{1,0:T(8,128)S(1)}, u32[]{:S(2)}, u32[]{:S(2)}) collective-permute-start(f32[496,128]{1,0:T(8,128)S(1)} %fusion.15), channel_id=1, source_target_pairs={{0,8},{4,12},{8,0},{12,4},{16,24},{20,28},{24,16},{28,20},{1,9},{5... | collective-permute-start | bytes 761864 | tf_op jit(solution)/shard_map/ppermute | solution.py:20
  61.2 14.3 %collective-permute-start.19 = (f32[496,128]{1,0:T(8,128)S(1)}, f32[496,128]{1,0:T(8,128)S(1)}, u32[]{:S(2)}, u32[]{:S(2)}) collective-permute-start(f32[496,128]{1,0:T(8,128)S(1)} %fusion.15), channel_id=1, source_target_pairs={{0,16},{4,20},{8,24},{12,28},{16,0},{20,4},{24,8},{28,12},{1,17},{... | collective-permute-start | bytes 761864 | tf_op jit(solution)/shard_map/ppermute | solution.py:20
  63.3 12.8 %collective-permute-start.20 = (f32[496,128]{1,0:T(8,128)S(1)}, f32[496,128]{1,0:T(8,128)S(1)}, u32[]{:S(2)}, u32[]{:S(2)}) collective-permute-start(f32[496,128]{1,0:T(8,128)S(1)} %fusion.15), channel_id=1, source_target_pairs={{0,24},{4,28},{8,16},{12,20},{16,8},{20,12},{24,0},{28,4},{1,25},{... | collective-permute-start | bytes 761864 | tf_op jit(solution)/shard_map/ppermute | solution.py:20
  64.4 14.8 %collective-permute-start.8 = (f32[504,128]{1,0:T(8,128)S(1)}, f32[504,128]{1,0:T(8,128)S(1)}, u32[]{:S(2)}, u32[]{:S(2)}) collective-permute-start(f32[504,128]{1,0:T(8,128)S(1)} %fusion.11), channel_id=1, source_target_pairs={{0,8},{4,12},{8,0},{12,4},{16,24},{20,28},{24,16},{28,20},{1,9},{5... | collective-permute-start | bytes 774152 | tf_op jit(solution)/shard_map/ppermute | solution.py:20
  65.4 17.6 %collective-permute-start.9 = (f32[504,128]{1,0:T(8,128)S(1)}, f32[504,128]{1,0:T(8,128)S(1)}, u32[]{:S(2)}, u32[]{:S(2)}) collective-permute-start(f32[504,128]{1,0:T(8,128)S(1)} %fusion.11), channel_id=1, source_target_pairs={{0,16},{4,20},{8,24},{12,28},{16,0},{20,4},{24,8},{28,12},{1,17},{... | collective-permute-start | bytes 774152 | tf_op jit(solution)/shard_map/ppermute | solution.py:20
  69.4 14.3 %collective-permute-start.10 = (f32[504,128]{1,0:T(8,128)S(1)}, f32[504,128]{1,0:T(8,128)S(1)}, u32[]{:S(2)}, u32[]{:S(2)}) collective-permute-start(f32[504,128]{1,0:T(8,128)S(1)} %fusion.11), channel_id=1, source_target_pairs={{0,24},{4,28},{8,16},{12,20},{16,8},{20,12},{24,0},{28,4},{1,25},{... | collective-permute-start | bytes 774152 | tf_op jit(solution)/shard_map/ppermute | solution.py:20
  77.3 7.7 %collective-permute-start.21 = (f32[496,256]{1,0:T(8,128)S(1)}, f32[496,256]{1,0:T(8,128)S(1)}, u32[]{:S(2)}, u32[]{:S(2)}) collective-permute-start(f32[496,256]{1,0:T(8,128)S(1)} %slice.49), channel_id=1, source_target_pairs={{0,4},{4,0},{8,12},{12,8},{16,20},{20,16},{24,28},{28,24},{1,5},{5... | collective-permute-start | bytes 1523720 | tf_op jit(solution)/shard_map/ppermute | solution.py:20
  84.9 3.7 %collective-permute-start.11 = (f32[504,256]{1,0:T(8,128)S(1)}, f32[504,256]{1,0:T(8,128)S(1)}, u32[]{:S(2)}, u32[]{:S(2)}) collective-permute-start(f32[504,256]{1,0:T(8,128)S(1)} %slice.45), channel_id=1, source_target_pairs={{0,4},{4,0},{8,12},{12,8},{16,20},{20,16},{24,28},{28,24},{1,5},{5... | collective-permute-start | bytes 1548296 | tf_op jit(solution)/shard_map/ppermute | solution.py:20
  85.1 15.4 %collective-permute-start.22 = (f32[496,256]{1,0:T(8,128)S(1)}, f32[496,256]{1,0:T(8,128)S(1)}, u32[]{:S(2)}, u32[]{:S(2)}) collective-permute-start(f32[496,256]{1,0:T(8,128)S(1)} %fusion.18), channel_id=1, source_target_pairs={{0,1},{3,2},{4,5},{7,6},{8,9},{11,10},{12,13},{15,14},{16,17},{19,... | collective-permute-start | bytes 1523720 | tf_op jit(solution)/shard_map/ppermute | solution.py:26
  88.7 22.4 %collective-permute-start.12 = (f32[504,256]{1,0:T(8,128)S(1)}, f32[504,256]{1,0:T(8,128)S(1)}, u32[]{:S(2)}, u32[]{:S(2)}) collective-permute-start(f32[504,256]{1,0:T(8,128)S(1)} %fusion.17), channel_id=1, source_target_pairs={{0,1},{3,2},{4,5},{7,6},{8,9},{11,10},{12,13},{15,14},{16,17},{19,... | collective-permute-start | bytes 1548296 | tf_op jit(solution)/shard_map/ppermute | solution.py:26
  100.5 11.4 %collective-permute-start.23 = (f32[496,256]{1,0:T(8,128)S(1)}, f32[496,256]{1,0:T(8,128)S(1)}, u32[]{:S(2)}, u32[]{:S(2)}) collective-permute-start(f32[496,256]{1,0:T(8,128)S(1)} %add.149), channel_id=1, source_target_pairs={{1,2},{2,1},{5,6},{6,5},{9,10},{10,9},{13,14},{14,13},{17,18},{18,... | collective-permute-start | bytes 1523720 | tf_op jit(solution)/shard_map/ppermute | solution.py:27
  112.0 17.7 %collective-permute-start.24 = (f32[496,256]{1,0:T(8,128)S(1)}, f32[496,256]{1,0:T(8,128)S(1)}, u32[]{:S(2)}, u32[]{:S(2)}) collective-permute-start(f32[496,256]{1,0:T(8,128)S(1)} %add.150), channel_id=1, source_target_pairs={{1,0},{2,3},{5,4},{6,7},{9,8},{10,11},{13,12},{14,15},{17,16},{18,... | collective-permute-start | bytes 1523720 | tf_op jit(solution)/shard_map/ppermute | solution.py:28
  113.4 27.6 %collective-permute-start.14 = (f32[504,256]{1,0:T(8,128)S(1)}, f32[504,256]{1,0:T(8,128)S(1)}, u32[]{:S(2)}, u32[]{:S(2)}) collective-permute-start(f32[504,256]{1,0:T(8,128)S(1)} %add.140), channel_id=1, source_target_pairs={{1,0},{2,3},{5,4},{6,7},{9,8},{10,11},{13,12},{14,15},{17,16},{18,... | collective-permute-start | bytes 1548296 | tf_op jit(solution)/shard_map/ppermute | solution.py:28
  (5 other events, 66.3 us)

commit v2 on v1

v2 whole, which is shorter than its diff:
```python
import math

import jax
import jax.numpy as jnp
from jax import lax
from jax.sharding import Mesh, PartitionSpec as P

HIGHEST = lax.Precision.HIGHEST
HIGH = lax.Precision.HIGH
PIECES = 2


def dot(a, b, dims, precision):
    return lax.dot_general(
        a, b, (dims, ((), ())), precision=precision, preferred_element_type=jnp.float32
    )


def swap_core(value):
    return lax.ppermute(value, "core", [(0, 1), (1, 0)])


def sum_col(value, depth):
    if depth != 4:
        return lax.psum(value, "col")
    inner = value + lax.ppermute(value, "col", [(0, 1), (3, 2)])
    total = inner + lax.ppermute(inner, "col", [(1, 2), (2, 1)])
    back = lax.ppermute(total, "col", [(1, 0), (2, 3)])
    place = lax.axis_index("col")
    return jnp.where((place == 0) | (place == 3), back, total)


def cuts(size, pieces):
    step = -(-size // pieces // 8) * 8
    edges = list(range(0, size, step)) + [size]
    return list(zip(edges[:-1], edges[1:]))


def per_device(batch, running, targets, centers, weights):
    rows_here, feature_count = batch.shape
    chips = lax.axis_size("chip")
    depth = lax.axis_size("col")
    length_scale = math.sqrt(feature_count) / 4.0
    factor = 1.0 / math.sqrt(rows_here * chips * 2 * depth)

    rows = lax.all_gather(batch, "chip", axis=0, tiled=True)
    cent = jnp.concatenate([centers, swap_core(centers)], axis=0)
    weights_t = weights.T
    weight = jnp.concatenate([weights_t, swap_core(weights_t)], axis=1)
    cent_sq = jnp.sum(cent * cent, axis=1)

    crossed = dot(rows, cent, ((1,), (1,)), HIGHEST)
    row_sq = jnp.sum(rows * rows, axis=1, keepdims=True)
    dist_sq = row_sq + cent_sq[None, :] - 2.0 * crossed
    kernel = jnp.exp(-jnp.sqrt(dist_sq + 1.0) / length_scale)

    running_t, targets_t = running.T, targets.T
    residuals, gradients = [], []
    for low, high in cuts(weights.shape[1], PIECES):
        shares = dot(weight[low:high], kernel, ((1,), (1,)), HIGH)
        shares = shares.reshape(high - low, chips, rows_here).transpose(1, 0, 2)
        predicted = running_t[low:high] + lax.psum_scatter(
            shares, "chip", scatter_dimension=0, tiled=False
        )
        residual = predicted - targets_t[low:high]
        residuals.append(residual)
        moved = lax.all_gather(residual, "chip", axis=0, tiled=False)
        moved = moved.transpose(1, 0, 2).reshape(high - low, chips * rows_here)
        gradient = dot(moved, kernel, ((1,), (0,)), HIGH)
        half = centers.shape[0]
        owned = gradient[:, :half] + swap_core(gradient[:, half:])
        gradients.append(sum_col(owned * factor, depth))
    return (
        jnp.concatenate(gradients, axis=0).T,
        jnp.concatenate(residuals, axis=0).T,
    )


def solution(mesh):
    owners, depth = mesh.shape["row"], mesh.shape["col"]
    split = Mesh(mesh.devices.reshape(owners // 2, 2, depth), ("chip", "core", "col"))
    everywhere = P(("chip", "core", "col"), None)
    owned = P(("chip", "core"), None)
    return jax.shard_map(
        per_device,
        mesh=split,
        in_specs=(everywhere, everywhere, everywhere, owned, owned),
        out_specs=(owned, everywhere),
        check_vma=False,
    )
```

time: 142 us -> 199 us (1.40)
  blocking collectives: 0 us -> 31.2 us
  waiting for transfers between devices: 87.9 us -> 116 us
  starting transfers between devices: 30.4 us -> 9.63 us
  between operations: 1.06 us -> 14.1 us
  local copies, waits for them, and re-layouts: 1.5 us -> 6.67 us
  matrix products: 16.8 us -> 11.8 us
  other arithmetic: 4.43 us -> 8.89 us
    ppermute x19 -> x4, waiting for transfers between devices: 42.6 us -> 1.84 us  [swap_core(): return lax.ppermute(value, 'core', [(0, 1), (1, 0)])]
    all_gather x0 -> x1, waiting for transfers between devices: none -> 35.9 us  [per_device(): rows = lax.all_gather(batch, 'chip', axis=0, tiled=True)]
    unnamed x0 -> x5, waiting for transfers between devices: none -> 34.2 us
    all_gather x0 -> x2, blocking collectives: none -> 31.2 us  [per_device(): moved = lax.all_gather(residual, 'chip', axis=0, tiled=False)]
    ppermute x19 -> x4, starting transfers between devices: 21.1 us -> 0.67 us  [swap_core(): return lax.ppermute(value, 'core', [(0, 1), (1, 0)])]
    dot_general x20 -> x5, matrix products: 16.8 us -> 11.8 us  [dot(): lax.dot_general(a, b, (dims, ((), ())), precision=precision, preferred_el...]
    sub x0 -> x2, other arithmetic: none -> 2.21 us  [per_device(): residual = predicted - targets_t[low:high]]
    reshape x0 -> x2, local copies, waits for them, and re-layouts: none -> 2.06 us  [per_device(): shares = shares.reshape(high - low, chips, rows_here).transpose(1, 0, 2)]
  transfers between devices with their start and end apart: 25 -> 13, of which waited for: 12 -> 8; matrix products, arithmetic and copies ran while one was open for 11% -> 11% of each run, Pallas kernels for 0% -> 0%
where the time goes in v2:
time: 199 us
  waiting for transfers between devices  116 us (58%)
  blocking collectives  31.2 us (16%)
  between operations  14.1 us (7%)
  matrix products  11.8 us (6%)
  starting transfers between devices  9.63 us (5%)
  other arithmetic  8.89 us (4%)
  local copies, waits for them, and re-layouts  6.67 us (3%)
    all_gather x1, waiting for transfers between devices, per_device(): rows = lax.all_gather(batch, 'chip', axis=0, tiled=True)  35.9 us
    unnamed x5, waiting for transfers between devices  34.2 us
    all_gather x2, blocking collectives, per_device(): moved = lax.all_gather(residual, 'chip', axis=0, tiled=False)  31.2 us
    ppermute x2, waiting for transfers between devices, sum_col(): back = lax.ppermute(total, 'col', [(1, 0), (2, 3)])  24.4 us
    ppermute x2, waiting for transfers between devices, sum_col(): inner = value + lax.ppermute(value, 'col', [(0, 1), (3, 2)])  20.1 us
    dot_general x5, matrix products, dot(): lax.dot_general(a, b, (dims, ((), ())), precision=precision, preferred_el...  11.8 us
    ppermute x2, starting transfers between devices, sum_col(): inner = value + lax.ppermute(value, 'col', [(0, 1), (3, 2)])  4.74 us
  transfers between devices with their start and end apart: 13, of which 8 were waited for; matrix products, arithmetic and copies ran while one was open for 11% of the time, Pallas kernels for 0%

profile of v2, /device:TPU:0, one launch (start us, length us, event | category | flops | bytes accessed | tf_op | source)
XLA Modules:
  0.0 198.7 jit_solution(14281096822619176917)
XLA Ops:
  8.5 1.3 constant_dynamic-update-slice_fusion.1
  9.8 1.8 collective-permute-done.1
  12.0 35.9 %all-gather.4.cloned.1.call-done = f32[512,1024]{1,0:T(8,128)} async-done(((f32[128,1024]{1,0:T(8,128)}), f32[512,1024]{1,0:T(8,128)}) %all-gather.4.cloned.1.call-update) | async-done | bytes 2097168 | tf_op jit(solution)/shard_map/all_gather | solution.py:46
  47.9 2.0 multiply_reduce_fusion.1
  50.1 3.9 %multiply_exponential_fusion = f32[512,512]{0,1:T(8,128)S(1)} fusion(f32[512,1024]{1,0:T(8,128)S(1)} %constant_dynamic-update-slice_fusion, f32[512,1024]{1,0:T(8,128)S(1)} %copy-done, f32[512]{0:T(512)S(1)} %multiply_reduce_fusion, f32[512]{0:T(512)S(1)} %multiply_reduce_fusion.1), kind=kOutput, calls=%fused_computation.8 | convolution fusion | flops 3222798336 | bytes 5246976 | tf_op jit(solution)/shard_map/dot_general | solution.py:14
  54.1 2.0 %convolution_bitcast_fusion.1 = f32[62,4,8,128]{3,2,1,0:T(8,128)S(1)} fusion(f32[512,512]{0,1:T(8,128)S(1)} %multiply_exponential_fusion, f32[1000,256]{1,0:T(8,128)} %collective-permute-done, f32[1000,256]{1,0:T(8,128)S(1)} %bitcast.53), kind=kOutput, calls=%fused_computation.7 | convolution fusion | flops 780394496 | bytes 4112384 | tf_op jit(solution)/shard_map/dot_general | solution.py:14
  57.7 2.0 %convolution_bitcast_fusion = f32[63,4,8,128]{3,2,1,0:T(8,128)S(1)} fusion(f32[512,512]{0,1:T(8,128)S(1)} %multiply_exponential_fusion, f32[1000,256]{1,0:T(8,128)S(1)} %bitcast.54, f32[1000,256]{1,0:T(8,128)} %collective-permute-done), kind=kOutput, calls=%fused_computation.6 | convolution fusion | flops 792981504 | bytes 4128768 | tf_op jit(solution)/shard_map/dot_general | solution.py:14
  60.8 24.0 %reduce-scatter.9.cloned.1.call-done = f32[1,496,128]{2,1,0:T(8,128)} async-done(((f32[4,496,128]{2,1,0:T(8,128)}), f32[1,496,128]{2,1,0:T(8,128)}) %reduce-scatter.9.cloned.1.call-update) | async-done | bytes 253968
  84.9 1.2 slice_subtract_fusion.1
  86.1 17.6 %all-gather.1 = f32[1984,128]{1,0:T(8,128)S(1)} all-gather(f32[496,128]{1,0:T(8,128)S(1)} %slice_subtract_fusion.1), channel_id=3, replica_groups=mesh['chip'=4,'core'=2,'col'=4] {'chip'}, dimensions={0}, use_global_device_ids=true | all-gather | bytes 1269760 | tf_op jit(solution)/shard_map/all_gather | solution.py:67
  104.1 1.9 fusion.9
  107.7 9.5 %reduce-scatter.7.cloned.1.call-done = f32[1,504,128]{2,1,0:T(8,128)} async-done(((f32[4,504,128]{2,1,0:T(8,128)}), f32[1,504,128]{2,1,0:T(8,128)}) %reduce-scatter.7.cloned.1.call-update) | async-done | bytes 258064
  118.2 13.6 %all-gather = f32[2016,128]{1,0:T(8,128)S(1)} all-gather(f32[504,128]{1,0:T(8,128)S(1)} %slice_subtract_fusion), channel_id=2, replica_groups=mesh['chip'=4,'core'=2,'col'=4] {'chip'}, dimensions={0}, use_global_device_ids=true | all-gather | bytes 1290240 | tf_op jit(solution)/shard_map/all_gather | solution.py:67
  132.1 1.9 fusion.8
  134.2 1.1 fusion.5
  135.3 3.4 %collective-permute-start.7 = (f32[496,256]{1,0:T(8,128)S(1)}, f32[496,256]{1,0:T(8,128)S(1)}, u32[]{:S(2)}, u32[]{:S(2)}) collective-permute-start(f32[496,256]{1,0:T(8,128)S(1)} %fusion.5), channel_id=1, source_target_pairs={{0,1},{3,2},{4,5},{7,6},{8,9},{11,10},{12,13},{15,14},{16,17},{19,... | collective-permute-start | bytes 1523720 | tf_op jit(solution)/shard_map/ppermute | solution.py:26
  138.9 1.3 collective-permute-start.3
  140.2 10.4 %collective-permute-done.7 = f32[496,256]{1,0:T(8,128)S(1)} collective-permute-done((f32[496,256]{1,0:T(8,128)S(1)}, f32[496,256]{1,0:T(8,128)S(1)}, u32[]{:S(2)}, u32[]{:S(2)}) %collective-permute-start.7) | collective-permute-done | bytes 507936 | tf_op jit(solution)/shard_map/ppermute | solution.py:26
  151.5 9.7 %collective-permute-done.3 = f32[504,256]{1,0:T(8,128)S(1)} collective-permute-done((f32[504,256]{1,0:T(8,128)S(1)}, f32[504,256]{1,0:T(8,128)S(1)}, u32[]{:S(2)}, u32[]{:S(2)}) %collective-permute-start.3) | collective-permute-done | bytes 516128 | tf_op jit(solution)/shard_map/ppermute | solution.py:26
  162.1 1.3 collective-permute-start.9
  163.5 1.3 collective-permute-start.5
  165.6 14.2 %collective-permute-done.9 = f32[496,256]{1,0:T(8,128)} collective-permute-done((f32[496,256]{1,0:T(8,128)S(1)}, f32[496,256]{1,0:T(8,128)}, u32[]{:S(2)}, u32[]{:S(2)}) %collective-permute-start.9) | collective-permute-done | bytes 507936 | tf_op jit(solution)/shard_map/ppermute | solution.py:28
  179.8 1.1 broadcast_select_fusion.1
  180.9 10.2 %collective-permute-done.5 = f32[504,256]{1,0:T(8,128)S(1)} collective-permute-done((f32[504,256]{1,0:T(8,128)S(1)}, f32[504,256]{1,0:T(8,128)S(1)}, u32[]{:S(2)}, u32[]{:S(2)}) %collective-permute-start.5) | collective-permute-done | bytes 516128 | tf_op jit(solution)/shard_map/ppermute | solution.py:28
  (52 shorter events, 11.9 us)
Async XLA Ops:
  7.2 40.7 %all-gather.4.cloned.1.call-start = ((), (), s32[]{:S(2)}) async-start(), calls=%async_computation.2 | async-start | bytes 2621440 | tf_op jit(solution)/shard_map/all_gather | solution.py:46
  7.9 77.0 %reduce-scatter.9.cloned.1.call-start = ((), (), s32[]{:S(2)}) async-start(), calls=%async_computation.4 | async-start | bytes 1269760
  7.9 3.7 %collective-permute-start.1 = (f32[256,1024]{1,0:T(8,128)}, f32[256,1024]{1,0:T(8,128)S(1)}, u32[]{:S(2)}, u32[]{:S(2)}) collective-permute-start(f32[256,1024]{1,0:T(8,128)} %param.8), channel_id=1, source_target_pairs={{0,4},{4,0},{1,5},{5,1},{2,6},{6,2},{3,7},{7,3},{8,12},{12,8},{9,1... | collective-permute-start | bytes 3145736 | tf_op jit(solution)/shard_map/ppermute | solution.py:20
  8.5 45.6 %collective-permute-start = (f32[1000,256]{1,0:T(8,128)}, f32[1000,256]{1,0:T(8,128)}, u32[]{:S(2)}, u32[]{:S(2)}) collective-permute-start(f32[1000,256]{1,0:T(8,128)} %bitcast.52), channel_id=1, source_target_pairs={{0,4},{4,0},{1,5},{5,1},{2,6},{6,2},{3,7},{7,3},{8,12},{12,8},{9,1... | collective-permute-start | bytes 3072008 | tf_op jit(solution)/shard_map/ppermute | solution.py:20
  47.9 2.2 %copy-start = (f32[512,1024]{1,0:T(8,128)S(1)}, f32[512,1024]{1,0:T(8,128)}, u32[]{:S(2)}) copy-start(f32[512,1024]{1,0:T(8,128)} %all-gather.4.cloned.1.call-done) | copy-start | bytes 6291460
  50.1 4.0 %copy-start.1 = (f32[256,1000]{0,1:T(8,128)S(1)}, f32[256,1000]{0,1:T(8,128)}, u32[]{:S(2)}) copy-start(f32[256,1000]{0,1:T(8,128)} %param.9) | copy-start | bytes 3072004
  56.1 1.6 copy-start.2
  57.2 60.0 %reduce-scatter.7.cloned.1.call-start = ((), (), s32[]{:S(2)}) async-start(), calls=%async_computation.3 | async-start | bytes 1290240
  86.1 17.6 %copy-start.5 = (f32[496,128]{1,0:T(8,128)}, f32[496,128]{1,0:T(8,128)S(1)}, u32[]{:S(2)}) copy-start(f32[496,128]{1,0:T(8,128)S(1)} %slice_subtract_fusion.1) | copy-start | bytes 761860
  104.0 13.2 %copy-start.7 = (f32[128,1000]{0,1:T(8,128)S(1)}, f32[128,1000]{0,1:T(8,128)}, u32[]{:S(2)}) copy-start(f32[128,1000]{0,1:T(8,128)} %param.7) | copy-start | bytes 1536004
  104.0 13.2 %copy-start.8 = (f32[128,1000]{0,1:T(8,128)S(1)}, f32[128,1000]{0,1:T(8,128)}, u32[]{:S(2)}) copy-start(f32[128,1000]{0,1:T(8,128)} %param.6) | copy-start | bytes 1536004
  106.0 1.0 copy-start.3
  107.7 26.5 %collective-permute-start.6 = (f32[496,256]{1,0:T(8,128)}, f32[496,256]{1,0:T(8,128)}, u32[]{:S(2)}, u32[]{:S(2)}) collective-permute-start(f32[496,256]{1,0:T(8,128)} %slice.49), channel_id=1, source_target_pairs={{0,4},{4,0},{1,5},{5,1},{2,6},{6,2},{3,7},{7,3},{8,12},{12,8},{9,1... | collective-permute-start | bytes 1523720 | tf_op jit(solution)/shard_map/ppermute | solution.py:20
  132.1 2.1 %copy-start.4 = (f32[496,512]{1,0:T(8,128)S(1)}, f32[496,512]{1,0:T(8,128)}, u32[]{:S(2)}) copy-start(f32[496,512]{1,0:T(8,128)} %copy-done.3) | copy-start | bytes 3047428
  134.1 4.7 %collective-permute-start.2 = (f32[504,256]{1,0:T(8,128)S(1)}, f32[504,256]{1,0:T(8,128)S(1)}, u32[]{:S(2)}, u32[]{:S(2)}) collective-permute-start(f32[504,256]{1,0:T(8,128)S(1)} %slice.45), channel_id=1, source_target_pairs={{0,4},{4,0},{1,5},{5,1},{2,6},{6,2},{3,7},{7,3},{8,12},{12,8},{9,1... | collective-permute-start | bytes 1548296 | tf_op jit(solution)/shard_map/ppermute | solution.py:20
  135.3 15.3 %collective-permute-start.7 = (f32[496,256]{1,0:T(8,128)S(1)}, f32[496,256]{1,0:T(8,128)S(1)}, u32[]{:S(2)}, u32[]{:S(2)}) collective-permute-start(f32[496,256]{1,0:T(8,128)S(1)} %fusion.5), channel_id=1, source_target_pairs={{0,1},{3,2},{4,5},{7,6},{8,9},{11,10},{12,13},{15,14},{16,17},{19,... | collective-permute-start | bytes 1523720 | tf_op jit(solution)/shard_map/ppermute | solution.py:26
  138.9 22.4 %collective-permute-start.3 = (f32[504,256]{1,0:T(8,128)S(1)}, f32[504,256]{1,0:T(8,128)S(1)}, u32[]{:S(2)}, u32[]{:S(2)}) collective-permute-start(f32[504,256]{1,0:T(8,128)S(1)} %fusion.4), channel_id=1, source_target_pairs={{0,1},{3,2},{4,5},{7,6},{8,9},{11,10},{12,13},{15,14},{16,17},{19,... | collective-permute-start | bytes 1548296 | tf_op jit(solution)/shard_map/ppermute | solution.py:26
  150.7 14.1 %copy-start.6 = (f32[496,128]{1,0:T(8,128)S(1)}, f32[496,128]{1,0:T(8,128)}, u32[]{:S(2)}) copy-start(f32[496,128]{1,0:T(8,128)} %copy-done.5) | copy-start | bytes 761860
  150.7 11.3 %collective-permute-start.8 = (f32[496,256]{1,0:T(8,128)S(1)}, f32[496,256]{1,0:T(8,128)S(1)}, u32[]{:S(2)}, u32[]{:S(2)}) collective-permute-start(f32[496,256]{1,0:T(8,128)S(1)} %add.58), channel_id=1, source_target_pairs={{1,2},{2,1},{5,6},{6,5},{9,10},{10,9},{13,14},{14,13},{17,18},{18,... | collective-permute-start | bytes 1523720 | tf_op jit(solution)/shard_map/ppermute | solution.py:27
  161.3 2.1 %collective-permute-start.4 = (f32[504,256]{1,0:T(8,128)S(1)}, f32[504,256]{1,0:T(8,128)S(1)}, u32[]{:S(2)}, u32[]{:S(2)}) collective-permute-start(f32[504,256]{1,0:T(8,128)S(1)} %add.54), channel_id=1, source_target_pairs={{1,2},{2,1},{5,6},{6,5},{9,10},{10,9},{13,14},{14,13},{17,18},{18,... | collective-permute-start | bytes 1548296 | tf_op jit(solution)/shard_map/ppermute | solution.py:27
  162.1 17.7 %collective-permute-start.9 = (f32[496,256]{1,0:T(8,128)S(1)}, f32[496,256]{1,0:T(8,128)}, u32[]{:S(2)}, u32[]{:S(2)}) collective-permute-start(f32[496,256]{1,0:T(8,128)S(1)} %add.59), channel_id=1, source_target_pairs={{1,0},{2,3},{5,4},{6,7},{9,8},{10,11},{13,12},{14,15},{17,16},{18,... | collective-permute-start | bytes 1523720 | tf_op jit(solution)/shard_map/ppermute | solution.py:28
  163.5 27.6 %collective-permute-start.5 = (f32[504,256]{1,0:T(8,128)S(1)}, f32[504,256]{1,0:T(8,128)S(1)}, u32[]{:S(2)}, u32[]{:S(2)}) collective-permute-start(f32[504,256]{1,0:T(8,128)S(1)} %add.55), channel_id=1, source_target_pairs={{1,0},{2,3},{5,4},{6,7},{9,8},{10,11},{13,12},{14,15},{17,16},{18,... | collective-permute-start | bytes 1548296 | tf_op jit(solution)/shard_map/ppermute | solution.py:28
Sparse Core Ops, SparseCore 0:
  9.8 38.0 all-gather.3
  57.3 27.5 reduce-scatter.8
  88.1 29.0 reduce-scatter.6

commit v3 on v2

v3 whole, which is shorter than its diff:
```python
import math

import jax
import jax.numpy as jnp
from jax import lax
from jax.sharding import Mesh, PartitionSpec as P

HIGHEST = lax.Precision.HIGHEST
HIGH = lax.Precision.HIGH
ROUNDS = (400, 352, 248)


def dot(a, b, dims, precision):
    return lax.dot_general(
        a, b, (dims, ((), ())), precision=precision, preferred_element_type=jnp.float32
    )


def swap(value, axis, flip=1):
    size = lax.axis_size(axis)
    return lax.ppermute(value, axis, [(i, i ^ flip) for i in range(size)])


def after(value, *earlier):
    return lax.optimization_barrier((value,) + earlier)[0]


def sum_col(value):
    if lax.axis_size("col") != 4:
        return lax.psum(value, "col")
    inner = value + lax.ppermute(value, "col", [(0, 1), (3, 2)])
    total = inner + lax.ppermute(inner, "col", [(1, 2), (2, 1)])
    back = lax.ppermute(total, "col", [(1, 0), (2, 3)])
    place = lax.axis_index("col")
    return jnp.where((place == 0) | (place == 3), back, total)


def kernel_of(rows, cent, cent_sq):
    length_scale = math.sqrt(rows.shape[1]) / 4.0
    crossed = dot(rows, cent, ((1,), (1,)), HIGHEST)
    row_sq = jnp.sum(rows * rows, axis=1, keepdims=True)
    dist_sq = row_sq + cent_sq[None, :] - 2.0 * crossed
    return jnp.exp(-jnp.sqrt(dist_sq + 1.0) / length_scale)


def any_plane(batch, start_t, cent, cent_sq, weight):
    rows_here, chips = batch.shape[0], lax.axis_size("chip")
    rows = lax.all_gather(batch, "chip", axis=0, tiled=True)
    kernel = kernel_of(rows, cent, cent_sq)
    shares = dot(weight, kernel, ((1,), (1,)), HIGH)
    shares = shares.reshape(weight.shape[0], chips, rows_here).transpose(1, 0, 2)
    residual = start_t + lax.psum_scatter(shares, "chip", scatter_dimension=0, tiled=False)
    moved = lax.all_gather(residual, "chip", axis=0, tiled=False)
    moved = moved.transpose(1, 0, 2).reshape(weight.shape[0], chips * rows_here)
    gradient = dot(moved, kernel, ((1,), (0,)), HIGH)
    half = cent.shape[0] // 2
    owned = gradient[:, :half] + swap(gradient[:, half:], "core")
    return sum_col(owned), residual


def square(batch, start_t, cent, cent_sq, weight):
    rows, half, out = batch.shape[0], cent.shape[0] // 2, weight.shape[0]
    block_x = swap(batch, "chip", 1)
    block_y = swap(batch, "chip", 2)
    own = kernel_of(batch, cent, cent_sq)
    low = swap(after(block_x[: rows // 2], own), "chip", 2)
    high = swap(after(block_y[rows // 2 :], own), "chip", 1)
    side_x = kernel_of(block_x, cent, cent_sq)
    side_y = kernel_of(block_y, cent, cent_sq)
    far = kernel_of(jnp.concatenate([low, high], axis=0), cent, cent_sq)
    stay = (jnp.concatenate([own, side_y]), jnp.concatenate([own, side_x]))
    goes = (jnp.concatenate([side_x, far]), jnp.concatenate([side_y, far]))

    edges, at = [], 0
    for size in ROUNDS:
        size = min(size, out - at)
        middle = at + -(-size // 2 // 8) * 8
        edges.append(((at, middle), (middle, at + size)))
        at += size

    def shares(r):
        return [dot(weight[a:b], goes[i], ((1,), (1,)), HIGH) for i, (a, b) in enumerate(edges[r])]

    def begin(r):
        kept = []
        for i, (a, b) in enumerate(edges[r]):
            base = jnp.pad(start_t[a:b], ((0, 0), (0, rows)))
            kept.append(dot(weight[a:b], stay[i], ((1,), (1,)), HIGH) + base)
        return kept

    def turned(pair):
        return jnp.concatenate([pair[:, rows:], pair[:, :rows]], axis=1)

    axes = ((1, 2), (2, 1))
    gradients, residuals = [], []
    sent = shares(0)
    coming = [swap(sent[i], "chip", axes[i][0]) for i in (0, 1)]
    for r in range(len(edges)):
        partial = [k + c for k, c in zip(begin(r), coming)]
        full = [partial[i] + turned(swap(partial[i], "chip", axes[i][1])) for i in (0, 1)]
        if r + 1 < len(edges):
            sent = after(tuple(shares(r + 1)), *partial)
            coming = [swap(sent[i], "chip", axes[i][0]) for i in (0, 1)]
        residuals += [f[:, :rows] for f in full]
        if r:
            full = after(tuple(full), gone)
        other = [swap(full[i], "chip", axes[i][0]) for i in (0, 1)]
        if r:
            other = after(tuple(other), owned)
        gone, here = [
            jnp.concatenate(
                [
                    dot(full[i], stay[i][:, cols], ((1,), (0,)), HIGH)
                    + dot(other[i], goes[i][:, cols], ((1,), (0,)), HIGH)
                    for i in (0, 1)
                ]
            )
            for cols in (slice(half, None), slice(0, half))
        ]
        owned = here + swap(gone, "core")
        gradients.append(sum_col(owned))
    return jnp.concatenate(gradients), jnp.concatenate(residuals)


def per_device(batch, running, targets, centers, weights):
    chips, depth = lax.axis_size("chip"), lax.axis_size("col")
    factor = 1.0 / math.sqrt(batch.shape[0] * chips * 2 * depth)
    cent = jnp.concatenate([centers, swap(centers, "core")], axis=0)
    cent_sq = jnp.sum(cent * cent, axis=1)
    weights_t = weights.T
    weight = jnp.concatenate([weights_t, swap(weights_t, "core")], axis=1)
    plane = square if chips == 4 else any_plane
    gradient, residual = plane(batch, (running - targets).T, cent, cent_sq, weight)
    return (gradient * factor).T, residual.T


def solution(mesh):
    owners, depth = mesh.shape["row"], mesh.shape["col"]
    split = Mesh(mesh.devices.reshape(owners // 2, 2, depth), ("chip", "core", "col"))
    everywhere = P(("chip", "core", "col"), None)
    owned = P(("chip", "core"), None)
    return jax.shard_map(
        per_device,
        mesh=split,
        in_specs=(everywhere, everywhere, everywhere, owned, owned),
        out_specs=(owned, everywhere),
        check_vma=False,
    )
```

time: 199 us -> 122 us (0.61)
  waiting for transfers between devices: 116 us -> 44 us
  starting transfers between devices: 9.63 us -> 45.2 us
  blocking collectives: 31.2 us -> 0 us
  between operations: 14.1 us -> 1.52 us
  matrix products: 11.8 us -> 20.6 us
  other arithmetic: 8.89 us -> 3.77 us
    all_gather x1 -> x0, waiting for transfers between devices: 35.9 us -> none  [per_device(): rows = lax.all_gather(batch, 'chip', axis=0, tiled=True)]
    unnamed x5 -> x0, waiting for transfers between devices: 34.2 us -> none
    all_gather x2 -> x0, blocking collectives: 31.2 us -> none  [per_device(): moved = lax.all_gather(residual, 'chip', axis=0, tiled=False)]
    ppermute x4 -> x27, starting transfers between devices: 0.67 us -> 25 us  [swap(): return lax.ppermute(value, axis, [(i, i ^ flip) for i in range(size)])]
    ppermute x4 -> x27, waiting for transfers between devices: 1.84 us -> 20.8 us  [swap(): return lax.ppermute(value, axis, [(i, i ^ flip) for i in range(size)])]
    ppermute x2 -> x3, waiting for transfers between devices: 20.1 us -> 3.14 us  [sum_col(): inner = value + lax.ppermute(value, 'col', [(0, 1), (3, 2)])]
    ppermute x2 -> x3, starting transfers between devices: 4.74 us -> 14.2 us  [sum_col(): inner = value + lax.ppermute(value, 'col', [(0, 1), (3, 2)])]
    dot_general x5 -> x40, matrix products: 11.8 us -> 20.6 us  [dot(): lax.dot_general(a, b, (dims, ((), ())), precision=precision, preferred_el...]
  transfers between devices with their start and end apart: 13 -> 36, of which waited for: 8 -> 13; matrix products, arithmetic and copies ran while one was open for 11% -> 18% of each run, Pallas kernels for 0% -> 0%
where the time goes in v3:
time: 122 us; the launch traced here: 121 us
  starting transfers between devices  45.2 us (37%)
  waiting for transfers between devices  44 us (36%)
  matrix products  20.6 us (17%)
  local copies, waits for them, and re-layouts  6.08 us (5%)
  other arithmetic  3.77 us (3%)
  between operations  1.52 us (1%)
    ppermute x27, starting transfers between devices, swap(): return lax.ppermute(value, axis, [(i, i ^ flip) for i in range(size)])  25 us
    ppermute x27, waiting for transfers between devices, swap(): return lax.ppermute(value, axis, [(i, i ^ flip) for i in range(size)])  20.8 us
    dot_general x40, matrix products, dot(): lax.dot_general(a, b, (dims, ((), ())), precision=precision, preferred_el...  20.6 us
    ppermute x3, waiting for transfers between devices, sum_col(): back = lax.ppermute(total, 'col', [(1, 0), (2, 3)])  20 us
    ppermute x3, starting transfers between devices, sum_col(): inner = value + lax.ppermute(value, 'col', [(0, 1), (3, 2)])  14.2 us
    ppermute x3, starting transfers between devices, sum_col(): back = lax.ppermute(total, 'col', [(1, 0), (2, 3)])  3.87 us
    ppermute x3, waiting for transfers between devices, sum_col(): inner = value + lax.ppermute(value, 'col', [(0, 1), (3, 2)])  3.14 us
    unnamed x19, local copies, waits for them, and re-layouts  2.6 us
  transfers between devices with their start and end apart: 36, of which 13 were waited for; matrix products, arithmetic and copies ran while one was open for 18% of the time, Pallas kernels for 0%

profile of v3, /device:TPU:0, one launch (start us, length us, event | category | flops | bytes accessed | tf_op | source)
XLA Modules:
  0.0 121.1 jit_solution(4211473942615210806)
XLA Ops:
  0.6 3.0 %collective-permute-start.2 = (f32[128,1024]{1,0:T(8,128)}, f32[128,1024]{1,0:T(8,128)S(1)}, u32[]{:S(2)}, u32[]{:S(2)}) collective-permute-start(f32[128,1024]{1,0:T(8,128)} %param.5), channel_id=1, source_target_pairs={{0,16},{8,24},{16,0},{24,8},{1,17},{9,25},{17,1},{25,9},{2,18},{10... | collective-permute-start | bytes 1572872 | tf_op jit(solution)/shard_map/ppermute | solution.py:21
  3.7 1.5 %collective-permute-start.3 = (f32[128,1024]{1,0:T(8,128)}, f32[128,1024]{1,0:T(8,128)S(1)}, u32[]{:S(2)}, u32[]{:S(2)}) collective-permute-start(f32[128,1024]{1,0:T(8,128)} %param.5), channel_id=1, source_target_pairs={{0,8},{8,0},{16,24},{24,16},{1,9},{9,1},{17,25},{25,17},{2,10},{10... | collective-permute-start | bytes 1572872 | tf_op jit(solution)/shard_map/ppermute | solution.py:21
  6.9 2.5 %constant_dynamic-update-slice_fusion.1 = f32[512,1024]{1,0:T(8,128)} fusion(f32[256,1024]{1,0:T(8,128)} %param.8), kind=kLoop, calls=%fused_computation.111 | loop fusion | bytes 2097152
  11.6 4.2 %collective-permute-done.2 = f32[128,1024]{1,0:T(8,128)S(1)} collective-permute-done((f32[128,1024]{1,0:T(8,128)}, f32[128,1024]{1,0:T(8,128)S(1)}, u32[]{:S(2)}, u32[]{:S(2)}) %collective-permute-start.2) | collective-permute-done | bytes 524320 | tf_op jit(solution)/shard_map/ppermute | solution.py:21
  15.8 1.4 %collective-permute-done.3 = f32[128,1024]{1,0:T(8,128)S(1)} collective-permute-done((f32[128,1024]{1,0:T(8,128)}, f32[128,1024]{1,0:T(8,128)S(1)}, u32[]{:S(2)}, u32[]{:S(2)}) %collective-permute-start.3) | collective-permute-done | bytes 524320 | tf_op jit(solution)/shard_map/ppermute | solution.py:21
  17.6 1.3 %constant_dynamic-update-slice_fusion = f32[512,1024]{1,0:T(8,128)S(1)} fusion(f32[512,1024]{1,0:T(8,128)S(1)} %copy-done.1, f32[256,1024]{1,0:T(8,128)} %collective-permute-done.1), kind=kLoop, calls=%fused_computation.110 | loop fusion | bytes 2097152 | tf_op jit(solution)/shard_map/concatenate | solution.py:128
  19.2 2.4 %multiply_exponential_fusion.3 = f32[128,512]{1,0:T(8,128)S(1)} fusion(f32[512,1024]{1,0:T(8,128)S(1)} %constant_dynamic-update-slice_fusion, f32[128,1024]{1,0:T(8,128)S(1)} %copy-done.3, f32[512]{0:T(512)S(1)} %multiply_reduce_fusion, f32[128]{0:T(128)S(1)} %multiply_reduce_fusion.4), kind=kOutput, calls=%fused_computation.91 | convolution fusion | flops 805699584 | bytes 2886144 | tf_op jit(solution)/shard_map/dot_general | solution.py:14
  21.6 1.6 %collective-permute-start.5 = (f32[64,1024]{1,0:T(8,128)S(1)}, f32[64,1024]{1,0:T(8,128)S(1)}, u32[]{:S(2)}, u32[]{:S(2)}) collective-permute-start(f32[64,1024]{1,0:T(8,128)S(1)} %slice.186), channel_id=1, source_target_pairs={{0,8},{8,0},{16,24},{24,16},{1,9},{9,1},{17,25},{25,17},{2,10},{10... | collective-permute-start | bytes 786440 | tf_op jit(solution)/shard_map/ppermute | solution.py:21
  23.6 2.4 %multiply_exponential_fusion.1 = f32[128,512]{1,0:T(8,128)S(1)} fusion(f32[128]{0:T(128)S(1)} %multiply_reduce_fusion.2, f32[512,1024]{1,0:T(8,128)S(1)} %constant_dynamic-update-slice_fusion, f32[128,1024]{1,0:T(8,128)S(1)} %collective-permute-done.3, f32[512]{0:T(512)S(1)} %multiply_reduce_fusion), kind=kOutput, calls=%fused_computation.89 | convolution fusion | flops 805699584 | bytes 2886144 | tf_op jit(solution)/shard_map/dot_general | solution.py:14
  26.0 2.4 %multiply_exponential_fusion.2 = f32[128,512]{1,0:T(8,128)S(1)} fusion(f32[128]{0:T(128)S(1)} %multiply_reduce_fusion.3, f32[512,1024]{1,0:T(8,128)S(1)} %constant_dynamic-update-slice_fusion, f32[128,1024]{1,0:T(8,128)S(1)} %collective-permute-done.2, f32[512]{0:T(512)S(1)} %multiply_reduce_fusion), kind=kOutput, calls=%fused_computation.90 | convolution fusion | flops 805699584 | bytes 2886144 | tf_op jit(solution)/shard_map/dot_general | solution.py:14
  29.9 2.4 %multiply_exponential_fusion = f32[128,512]{1,0:T(8,128)S(1)} fusion(f32[128,1024]{1,0:T(8,128)S(1)} %constant_dynamic-update-slice_fusion.2, f32[512,1024]{1,0:T(8,128)S(1)} %constant_dynamic-update-slice_fusion, f32[128]{0:T(128)S(1)} %multiply_reduce_fusion.1, f32[512]{0:T(512)S(1)} %multiply_reduce_fusion), kind=kOutput, calls=%fused_computation.88 | convolution fusion | flops 805699584 | bytes 2886144 | tf_op jit(solution)/shard_map/dot_general | solution.py:14
  35.7 2.8 %collective-permute-done.6 = f32[200,256]{1,0:T(8,128)S(1)} collective-permute-done((f32[200,256]{1,0:T(8,128)S(1)}, f32[200,256]{1,0:T(8,128)S(1)}, u32[]{:S(2)}, u32[]{:S(2)}) %collective-permute-start.6) | collective-permute-done | bytes 204832 | tf_op jit(solution)/shard_map/ppermute | solution.py:21
  40.0 1.6 %collective-permute-start.16 = (f32[176,256]{1,0:T(8,128)S(1)}, f32[176,256]{1,0:T(8,128)S(1)}, u32[]{:S(2)}, u32[]{:S(2)}) collective-permute-start(f32[176,256]{1,0:T(8,128)S(1)} %fusion.14), channel_id=1, source_target_pairs={{0,8},{8,0},{16,24},{24,16},{1,9},{9,1},{17,25},{25,17},{2,10},{10... | collective-permute-start | bytes 540680 | tf_op jit(solution)/shard_map/ppermute | solution.py:21
  43.2 1.3 %collective-permute-start.18 = (f32[176,256]{1,0:T(8,128)S(1)}, f32[176,256]{1,0:T(8,128)S(1)}, u32[]{:S(2)}, u32[]{:S(2)}) collective-permute-start(f32[176,256]{1,0:T(8,128)S(1)} %fusion.17), channel_id=1, source_target_pairs={{0,16},{8,24},{16,0},{24,8},{1,17},{9,25},{17,1},{25,9},{2,18},{10... | collective-permute-start | bytes 540680 | tf_op jit(solution)/shard_map/ppermute | solution.py:21
  47.0 4.9 %collective-permute-done.18 = f32[176,256]{1,0:T(8,128)S(1)} collective-permute-done((f32[176,256]{1,0:T(8,128)S(1)}, f32[176,256]{1,0:T(8,128)S(1)}, u32[]{:S(2)}, u32[]{:S(2)}) %collective-permute-start.18) | collective-permute-done | bytes 180256 | tf_op jit(solution)/shard_map/ppermute | solution.py:21
  53.3 1.4 %collective-permute-start.26 = (f32[128,256]{1,0:T(8,128)S(1)}, f32[128,256]{1,0:T(8,128)S(1)}, u32[]{:S(2)}, u32[]{:S(2)}) collective-permute-start(f32[128,256]{1,0:T(8,128)S(1)} %fusion.15), channel_id=1, source_target_pairs={{0,8},{8,0},{16,24},{24,16},{1,9},{9,1},{17,25},{25,17},{2,10},{10... | collective-permute-start | bytes 393224 | tf_op jit(solution)/shard_map/ppermute | solution.py:21
  56.4 3.5 %collective-permute-done.28 = f32[120,256]{1,0:T(8,128)S(1)} collective-permute-done((f32[120,256]{1,0:T(8,128)S(1)}, f32[120,256]{1,0:T(8,128)S(1)}, u32[]{:S(2)}, u32[]{:S(2)}) %collective-permute-start.28) | collective-permute-done | bytes 122912 | tf_op jit(solution)/shard_map/ppermute | solution.py:21
  61.3 1.4 %collective-permute-start.29 = (f32[120,256]{1,0:T(8,128)S(1)}, f32[120,256]{1,0:T(8,128)S(1)}, u32[]{:S(2)}, u32[]{:S(2)}) collective-permute-start(f32[120,256]{1,0:T(8,128)S(1)} %fusion.8), channel_id=1, source_target_pairs={{0,8},{8,0},{16,24},{24,16},{1,9},{9,1},{17,25},{25,17},{2,10},{10... | collective-permute-start | bytes 368648 | tf_op jit(solution)/shard_map/ppermute | solution.py:21
  70.9 3.5 %collective-permute-start.13 = (f32[400,256]{1,0:T(8,128)S(1)}, f32[400,256]{1,0:T(8,128)S(1)}, u32[]{:S(2)}, u32[]{:S(2)}) collective-permute-start(f32[400,256]{1,0:T(8,128)S(1)} %maximum_add_fusion), channel_id=1, source_target_pairs={{0,1},{3,2},{4,5},{7,6},{8,9},{11,10},{12,13},{15,14},{16,17},{19,... | collective-permute-start | bytes 1228808 | tf_op jit(solution)/shard_map/ppermute | solution.py:31
  78.5 3.5 %collective-permute-start.23 = (f32[352,256]{1,0:T(8,128)S(1)}, f32[352,256]{1,0:T(8,128)S(1)}, u32[]{:S(2)}, u32[]{:S(2)}) collective-permute-start(f32[352,256]{1,0:T(8,128)S(1)} %maximum_add_fusion.1), channel_id=1, source_target_pairs={{0,1},{3,2},{4,5},{7,6},{8,9},{11,10},{12,13},{15,14},{16,17},{19,... | collective-permute-start | bytes 1081352 | tf_op jit(solution)/shard_map/ppermute | solution.py:31
  85.1 7.2 %collective-permute-start.33 = (f32[248,256]{1,0:T(8,128)S(1)}, f32[248,256]{1,0:T(8,128)S(1)}, u32[]{:S(2)}, u32[]{:S(2)}) collective-permute-start(f32[248,256]{1,0:T(8,128)S(1)} %maximum_add_fusion.2), channel_id=1, source_target_pairs={{0,1},{3,2},{4,5},{7,6},{8,9},{11,10},{12,13},{15,14},{16,17},{19,... | collective-permute-start | bytes 761864 | tf_op jit(solution)/shard_map/ppermute | solution.py:31
  94.4 2.0 %collective-permute-done.33 = f32[248,256]{1,0:T(8,128)S(1)} collective-permute-done((f32[248,256]{1,0:T(8,128)S(1)}, f32[248,256]{1,0:T(8,128)S(1)}, u32[]{:S(2)}, u32[]{:S(2)}) %collective-permute-start.33) | collective-permute-done | bytes 253984 | tf_op jit(solution)/shard_map/ppermute | solution.py:31
  99.9 6.9 %collective-permute-done.15 = f32[400,256]{1,0:T(8,128)S(1)} collective-permute-done((f32[400,256]{1,0:T(8,128)S(1)}, f32[400,256]{1,0:T(8,128)S(1)}, u32[]{:S(2)}, u32[]{:S(2)}) %collective-permute-start.15) | collective-permute-done | bytes 409632 | tf_op jit(solution)/shard_map/ppermute | solution.py:33
  106.8 13.2 %collective-permute-done.35 = f32[248,256]{1,0:T(8,128)S(1)} collective-permute-done((f32[248,256]{1,0:T(8,128)S(1)}, f32[248,256]{1,0:T(8,128)S(1)}, u32[]{:S(2)}, u32[]{:S(2)}) %collective-permute-start.35) | collective-permute-done | bytes 253984 | tf_op jit(solution)/shard_map/ppermute | solution.py:33
  (153 shorter events, 41.2 us)
Async XLA Ops:
  0.6 15.2 %collective-permute-start.2 = (f32[128,1024]{1,0:T(8,128)}, f32[128,1024]{1,0:T(8,128)S(1)}, u32[]{:S(2)}, u32[]{:S(2)}) collective-permute-start(f32[128,1024]{1,0:T(8,128)} %param.5), channel_id=1, source_target_pairs={{0,16},{8,24},{16,0},{24,8},{1,17},{9,25},{17,1},{25,9},{2,18},{10... | collective-permute-start | bytes 1572872 | tf_op jit(solution)/shard_map/ppermute | solution.py:21
  3.7 13.6 %collective-permute-start.3 = (f32[128,1024]{1,0:T(8,128)}, f32[128,1024]{1,0:T(8,128)S(1)}, u32[]{:S(2)}, u32[]{:S(2)}) collective-permute-start(f32[128,1024]{1,0:T(8,128)} %param.5), channel_id=1, source_target_pairs={{0,8},{8,0},{16,24},{24,16},{1,9},{9,1},{17,25},{25,17},{2,10},{10... | collective-permute-start | bytes 1572872 | tf_op jit(solution)/shard_map/ppermute | solution.py:21
  5.2 12.4 %collective-permute-start.1 = (f32[256,1024]{1,0:T(8,128)}, f32[256,1024]{1,0:T(8,128)}, u32[]{:S(2)}, u32[]{:S(2)}) collective-permute-start(f32[256,1024]{1,0:T(8,128)} %param.8), channel_id=1, source_target_pairs={{0,4},{4,0},{1,5},{5,1},{2,6},{6,2},{3,7},{7,3},{8,12},{12,8},{9,1... | collective-permute-start | bytes 3145736 | tf_op jit(solution)/shard_map/ppermute | solution.py:21
  5.2 12.4 %collective-permute-start = (f32[1000,256]{1,0:T(8,128)}, f32[1000,256]{1,0:T(8,128)S(1)}, u32[]{:S(2)}, u32[]{:S(2)}) collective-permute-start(f32[1000,256]{1,0:T(8,128)} %bitcast.52), channel_id=1, source_target_pairs={{0,4},{4,0},{1,5},{5,1},{2,6},{6,2},{3,7},{7,3},{8,12},{12,8},{9,1... | collective-permute-start | bytes 3072008 | tf_op jit(solution)/shard_map/ppermute | solution.py:21
  21.6 8.2 %collective-permute-start.5 = (f32[64,1024]{1,0:T(8,128)S(1)}, f32[64,1024]{1,0:T(8,128)S(1)}, u32[]{:S(2)}, u32[]{:S(2)}) collective-permute-start(f32[64,1024]{1,0:T(8,128)S(1)} %slice.186), channel_id=1, source_target_pairs={{0,8},{8,0},{16,24},{24,16},{1,9},{9,1},{17,25},{25,17},{2,10},{10... | collective-permute-start | bytes 786440 | tf_op jit(solution)/shard_map/ppermute | solution.py:21
  42.0 12.7 %collective-permute-start.7 = (f32[200,256]{1,0:T(8,128)S(1)}, f32[200,256]{1,0:T(8,128)S(1)}, u32[]{:S(2)}, u32[]{:S(2)}) collective-permute-start(f32[200,256]{1,0:T(8,128)S(1)} %fusion.3), channel_id=1, source_target_pairs={{0,16},{8,24},{16,0},{24,8},{1,17},{9,25},{17,1},{25,9},{2,18},{10... | collective-permute-start | bytes 614408 | tf_op jit(solution)/shard_map/ppermute | solution.py:21
  42.7 13.0 %collective-permute-start.10 = (f32[200,256]{1,0:T(8,128)S(1)}, f32[200,256]{1,0:T(8,128)S(1)}, u32[]{:S(2)}, u32[]{:S(2)}) collective-permute-start(f32[200,256]{1,0:T(8,128)S(1)} %fusion.4), channel_id=1, source_target_pairs={{0,8},{8,0},{16,24},{24,16},{1,9},{9,1},{17,25},{25,17},{2,10},{10... | collective-permute-start | bytes 614408 | tf_op jit(solution)/shard_map/ppermute | solution.py:21
  43.2 8.7 %collective-permute-start.18 = (f32[176,256]{1,0:T(8,128)S(1)}, f32[176,256]{1,0:T(8,128)S(1)}, u32[]{:S(2)}, u32[]{:S(2)}) collective-permute-start(f32[176,256]{1,0:T(8,128)S(1)} %fusion.17), channel_id=1, source_target_pairs={{0,16},{8,24},{16,0},{24,8},{1,17},{9,25},{17,1},{25,9},{2,18},{10... | collective-permute-start | bytes 540680 | tf_op jit(solution)/shard_map/ppermute | solution.py:21
  46.0 17.1 %collective-permute-start.17 = (f32[176,256]{1,0:T(8,128)S(1)}, f32[176,256]{1,0:T(8,128)S(1)}, u32[]{:S(2)}, u32[]{:S(2)}) collective-permute-start(f32[176,256]{1,0:T(8,128)S(1)} %fusion.5), channel_id=1, source_target_pairs={{0,16},{8,24},{16,0},{24,8},{1,17},{9,25},{17,1},{25,9},{2,18},{10... | collective-permute-start | bytes 540680 | tf_op jit(solution)/shard_map/ppermute | solution.py:21
  52.6 11.6 %collective-permute-start.19 = (f32[176,256]{1,0:T(8,128)S(1)}, f32[176,256]{1,0:T(8,128)S(1)}, u32[]{:S(2)}, u32[]{:S(2)}) collective-permute-start(f32[176,256]{1,0:T(8,128)S(1)} %fusion.6), channel_id=1, source_target_pairs={{0,8},{8,0},{16,24},{24,16},{1,9},{9,1},{17,25},{25,17},{2,10},{10... | collective-permute-start | bytes 540680 | tf_op jit(solution)/shard_map/ppermute | solution.py:21
  53.3 8.0 %collective-permute-start.26 = (f32[128,256]{1,0:T(8,128)S(1)}, f32[128,256]{1,0:T(8,128)S(1)}, u32[]{:S(2)}, u32[]{:S(2)}) collective-permute-start(f32[128,256]{1,0:T(8,128)S(1)} %fusion.15), channel_id=1, source_target_pairs={{0,8},{8,0},{16,24},{24,16},{1,9},{9,1},{17,25},{25,17},{2,10},{10... | collective-permute-start | bytes 393224 | tf_op jit(solution)/shard_map/ppermute | solution.py:21
  55.6 8.6 %collective-permute-start.8 = (f32[200,256]{1,0:T(8,128)S(1)}, f32[200,256]{1,0:T(8,128)S(1)}, u32[]{:S(2)}, u32[]{:S(2)}) collective-permute-start(f32[200,256]{1,0:T(8,128)S(1)} %maximum_add_fusion.3), channel_id=1, source_target_pairs={{0,8},{8,0},{16,24},{24,16},{1,9},{9,1},{17,25},{25,17},{2,10},{10... | collective-permute-start | bytes 614408 | tf_op jit(solution)/shard_map/ppermute | solution.py:21
  61.3 9.5 %collective-permute-start.29 = (f32[120,256]{1,0:T(8,128)S(1)}, f32[120,256]{1,0:T(8,128)S(1)}, u32[]{:S(2)}, u32[]{:S(2)}) collective-permute-start(f32[120,256]{1,0:T(8,128)S(1)} %fusion.8), channel_id=1, source_target_pairs={{0,8},{8,0},{16,24},{24,16},{1,9},{9,1},{17,25},{25,17},{2,10},{10... | collective-permute-start | bytes 368648 | tf_op jit(solution)/shard_map/ppermute | solution.py:21
  63.1 7.7 %collective-permute-start.27 = (f32[128,256]{1,0:T(8,128)S(1)}, f32[128,256]{1,0:T(8,128)S(1)}, u32[]{:S(2)}, u32[]{:S(2)}) collective-permute-start(f32[128,256]{1,0:T(8,128)S(1)} %fusion.7), channel_id=1, source_target_pairs={{0,16},{8,24},{16,0},{24,8},{1,17},{9,25},{17,1},{25,9},{2,18},{10... | collective-permute-start | bytes 393224 | tf_op jit(solution)/shard_map/ppermute | solution.py:21
  66.6 7.9 %collective-permute-start.20 = (f32[176,256]{1,0:T(8,128)S(1)}, f32[176,256]{1,0:T(8,128)S(1)}, u32[]{:S(2)}, u32[]{:S(2)}) collective-permute-start(f32[176,256]{1,0:T(8,128)S(1)} %maximum_add_fusion.5), channel_id=1, source_target_pairs={{0,8},{8,0},{16,24},{24,16},{1,9},{9,1},{17,25},{25,17},{2,10},{10... | collective-permute-start | bytes 540680 | tf_op jit(solution)/shard_map/ppermute | solution.py:21
  67.8 6.7 %collective-permute-start.21 = (f32[176,256]{1,0:T(8,128)S(1)}, f32[176,256]{1,0:T(8,128)S(1)}, u32[]{:S(2)}, u32[]{:S(2)}) collective-permute-start(f32[176,256]{1,0:T(8,128)S(1)} %maximum_add_fusion.6), channel_id=1, source_target_pairs={{0,16},{8,24},{16,0},{24,8},{1,17},{9,25},{17,1},{25,9},{2,18},{10... | collective-permute-start | bytes 540680 | tf_op jit(solution)/shard_map/ppermute | solution.py:21
  70.9 13.3 %collective-permute-start.13 = (f32[400,256]{1,0:T(8,128)S(1)}, f32[400,256]{1,0:T(8,128)S(1)}, u32[]{:S(2)}, u32[]{:S(2)}) collective-permute-start(f32[400,256]{1,0:T(8,128)S(1)} %maximum_add_fusion), channel_id=1, source_target_pairs={{0,1},{3,2},{4,5},{7,6},{8,9},{11,10},{12,13},{15,14},{16,17},{19,... | collective-permute-start | bytes 1228808 | tf_op jit(solution)/shard_map/ppermute | solution.py:31
  75.4 6.7 %collective-permute-start.30 = (f32[128,256]{1,0:T(8,128)S(1)}, f32[128,256]{1,0:T(8,128)S(1)}, u32[]{:S(2)}, u32[]{:S(2)}) collective-permute-start(f32[128,256]{1,0:T(8,128)S(1)} %maximum_add_fusion.7), channel_id=1, source_target_pairs={{0,8},{8,0},{16,24},{24,16},{1,9},{9,1},{17,25},{25,17},{2,10},{10... | collective-permute-start | bytes 393224 | tf_op jit(solution)/shard_map/ppermute | solution.py:21
  78.5 13.8 %collective-permute-start.23 = (f32[352,256]{1,0:T(8,128)S(1)}, f32[352,256]{1,0:T(8,128)S(1)}, u32[]{:S(2)}, u32[]{:S(2)}) collective-permute-start(f32[352,256]{1,0:T(8,128)S(1)} %maximum_add_fusion.1), channel_id=1, source_target_pairs={{0,1},{3,2},{4,5},{7,6},{8,9},{11,10},{12,13},{15,14},{16,17},{19,... | collective-permute-start | bytes 1081352 | tf_op jit(solution)/shard_map/ppermute | solution.py:31
  84.3 8.7 %collective-permute-start.14 = (f32[400,256]{1,0:T(8,128)S(1)}, f32[400,256]{1,0:T(8,128)S(1)}, u32[]{:S(2)}, u32[]{:S(2)}) collective-permute-start(f32[400,256]{1,0:T(8,128)S(1)} %add.211), channel_id=1, source_target_pairs={{1,2},{2,1},{5,6},{6,5},{9,10},{10,9},{13,14},{14,13},{17,18},{18,... | collective-permute-start | bytes 1228808 | tf_op jit(solution)/shard_map/ppermute | solution.py:32
  85.1 11.3 %collective-permute-start.33 = (f32[248,256]{1,0:T(8,128)S(1)}, f32[248,256]{1,0:T(8,128)S(1)}, u32[]{:S(2)}, u32[]{:S(2)}) collective-permute-start(f32[248,256]{1,0:T(8,128)S(1)} %maximum_add_fusion.2), channel_id=1, source_target_pairs={{0,1},{3,2},{4,5},{7,6},{8,9},{11,10},{12,13},{15,14},{16,17},{19,... | collective-permute-start | bytes 761864 | tf_op jit(solution)/shard_map/ppermute | solution.py:31
  93.1 13.6 %collective-permute-start.15 = (f32[400,256]{1,0:T(8,128)S(1)}, f32[400,256]{1,0:T(8,128)S(1)}, u32[]{:S(2)}, u32[]{:S(2)}) collective-permute-start(f32[400,256]{1,0:T(8,128)S(1)} %add.212), channel_id=1, source_target_pairs={{1,0},{2,3},{5,4},{6,7},{9,8},{10,11},{13,12},{14,15},{17,16},{18,... | collective-permute-start | bytes 1228808 | tf_op jit(solution)/shard_map/ppermute | solution.py:33
  97.2 22.8 %collective-permute-start.25 = (f32[352,256]{1,0:T(8,128)S(1)}, f32[352,256]{1,0:T(8,128)S(1)}, u32[]{:S(2)}, u32[]{:S(2)}) collective-permute-start(f32[352,256]{1,0:T(8,128)S(1)} %add.225), channel_id=1, source_target_pairs={{1,0},{2,3},{5,4},{6,7},{9,8},{10,11},{13,12},{14,15},{17,16},{18,... | collective-permute-start | bytes 1081352 | tf_op jit(solution)/shard_map/ppermute | solution.py:33
  98.6 21.4 %collective-permute-start.35 = (f32[248,256]{1,0:T(8,128)S(1)}, f32[248,256]{1,0:T(8,128)S(1)}, u32[]{:S(2)}, u32[]{:S(2)}) collective-permute-start(f32[248,256]{1,0:T(8,128)S(1)} %add.238), channel_id=1, source_target_pairs={{1,0},{2,3},{5,4},{6,7},{9,8},{10,11},{13,12},{14,15},{17,16},{18,... | collective-permute-start | bytes 761864 | tf_op jit(solution)/shard_map/ppermute | solution.py:33
  (20 other events, 127.1 us)

commit v4 on v2

v4 whole, which is shorter than its diff:
```python
import functools
import math

import jax
import jax.numpy as jnp
from jax import lax
from jax.experimental import pallas as pl
from jax.experimental.pallas import tpu as pltpu
from jax.sharding import Mesh, PartitionSpec as P

HIGHEST = lax.Precision.HIGHEST
HIGH = lax.Precision.HIGH
ROUNDS = (0.32, 0.32, 0.24)
BF16, F32 = jnp.bfloat16, jnp.float32
NT = (((1,), (1,)), ((), ()))
NN = (((1,), (0,)), ((), ()))


def swap(value, axis, flip=1):
    size = lax.axis_size(axis)
    return lax.ppermute(value, axis, [(i, i ^ flip) for i in range(size)])


class Line:
    def __init__(self):
        self.last = None

    def hold(self, args):
        if self.last is None:
            return args
        return lax.optimization_barrier((args, self.last))[0]

    def __call__(self, step, *args):
        out = step(*self.hold(args))
        self.last = jax.tree.leaves(out)[0]
        return out


def halves(value):
    high = value.astype(BF16)
    return high, (value - high.astype(F32)).astype(BF16)


def mul(a, b, dims):
    return lax.dot_general(a, b, dims, preferred_element_type=F32)


def mul3(a, b, dims):
    return mul(a[0], b[0], dims) + (mul(a[0], b[1], dims) + mul(a[1], b[0], dims))


def call(body, outs, args, flops=0, scratch=(), aliases=None):
    moved = sum(x.size * x.dtype.itemsize for x in (*args, *outs))
    vmem = pl.BlockSpec(memory_space=pltpu.VMEM)
    return pl.pallas_call(
        body,
        out_shape=outs,
        in_specs=[vmem] * len(args),
        out_specs=[vmem] * len(outs),
        scratch_shapes=list(scratch),
        input_output_aliases=aliases or {},
        cost_estimate=pl.CostEstimate(flops=flops, bytes_accessed=moved, transcendentals=0),
        compiler_params=pltpu.CompilerParams(vmem_limit_bytes=40 * 2**20),
    )(*args)


def shaped(shape, dtype=F32):
    return jax.ShapeDtypeStruct(shape, dtype)


def cent_body(mine_ref, theirs_ref, high_ref, low_ref, sq_ref):
    half = mine_ref.shape[0]
    for i, ref in enumerate((mine_ref, theirs_ref)):
        for at in range(0, half, 128):
            to = pl.ds(i * half + at, 128)
            value = ref[pl.ds(at, 128)]
            high_ref[to], low_ref[to] = halves(value)
            total = jnp.sum(value * value, axis=1, keepdims=True)
            sq_ref[:, to] = jnp.broadcast_to(total, (128, 128)).T[:8]


def split_cent(mine, theirs):
    half, width = mine.shape
    pair = [shaped((2 * half, width), BF16)] * 2
    return call(cent_body, pair + [shaped((8, 2 * half))], (mine, theirs))


def kernel_rows(high, low, row_sq, cent_refs, put):
    cent_high, cent_low, cent_sq = cent_refs
    scale = -4.0 / math.sqrt(cent_high.shape[1])
    for at in range(0, cent_high.shape[0], 256):
        to = pl.ds(at, 256)
        ch, cl = cent_high[to], cent_low[to]
        crossed = mul(high, ch, NT) + (mul(high, cl, NT) + mul(low, ch, NT) + mul(low, cl, NT))
        dist_sq = row_sq + cent_sq[0:1, to] - 2.0 * crossed
        put(to, halves(jnp.exp(jnp.sqrt(dist_sq + 1.0) * scale)))


def fill(refs, high_ref, low_ref, sq_ref):
    at = 0
    for ref in refs:
        to = pl.ds(at, ref.shape[0])
        value = ref[...]
        high_ref[to], low_ref[to] = halves(value)
        sq_ref[to] = jnp.broadcast_to(jnp.sum(value * value, axis=1, keepdims=True), (ref.shape[0], 128))
        at += ref.shape[0]


def near_body(x0, x1, own, y0, y1, c_high, c_low, c_sq, near_high, near_low, high, low, row_sq):
    fill((x0, x1, own, y0, y1), high, low, row_sq)

    def put(to, pair):
        near_high[:, to], near_low[:, to] = pair

    kernel_rows(high[...], low[...], row_sq[:, 0:1], (c_high, c_low, c_sq), put)


def near_kernels(x0, x1, own, y0, y1, cent):
    rows, width = own.shape
    total, wide = 3 * rows, cent[0].shape[0]
    return call(
        near_body,
        [shaped((total, wide), BF16)] * 2,
        (x0, x1, own, y0, y1, *cent),
        flops=8 * total * wide * width,
        scratch=[pltpu.VMEM((total, width), BF16)] * 2 + [pltpu.VMEM((total, 128), F32)],
    )


def share(w_refs, cols, k_refs, rows):
    half = w_refs[0].shape[1]
    total = None
    for i, ref in enumerate(w_refs):
        kept = pl.ds(i * half, half)
        part = mul3(halves(ref[cols]), (k_refs[0][rows, kept], k_refs[1][rows, kept]), NT)
        total = part if total is None else total + part
    return total


def stays(rows):
    return pl.ds(rows, 2 * rows), pl.ds(0, 2 * rows)


def goes(rows):
    return pl.ds(0, 2 * rows), pl.ds(rows, 2 * rows)


def keep_body(edges, rows, w0, w1, running, targets, near_high, near_low, *kept):
    for i, (a, b) in enumerate(edges):
        cols = pl.ds(a, b - a)
        value = share((w0, w1), cols, (near_high, near_low), stays(rows)[i % 2])
        own = slice(0, rows) if i % 2 == 0 else slice(rows, 2 * rows)
        other = slice(rows, 2 * rows) if i % 2 == 0 else slice(0, rows)
        kept[i][:, own] = value[:, own] + (running[cols] - targets[cols])
        kept[i][:, other] = value[:, other]


def keep_shares(edges, w0, w1, running, targets, near):
    rows = running.shape[1]
    outs = [shaped((b - a, 2 * rows)) for a, b in edges]
    flops = 12 * rows * near[0].shape[1] * w0.shape[0]
    return call(
        functools.partial(keep_body, edges, rows), outs, (w0, w1, running, targets, *near), flops
    )


def far_body(edges, low_rows, high_rows, c_high, c_low, c_sq, near_high, near_low, w0, w1, *rest):
    outs, (high, low, row_sq) = rest[:-3], rest[-3:]
    far_high, far_low, sent = outs[0], outs[1], outs[2:]
    rows = low.shape[0]
    fill((low_rows, high_rows), high, low, row_sq)
    for far, near in ((far_high, near_high), (far_low, near_low)):
        far[pl.ds(0, rows)] = near[pl.ds(0, rows)]
        far[pl.ds(2 * rows, rows)] = near[pl.ds(2 * rows, rows)]

    def put(to, pair):
        far_high[pl.ds(rows, rows), to], far_low[pl.ds(rows, rows), to] = pair

    kernel_rows(high[...], low[...], row_sq[:, 0:1], (c_high, c_low, c_sq), put)
    for i, (a, b) in enumerate(edges):
        sent[i][...] = share((w0, w1), pl.ds(a, b - a), (far_high, far_low), goes(rows)[i % 2])


def far_kernels(edges, low, high, cent, near, w0, w1):
    rows, width = 2 * low.shape[0], low.shape[1]
    wide = cent[0].shape[0]
    outs = [shaped(near[0].shape, BF16)] * 2 + [shaped((b - a, 2 * rows)) for a, b in edges]
    out = call(
        functools.partial(far_body, edges),
        outs,
        (low, high, *cent, *near, w0, w1),
        flops=8 * rows * wide * width,
        scratch=[pltpu.VMEM((rows, width), BF16)] * 2 + [pltpu.VMEM((rows, 128), F32)],
    )
    return out[:2], out[2:]


def send_body(edges, rows, w0, w1, far_high, far_low, *sent):
    for i, (a, b) in enumerate(edges):
        sent[i][...] = share((w0, w1), pl.ds(a, b - a), (far_high, far_low), goes(rows)[i % 2])


def send_shares(edges, w0, w1, far):
    rows = far[0].shape[0] // 3
    outs = [shaped((b - a, 2 * rows)) for a, b in edges]
    flops = sum(12 * rows * far[0].shape[1] * (b - a) for a, b in edges)
    return call(functools.partial(send_body, edges, rows), outs, (w0, w1, *far), flops)


def grad_body(factor, full_a, full_b, other_a, other_b, near_high, near_low, far_high, far_low, gone, here):
    rows, half = full_a.shape[1] // 2, gone.shape[1]
    at = 0
    for i, (full, other) in enumerate(((full_a, other_a), (full_b, other_b))):
        to = pl.ds(at, full.shape[0])
        at += full.shape[0]
        full_pair, other_pair = halves(full[...]), halves(other[...])
        stay, go = stays(rows)[i], goes(rows)[i]
        for out, cols in ((gone, pl.ds(half, half)), (here, pl.ds(0, half))):
            out[to] = factor * (
                mul3(full_pair, (near_high[stay, cols], near_low[stay, cols]), NN)
                + mul3(other_pair, (far_high[go, cols], far_low[go, cols]), NN)
            )


def grad_parts(factor, full, other, near, far):
    cols, half = full[0].shape[0] + full[1].shape[0], near[0].shape[1] // 2
    flops = 12 * cols * full[0].shape[1] * 2 * half
    outs = [shaped((cols, half))] * 2
    return call(functools.partial(grad_body, factor), outs, (*full, *other, *near, *far), flops)


def line_of_four(value, hop):
    pairs = ([(0, 1), (3, 2)], [(1, 2), (2, 1)], [(1, 0), (2, 3)])[hop]
    return lax.ppermute(value, "col", pairs)


def add(a, b):
    return a + b


def cut(out):
    edges, at = [], 0
    for part in ROUNDS + (1.0,):
        left = out - at
        both = left if part == 1.0 else min(left, round(out * part / 16) * 16)
        first = -(-both // 16) * 8
        edges += [(at, at + first), (at + first, at + both)]
        at += both
    return edges


def square(batch, running_t, targets_t, centers, weights_t, factor):
    rows, out = batch.shape[0], weights_t.shape[0]
    mid = rows // 2
    edges = cut(out)
    line = Line()
    x0 = swap(batch[:mid], "chip", 1)
    y1 = swap(batch[mid:], "chip", 2)
    x1 = swap(batch[mid:], "chip", 1)
    y0 = swap(batch[:mid], "chip", 2)
    cent_theirs = swap(centers, "core")
    cent = line(split_cent, centers, cent_theirs)
    w0 = weights_t
    w1 = swap(lax.optimization_barrier((weights_t, x0, y1, cent[0]))[0], "core")
    low = swap(x0, "chip", 2)
    high = swap(y1, "chip", 1)
    near = line(near_kernels, x0, x1, batch, y0, y1, cent)
    kept = line(lambda *a: keep_shares(edges, *a), w0, w1, running_t, targets_t, near)
    far, sent = line(lambda *a: far_kernels(edges[:4], *a), low, high, cent, near, w0, w1)

    axes = ((1, 2), (2, 1))

    def both(pair, step):
        return [swap(pair[i], "chip", axes[i][step]) for i in (0, 1)]

    def turned(a, b):
        return a + jnp.concatenate([b[:, rows:], b[:, :rows]], axis=1)

    rounds = len(edges) // 2
    coming, full, other, owned = [None] * rounds, [None] * rounds, [None] * rounds, [None] * rounds
    gone, here, inner, total, back = ([None] * rounds for _ in range(5))
    partial, crossing = [None] * rounds, [None] * rounds

    def do_partial(r):
        partial[r] = [line(add, kept[2 * r + i], coming[r][i]) for i in (0, 1)]
        crossing[r] = both(partial[r], 1)

    def do_full(r):
        full[r] = [line(turned, partial[r][i], crossing[r][i]) for i in (0, 1)]
        other[r] = both(full[r], 0)

    def do_grad(r):
        gone[r], here[r] = line(lambda *a: grad_parts(factor, *a), full[r], other[r], near, far)
        gone[r] = swap(gone[r], "core")

    def do_owned(r):
        owned[r] = line(add, here[r], gone[r])
        inner[r] = line_of_four(owned[r], 0)

    def do_inner(r):
        inner[r] = line(add, owned[r], inner[r])
        total[r] = line_of_four(inner[r], 1)

    def do_total(r):
        total[r] = line(add, inner[r], total[r])
        back[r] = line_of_four(total[r], 2)

    coming[0] = both(sent[0:2], 0)
    coming[1] = both(line.hold(tuple(sent[2:4])), 0)
    sent = list(sent) + list(line(lambda *a: send_shares(edges[4:], *a), w0, w1, far))
    do_partial(0)
    do_partial(1)
    do_full(0)
    coming[2] = both(line.hold(tuple(sent[4:6])), 0)
    do_full(1)
    do_grad(0)
    do_partial(2)
    coming[3] = both(line.hold(tuple(sent[6:8])), 0)
    do_owned(0)
    do_grad(1)
    do_full(2)
    do_owned(1)
    do_partial(3)
    do_inner(0)
    do_grad(2)
    do_full(3)
    do_owned(2)
    do_inner(1)
    do_total(0)
    do_grad(3)
    do_owned(3)
    do_inner(2)
    do_total(1)
    do_inner(3)
    do_total(2)
    do_total(3)

    place = lax.axis_index("col")
    ends = (place == 0) | (place == 3)
    gradient = jnp.concatenate([jnp.where(ends, b, t) for b, t in zip(back, total)])
    own = (slice(0, rows), slice(rows, None))
    residual = jnp.concatenate([f[i][:, own[i]] for f in full for i in (0, 1)])
    return gradient, residual


def any_plane(batch, running_t, targets_t, centers, weights_t, factor):
    def dot(a, b, dims, precision):
        return lax.dot_general(a, b, dims, precision=precision, preferred_element_type=F32)

    rows_here, chips = batch.shape[0], lax.axis_size("chip")
    half, out = centers.shape[0], weights_t.shape[0]
    cent = jnp.concatenate([centers, swap(centers, "core")], axis=0)
    weight = jnp.concatenate([weights_t, swap(weights_t, "core")], axis=1)
    rows = lax.all_gather(batch, "chip", axis=0, tiled=True)
    row_sq = jnp.sum(rows * rows, axis=1, keepdims=True)
    dist_sq = row_sq + jnp.sum(cent * cent, axis=1)[None, :] - 2.0 * dot(rows, cent, NT, HIGHEST)
    kernel = jnp.exp(-jnp.sqrt(dist_sq + 1.0) / (math.sqrt(rows.shape[1]) / 4.0))
    shares = dot(weight, kernel, NT, HIGH).reshape(out, chips, rows_here).transpose(1, 0, 2)
    residual = running_t - targets_t + lax.psum_scatter(shares, "chip", scatter_dimension=0, tiled=False)
    moved = lax.all_gather(residual, "chip", axis=0, tiled=False)
    moved = moved.transpose(1, 0, 2).reshape(out, chips * rows_here)
    gradient = dot(moved, kernel, NN, HIGH) * factor
    owned = gradient[:, :half] + swap(gradient[:, half:], "core")
    return lax.psum(owned, "col"), residual


def per_device(batch, running, targets, centers, weights):
    chips, depth = lax.axis_size("chip"), lax.axis_size("col")
    factor = 1.0 / math.sqrt(batch.shape[0] * chips * 2 * depth)
    plane = square if (chips, depth) == (4, 4) else any_plane
    gradient, residual = plane(batch, running.T, targets.T, centers, weights.T, factor)
    return gradient.T, residual.T


def solution(mesh):
    owners, depth = mesh.shape["row"], mesh.shape["col"]
    split = Mesh(mesh.devices.reshape(owners // 2, 2, depth), ("chip", "core", "col"))
    everywhere = P(("chip", "core", "col"), None)
    owned = P(("chip", "core"), None)
    return jax.shard_map(
        per_device,
        mesh=split,
        in_specs=(everywhere, everywhere, everywhere, owned, owned),
        out_specs=(owned, everywhere),
        check_vma=False,
    )
```

time: 199 us -> 120 us (0.60)
  waiting for transfers between devices: 116 us -> 42.5 us
  starting transfers between devices: 9.63 us -> 58 us
  blocking collectives: 31.2 us -> 0 us
  between operations: 14.1 us -> 1.27 us
  matrix products: 11.8 us -> 0 us
  Pallas kernels: 0 us -> 11.1 us
  local copies, waits for them, and re-layouts: 6.67 us -> 2.14 us
  other arithmetic: 8.89 us -> 4.6 us
    ppermute x10 -> x48, starting transfers between devices: 9.52 us -> 58 us  [the longest x36 35.7 us: swap(): return lax.ppermute(value, axis, [(i, i ^ flip) for i in range(size)])]
    all_gather x1 -> x0, waiting for transfers between devices: 35.9 us -> none  [per_device(): rows = lax.all_gather(batch, 'chip', axis=0, tiled=True)]
    unnamed x5 -> x0, waiting for transfers between devices: 34.2 us -> none
    all_gather x2 -> x0, blocking collectives: 31.2 us -> none  [per_device(): moved = lax.all_gather(residual, 'chip', axis=0, tiled=False)]
    dot_general x5 -> x0, matrix products: 11.8 us -> none  [dot(): lax.dot_general(a, b, (dims, ((), ())), precision=precision, preferred_el...]
    pallas_call x0 -> x9, Pallas kernels: none -> 11.1 us  [call(): pl.pallas_call(body, out_shape=outs, in_specs=[vmem] * len(args), out_spe...]
    ppermute x10 -> x48, waiting for transfers between devices: 46.3 us -> 42.5 us  [the longest x36 24.1 us: swap(): return lax.ppermute(value, axis, [(i, i ^ flip) for i in range(size)])]
    add x4 -> x28, other arithmetic: 0.27 us -> 3.44 us  [the longest x20 3.29 us: add(): return a + b]
  transfers between devices with their start and end apart: 13 -> 48, of which waited for: 8 -> 17; matrix products, arithmetic and copies ran while one was open for 11% -> 5% of each run, Pallas kernels for 0% -> 7%
where the time goes in v4:
time: 120 us
  starting transfers between devices  58 us (48%)
  waiting for transfers between devices  42.5 us (35%)
  Pallas kernels  11.1 us (9%)
  other arithmetic  4.6 us (4%)
  local copies, waits for them, and re-layouts  2.14 us (2%)
  between operations  1.27 us (1%)
    ppermute x36, starting transfers between devices, swap(): return lax.ppermute(value, axis, [(i, i ^ flip) for i in range(size)])  35.7 us
    ppermute x36, waiting for transfers between devices, swap(): return lax.ppermute(value, axis, [(i, i ^ flip) for i in range(size)])  24.1 us
    ppermute x12, starting transfers between devices, line_of_four(): return lax.ppermute(value, 'col', pairs)  22.3 us
    ppermute x12, waiting for transfers between devices, line_of_four(): return lax.ppermute(value, 'col', pairs)  18.4 us
    pallas_call x9, Pallas kernels, call(): pl.pallas_call(body, out_shape=outs, in_specs=[vmem] * len(args), out_spe...  11.1 us
    add x20, other arithmetic, add(): return a + b  3.29 us
  transfers between devices with their start and end apart: 48, of which 17 were waited for; matrix products, arithmetic and copies ran while one was open for 5% of the time, Pallas kernels for 7%

profile of v4, /device:TPU:0, one launch (start us, length us, event | category | flops | bytes accessed | tf_op | source)
XLA Modules:
  0.0 119.6 jit_solution(11424196202591276313)
XLA Ops:
  2.2 2.6 %collective-permute-start = (f32[64,1024]{1,0:T(8,128)S(1)}, f32[64,1024]{1,0:T(8,128)S(1)}, u32[]{:S(2)}, u32[]{:S(2)}) collective-permute-start(f32[64,1024]{1,0:T(8,128)S(1)} %get-tuple-element.309), channel_id=1, source_target_pairs={{0,8},{8,0},{16,24},{24,16},{1,9},{9,1},{17,25},{25,17},{2,10},{10... | collective-permute-start | bytes 786440 | tf_op jit(solution)/shard_map/ppermute | solution.py:21
  4.9 1.5 %collective-permute-start.1 = (f32[64,1024]{1,0:T(8,128)S(1)}, f32[64,1024]{1,0:T(8,128)S(1)}, u32[]{:S(2)}, u32[]{:S(2)}) collective-permute-start(f32[64,1024]{1,0:T(8,128)S(1)} %get-tuple-element.308), channel_id=1, source_target_pairs={{0,16},{8,24},{16,0},{24,8},{1,17},{9,25},{17,1},{25,9},{2,18},{10... | collective-permute-start | bytes 786440 | tf_op jit(solution)/shard_map/ppermute | solution.py:21
  6.9 4.9 %collective-permute-done.x0 = f32[64,1024]{1,0:T(8,128)S(1)} collective-permute-done((f32[64,1024]{1,0:T(8,128)S(1)}, f32[64,1024]{1,0:T(8,128)S(1)}, u32[]{:S(2)}, u32[]{:S(2)}) %collective-permute-start) | collective-permute-done | bytes 262176 | tf_op jit(solution)/shard_map/ppermute | solution.py:21
  13.6 1.7 %collective-permute-start.5 = (f32[64,1024]{1,0:T(8,128)S(1)}, f32[64,1024]{1,0:T(8,128)S(1)}, u32[]{:S(2)}, u32[]{:S(2)}) collective-permute-start(f32[64,1024]{1,0:T(8,128)S(1)} %get-tuple-element.309), channel_id=1, source_target_pairs={{0,16},{8,24},{16,0},{24,8},{1,17},{9,25},{17,1},{25,9},{2,18},{10... | collective-permute-start | bytes 786440 | tf_op jit(solution)/shard_map/ppermute | solution.py:21
  15.7 1.6 %collective-permute-start.7 = (f32[64,1024]{1,0:T(8,128)S(1)}, f32[64,1024]{1,0:T(8,128)S(1)}, u32[]{:S(2)}, u32[]{:S(2)}) collective-permute-start(f32[64,1024]{1,0:T(8,128)S(1)} %collective-permute-done.1.y1), channel_id=1, source_target_pairs={{0,8},{8,0},{16,24},{24,16},{1,9},{9,1},{17,25},{25,17},{2,10},{10... | collective-permute-start | bytes 786440 | tf_op jit(solution)/shard_map/ppermute | solution.py:21
  17.3 5.0 %collective-permute-done.4.x1 = f32[64,1024]{1,0:T(8,128)S(1)} collective-permute-done((f32[64,1024]{1,0:T(8,128)S(1)}, f32[64,1024]{1,0:T(8,128)S(1)}, u32[]{:S(2)}, u32[]{:S(2)}) %collective-permute-start.4) | collective-permute-done | bytes 262176 | tf_op jit(solution)/shard_map/ppermute | solution.py:21
  22.8 2.2 %shard_map.69 = (bf16[384,512]{1,0:T(8,128)(2,1)S(1)}, bf16[384,512]{1,0:T(8,128)(2,1)S(1)}) custom-call(f32[64,1024]{1,0:T(8,128)S(1)} %collective-permute-done.x0, f32[64,1024]{1,0:T(8,128)S(1)} %collective-permute-done.4.x1, f32[128,1024]{1,0:T(8,128)S(1)} %copy-done.2, f32[64,1024]{1,0:T(8,128)S(1)} %collective-permute-done.5.y0, ...), custom_call_target="tpu_custom_call" | custom-call | flops 1610612736 | bytes 4472832 | tf_op jit(solution)/shard_map/pallas_call | solution.py:55
  25.1 2.1 %shard_map.70 = (f32[160,256]{1,0:T(8,128)S(1)}, f32[160,256]{1,0:T(8,128)S(1)}, f32[160,256]{1,0:T(8,128)S(1)}, f32[160,256]{1,0:T(8,128)S(1)}, f32[120,256]{1,...) custom-call(f32[1000,256]{1,0:T(8,128)S(1)} %bitcast.7, ...), custom_call_target="tpu_custom_call" | custom-call | flops 786432000 | bytes 4882432 | tf_op jit(solution)/shard_map/pallas_call | solution.py:55
  27.7 2.6 %shard_map.71 = (bf16[384,512]{1,0:T(8,128)(2,1)S(1)}, bf16[384,512]{1,0:T(8,128)(2,1)S(1)}, f32[160,256]{1,0:T(8,128)S(1)}, f32[160,256]{1,0:T(8,128)S(1)}, f32...) custom-call(f32[64,1024]{1,0:T(8,128)S(1)} %collective-permute-done.6.low_rows, ...), custom_call_target="tpu_custom_call" | custom-call | flops 536870912 | bytes 6914048 | tf_op jit(solution)/shard_map/pallas_call | solution.py:55
  30.3 1.7 %collective-permute-start.8 = (f32[160,256]{1,0:T(8,128)S(1)}, f32[160,256]{1,0:T(8,128)S(1)}, u32[]{:S(2)}, u32[]{:S(2)}) collective-permute-start(f32[160,256]{1,0:T(8,128)S(1)} %get-tuple-element.185), channel_id=1, source_target_pairs={{0,8},{8,0},{16,24},{24,16},{1,9},{9,1},{17,25},{25,17},{2,10},{10... | collective-permute-start | bytes 491528 | tf_op jit(solution)/shard_map/ppermute | solution.py:21
  32.3 1.7 %collective-permute-start.12 = (f32[160,256]{1,0:T(8,128)S(1)}, f32[160,256]{1,0:T(8,128)}, u32[]{:S(2)}, u32[]{:S(2)}) collective-permute-start(f32[160,256]{1,0:T(8,128)S(1)} %get-tuple-element.202), channel_id=1, source_target_pairs={{0,16},{8,24},{16,0},{24,8},{1,17},{9,25},{17,1},{25,9},{2,18},{10... | collective-permute-start | bytes 491528 | tf_op jit(solution)/shard_map/ppermute | solution.py:21
  35.5 2.0 %collective-permute-done.8 = f32[160,256]{1,0:T(8,128)S(1)} collective-permute-done((f32[160,256]{1,0:T(8,128)S(1)}, f32[160,256]{1,0:T(8,128)S(1)}, u32[]{:S(2)}, u32[]{:S(2)}) %collective-permute-start.8) | collective-permute-done | bytes 163872 | tf_op jit(solution)/shard_map/ppermute | solution.py:21
  37.5 1.8 %collective-permute-start.9 = (f32[160,256]{1,0:T(8,128)S(1)}, f32[160,256]{1,0:T(8,128)}, u32[]{:S(2)}, u32[]{:S(2)}) collective-permute-start(f32[160,256]{1,0:T(8,128)S(1)} %add.84), channel_id=1, source_target_pairs={{0,16},{8,24},{16,0},{24,8},{1,17},{9,25},{17,1},{25,9},{2,18},{10... | collective-permute-start | bytes 491528 | tf_op jit(solution)/shard_map/ppermute | solution.py:21
  40.5 1.7 %collective-permute-start.13 = (f32[160,256]{1,0:T(8,128)S(1)}, f32[160,256]{1,0:T(8,128)S(1)}, u32[]{:S(2)}, u32[]{:S(2)}) collective-permute-start(f32[160,256]{1,0:T(8,128)S(1)} %add.85), channel_id=1, source_target_pairs={{0,8},{8,0},{16,24},{24,16},{1,9},{9,1},{17,25},{25,17},{2,10},{10... | collective-permute-start | bytes 491528 | tf_op jit(solution)/shard_map/ppermute | solution.py:21
  43.2 1.6 %collective-permute-start.17 = (f32[160,256]{1,0:T(8,128)S(1)}, f32[160,256]{1,0:T(8,128)S(1)}, u32[]{:S(2)}, u32[]{:S(2)}) collective-permute-start(f32[160,256]{1,0:T(8,128)S(1)} %add.86), channel_id=1, source_target_pairs={{0,16},{8,24},{16,0},{24,8},{1,17},{9,25},{17,1},{25,9},{2,18},{10... | collective-permute-start | bytes 491528 | tf_op jit(solution)/shard_map/ppermute | solution.py:21
  48.9 1.6 %collective-permute-start.15 = (f32[160,256]{1,0:T(8,128)S(1)}, f32[160,256]{1,0:T(8,128)S(1)}, u32[]{:S(2)}, u32[]{:S(2)}) collective-permute-start(f32[160,256]{1,0:T(8,128)S(1)} %maximum_add_fusion.1.full_b), channel_id=1, source_target_pairs={{0,16},{8,24},{16,0},{24,8},{1,17},{9,25},{17,1},{25,9},{2,18},{10... | collective-permute-start | bytes 491528 | tf_op jit(solution)/shard_map/ppermute | solution.py:21
  51.2 1.7 %collective-permute-done.16 = f32[160,256]{1,0:T(8,128)S(1)} collective-permute-done((f32[160,256]{1,0:T(8,128)S(1)}, f32[160,256]{1,0:T(8,128)S(1)}, u32[]{:S(2)}, u32[]{:S(2)}) %collective-permute-start.16) | collective-permute-done | bytes 163872 | tf_op jit(solution)/shard_map/ppermute | solution.py:21
  57.4 1.5 %collective-permute-done.20 = f32[120,256]{1,0:T(8,128)S(1)} collective-permute-done((f32[120,256]{1,0:T(8,128)S(1)}, f32[120,256]{1,0:T(8,128)S(1)}, u32[]{:S(2)}, u32[]{:S(2)}) %collective-permute-start.20) | collective-permute-done | bytes 122912 | tf_op jit(solution)/shard_map/ppermute | solution.py:21
  59.7 3.1 %collective-permute-done.19 = f32[120,256]{1,0:T(8,128)S(1)} collective-permute-done((f32[120,256]{1,0:T(8,128)S(1)}, f32[120,256]{1,0:T(8,128)S(1)}, u32[]{:S(2)}, u32[]{:S(2)}) %collective-permute-start.19) | collective-permute-done | bytes 122912 | tf_op jit(solution)/shard_map/ppermute | solution.py:21
  65.8 3.3 %collective-permute-start.21 = (f32[320,256]{1,0:T(8,128)S(1)}, f32[320,256]{1,0:T(8,128)S(1)}, u32[]{:S(2)}, u32[]{:S(2)}) collective-permute-start(f32[320,256]{1,0:T(8,128)S(1)} %add.94), channel_id=1, source_target_pairs={{0,1},{3,2},{4,5},{7,6},{8,9},{11,10},{12,13},{15,14},{16,17},{19,... | collective-permute-start | bytes 983048 | tf_op jit(solution)/shard_map/ppermute | solution.py:234
  81.8 5.2 %collective-permute-start.38 = (f32[240,256]{1,0:T(8,128)S(1)}, f32[240,256]{1,0:T(8,128)S(1)}, u32[]{:S(2)}, u32[]{:S(2)}) collective-permute-start(f32[240,256]{1,0:T(8,128)S(1)} %add.103), channel_id=1, source_target_pairs={{0,1},{3,2},{4,5},{7,6},{8,9},{11,10},{12,13},{15,14},{16,17},{19,... | collective-permute-start | bytes 737288 | tf_op jit(solution)/shard_map/ppermute | solution.py:234
  89.9 4.6 %collective-permute-start.44 = (f32[120,256]{1,0:T(8,128)S(1)}, f32[120,256]{1,0:T(8,128)S(1)}, u32[]{:S(2)}, u32[]{:S(2)}) collective-permute-start(f32[120,256]{1,0:T(8,128)S(1)} %add.106), channel_id=1, source_target_pairs={{0,1},{3,2},{4,5},{7,6},{8,9},{11,10},{12,13},{15,14},{16,17},{19,... | collective-permute-start | bytes 368648 | tf_op jit(solution)/shard_map/ppermute | solution.py:234
  95.3 2.1 %collective-permute-done.44 = f32[120,256]{1,0:T(8,128)S(1)} collective-permute-done((f32[120,256]{1,0:T(8,128)S(1)}, f32[120,256]{1,0:T(8,128)S(1)}, u32[]{:S(2)}, u32[]{:S(2)}) %collective-permute-start.44) | collective-permute-done | bytes 122912 | tf_op jit(solution)/shard_map/ppermute | solution.py:234
  102.2 16.2 %collective-permute-done.47 = f32[120,256]{1,0:T(8,128)S(1)} collective-permute-done((f32[120,256]{1,0:T(8,128)S(1)}, f32[120,256]{1,0:T(8,128)S(1)}, u32[]{:S(2)}, u32[]{:S(2)}) %collective-permute-start.47) | collective-permute-done | bytes 122912 | tf_op jit(solution)/shard_map/ppermute | solution.py:234
  (143 shorter events, 44.1 us)
Async XLA Ops:
  2.2 9.5 %collective-permute-start = (f32[64,1024]{1,0:T(8,128)S(1)}, f32[64,1024]{1,0:T(8,128)S(1)}, u32[]{:S(2)}, u32[]{:S(2)}) collective-permute-start(f32[64,1024]{1,0:T(8,128)S(1)} %get-tuple-element.309), channel_id=1, source_target_pairs={{0,8},{8,0},{16,24},{24,16},{1,9},{9,1},{17,25},{25,17},{2,10},{10... | collective-permute-start | bytes 786440 | tf_op jit(solution)/shard_map/ppermute | solution.py:21
  13.2 11.8 %collective-permute-start.3 = (f32[1000,256]{1,0:T(8,128)S(1)}, f32[1000,256]{1,0:T(8,128)S(1)}, u32[]{:S(2)}, u32[]{:S(2)}) collective-permute-start(f32[1000,256]{1,0:T(8,128)S(1)} %bitcast.6), channel_id=1, source_target_pairs={{0,4},{4,0},{1,5},{5,1},{2,6},{6,2},{3,7},{7,3},{8,12},{12,8},{9,1... | collective-permute-start | bytes 3072008 | tf_op jit(solution)/shard_map/ppermute | solution.py:21
  13.2 9.1 %collective-permute-start.4 = (f32[64,1024]{1,0:T(8,128)S(1)}, f32[64,1024]{1,0:T(8,128)S(1)}, u32[]{:S(2)}, u32[]{:S(2)}) collective-permute-start(f32[64,1024]{1,0:T(8,128)S(1)} %get-tuple-element.308), channel_id=1, source_target_pairs={{0,8},{8,0},{16,24},{24,16},{1,9},{9,1},{17,25},{25,17},{2,10},{10... | collective-permute-start | bytes 786440 | tf_op jit(solution)/shard_map/ppermute | solution.py:21
  13.6 9.1 %collective-permute-start.5 = (f32[64,1024]{1,0:T(8,128)S(1)}, f32[64,1024]{1,0:T(8,128)S(1)}, u32[]{:S(2)}, u32[]{:S(2)}) collective-permute-start(f32[64,1024]{1,0:T(8,128)S(1)} %get-tuple-element.309), channel_id=1, source_target_pairs={{0,16},{8,24},{16,0},{24,8},{1,17},{9,25},{17,1},{25,9},{2,18},{10... | collective-permute-start | bytes 786440 | tf_op jit(solution)/shard_map/ppermute | solution.py:21
  15.3 12.4 %collective-permute-start.6 = (f32[64,1024]{1,0:T(8,128)S(1)}, f32[64,1024]{1,0:T(8,128)S(1)}, u32[]{:S(2)}, u32[]{:S(2)}) collective-permute-start(f32[64,1024]{1,0:T(8,128)S(1)} %collective-permute-done.x0), channel_id=1, source_target_pairs={{0,16},{8,24},{16,0},{24,8},{1,17},{9,25},{17,1},{25,9},{2,18},{10... | collective-permute-start | bytes 786440 | tf_op jit(solution)/shard_map/ppermute | solution.py:21
  15.7 12.0 %collective-permute-start.7 = (f32[64,1024]{1,0:T(8,128)S(1)}, f32[64,1024]{1,0:T(8,128)S(1)}, u32[]{:S(2)}, u32[]{:S(2)}) collective-permute-start(f32[64,1024]{1,0:T(8,128)S(1)} %collective-permute-done.1.y1), channel_id=1, source_target_pairs={{0,8},{8,0},{16,24},{24,16},{1,9},{9,1},{17,25},{25,17},{2,10},{10... | collective-permute-start | bytes 786440 | tf_op jit(solution)/shard_map/ppermute | solution.py:21
  32.0 10.3 %collective-permute-start.11 = (f32[160,256]{1,0:T(8,128)S(1)}, f32[160,256]{1,0:T(8,128)}, u32[]{:S(2)}, u32[]{:S(2)}) collective-permute-start(f32[160,256]{1,0:T(8,128)S(1)} %get-tuple-element.200), channel_id=1, source_target_pairs={{0,8},{8,0},{16,24},{24,16},{1,9},{9,1},{17,25},{25,17},{2,10},{10... | collective-permute-start | bytes 491528 | tf_op jit(solution)/shard_map/ppermute | solution.py:21
  34.0 10.8 %collective-permute-start.10 = (f32[160,256]{1,0:T(8,128)S(1)}, f32[160,256]{1,0:T(8,128)}, u32[]{:S(2)}, u32[]{:S(2)}) collective-permute-start(f32[160,256]{1,0:T(8,128)S(1)} %get-tuple-element.198), channel_id=1, source_target_pairs={{0,16},{8,24},{16,0},{24,8},{1,17},{9,25},{17,1},{25,9},{2,18},{10... | collective-permute-start | bytes 491528 | tf_op jit(solution)/shard_map/ppermute | solution.py:21
  37.5 8.9 %collective-permute-start.9 = (f32[160,256]{1,0:T(8,128)S(1)}, f32[160,256]{1,0:T(8,128)}, u32[]{:S(2)}, u32[]{:S(2)}) collective-permute-start(f32[160,256]{1,0:T(8,128)S(1)} %add.84), channel_id=1, source_target_pairs={{0,16},{8,24},{16,0},{24,8},{1,17},{9,25},{17,1},{25,9},{2,18},{10... | collective-permute-start | bytes 491528 | tf_op jit(solution)/shard_map/ppermute | solution.py:21
  47.4 8.5 %collective-permute-start.14 = (f32[160,256]{1,0:T(8,128)S(1)}, f32[160,256]{1,0:T(8,128)S(1)}, u32[]{:S(2)}, u32[]{:S(2)}) collective-permute-start(f32[160,256]{1,0:T(8,128)S(1)} %maximum_add_fusion.full_a), channel_id=1, source_target_pairs={{0,8},{8,0},{16,24},{24,16},{1,9},{9,1},{17,25},{25,17},{2,10},{10... | collective-permute-start | bytes 491528 | tf_op jit(solution)/shard_map/ppermute | solution.py:21
  50.5 15.2 %collective-permute-start.24 = (f32[160,256]{1,0:T(8,128)S(1)}, f32[160,256]{1,0:T(8,128)S(1)}, u32[]{:S(2)}, u32[]{:S(2)}) collective-permute-start(f32[160,256]{1,0:T(8,128)S(1)} %maximum_add_fusion.2.full_a), channel_id=1, source_target_pairs={{0,8},{8,0},{16,24},{24,16},{1,9},{9,1},{17,25},{25,17},{2,10},{10... | collective-permute-start | bytes 491528 | tf_op jit(solution)/shard_map/ppermute | solution.py:21
  53.5 11.5 %collective-permute-start.25 = (f32[160,256]{1,0:T(8,128)S(1)}, f32[160,256]{1,0:T(8,128)S(1)}, u32[]{:S(2)}, u32[]{:S(2)}) collective-permute-start(f32[160,256]{1,0:T(8,128)S(1)} %maximum_add_fusion.3.full_b), channel_id=1, source_target_pairs={{0,16},{8,24},{16,0},{24,8},{1,17},{9,25},{17,1},{25,9},{2,18},{10... | collective-permute-start | bytes 491528 | tf_op jit(solution)/shard_map/ppermute | solution.py:21
  59.0 10.8 %collective-permute-start.28 = (f32[120,256]{1,0:T(8,128)S(1)}, f32[120,256]{1,0:T(8,128)S(1)}, u32[]{:S(2)}, u32[]{:S(2)}) collective-permute-start(f32[120,256]{1,0:T(8,128)S(1)} %add.92), channel_id=1, source_target_pairs={{0,16},{8,24},{16,0},{24,8},{1,17},{9,25},{17,1},{25,9},{2,18},{10... | collective-permute-start | bytes 368648 | tf_op jit(solution)/shard_map/ppermute | solution.py:21
  64.0 9.1 %collective-permute-start.23 = (f32[64,256]{1,0:T(8,128)S(1)}, f32[64,256]{1,0:T(8,128)S(1)}, u32[]{:S(2)}, u32[]{:S(2)}) collective-permute-start(f32[64,256]{1,0:T(8,128)S(1)} %get-tuple-element.243), channel_id=1, source_target_pairs={{0,8},{8,0},{16,24},{24,16},{1,9},{9,1},{17,25},{25,17},{2,10},{10... | collective-permute-start | bytes 196616 | tf_op jit(solution)/shard_map/ppermute | solution.py:21
  65.0 8.7 %collective-permute-start.22 = (f32[56,256]{1,0:T(8,128)S(1)}, f32[56,256]{1,0:T(8,128)S(1)}, u32[]{:S(2)}, u32[]{:S(2)}) collective-permute-start(f32[56,256]{1,0:T(8,128)S(1)} %get-tuple-element.241), channel_id=1, source_target_pairs={{0,16},{8,24},{16,0},{24,8},{1,17},{9,25},{17,1},{25,9},{2,18},{10... | collective-permute-start | bytes 172040 | tf_op jit(solution)/shard_map/ppermute | solution.py:21
  65.8 9.3 %collective-permute-start.21 = (f32[320,256]{1,0:T(8,128)S(1)}, f32[320,256]{1,0:T(8,128)S(1)}, u32[]{:S(2)}, u32[]{:S(2)}) collective-permute-start(f32[320,256]{1,0:T(8,128)S(1)} %add.94), channel_id=1, source_target_pairs={{0,1},{3,2},{4,5},{7,6},{8,9},{11,10},{12,13},{15,14},{16,17},{19,... | collective-permute-start | bytes 983048 | tf_op jit(solution)/shard_map/ppermute | solution.py:234
  73.7 13.3 %collective-permute-start.30 = (f32[320,256]{1,0:T(8,128)S(1)}, f32[320,256]{1,0:T(8,128)S(1)}, u32[]{:S(2)}, u32[]{:S(2)}) collective-permute-start(f32[320,256]{1,0:T(8,128)S(1)} %add.97), channel_id=1, source_target_pairs={{0,1},{3,2},{4,5},{7,6},{8,9},{11,10},{12,13},{15,14},{16,17},{19,... | collective-permute-start | bytes 983048 | tf_op jit(solution)/shard_map/ppermute | solution.py:234
  77.6 10.1 %collective-permute-start.29 = (f32[320,256]{1,0:T(8,128)S(1)}, f32[320,256]{1,0:T(8,128)S(1)}, u32[]{:S(2)}, u32[]{:S(2)}) collective-permute-start(f32[320,256]{1,0:T(8,128)S(1)} %add.100), channel_id=1, source_target_pairs={{1,2},{2,1},{5,6},{6,5},{9,10},{10,9},{13,14},{14,13},{17,18},{18,... | collective-permute-start | bytes 983048 | tf_op jit(solution)/shard_map/ppermute | solution.py:234
  79.0 8.8 %collective-permute-start.39 = (f32[64,256]{1,0:T(8,128)S(1)}, f32[64,256]{1,0:T(8,128)S(1)}, u32[]{:S(2)}, u32[]{:S(2)}) collective-permute-start(f32[64,256]{1,0:T(8,128)S(1)} %maximum_add_fusion.6.full_a), channel_id=1, source_target_pairs={{0,8},{8,0},{16,24},{24,16},{1,9},{9,1},{17,25},{25,17},{2,10},{10... | collective-permute-start | bytes 196616 | tf_op jit(solution)/shard_map/ppermute | solution.py:21
  81.8 12.7 %collective-permute-start.38 = (f32[240,256]{1,0:T(8,128)S(1)}, f32[240,256]{1,0:T(8,128)S(1)}, u32[]{:S(2)}, u32[]{:S(2)}) collective-permute-start(f32[240,256]{1,0:T(8,128)S(1)} %add.103), channel_id=1, source_target_pairs={{0,1},{3,2},{4,5},{7,6},{8,9},{11,10},{12,13},{15,14},{16,17},{19,... | collective-permute-start | bytes 737288 | tf_op jit(solution)/shard_map/ppermute | solution.py:234
  88.6 13.5 %collective-permute-start.36 = (f32[320,256]{1,0:T(8,128)S(1)}, f32[320,256]{1,0:T(8,128)S(1)}, u32[]{:S(2)}, u32[]{:S(2)}) collective-permute-start(f32[320,256]{1,0:T(8,128)S(1)} %add.105), channel_id=1, source_target_pairs={{1,0},{2,3},{5,4},{6,7},{9,8},{10,11},{13,12},{14,15},{17,16},{18,... | collective-permute-start | bytes 983048 | tf_op jit(solution)/shard_map/ppermute | solution.py:234
  98.1 20.4 %collective-permute-start.42 = (f32[320,256]{1,0:T(8,128)S(1)}, f32[320,256]{1,0:T(8,128)S(1)}, u32[]{:S(2)}, u32[]{:S(2)}) collective-permute-start(f32[320,256]{1,0:T(8,128)S(1)} %add.108), channel_id=1, source_target_pairs={{1,0},{2,3},{5,4},{6,7},{9,8},{10,11},{13,12},{14,15},{17,16},{18,... | collective-permute-start | bytes 983048 | tf_op jit(solution)/shard_map/ppermute | solution.py:234
  99.5 19.0 %collective-permute-start.45 = (f32[240,256]{1,0:T(8,128)S(1)}, f32[240,256]{1,0:T(8,128)S(1)}, u32[]{:S(2)}, u32[]{:S(2)}) collective-permute-start(f32[240,256]{1,0:T(8,128)S(1)} %add.110), channel_id=1, source_target_pairs={{1,0},{2,3},{5,4},{6,7},{9,8},{10,11},{13,12},{14,15},{17,16},{18,... | collective-permute-start | bytes 737288 | tf_op jit(solution)/shard_map/ppermute | solution.py:234
  100.8 17.6 %collective-permute-start.47 = (f32[120,256]{1,0:T(8,128)S(1)}, f32[120,256]{1,0:T(8,128)S(1)}, u32[]{:S(2)}, u32[]{:S(2)}) collective-permute-start(f32[120,256]{1,0:T(8,128)S(1)} %add.111), channel_id=1, source_target_pairs={{1,0},{2,3},{5,4},{6,7},{9,8},{10,11},{13,12},{14,15},{17,16},{18,... | collective-permute-start | bytes 368648 | tf_op jit(solution)/shard_map/ppermute | solution.py:234
  (30 other events, 186.1 us)

commit v5 on v4

--- a/solution.py
+++ b/solution.py
@@ -10,7 +10,7 @@
 
 HIGHEST = lax.Precision.HIGHEST
 HIGH = lax.Precision.HIGH
-ROUNDS = (0.32, 0.32, 0.24)
+ROUNDS = (0.52,)
 BF16, F32 = jnp.bfloat16, jnp.float32
 NT = (((1,), (1,)), ((), ()))
 NN = (((1,), (0,)), ((), ()))
@@ -50,7 +50,6 @@
 
 
 def call(body, outs, args, flops=0, scratch=(), aliases=None):
-    moved = sum(x.size * x.dtype.itemsize for x in (*args, *outs))
     vmem = pl.BlockSpec(memory_space=pltpu.VMEM)
     return pl.pallas_call(
         body,
@@ -59,7 +58,7 @@
         out_specs=[vmem] * len(outs),
         scratch_shapes=list(scratch),
         input_output_aliases=aliases or {},
-        cost_estimate=pl.CostEstimate(flops=flops, bytes_accessed=moved, transcendentals=0),
+        cost_estimate=pl.CostEstimate(flops=flops // 2**20, bytes_accessed=0, transcendentals=0),
         compiler_params=pltpu.CompilerParams(vmem_limit_bytes=40 * 2**20),
     )(*args)
 
@@ -106,24 +105,54 @@
         at += ref.shape[0]
 
 
-def near_body(x0, x1, own, y0, y1, c_high, c_low, c_sq, near_high, near_low, high, low, row_sq):
-    fill((x0, x1, own, y0, y1), high, low, row_sq)
+def own_body(own, c_high, c_low, c_sq, own_high, own_low, high, low, row_sq):
+    fill((own,), high, low, row_sq)
 
     def put(to, pair):
-        near_high[:, to], near_low[:, to] = pair
+        own_high[:, to], own_low[:, to] = pair
 
     kernel_rows(high[...], low[...], row_sq[:, 0:1], (c_high, c_low, c_sq), put)
 
 
-def near_kernels(x0, x1, own, y0, y1, cent):
+def row_scratch(rows, width):
+    return [pltpu.VMEM((rows, width), BF16)] * 2 + [pltpu.VMEM((rows, 128), F32)]
+
+
+def own_kernels(own, cent):
     rows, width = own.shape
-    total, wide = 3 * rows, cent[0].shape[0]
+    wide = cent[0].shape[0]
+    return call(
+        own_body,
+        [shaped((rows, wide), BF16)] * 2,
+        (own, *cent),
+        flops=8 * rows * wide * width,
+        scratch=row_scratch(rows, width),
+    )
+
+
+def near_body(x, y, c_high, c_low, c_sq, own_high, own_low, near_high, near_low, high, low, row_sq):
+    rows = x.shape[0]
+    fill((x, y), high, low, row_sq)
+    near_high[pl.ds(rows, rows)] = own_high[...]
+    near_low[pl.ds(rows, rows)] = own_low[...]
+
+    def put(to, pair):
+        for ref, value in zip((near_high, near_low), pair):
+            ref[pl.ds(0, rows), to] = value[:rows]
+            ref[pl.ds(2 * rows, rows), to] = value[rows:]
+
+    kernel_rows(high[...], low[...], row_sq[:, 0:1], (c_high, c_low, c_sq), put)
+
+
+def near_kernels(x, y, cent, own):
+    rows, width = x.shape
+    wide = cent[0].shape[0]
     return call(
         near_body,
-        [shaped((total, wide), BF16)] * 2,
-        (x0, x1, own, y0, y1, *cent),
-        flops=8 * total * wide * width,
-        scratch=[pltpu.VMEM((total, width), BF16)] * 2 + [pltpu.VMEM((total, 128), F32)],
+        [shaped((3 * rows, wide), BF16)] * 2,
+        (x, y, *cent, *own),
+        flops=16 * rows * wide * width,
+        scratch=row_scratch(2 * rows, width),
     )
 
 
@@ -190,7 +219,7 @@
         outs,
         (low, high, *cent, *near, w0, w1),
         flops=8 * rows * wide * width,
-        scratch=[pltpu.VMEM((rows, width), BF16)] * 2 + [pltpu.VMEM((rows, 128), F32)],
+        scratch=row_scratch(rows, width),
     )
     return out[:2], out[2:]
 
@@ -229,9 +258,12 @@
     return call(functools.partial(grad_body, factor), outs, (*full, *other, *near, *far), flops)
 
 
-def line_of_four(value, hop):
-    pairs = ([(0, 1), (3, 2)], [(1, 2), (2, 1)], [(1, 0), (2, 3)])[hop]
+def pass_line(value, pairs):
     return lax.ppermute(value, "col", pairs)
+
+
+BESIDE = [(0, 1), (1, 0), (2, 3), (3, 2)]
+ACROSS = [(0, 3), (3, 0), (1, 2), (2, 1)]
 
 
 def add(a, b):
@@ -251,24 +283,24 @@
 
 def square(batch, running_t, targets_t, centers, weights_t, factor):
     rows, out = batch.shape[0], weights_t.shape[0]
-    mid = rows // 2
+    mid, quarter = rows // 2, centers.shape[0] // 2
     edges = cut(out)
+    rounds = len(edges) // 2
     line = Line()
-    x0 = swap(batch[:mid], "chip", 1)
-    y1 = swap(batch[mid:], "chip", 2)
-    x1 = swap(batch[mid:], "chip", 1)
-    y0 = swap(batch[:mid], "chip", 2)
+    block_x = swap(batch, "chip", 1)
+    block_y = swap(batch, "chip", 2)
     cent_theirs = swap(centers, "core")
+    w0, w1 = weights_t, swap(weights_t, "core")
     cent = line(split_cent, centers, cent_theirs)
-    w0 = weights_t
-    w1 = swap(lax.optimization_barrier((weights_t, x0, y1, cent[0]))[0], "core")
-    low = swap(x0, "chip", 2)
-    high = swap(y1, "chip", 1)
-    near = line(near_kernels, x0, x1, batch, y0, y1, cent)
-    kept = line(lambda *a: keep_shares(edges, *a), w0, w1, running_t, targets_t, near)
+    own = line(own_kernels, batch, cent)
+    low = swap(block_x[:mid], "chip", 2)
+    high = swap(block_y[mid:], "chip", 1)
+    near = line(near_kernels, block_x, block_y, cent, own)
     far, sent = line(lambda *a: far_kernels(edges[:4], *a), low, high, cent, near, w0, w1)
 
     axes = ((1, 2), (2, 1))
+    place = lax.axis_index("col")
+    ends = (place == 0) | (place == 3)
 
     def both(pair, step):
         return [swap(pair[i], "chip", axes[i][step]) for i in (0, 1)]
@@ -276,10 +308,8 @@
     def turned(a, b):
         return a + jnp.concatenate([b[:, rows:], b[:, :rows]], axis=1)
 
-    rounds = len(edges) // 2
-    coming, full, other, owned = [None] * rounds, [None] * rounds, [None] * rounds, [None] * rounds
-    gone, here, inner, total, back = ([None] * rounds for _ in range(5))
-    partial, crossing = [None] * rounds, [None] * rounds
+    coming, crossing, beside, across, back = ([None] * rounds for _ in range(5))
+    partial, full, other, gone, here, mine, total = ([None] * rounds for _ in range(7))
 
     def do_partial(r):
         partial[r] = [line(add, kept[2 * r + i], coming[r][i]) for i in (0, 1)]
@@ -293,53 +323,58 @@
         gone[r], here[r] = line(lambda *a: grad_parts(factor, *a), full[r], other[r], near, far)
         gone[r] = swap(gone[r], "core")
 
+    def split(a, b):
+        first, second = a[:, :quarter] + b[:, :quarter], a[:, quarter:] + b[:, quarter:]
+        return jnp.where(ends, second, first), jnp.where(ends, first, second)
+
     def do_owned(r):
-        owned[r] = line(add, here[r], gone[r])
-        inner[r] = line_of_four(owned[r], 0)
-
-    def do_inner(r):
-        inner[r] = line(add, owned[r], inner[r])
-        total[r] = line_of_four(inner[r], 1)
+        sends, mine[r] = line(split, here[r], gone[r])
+        beside[r] = pass_line(sends, BESIDE)
+
+    def do_mine(r):
+        mine[r] = line(add, mine[r], beside[r])
+        across[r] = pass_line(mine[r], ACROSS)
 
     def do_total(r):
-        total[r] = line(add, inner[r], total[r])
-        back[r] = line_of_four(total[r], 2)
+        total[r] = line(add, mine[r], across[r])
+        back[r] = pass_line(total[r], BESIDE)
 
     coming[0] = both(sent[0:2], 0)
     coming[1] = both(line.hold(tuple(sent[2:4])), 0)
-    sent = list(sent) + list(line(lambda *a: send_shares(edges[4:], *a), w0, w1, far))
+    kept = line(lambda *a: keep_shares(edges, *a), w0, w1, running_t, targets_t, near)
+    if rounds == 3:
+        sent = list(sent) + list(line(lambda *a: send_shares(edges[4:], *a), w0, w1, far))
     do_partial(0)
     do_partial(1)
     do_full(0)
-    coming[2] = both(line.hold(tuple(sent[4:6])), 0)
+    if rounds == 3:
+        coming[2] = both(line.hold(tuple(sent[4:6])), 0)
     do_full(1)
     do_grad(0)
-    do_partial(2)
-    coming[3] = both(line.hold(tuple(sent[6:8])), 0)
     do_owned(0)
+    if rounds == 3:
+        do_partial(2)
     do_grad(1)
-    do_full(2)
     do_owned(1)
-    do_partial(3)
-    do_inner(0)
-    do_grad(2)
-    do_full(3)
-    do_owned(2)
-    do_inner(1)
+    if rounds == 3:
+        do_full(2)
+    do_mine(0)
+    if rounds == 3:
+        do_grad(2)
+        do_owned(2)
+    do_mine(1)
     do_total(0)
-    do_grad(3)
-    do_owned(3)
-    do_inner(2)
+    if rounds == 3:
+        do_mine(2)
     do_total(1)
-    do_inner(3)
-    do_total(2)
-    do_total(3)
-
-    place = lax.axis_index("col")
-    ends = (place == 0) | (place == 3)
-    gradient = jnp.concatenate([jnp.where(ends, b, t) for b, t in zip(back, total)])
-    own = (slice(0, rows), slice(rows, None))
-    residual = jnp.concatenate([f[i][:, own[i]] for f in full for i in (0, 1)])
+    if rounds == 3:
+        do_total(2)
+
+    first = [jnp.where(ends, t, b) for t, b in zip(total, back)]
+    second = [jnp.where(ends, b, t) for t, b in zip(total, back)]
+    gradient = jnp.concatenate([jnp.concatenate(first), jnp.concatenate(second)], axis=1)
+    mine_rows = (slice(0, rows), slice(rows, None))
+    residual = jnp.concatenate([f[i][:, mine_rows[i]] for f in full for i in (0, 1)])
     return gradient, residual
 
 

time: 120 us -> 117 us (0.975)
  waiting for transfers between devices: 42.5 us -> 70.8 us
  starting transfers between devices: 58 us -> 31 us
  local copies, waits for them, and re-layouts: 2.14 us -> 0.17 us
    ppermute x36 -> x20, starting transfers between devices: 35.7 us -> 21 us  [swap(): return lax.ppermute(value, axis, [(i, i ^ flip) for i in range(size)])]
    ppermute x12 -> x6, waiting for transfers between devices: 18.4 us -> 33 us  [pass_line(): return lax.ppermute(value, 'col', pairs)]
    ppermute x36 -> x20, waiting for transfers between devices: 24.1 us -> 37.8 us  [swap(): return lax.ppermute(value, axis, [(i, i ^ flip) for i in range(size)])]
    ppermute x12 -> x6, starting transfers between devices: 22.3 us -> 10 us  [pass_line(): return lax.ppermute(value, 'col', pairs)]
    add x20 -> x8, other arithmetic: 3.29 us -> 0.27 us  [add(): return a + b]
    pallas_call x9 -> x7, Pallas kernels: 11.1 us -> 10.1 us  [call(): pl.pallas_call(body, out_shape=outs, in_specs=[vmem] * len(args), out_spe...]
  transfers between devices with their start and end apart: 48 -> 26, of which waited for: 17 -> 17; matrix products, arithmetic and copies ran while one was open for 5% -> 2% of each run, Pallas kernels for 7% -> 4%
where the time goes in v5:
time: 117 us; the launch traced here: 116 us
  waiting for transfers between devices  70.8 us (61%)
  starting transfers between devices  31 us (26%)
  Pallas kernels  10.1 us (9%)
  other arithmetic  3.53 us (3%)
    ppermute x20, waiting for transfers between devices, swap(): return lax.ppermute(value, axis, [(i, i ^ flip) for i in range(size)])  37.8 us
    ppermute x6, waiting for transfers between devices, pass_line(): return lax.ppermute(value, 'col', pairs)  33 us
    ppermute x20, starting transfers between devices, swap(): return lax.ppermute(value, axis, [(i, i ^ flip) for i in range(size)])  21 us
    pallas_call x7, Pallas kernels, call(): pl.pallas_call(body, out_shape=outs, in_specs=[vmem] * len(args), out_spe...  10.1 us
    ppermute x6, starting transfers between devices, pass_line(): return lax.ppermute(value, 'col', pairs)  10 us
  transfers between devices with their start and end apart: 26, of which 17 were waited for; matrix products, arithmetic and copies ran while one was open for 2% of the time, Pallas kernels for 4%

profile of v5, /device:TPU:0, one launch (start us, length us, event | category | flops | bytes accessed | tf_op | source)
XLA Modules:
  0.0 116.5 jit_solution(1460370698627390782)
XLA Ops:
  1.2 2.9 %collective-permute-start.1 = (f32[128,1024]{1,0:T(8,128)}, f32[128,1024]{1,0:T(8,128)S(1)}, u32[]{:S(2)}, u32[]{:S(2)}) collective-permute-start(f32[128,1024]{1,0:T(8,128)} %own), channel_id=1, source_target_pairs={{0,8},{8,0},{16,24},{24,16},{1,9},{9,1},{17,25},{25,17},{2,10},{10... | collective-permute-start | bytes 1572872 | tf_op jit(solution)/shard_map/ppermute | solution.py:21
  5.7 10.9 %collective-permute-done.1.x = f32[128,1024]{1,0:T(8,128)S(1)} collective-permute-done((f32[128,1024]{1,0:T(8,128)}, f32[128,1024]{1,0:T(8,128)S(1)}, u32[]{:S(2)}, u32[]{:S(2)}) %collective-permute-start.1) | collective-permute-done | bytes 524320 | tf_op jit(solution)/shard_map/ppermute | solution.py:21
  16.6 1.8 %collective-permute-start.4 = (f32[64,1024]{1,0:T(8,128)S(1)}, f32[64,1024]{1,0:T(8,128)S(1)}, u32[]{:S(2)}, u32[]{:S(2)}) collective-permute-start(f32[64,1024]{1,0:T(8,128)S(1)} %slice.88), channel_id=1, source_target_pairs={{0,16},{8,24},{16,0},{24,8},{1,17},{9,25},{17,1},{25,9},{2,18},{10... | collective-permute-start | bytes 786440 | tf_op jit(solution)/shard_map/ppermute | solution.py:21
  18.4 1.6 %collective-permute-start.5 = (f32[64,1024]{1,0:T(8,128)S(1)}, f32[64,1024]{1,0:T(8,128)S(1)}, u32[]{:S(2)}, u32[]{:S(2)}) collective-permute-start(f32[64,1024]{1,0:T(8,128)S(1)} %slice.89), channel_id=1, source_target_pairs={{0,8},{8,0},{16,24},{24,16},{1,9},{9,1},{17,25},{25,17},{2,10},{10... | collective-permute-start | bytes 786440 | tf_op jit(solution)/shard_map/ppermute | solution.py:21
  20.5 1.7 %shard_map.69 = (bf16[128,512]{1,0:T(8,128)(2,1)S(1)}, bf16[128,512]{1,0:T(8,128)(2,1)S(1)}) custom-call(f32[128,1024]{1,0:T(8,128)S(1)} %copy-done.2, bf16[512,1024]{1,0:T(8,128)(2,1)S(1)} %get-tuple-element.115.c_high, bf16[512,1024]{1,0:T(8,128)(2,1)S(1)} %get-tuple-element.116.c_low, f32[8,512]{1,0:T(8,128)S(1)} %get-tuple-element.117.c_sq), custom_call_target="tpu_custom_call" | custom-call | flops 512 | tf_op jit(solution)/shard_map/pallas_call | solution.py:54
  22.2 1.6 %shard_map.70 = (bf16[384,512]{1,0:T(8,128)(2,1)S(1)}, bf16[384,512]{1,0:T(8,128)(2,1)S(1)}) custom-call(f32[128,1024]{1,0:T(8,128)S(1)} %collective-permute-done.1.x, f32[128,1024]{1,0:T(8,128)S(1)} %collective-permute-done.2.y, bf16[512,1024]{1,0:T(8,128)(2,1)S(1)} %get-tuple-element.115.c_high, bf16[512,1024]{1,0:T(8,128)(2,1)S(1)} %get-tuple-element.116.c_low, ...), custom_call_target="tpu_custom_call" | custom-call | flops 1024 | tf_op jit(solution)/shard_map/pallas_call | solution.py:54
  25.7 2.6 %shard_map.71 = (bf16[384,512]{1,0:T(8,128)(2,1)S(1)}, bf16[384,512]{1,0:T(8,128)(2,1)S(1)}, f32[256,256]{1,0:T(8,128)S(1)}, f32[256,256]{1,0:T(8,128)S(1)}, f32...) custom-call(f32[64,1024]{1,0:T(8,128)S(1)} %collective-permute-done.4.low_rows, ...), custom_call_target="tpu_custom_call" | custom-call | flops 512 | tf_op jit(solution)/shard_map/pallas_call | solution.py:54
  31.4 3.3 %collective-permute-done.6 = f32[256,256]{1,0:T(8,128)S(1)} collective-permute-done((f32[256,256]{1,0:T(8,128)S(1)}, f32[256,256]{1,0:T(8,128)S(1)}, u32[]{:S(2)}, u32[]{:S(2)}) %collective-permute-start.6) | collective-permute-done | bytes 262176 | tf_op jit(solution)/shard_map/ppermute | solution.py:21
  36.8 1.6 %collective-permute-start.8 = (f32[240,256]{1,0:T(8,128)S(1)}, f32[240,256]{1,0:T(8,128)S(1)}, u32[]{:S(2)}, u32[]{:S(2)}) collective-permute-start(f32[240,256]{1,0:T(8,128)S(1)} %get-tuple-element.136), channel_id=1, source_target_pairs={{0,16},{8,24},{16,0},{24,8},{1,17},{9,25},{17,1},{25,9},{2,18},{10... | collective-permute-start | bytes 737288 | tf_op jit(solution)/shard_map/ppermute | solution.py:21
  39.0 4.3 %collective-permute-done.9 = f32[248,256]{1,0:T(8,128)S(1)} collective-permute-done((f32[248,256]{1,0:T(8,128)S(1)}, f32[248,256]{1,0:T(8,128)S(1)}, u32[]{:S(2)}, u32[]{:S(2)}) %collective-permute-start.9) | collective-permute-done | bytes 253984 | tf_op jit(solution)/shard_map/ppermute | solution.py:21
  44.4 4.9 %collective-permute-done.8 = f32[240,256]{1,0:T(8,128)S(1)} collective-permute-done((f32[240,256]{1,0:T(8,128)S(1)}, f32[240,256]{1,0:T(8,128)S(1)}, u32[]{:S(2)}, u32[]{:S(2)}) %collective-permute-start.8) | collective-permute-done | bytes 245792 | tf_op jit(solution)/shard_map/ppermute | solution.py:21
  49.4 1.7 %collective-permute-start.14 = (f32[240,256]{1,0:T(8,128)S(1)}, f32[240,256]{1,0:T(8,128)S(1)}, u32[]{:S(2)}, u32[]{:S(2)}) collective-permute-start(f32[240,256]{1,0:T(8,128)S(1)} %add.51), channel_id=1, source_target_pairs={{0,8},{8,0},{16,24},{24,16},{1,9},{9,1},{17,25},{25,17},{2,10},{10... | collective-permute-start | bytes 737288 | tf_op jit(solution)/shard_map/ppermute | solution.py:21
  52.8 2.0 %collective-permute-done.15 = f32[248,256]{1,0:T(8,128)S(1)} collective-permute-done((f32[248,256]{1,0:T(8,128)S(1)}, f32[248,256]{1,0:T(8,128)S(1)}, u32[]{:S(2)}, u32[]{:S(2)}) %collective-permute-start.15) | collective-permute-done | bytes 253984 | tf_op jit(solution)/shard_map/ppermute | solution.py:21
  55.8 2.4 %collective-permute-done.13.other_b = f32[256,256]{1,0:T(8,128)S(1)} collective-permute-done((f32[256,256]{1,0:T(8,128)S(1)}, f32[256,256]{1,0:T(8,128)S(1)}, u32[]{:S(2)}, u32[]{:S(2)}) %collective-permute-start.13) | collective-permute-done | bytes 262176 | tf_op jit(solution)/shard_map/ppermute | solution.py:21
  58.6 1.8 %shard_map.73 = (f32[512,256]{1,0:T(8,128)}, f32[512,256]{1,0:T(8,128)S(1)}) custom-call(f32[256,256]{1,0:T(8,128)S(1)} %maximum_add_fusion.full_a, f32[256,256]{1,0:T(8,128)S(1)} %maximum_add_fusion.1.full_b, f32[256,256]{1,0:T(8,128)S(1)} %collective-permute-done.12.other_a, f32[256,256]{1,0:T(8,128)S(1)} %collective-permute-done.13.other_b, ...), custom_call_target="tpu_custom_call" | custom-call | flops 768 | tf_op jit(solution)/shard_map/pallas_call | solution.py:54
  63.7 6.2 %collective-permute-done.19.other_b = f32[240,256]{1,0:T(8,128)S(1)} collective-permute-done((f32[240,256]{1,0:T(8,128)S(1)}, f32[240,256]{1,0:T(8,128)S(1)}, u32[]{:S(2)}, u32[]{:S(2)}) %collective-permute-start.19) | collective-permute-done | bytes 245792 | tf_op jit(solution)/shard_map/ppermute | solution.py:21
  71.0 1.6 %collective-permute-start.17 = (f32[512,128]{1,0:T(8,128)S(1)}, f32[512,128]{1,0:T(8,128)S(1)}, u32[]{:S(2)}, u32[]{:S(2)}) collective-permute-start(f32[512,128]{1,0:T(8,128)S(1)} %get-tuple-element.189), channel_id=1, source_target_pairs={{0,1},{1,0},{2,3},{3,2},{4,5},{5,4},{6,7},{7,6},{8,9},{9,8},{10,11... | collective-permute-start | bytes 786440 | tf_op jit(solution)/shard_map/ppermute | solution.py:262
  72.9 6.8 %collective-permute-done.17 = f32[512,128]{1,0:T(8,128)S(1)} collective-permute-done((f32[512,128]{1,0:T(8,128)S(1)}, f32[512,128]{1,0:T(8,128)S(1)}, u32[]{:S(2)}, u32[]{:S(2)}) %collective-permute-start.17) | collective-permute-done | bytes 262176 | tf_op jit(solution)/shard_map/ppermute | solution.py:262
  79.7 3.7 %collective-permute-start.21 = (f32[512,128]{1,0:T(8,128)S(1)}, f32[512,128]{1,0:T(8,128)S(1)}, u32[]{:S(2)}, u32[]{:S(2)}) collective-permute-start(f32[512,128]{1,0:T(8,128)S(1)} %add.60), channel_id=1, source_target_pairs={{0,3},{3,0},{1,2},{2,1},{4,7},{7,4},{5,6},{6,5},{8,11},{11,8},{9,1... | collective-permute-start | bytes 786440 | tf_op jit(solution)/shard_map/ppermute | solution.py:262
  83.4 11.6 %collective-permute-done.22 = f32[488,128]{1,0:T(8,128)S(1)} collective-permute-done((f32[488,128]{1,0:T(8,128)S(1)}, f32[488,128]{1,0:T(8,128)S(1)}, u32[]{:S(2)}, u32[]{:S(2)}) %collective-permute-start.22) | collective-permute-done | bytes 249888 | tf_op jit(solution)/shard_map/ppermute | solution.py:262
  95.1 1.8 %collective-permute-start.23 = (f32[512,128]{1,0:T(8,128)S(1)}, f32[512,128]{1,0:T(8,128)S(1)}, u32[]{:S(2)}, u32[]{:S(2)}) collective-permute-start(f32[512,128]{1,0:T(8,128)S(1)} %add.62), channel_id=1, source_target_pairs={{0,1},{1,0},{2,3},{3,2},{4,5},{5,4},{6,7},{7,6},{8,9},{9,8},{10,11... | collective-permute-start | bytes 786440 | tf_op jit(solution)/shard_map/ppermute | solution.py:262
  98.3 9.6 %collective-permute-done.24 = f32[488,128]{1,0:T(8,128)S(1)} collective-permute-done((f32[488,128]{1,0:T(8,128)S(1)}, f32[488,128]{1,0:T(8,128)S(1)}, u32[]{:S(2)}, u32[]{:S(2)}) %collective-permute-start.24) | collective-permute-done | bytes 249888 | tf_op jit(solution)/shard_map/ppermute | solution.py:262
  107.9 2.4 %collective-permute-start.25 = (f32[488,128]{1,0:T(8,128)S(1)}, f32[488,128]{1,0:T(8,128)S(1)}, u32[]{:S(2)}, u32[]{:S(2)}) collective-permute-start(f32[488,128]{1,0:T(8,128)S(1)} %add.63), channel_id=1, source_target_pairs={{0,1},{1,0},{2,3},{3,2},{4,5},{5,4},{6,7},{7,6},{8,9},{9,8},{10,11... | collective-permute-start | bytes 749576 | tf_op jit(solution)/shard_map/ppermute | solution.py:262
  110.4 5.0 %collective-permute-done.25 = f32[488,128]{1,0:T(8,128)S(1)} collective-permute-done((f32[488,128]{1,0:T(8,128)S(1)}, f32[488,128]{1,0:T(8,128)S(1)}, u32[]{:S(2)}, u32[]{:S(2)}) %collective-permute-start.25) | collective-permute-done | bytes 249888 | tf_op jit(solution)/shard_map/ppermute | solution.py:262
  (73 shorter events, 21.9 us)
Async XLA Ops:
  0.6 19.3 %collective-permute-start.3 = (f32[256,1024]{1,0:T(8,128)}, f32[256,1024]{1,0:T(8,128)S(1)}, u32[]{:S(2)}, u32[]{:S(2)}) collective-permute-start(f32[256,1024]{1,0:T(8,128)} %mine_ref.1), channel_id=1, source_target_pairs={{0,4},{4,0},{1,5},{5,1},{2,6},{6,2},{3,7},{7,3},{8,12},{12,8},{9,1... | collective-permute-start | bytes 3145736 | tf_op jit(solution)/shard_map/ppermute | solution.py:21
  1.2 24.5 %collective-permute-start = (f32[1000,256]{1,0:T(8,128)}, f32[1000,256]{1,0:T(8,128)S(1)}, u32[]{:S(2)}, u32[]{:S(2)}) collective-permute-start(f32[1000,256]{1,0:T(8,128)} %bitcast.7), channel_id=1, source_target_pairs={{0,4},{4,0},{1,5},{5,1},{2,6},{6,2},{3,7},{7,3},{8,12},{12,8},{9,1... | collective-permute-start | bytes 3072008 | tf_op jit(solution)/shard_map/ppermute | solution.py:21
  1.2 15.3 %collective-permute-start.1 = (f32[128,1024]{1,0:T(8,128)}, f32[128,1024]{1,0:T(8,128)S(1)}, u32[]{:S(2)}, u32[]{:S(2)}) collective-permute-start(f32[128,1024]{1,0:T(8,128)} %own), channel_id=1, source_target_pairs={{0,8},{8,0},{16,24},{24,16},{1,9},{9,1},{17,25},{25,17},{2,10},{10... | collective-permute-start | bytes 1572872 | tf_op jit(solution)/shard_map/ppermute | solution.py:21
  4.2 14.2 %collective-permute-start.2 = (f32[128,1024]{1,0:T(8,128)}, f32[128,1024]{1,0:T(8,128)S(1)}, u32[]{:S(2)}, u32[]{:S(2)}) collective-permute-start(f32[128,1024]{1,0:T(8,128)} %own), channel_id=1, source_target_pairs={{0,16},{8,24},{16,0},{24,8},{1,17},{9,25},{17,1},{25,9},{2,18},{10... | collective-permute-start | bytes 1572872 | tf_op jit(solution)/shard_map/ppermute | solution.py:21
  16.6 7.8 %collective-permute-start.4 = (f32[64,1024]{1,0:T(8,128)S(1)}, f32[64,1024]{1,0:T(8,128)S(1)}, u32[]{:S(2)}, u32[]{:S(2)}) collective-permute-start(f32[64,1024]{1,0:T(8,128)S(1)} %slice.88), channel_id=1, source_target_pairs={{0,16},{8,24},{16,0},{24,8},{1,17},{9,25},{17,1},{25,9},{2,18},{10... | collective-permute-start | bytes 786440 | tf_op jit(solution)/shard_map/ppermute | solution.py:21
  18.4 7.2 %collective-permute-start.5 = (f32[64,1024]{1,0:T(8,128)S(1)}, f32[64,1024]{1,0:T(8,128)S(1)}, u32[]{:S(2)}, u32[]{:S(2)}) collective-permute-start(f32[64,1024]{1,0:T(8,128)S(1)} %slice.89), channel_id=1, source_target_pairs={{0,8},{8,0},{16,24},{24,16},{1,9},{9,1},{17,25},{25,17},{2,10},{10... | collective-permute-start | bytes 786440 | tf_op jit(solution)/shard_map/ppermute | solution.py:21
  28.3 6.4 %collective-permute-start.6 = (f32[256,256]{1,0:T(8,128)S(1)}, f32[256,256]{1,0:T(8,128)S(1)}, u32[]{:S(2)}, u32[]{:S(2)}) collective-permute-start(f32[256,256]{1,0:T(8,128)S(1)} %get-tuple-element.130), channel_id=1, source_target_pairs={{0,8},{8,0},{16,24},{24,16},{1,9},{9,1},{17,25},{25,17},{2,10},{10... | collective-permute-start | bytes 786440 | tf_op jit(solution)/shard_map/ppermute | solution.py:21
  29.9 8.6 %collective-permute-start.10 = (f32[256,256]{1,0:T(8,128)S(1)}, f32[256,256]{1,0:T(8,128)S(1)}, u32[]{:S(2)}, u32[]{:S(2)}) collective-permute-start(f32[256,256]{1,0:T(8,128)S(1)} %get-tuple-element.140), channel_id=1, source_target_pairs={{0,16},{8,24},{16,0},{24,8},{1,17},{9,25},{17,1},{25,9},{2,18},{10... | collective-permute-start | bytes 786440 | tf_op jit(solution)/shard_map/ppermute | solution.py:21
  34.8 16.3 %collective-permute-start.7 = (f32[256,256]{1,0:T(8,128)S(1)}, f32[256,256]{1,0:T(8,128)S(1)}, u32[]{:S(2)}, u32[]{:S(2)}) collective-permute-start(f32[256,256]{1,0:T(8,128)S(1)} %add.48), channel_id=1, source_target_pairs={{0,16},{8,24},{16,0},{24,8},{1,17},{9,25},{17,1},{25,9},{2,18},{10... | collective-permute-start | bytes 786440 | tf_op jit(solution)/shard_map/ppermute | solution.py:21
  35.9 7.4 %collective-permute-start.9 = (f32[248,256]{1,0:T(8,128)S(1)}, f32[248,256]{1,0:T(8,128)S(1)}, u32[]{:S(2)}, u32[]{:S(2)}) collective-permute-start(f32[248,256]{1,0:T(8,128)S(1)} %get-tuple-element.138), channel_id=1, source_target_pairs={{0,8},{8,0},{16,24},{24,16},{1,9},{9,1},{17,25},{25,17},{2,10},{10... | collective-permute-start | bytes 761864 | tf_op jit(solution)/shard_map/ppermute | solution.py:21
  36.8 12.5 %collective-permute-start.8 = (f32[240,256]{1,0:T(8,128)S(1)}, f32[240,256]{1,0:T(8,128)S(1)}, u32[]{:S(2)}, u32[]{:S(2)}) collective-permute-start(f32[240,256]{1,0:T(8,128)S(1)} %get-tuple-element.136), channel_id=1, source_target_pairs={{0,16},{8,24},{16,0},{24,8},{1,17},{9,25},{17,1},{25,9},{2,18},{10... | collective-permute-start | bytes 737288 | tf_op jit(solution)/shard_map/ppermute | solution.py:21
  38.5 13.1 %collective-permute-start.11 = (f32[256,256]{1,0:T(8,128)S(1)}, f32[256,256]{1,0:T(8,128)S(1)}, u32[]{:S(2)}, u32[]{:S(2)}) collective-permute-start(f32[256,256]{1,0:T(8,128)S(1)} %add.49), channel_id=1, source_target_pairs={{0,8},{8,0},{16,24},{24,16},{1,9},{9,1},{17,25},{25,17},{2,10},{10... | collective-permute-start | bytes 786440 | tf_op jit(solution)/shard_map/ppermute | solution.py:21
  43.4 11.4 %collective-permute-start.15 = (f32[248,256]{1,0:T(8,128)S(1)}, f32[248,256]{1,0:T(8,128)S(1)}, u32[]{:S(2)}, u32[]{:S(2)}) collective-permute-start(f32[248,256]{1,0:T(8,128)S(1)} %add.50), channel_id=1, source_target_pairs={{0,16},{8,24},{16,0},{24,8},{1,17},{9,25},{17,1},{25,9},{2,18},{10... | collective-permute-start | bytes 761864 | tf_op jit(solution)/shard_map/ppermute | solution.py:21
  49.4 6.4 %collective-permute-start.14 = (f32[240,256]{1,0:T(8,128)S(1)}, f32[240,256]{1,0:T(8,128)S(1)}, u32[]{:S(2)}, u32[]{:S(2)}) collective-permute-start(f32[240,256]{1,0:T(8,128)S(1)} %add.51), channel_id=1, source_target_pairs={{0,8},{8,0},{16,24},{24,16},{1,9},{9,1},{17,25},{25,17},{2,10},{10... | collective-permute-start | bytes 737288 | tf_op jit(solution)/shard_map/ppermute | solution.py:21
  51.1 7.4 %collective-permute-start.12 = (f32[256,256]{1,0:T(8,128)S(1)}, f32[256,256]{1,0:T(8,128)S(1)}, u32[]{:S(2)}, u32[]{:S(2)}) collective-permute-start(f32[256,256]{1,0:T(8,128)S(1)} %maximum_add_fusion.full_a), channel_id=1, source_target_pairs={{0,8},{8,0},{16,24},{24,16},{1,9},{9,1},{17,25},{25,17},{2,10},{10... | collective-permute-start | bytes 786440 | tf_op jit(solution)/shard_map/ppermute | solution.py:21
  51.7 6.5 %collective-permute-start.13 = (f32[256,256]{1,0:T(8,128)S(1)}, f32[256,256]{1,0:T(8,128)S(1)}, u32[]{:S(2)}, u32[]{:S(2)}) collective-permute-start(f32[256,256]{1,0:T(8,128)S(1)} %maximum_add_fusion.1.full_b), channel_id=1, source_target_pairs={{0,16},{8,24},{16,0},{24,8},{1,17},{9,25},{17,1},{25,9},{2,18},{10... | collective-permute-start | bytes 786440 | tf_op jit(solution)/shard_map/ppermute | solution.py:21
  60.3 9.6 %collective-permute-start.18 = (f32[248,256]{1,0:T(8,128)S(1)}, f32[248,256]{1,0:T(8,128)S(1)}, u32[]{:S(2)}, u32[]{:S(2)}) collective-permute-start(f32[248,256]{1,0:T(8,128)S(1)} %maximum_add_fusion.2.full_a), channel_id=1, source_target_pairs={{0,8},{8,0},{16,24},{24,16},{1,9},{9,1},{17,25},{25,17},{2,10},{10... | collective-permute-start | bytes 761864 | tf_op jit(solution)/shard_map/ppermute | solution.py:21
  61.9 8.1 %collective-permute-start.19 = (f32[240,256]{1,0:T(8,128)S(1)}, f32[240,256]{1,0:T(8,128)S(1)}, u32[]{:S(2)}, u32[]{:S(2)}) collective-permute-start(f32[240,256]{1,0:T(8,128)S(1)} %maximum_add_fusion.3.full_b), channel_id=1, source_target_pairs={{0,16},{8,24},{16,0},{24,8},{1,17},{9,25},{17,1},{25,9},{2,18},{10... | collective-permute-start | bytes 737288 | tf_op jit(solution)/shard_map/ppermute | solution.py:21
  71.0 8.7 %collective-permute-start.17 = (f32[512,128]{1,0:T(8,128)S(1)}, f32[512,128]{1,0:T(8,128)S(1)}, u32[]{:S(2)}, u32[]{:S(2)}) collective-permute-start(f32[512,128]{1,0:T(8,128)S(1)} %get-tuple-element.189), channel_id=1, source_target_pairs={{0,1},{1,0},{2,3},{3,2},{4,5},{5,4},{6,7},{7,6},{8,9},{9,8},{10,11... | collective-permute-start | bytes 786440 | tf_op jit(solution)/shard_map/ppermute | solution.py:262
  79.7 15.3 %collective-permute-start.21 = (f32[512,128]{1,0:T(8,128)S(1)}, f32[512,128]{1,0:T(8,128)S(1)}, u32[]{:S(2)}, u32[]{:S(2)}) collective-permute-start(f32[512,128]{1,0:T(8,128)S(1)} %add.60), channel_id=1, source_target_pairs={{0,3},{3,0},{1,2},{2,1},{4,7},{7,4},{5,6},{6,5},{8,11},{11,8},{9,1... | collective-permute-start | bytes 786440 | tf_op jit(solution)/shard_map/ppermute | solution.py:262
  83.4 11.6 %collective-permute-start.22 = (f32[488,128]{1,0:T(8,128)S(1)}, f32[488,128]{1,0:T(8,128)S(1)}, u32[]{:S(2)}, u32[]{:S(2)}) collective-permute-start(f32[488,128]{1,0:T(8,128)S(1)} %get-tuple-element.190), channel_id=1, source_target_pairs={{0,1},{1,0},{2,3},{3,2},{4,5},{5,4},{6,7},{7,6},{8,9},{9,8},{10,11... | collective-permute-start | bytes 749576 | tf_op jit(solution)/shard_map/ppermute | solution.py:262
  95.1 15.2 %collective-permute-start.23 = (f32[512,128]{1,0:T(8,128)S(1)}, f32[512,128]{1,0:T(8,128)S(1)}, u32[]{:S(2)}, u32[]{:S(2)}) collective-permute-start(f32[512,128]{1,0:T(8,128)S(1)} %add.62), channel_id=1, source_target_pairs={{0,1},{1,0},{2,3},{3,2},{4,5},{5,4},{6,7},{7,6},{8,9},{9,8},{10,11... | collective-permute-start | bytes 786440 | tf_op jit(solution)/shard_map/ppermute | solution.py:262
  96.8 11.1 %collective-permute-start.24 = (f32[488,128]{1,0:T(8,128)S(1)}, f32[488,128]{1,0:T(8,128)S(1)}, u32[]{:S(2)}, u32[]{:S(2)}) collective-permute-start(f32[488,128]{1,0:T(8,128)S(1)} %add.61), channel_id=1, source_target_pairs={{0,3},{3,0},{1,2},{2,1},{4,7},{7,4},{5,6},{6,5},{8,11},{11,8},{9,1... | collective-permute-start | bytes 749576 | tf_op jit(solution)/shard_map/ppermute | solution.py:262
  107.9 7.4 %collective-permute-start.25 = (f32[488,128]{1,0:T(8,128)S(1)}, f32[488,128]{1,0:T(8,128)S(1)}, u32[]{:S(2)}, u32[]{:S(2)}) collective-permute-start(f32[488,128]{1,0:T(8,128)S(1)} %add.63), channel_id=1, source_target_pairs={{0,1},{1,0},{2,3},{3,2},{4,5},{5,4},{6,7},{7,6},{8,9},{9,8},{10,11... | collective-permute-start | bytes 749576 | tf_op jit(solution)/shard_map/ppermute | solution.py:262
  (7 other events, 38.6 us)

commit v6 on v5

--- a/solution.py
+++ b/solution.py
@@ -10,7 +10,7 @@
 
 HIGHEST = lax.Precision.HIGHEST
 HIGH = lax.Precision.HIGH
-ROUNDS = (0.52,)
+ROUNDS = (0.48,)
 BF16, F32 = jnp.bfloat16, jnp.float32
 NT = (((1,), (1,)), ((), ()))
 NN = (((1,), (0,)), ((), ()))
@@ -236,26 +236,43 @@
     return call(functools.partial(send_body, edges, rows), outs, (w0, w1, *far), flops)
 
 
-def grad_body(factor, full_a, full_b, other_a, other_b, near_high, near_low, far_high, far_low, gone, here):
-    rows, half = full_a.shape[1] // 2, gone.shape[1]
+PARTS = 3
+
+
+def part_rows(size):
+    step = -(-size // PARTS // 8) * 8
+    return [(at, min(size, at + step)) for at in range(0, size, step)]
+
+
+def grad_body(factor, full_a, full_b, other_a, other_b, near_high, near_low, far_high, far_low, here, *gone):
+    rows, half = full_a.shape[1] // 2, here.shape[1]
     at = 0
     for i, (full, other) in enumerate(((full_a, other_a), (full_b, other_b))):
         to = pl.ds(at, full.shape[0])
         at += full.shape[0]
         full_pair, other_pair = halves(full[...]), halves(other[...])
         stay, go = stays(rows)[i], goes(rows)[i]
-        for out, cols in ((gone, pl.ds(half, half)), (here, pl.ds(0, half))):
-            out[to] = factor * (
+        for away, cols in ((True, pl.ds(half, half)), (False, pl.ds(0, half))):
+            value = factor * (
                 mul3(full_pair, (near_high[stay, cols], near_low[stay, cols]), NN)
                 + mul3(other_pair, (far_high[go, cols], far_low[go, cols]), NN)
             )
+            if not away:
+                here[to] = value
+                continue
+            start, end = at - full.shape[0], at
+            for ref, (low, high) in zip(gone, part_rows(here.shape[0])):
+                low_at, high_at = max(low, start), min(high, end)
+                if low_at < high_at:
+                    ref[pl.ds(low_at - low, high_at - low_at)] = value[low_at - start : high_at - start]
 
 
 def grad_parts(factor, full, other, near, far):
     cols, half = full[0].shape[0] + full[1].shape[0], near[0].shape[1] // 2
     flops = 12 * cols * full[0].shape[1] * 2 * half
-    outs = [shaped((cols, half))] * 2
-    return call(functools.partial(grad_body, factor), outs, (*full, *other, *near, *far), flops)
+    outs = [shaped((cols, half))] + [shaped((b - a, half)) for a, b in part_rows(cols)]
+    out = call(functools.partial(grad_body, factor), outs, (*full, *other, *near, *far), flops)
+    return out[1:], out[0]
 
 
 def pass_line(value, pairs):
@@ -266,8 +283,48 @@
 ACROSS = [(0, 3), (3, 0), (1, 2), (2, 1)]
 
 
-def add(a, b):
-    return a + b
+def add_body(*refs):
+    count = len(refs) // 3
+    for i in range(count):
+        refs[2 * count + i][...] = refs[i][...] + refs[count + i][...]
+
+
+def add(many, more):
+    return call(add_body, [shaped(a.shape) for a in many], (*many, *more))
+
+
+def turn_body(*refs):
+    for a, b, out in zip(refs[0:2], refs[2:4], refs[4:6]):
+        rows = a.shape[1] // 2
+        left, right = pl.ds(0, rows), pl.ds(rows, rows)
+        out[:, left] = a[:, left] + b[:, right]
+        out[:, right] = a[:, right] + b[:, left]
+
+
+def turn(many, more):
+    return call(turn_body, [shaped(a.shape) for a in many], (*many, *more))
+
+
+def split_body(here, *refs):
+    gone, sends, mine = refs[:-2], refs[-2], refs[-1]
+    place = lax.axis_index("col")
+    ends = (place == 0) | (place == 3)
+    quarter = mine.shape[1]
+    left, right = pl.ds(0, quarter), pl.ds(quarter, quarter)
+
+    def put(kept, sent):
+        for ref, (a, b) in zip(gone, part_rows(here.shape[0])):
+            to = pl.ds(a, b - a)
+            mine[to] = here[to, kept] + ref[:, kept]
+            sends[to] = here[to, sent] + ref[:, sent]
+
+    pl.when(ends)(lambda: put(left, right))
+    pl.when(~ends)(lambda: put(right, left))
+
+
+def split(here, gone):
+    outs = [shaped((here.shape[0], here.shape[1] // 2))] * 2
+    return call(split_body, outs, (here, *gone))
 
 
 def cut(out):
@@ -283,7 +340,7 @@
 
 def square(batch, running_t, targets_t, centers, weights_t, factor):
     rows, out = batch.shape[0], weights_t.shape[0]
-    mid, quarter = rows // 2, centers.shape[0] // 2
+    mid = rows // 2
     edges = cut(out)
     rounds = len(edges) // 2
     line = Line()
@@ -305,70 +362,48 @@
     def both(pair, step):
         return [swap(pair[i], "chip", axes[i][step]) for i in (0, 1)]
 
-    def turned(a, b):
-        return a + jnp.concatenate([b[:, rows:], b[:, :rows]], axis=1)
-
     coming, crossing, beside, across, back = ([None] * rounds for _ in range(5))
     partial, full, other, gone, here, mine, total = ([None] * rounds for _ in range(7))
 
     def do_partial(r):
-        partial[r] = [line(add, kept[2 * r + i], coming[r][i]) for i in (0, 1)]
+        partial[r] = line(add, kept[2 * r : 2 * r + 2], coming[r])
         crossing[r] = both(partial[r], 1)
 
     def do_full(r):
-        full[r] = [line(turned, partial[r][i], crossing[r][i]) for i in (0, 1)]
+        full[r] = line(turn, partial[r], crossing[r])
         other[r] = both(full[r], 0)
 
     def do_grad(r):
         gone[r], here[r] = line(lambda *a: grad_parts(factor, *a), full[r], other[r], near, far)
-        gone[r] = swap(gone[r], "core")
-
-    def split(a, b):
-        first, second = a[:, :quarter] + b[:, :quarter], a[:, quarter:] + b[:, quarter:]
-        return jnp.where(ends, second, first), jnp.where(ends, first, second)
+        gone[r] = [swap(part, "core") for part in gone[r]]
 
     def do_owned(r):
         sends, mine[r] = line(split, here[r], gone[r])
         beside[r] = pass_line(sends, BESIDE)
 
     def do_mine(r):
-        mine[r] = line(add, mine[r], beside[r])
+        (mine[r],) = line(add, [mine[r]], [beside[r]])
         across[r] = pass_line(mine[r], ACROSS)
 
     def do_total(r):
-        total[r] = line(add, mine[r], across[r])
+        (total[r],) = line(add, [mine[r]], [across[r]])
         back[r] = pass_line(total[r], BESIDE)
 
     coming[0] = both(sent[0:2], 0)
     coming[1] = both(line.hold(tuple(sent[2:4])), 0)
     kept = line(lambda *a: keep_shares(edges, *a), w0, w1, running_t, targets_t, near)
-    if rounds == 3:
-        sent = list(sent) + list(line(lambda *a: send_shares(edges[4:], *a), w0, w1, far))
     do_partial(0)
     do_partial(1)
     do_full(0)
-    if rounds == 3:
-        coming[2] = both(line.hold(tuple(sent[4:6])), 0)
     do_full(1)
     do_grad(0)
     do_owned(0)
-    if rounds == 3:
-        do_partial(2)
     do_grad(1)
+    do_mine(0)
     do_owned(1)
-    if rounds == 3:
-        do_full(2)
-    do_mine(0)
-    if rounds == 3:
-        do_grad(2)
-        do_owned(2)
     do_mine(1)
     do_total(0)
-    if rounds == 3:
-        do_mine(2)
     do_total(1)
-    if rounds == 3:
-        do_total(2)
 
     first = [jnp.where(ends, t, b) for t, b in zip(total, back)]
     second = [jnp.where(ends, b, t) for t, b in zip(total, back)]

time: 117 us -> 106 us (0.906)
  waiting for transfers between devices: 70.8 us -> 52.8 us
  starting transfers between devices: 31 us -> 40.1 us
  other arithmetic: 3.53 us -> 1.98 us
    ppermute x6, waiting for transfers between devices: 33 us -> 18.9 us  [pass_line(): return lax.ppermute(value, 'col', pairs)]
    ppermute x6, starting transfers between devices: 10 us -> 19.5 us  [pass_line(): return lax.ppermute(value, 'col', pairs)]
    ppermute x20 -> x24, waiting for transfers between devices: 37.8 us -> 33.9 us  [swap(): return lax.ppermute(value, axis, [(i, i ^ flip) for i in range(size)])]
    select_n x2 -> x0, other arithmetic: 1.19 us -> none  [split(): return (jnp.where(ends, second, first), jnp.where(ends, first, second))]
    ppermute x20 -> x24, starting transfers between devices: 21 us -> 20.6 us  [swap(): return lax.ppermute(value, axis, [(i, i ^ flip) for i in range(size)])]
    pallas_call x7 -> x17, Pallas kernels: 10.1 us -> 9.82 us  [call(): pl.pallas_call(body, out_shape=outs, in_specs=[vmem] * len(args), out_spe...]
  transfers between devices with their start and end apart: 26 -> 30, of which waited for: 17 -> 18; matrix products, arithmetic and copies ran while one was open for 2% -> 1% of each run, Pallas kernels for 4% -> 7%
where the time goes in v6:
time: 106 us
  waiting for transfers between devices  52.8 us (50%)
  starting transfers between devices  40.1 us (38%)
  Pallas kernels  9.82 us (9%)
  other arithmetic  1.98 us (2%)
    ppermute x24, waiting for transfers between devices, swap(): return lax.ppermute(value, axis, [(i, i ^ flip) for i in range(size)])  33.9 us
    ppermute x24, starting transfers between devices, swap(): return lax.ppermute(value, axis, [(i, i ^ flip) for i in range(size)])  20.6 us
    ppermute x6, starting transfers between devices, pass_line(): return lax.ppermute(value, 'col', pairs)  19.5 us
    ppermute x6, waiting for transfers between devices, pass_line(): return lax.ppermute(value, 'col', pairs)  18.9 us
    pallas_call x17, Pallas kernels, call(): pl.pallas_call(body, out_shape=outs, in_specs=[vmem] * len(args), out_spe...  9.82 us
  transfers between devices with their start and end apart: 30, of which 18 were waited for; matrix products, arithmetic and copies ran while one was open for 1% of the time, Pallas kernels for 7%

profile of v6, /device:TPU:0, one launch (start us, length us, event | category | flops | bytes accessed | tf_op | source)
XLA Modules:
  0.0 105.6 jit_solution(3345077452740258390)
XLA Ops:
  1.2 2.9 %collective-permute-start.1 = (f32[128,1024]{1,0:T(8,128)}, f32[128,1024]{1,0:T(8,128)S(1)}, u32[]{:S(2)}, u32[]{:S(2)}) collective-permute-start(f32[128,1024]{1,0:T(8,128)} %own), channel_id=1, source_target_pairs={{0,8},{8,0},{16,24},{24,16},{1,9},{9,1},{17,25},{25,17},{2,10},{10... | collective-permute-start | bytes 1572872 | tf_op jit(solution)/shard_map/ppermute | solution.py:21
  4.2 1.5 %collective-permute-start.2 = (f32[128,1024]{1,0:T(8,128)}, f32[128,1024]{1,0:T(8,128)S(1)}, u32[]{:S(2)}, u32[]{:S(2)}) collective-permute-start(f32[128,1024]{1,0:T(8,128)} %own), channel_id=1, source_target_pairs={{0,16},{8,24},{16,0},{24,8},{1,17},{9,25},{17,1},{25,9},{2,18},{10... | collective-permute-start | bytes 1572872 | tf_op jit(solution)/shard_map/ppermute | solution.py:21
  5.7 10.9 %collective-permute-done.1.x = f32[128,1024]{1,0:T(8,128)S(1)} collective-permute-done((f32[128,1024]{1,0:T(8,128)}, f32[128,1024]{1,0:T(8,128)S(1)}, u32[]{:S(2)}, u32[]{:S(2)}) %collective-permute-start.1) | collective-permute-done | bytes 524320 | tf_op jit(solution)/shard_map/ppermute | solution.py:21
  16.6 1.8 %collective-permute-start.4 = (f32[64,1024]{1,0:T(8,128)S(1)}, f32[64,1024]{1,0:T(8,128)S(1)}, u32[]{:S(2)}, u32[]{:S(2)}) collective-permute-start(f32[64,1024]{1,0:T(8,128)S(1)} %slice.24), channel_id=1, source_target_pairs={{0,16},{8,24},{16,0},{24,8},{1,17},{9,25},{17,1},{25,9},{2,18},{10... | collective-permute-start | bytes 786440 | tf_op jit(solution)/shard_map/ppermute | solution.py:21
  18.4 1.6 %collective-permute-start.5 = (f32[64,1024]{1,0:T(8,128)S(1)}, f32[64,1024]{1,0:T(8,128)S(1)}, u32[]{:S(2)}, u32[]{:S(2)}) collective-permute-start(f32[64,1024]{1,0:T(8,128)S(1)} %slice.25), channel_id=1, source_target_pairs={{0,8},{8,0},{16,24},{24,16},{1,9},{9,1},{17,25},{25,17},{2,10},{10... | collective-permute-start | bytes 786440 | tf_op jit(solution)/shard_map/ppermute | solution.py:21
  20.5 1.6 %shard_map.69 = (bf16[128,512]{1,0:T(8,128)(2,1)S(1)}, bf16[128,512]{1,0:T(8,128)(2,1)S(1)}) custom-call(f32[128,1024]{1,0:T(8,128)S(1)} %copy-done.2, bf16[512,1024]{1,0:T(8,128)(2,1)S(1)} %get-tuple-element.135.c_high, bf16[512,1024]{1,0:T(8,128)(2,1)S(1)} %get-tuple-element.136.c_low, f32[8,512]{1,0:T(8,128)S(1)} %get-tuple-element.137.c_sq), custom_call_target="tpu_custom_call" | custom-call | flops 512 | tf_op jit(solution)/shard_map/pallas_call | solution.py:54
  22.2 1.6 %shard_map.70 = (bf16[384,512]{1,0:T(8,128)(2,1)S(1)}, bf16[384,512]{1,0:T(8,128)(2,1)S(1)}) custom-call(f32[128,1024]{1,0:T(8,128)S(1)} %collective-permute-done.1.x, f32[128,1024]{1,0:T(8,128)S(1)} %collective-permute-done.2.y, bf16[512,1024]{1,0:T(8,128)(2,1)S(1)} %get-tuple-element.135.c_high, bf16[512,1024]{1,0:T(8,128)(2,1)S(1)} %get-tuple-element.136.c_low, ...), custom_call_target="tpu_custom_call" | custom-call | flops 1024 | tf_op jit(solution)/shard_map/pallas_call | solution.py:54
  25.7 2.6 %shard_map.71 = (bf16[384,512]{1,0:T(8,128)(2,1)S(1)}, bf16[384,512]{1,0:T(8,128)(2,1)S(1)}, f32[240,256]{1,0:T(8,128)S(1)}, f32[240,256]{1,0:T(8,128)S(1)}, f32...) custom-call(f32[64,1024]{1,0:T(8,128)S(1)} %collective-permute-done.4.low_rows, ...), custom_call_target="tpu_custom_call" | custom-call | flops 512 | tf_op jit(solution)/shard_map/pallas_call | solution.py:54
  28.3 1.6 %collective-permute-start.6 = (f32[240,256]{1,0:T(8,128)S(1)}, f32[240,256]{1,0:T(8,128)S(1)}, u32[]{:S(2)}, u32[]{:S(2)}) collective-permute-start(f32[240,256]{1,0:T(8,128)S(1)} %get-tuple-element.151), channel_id=1, source_target_pairs={{0,8},{8,0},{16,24},{24,16},{1,9},{9,1},{17,25},{25,17},{2,10},{10... | collective-permute-start | bytes 737288 | tf_op jit(solution)/shard_map/ppermute | solution.py:21
  33.5 3.8 %collective-permute-done.6.refs_2_ = f32[240,256]{1,0:T(8,128)S(1)} collective-permute-done((f32[240,256]{1,0:T(8,128)S(1)}, f32[240,256]{1,0:T(8,128)S(1)}, u32[]{:S(2)}, u32[]{:S(2)}) %collective-permute-start.6) | collective-permute-done | bytes 245792 | tf_op jit(solution)/shard_map/ppermute | solution.py:21
  37.3 1.5 %collective-permute-done.7.refs_3_ = f32[240,256]{1,0:T(8,128)S(1)} collective-permute-done((f32[240,256]{1,0:T(8,128)S(1)}, f32[240,256]{1,0:T(8,128)S(1)}, u32[]{:S(2)}, u32[]{:S(2)}) %collective-permute-start.7) | collective-permute-done | bytes 245792 | tf_op jit(solution)/shard_map/ppermute | solution.py:21
  40.5 3.9 %collective-permute-done.11.refs_3_ = f32[256,256]{1,0:T(8,128)S(1)} collective-permute-done((f32[256,256]{1,0:T(8,128)S(1)}, f32[256,256]{1,0:T(8,128)S(1)}, u32[]{:S(2)}, u32[]{:S(2)}) %collective-permute-start.11) | collective-permute-done | bytes 262176 | tf_op jit(solution)/shard_map/ppermute | solution.py:21
  46.1 3.5 %collective-permute-done.8.refs_2_ = f32[240,256]{1,0:T(8,128)S(1)} collective-permute-done((f32[240,256]{1,0:T(8,128)S(1)}, f32[240,256]{1,0:T(8,128)S(1)}, u32[]{:S(2)}, u32[]{:S(2)}) %collective-permute-start.8) | collective-permute-done | bytes 245792 | tf_op jit(solution)/shard_map/ppermute | solution.py:21
  51.4 2.9 %collective-permute-done.15.refs_3_ = f32[256,256]{1,0:T(8,128)S(1)} collective-permute-done((f32[256,256]{1,0:T(8,128)S(1)}, f32[256,256]{1,0:T(8,128)S(1)}, u32[]{:S(2)}, u32[]{:S(2)}) %collective-permute-start.15) | collective-permute-done | bytes 262176 | tf_op jit(solution)/shard_map/ppermute | solution.py:21
  57.2 1.9 %collective-permute-done.12.other_a = f32[240,256]{1,0:T(8,128)S(1)} collective-permute-done((f32[240,256]{1,0:T(8,128)S(1)}, f32[240,256]{1,0:T(8,128)S(1)}, u32[]{:S(2)}, u32[]{:S(2)}) %collective-permute-start.12) | collective-permute-done | bytes 245792 | tf_op jit(solution)/shard_map/ppermute | solution.py:21
  63.2 1.6 %collective-permute-start.19 = (f32[480,128]{1,0:T(8,128)S(1)}, f32[480,128]{1,0:T(8,128)S(1)}, u32[]{:S(2)}, u32[]{:S(2)}) collective-permute-start(f32[480,128]{1,0:T(8,128)S(1)} %get-tuple-element.200), channel_id=1, source_target_pairs={{0,1},{1,0},{2,3},{3,2},{4,5},{5,4},{6,7},{7,6},{8,9},{9,8},{10,11... | collective-permute-start | bytes 737288 | tf_op jit(solution)/shard_map/ppermute | solution.py:279
  66.5 4.8 %collective-permute-done.19.refs_1_ = f32[480,128]{1,0:T(8,128)S(1)} collective-permute-done((f32[480,128]{1,0:T(8,128)S(1)}, f32[480,128]{1,0:T(8,128)S(1)}, u32[]{:S(2)}, u32[]{:S(2)}) %collective-permute-start.19) | collective-permute-done | bytes 245792 | tf_op jit(solution)/shard_map/ppermute | solution.py:279
  71.5 1.6 %collective-permute-start.26 = (f32[520,128]{1,0:T(8,128)S(1)}, f32[520,128]{1,0:T(8,128)S(1)}, u32[]{:S(2)}, u32[]{:S(2)}) collective-permute-start(f32[520,128]{1,0:T(8,128)S(1)} %get-tuple-element.221), channel_id=1, source_target_pairs={{0,1},{1,0},{2,3},{3,2},{4,5},{5,4},{6,7},{7,6},{8,9},{9,8},{10,11... | collective-permute-start | bytes 798728 | tf_op jit(solution)/shard_map/ppermute | solution.py:279
  73.1 2.5 %collective-permute-start.22 = (f32[480,128]{1,0:T(8,128)S(1)}, f32[480,128]{1,0:T(8,128)S(1)}, u32[]{:S(2)}, u32[]{:S(2)}) collective-permute-start(f32[480,128]{1,0:T(8,128)S(1)} %shard_map.80.refs_0_), channel_id=1, source_target_pairs={{0,3},{3,0},{1,2},{2,1},{4,7},{7,4},{5,6},{6,5},{8,11},{11,8},{9,1... | collective-permute-start | bytes 737288 | tf_op jit(solution)/shard_map/ppermute | solution.py:279
  75.6 4.4 %collective-permute-done.26.refs_1_ = f32[520,128]{1,0:T(8,128)S(1)} collective-permute-done((f32[520,128]{1,0:T(8,128)S(1)}, f32[520,128]{1,0:T(8,128)S(1)}, u32[]{:S(2)}, u32[]{:S(2)}) %collective-permute-start.26) | collective-permute-done | bytes 266272 | tf_op jit(solution)/shard_map/ppermute | solution.py:279
  80.0 11.1 %collective-permute-start.28 = (f32[520,128]{1,0:T(8,128)S(1)}, f32[520,128]{1,0:T(8,128)S(1)}, u32[]{:S(2)}, u32[]{:S(2)}) collective-permute-start(f32[520,128]{1,0:T(8,128)S(1)} %shard_map.82.refs_0_), channel_id=1, source_target_pairs={{0,3},{3,0},{1,2},{2,1},{4,7},{7,4},{5,6},{6,5},{8,11},{11,8},{9,1... | collective-permute-start | bytes 798728 | tf_op jit(solution)/shard_map/ppermute | solution.py:279
  91.3 4.4 %collective-permute-done.28.refs_1_ = f32[520,128]{1,0:T(8,128)S(1)} collective-permute-done((f32[520,128]{1,0:T(8,128)S(1)}, f32[520,128]{1,0:T(8,128)S(1)}, u32[]{:S(2)}, u32[]{:S(2)}) %collective-permute-start.28) | collective-permute-done | bytes 266272 | tf_op jit(solution)/shard_map/ppermute | solution.py:279
  95.7 2.6 %collective-permute-start.29 = (f32[520,128]{1,0:T(8,128)S(1)}, f32[520,128]{1,0:T(8,128)S(1)}, u32[]{:S(2)}, u32[]{:S(2)}) collective-permute-start(f32[520,128]{1,0:T(8,128)S(1)} %shard_map.84), channel_id=1, source_target_pairs={{0,1},{1,0},{2,3},{3,2},{4,5},{5,4},{6,7},{7,6},{8,9},{9,8},{10,11... | collective-permute-start | bytes 798728 | tf_op jit(solution)/shard_map/ppermute | solution.py:279
  99.2 5.3 %collective-permute-done.29 = f32[520,128]{1,0:T(8,128)S(1)} collective-permute-done((f32[520,128]{1,0:T(8,128)S(1)}, f32[520,128]{1,0:T(8,128)S(1)}, u32[]{:S(2)}, u32[]{:S(2)}) %collective-permute-start.29) | collective-permute-done | bytes 266272 | tf_op jit(solution)/shard_map/ppermute | solution.py:279
  (73 shorter events, 22.8 us)
Async XLA Ops:
  0.6 19.3 %collective-permute-start.3 = (f32[256,1024]{1,0:T(8,128)}, f32[256,1024]{1,0:T(8,128)S(1)}, u32[]{:S(2)}, u32[]{:S(2)}) collective-permute-start(f32[256,1024]{1,0:T(8,128)} %mine_ref.1), channel_id=1, source_target_pairs={{0,4},{4,0},{1,5},{5,1},{2,6},{6,2},{3,7},{7,3},{8,12},{12,8},{9,1... | collective-permute-start | bytes 3145736 | tf_op jit(solution)/shard_map/ppermute | solution.py:21
  1.2 24.5 %collective-permute-start = (f32[1000,256]{1,0:T(8,128)}, f32[1000,256]{1,0:T(8,128)S(1)}, u32[]{:S(2)}, u32[]{:S(2)}) collective-permute-start(f32[1000,256]{1,0:T(8,128)} %bitcast.7), channel_id=1, source_target_pairs={{0,4},{4,0},{1,5},{5,1},{2,6},{6,2},{3,7},{7,3},{8,12},{12,8},{9,1... | collective-permute-start | bytes 3072008 | tf_op jit(solution)/shard_map/ppermute | solution.py:21
  1.2 15.3 %collective-permute-start.1 = (f32[128,1024]{1,0:T(8,128)}, f32[128,1024]{1,0:T(8,128)S(1)}, u32[]{:S(2)}, u32[]{:S(2)}) collective-permute-start(f32[128,1024]{1,0:T(8,128)} %own), channel_id=1, source_target_pairs={{0,8},{8,0},{16,24},{24,16},{1,9},{9,1},{17,25},{25,17},{2,10},{10... | collective-permute-start | bytes 1572872 | tf_op jit(solution)/shard_map/ppermute | solution.py:21
  4.2 14.2 %collective-permute-start.2 = (f32[128,1024]{1,0:T(8,128)}, f32[128,1024]{1,0:T(8,128)S(1)}, u32[]{:S(2)}, u32[]{:S(2)}) collective-permute-start(f32[128,1024]{1,0:T(8,128)} %own), channel_id=1, source_target_pairs={{0,16},{8,24},{16,0},{24,8},{1,17},{9,25},{17,1},{25,9},{2,18},{10... | collective-permute-start | bytes 1572872 | tf_op jit(solution)/shard_map/ppermute | solution.py:21
  16.6 7.8 %collective-permute-start.4 = (f32[64,1024]{1,0:T(8,128)S(1)}, f32[64,1024]{1,0:T(8,128)S(1)}, u32[]{:S(2)}, u32[]{:S(2)}) collective-permute-start(f32[64,1024]{1,0:T(8,128)S(1)} %slice.24), channel_id=1, source_target_pairs={{0,16},{8,24},{16,0},{24,8},{1,17},{9,25},{17,1},{25,9},{2,18},{10... | collective-permute-start | bytes 786440 | tf_op jit(solution)/shard_map/ppermute | solution.py:21
  18.4 7.2 %collective-permute-start.5 = (f32[64,1024]{1,0:T(8,128)S(1)}, f32[64,1024]{1,0:T(8,128)S(1)}, u32[]{:S(2)}, u32[]{:S(2)}) collective-permute-start(f32[64,1024]{1,0:T(8,128)S(1)} %slice.25), channel_id=1, source_target_pairs={{0,8},{8,0},{16,24},{24,16},{1,9},{9,1},{17,25},{25,17},{2,10},{10... | collective-permute-start | bytes 786440 | tf_op jit(solution)/shard_map/ppermute | solution.py:21
  28.3 9.0 %collective-permute-start.6 = (f32[240,256]{1,0:T(8,128)S(1)}, f32[240,256]{1,0:T(8,128)S(1)}, u32[]{:S(2)}, u32[]{:S(2)}) collective-permute-start(f32[240,256]{1,0:T(8,128)S(1)} %get-tuple-element.151), channel_id=1, source_target_pairs={{0,8},{8,0},{16,24},{24,16},{1,9},{9,1},{17,25},{25,17},{2,10},{10... | collective-permute-start | bytes 737288 | tf_op jit(solution)/shard_map/ppermute | solution.py:21
  29.9 8.9 %collective-permute-start.7 = (f32[240,256]{1,0:T(8,128)S(1)}, f32[240,256]{1,0:T(8,128)S(1)}, u32[]{:S(2)}, u32[]{:S(2)}) collective-permute-start(f32[240,256]{1,0:T(8,128)S(1)} %get-tuple-element.152), channel_id=1, source_target_pairs={{0,16},{8,24},{16,0},{24,8},{1,17},{9,25},{17,1},{25,9},{2,18},{10... | collective-permute-start | bytes 737288 | tf_op jit(solution)/shard_map/ppermute | solution.py:21
  30.4 14.0 %collective-permute-start.10 = (f32[264,256]{1,0:T(8,128)S(1)}, f32[264,256]{1,0:T(8,128)S(1)}, u32[]{:S(2)}, u32[]{:S(2)}) collective-permute-start(f32[264,256]{1,0:T(8,128)S(1)} %get-tuple-element.163), channel_id=1, source_target_pairs={{0,8},{8,0},{16,24},{24,16},{1,9},{9,1},{17,25},{25,17},{2,10},{10... | collective-permute-start | bytes 811016 | tf_op jit(solution)/shard_map/ppermute | solution.py:21
  31.5 12.9 %collective-permute-start.11 = (f32[256,256]{1,0:T(8,128)S(1)}, f32[256,256]{1,0:T(8,128)S(1)}, u32[]{:S(2)}, u32[]{:S(2)}) collective-permute-start(f32[256,256]{1,0:T(8,128)S(1)} %get-tuple-element.164), channel_id=1, source_target_pairs={{0,16},{8,24},{16,0},{24,8},{1,17},{9,25},{17,1},{25,9},{2,18},{10... | collective-permute-start | bytes 786440 | tf_op jit(solution)/shard_map/ppermute | solution.py:21
  38.8 10.8 %collective-permute-start.8 = (f32[240,256]{1,0:T(8,128)S(1)}, f32[240,256]{1,0:T(8,128)S(1)}, u32[]{:S(2)}, u32[]{:S(2)}) collective-permute-start(f32[240,256]{1,0:T(8,128)S(1)} %get-tuple-element.170.refs_0_), channel_id=1, source_target_pairs={{0,16},{8,24},{16,0},{24,8},{1,17},{9,25},{17,1},{25,9},{2,18},{10... | collective-permute-start | bytes 737288 | tf_op jit(solution)/shard_map/ppermute | solution.py:21
  39.4 10.3 %collective-permute-start.9 = (f32[240,256]{1,0:T(8,128)S(1)}, f32[240,256]{1,0:T(8,128)S(1)}, u32[]{:S(2)}, u32[]{:S(2)}) collective-permute-start(f32[240,256]{1,0:T(8,128)S(1)} %get-tuple-element.171.refs_1_), channel_id=1, source_target_pairs={{0,8},{8,0},{16,24},{24,16},{1,9},{9,1},{17,25},{25,17},{2,10},{10... | collective-permute-start | bytes 737288 | tf_op jit(solution)/shard_map/ppermute | solution.py:21
  44.4 11.0 %collective-permute-start.14 = (f32[264,256]{1,0:T(8,128)S(1)}, f32[264,256]{1,0:T(8,128)S(1)}, u32[]{:S(2)}, u32[]{:S(2)}) collective-permute-start(f32[264,256]{1,0:T(8,128)S(1)} %get-tuple-element.178.refs_0_), channel_id=1, source_target_pairs={{0,16},{8,24},{16,0},{24,8},{1,17},{9,25},{17,1},{25,9},{2,18},{10... | collective-permute-start | bytes 811016 | tf_op jit(solution)/shard_map/ppermute | solution.py:21
  45.0 9.2 %collective-permute-start.15 = (f32[256,256]{1,0:T(8,128)S(1)}, f32[256,256]{1,0:T(8,128)S(1)}, u32[]{:S(2)}, u32[]{:S(2)}) collective-permute-start(f32[256,256]{1,0:T(8,128)S(1)} %get-tuple-element.179.refs_1_), channel_id=1, source_target_pairs={{0,8},{8,0},{16,24},{24,16},{1,9},{9,1},{17,25},{25,17},{2,10},{10... | collective-permute-start | bytes 786440 | tf_op jit(solution)/shard_map/ppermute | solution.py:21
  49.7 9.4 %collective-permute-start.12 = (f32[240,256]{1,0:T(8,128)S(1)}, f32[240,256]{1,0:T(8,128)S(1)}, u32[]{:S(2)}, u32[]{:S(2)}) collective-permute-start(f32[240,256]{1,0:T(8,128)S(1)} %get-tuple-element.183.full_a), channel_id=1, source_target_pairs={{0,8},{8,0},{16,24},{24,16},{1,9},{9,1},{17,25},{25,17},{2,10},{10... | collective-permute-start | bytes 737288 | tf_op jit(solution)/shard_map/ppermute | solution.py:21
  50.3 9.9 %collective-permute-start.13 = (f32[240,256]{1,0:T(8,128)S(1)}, f32[240,256]{1,0:T(8,128)S(1)}, u32[]{:S(2)}, u32[]{:S(2)}) collective-permute-start(f32[240,256]{1,0:T(8,128)S(1)} %get-tuple-element.184.full_b), channel_id=1, source_target_pairs={{0,16},{8,24},{16,0},{24,8},{1,17},{9,25},{17,1},{25,9},{2,18},{10... | collective-permute-start | bytes 737288 | tf_op jit(solution)/shard_map/ppermute | solution.py:21
  55.5 9.3 %collective-permute-start.20 = (f32[264,256]{1,0:T(8,128)S(1)}, f32[264,256]{1,0:T(8,128)S(1)}, u32[]{:S(2)}, u32[]{:S(2)}) collective-permute-start(f32[264,256]{1,0:T(8,128)S(1)} %get-tuple-element.202.full_a), channel_id=1, source_target_pairs={{0,8},{8,0},{16,24},{24,16},{1,9},{9,1},{17,25},{25,17},{2,10},{10... | collective-permute-start | bytes 811016 | tf_op jit(solution)/shard_map/ppermute | solution.py:21
  56.1 8.8 %collective-permute-start.21 = (f32[256,256]{1,0:T(8,128)S(1)}, f32[256,256]{1,0:T(8,128)S(1)}, u32[]{:S(2)}, u32[]{:S(2)}) collective-permute-start(f32[256,256]{1,0:T(8,128)S(1)} %get-tuple-element.203.full_b), channel_id=1, source_target_pairs={{0,16},{8,24},{16,0},{24,8},{1,17},{9,25},{17,1},{25,9},{2,18},{10... | collective-permute-start | bytes 786440 | tf_op jit(solution)/shard_map/ppermute | solution.py:21
  63.2 8.2 %collective-permute-start.19 = (f32[480,128]{1,0:T(8,128)S(1)}, f32[480,128]{1,0:T(8,128)S(1)}, u32[]{:S(2)}, u32[]{:S(2)}) collective-permute-start(f32[480,128]{1,0:T(8,128)S(1)} %get-tuple-element.200), channel_id=1, source_target_pairs={{0,1},{1,0},{2,3},{3,2},{4,5},{5,4},{6,7},{7,6},{8,9},{9,8},{10,11... | collective-permute-start | bytes 737288 | tf_op jit(solution)/shard_map/ppermute | solution.py:279
  71.5 8.5 %collective-permute-start.26 = (f32[520,128]{1,0:T(8,128)S(1)}, f32[520,128]{1,0:T(8,128)S(1)}, u32[]{:S(2)}, u32[]{:S(2)}) collective-permute-start(f32[520,128]{1,0:T(8,128)S(1)} %get-tuple-element.221), channel_id=1, source_target_pairs={{0,1},{1,0},{2,3},{3,2},{4,5},{5,4},{6,7},{7,6},{8,9},{9,8},{10,11... | collective-permute-start | bytes 798728 | tf_op jit(solution)/shard_map/ppermute | solution.py:279
  73.1 18.0 %collective-permute-start.22 = (f32[480,128]{1,0:T(8,128)S(1)}, f32[480,128]{1,0:T(8,128)S(1)}, u32[]{:S(2)}, u32[]{:S(2)}) collective-permute-start(f32[480,128]{1,0:T(8,128)S(1)} %shard_map.80.refs_0_), channel_id=1, source_target_pairs={{0,3},{3,0},{1,2},{2,1},{4,7},{7,4},{5,6},{6,5},{8,11},{11,8},{9,1... | collective-permute-start | bytes 737288 | tf_op jit(solution)/shard_map/ppermute | solution.py:279
  80.0 15.7 %collective-permute-start.28 = (f32[520,128]{1,0:T(8,128)S(1)}, f32[520,128]{1,0:T(8,128)S(1)}, u32[]{:S(2)}, u32[]{:S(2)}) collective-permute-start(f32[520,128]{1,0:T(8,128)S(1)} %shard_map.82.refs_0_), channel_id=1, source_target_pairs={{0,3},{3,0},{1,2},{2,1},{4,7},{7,4},{5,6},{6,5},{8,11},{11,8},{9,1... | collective-permute-start | bytes 798728 | tf_op jit(solution)/shard_map/ppermute | solution.py:279
  91.2 8.0 %collective-permute-start.27 = (f32[480,128]{1,0:T(8,128)S(1)}, f32[480,128]{1,0:T(8,128)S(1)}, u32[]{:S(2)}, u32[]{:S(2)}) collective-permute-start(f32[480,128]{1,0:T(8,128)S(1)} %shard_map.83), channel_id=1, source_target_pairs={{0,1},{1,0},{2,3},{3,2},{4,5},{5,4},{6,7},{7,6},{8,9},{9,8},{10,11... | collective-permute-start | bytes 737288 | tf_op jit(solution)/shard_map/ppermute | solution.py:279
  95.7 8.8 %collective-permute-start.29 = (f32[520,128]{1,0:T(8,128)S(1)}, f32[520,128]{1,0:T(8,128)S(1)}, u32[]{:S(2)}, u32[]{:S(2)}) collective-permute-start(f32[520,128]{1,0:T(8,128)S(1)} %shard_map.84), channel_id=1, source_target_pairs={{0,1},{1,0},{2,3},{3,2},{4,5},{5,4},{6,7},{7,6},{8,9},{9,8},{10,11... | collective-permute-start | bytes 798728 | tf_op jit(solution)/shard_map/ppermute | solution.py:279
  (11 other events, 58.9 us)

commit v7 on v6

--- a/solution.py
+++ b/solution.py
@@ -10,7 +10,8 @@
 
 HIGHEST = lax.Precision.HIGHEST
 HIGH = lax.Precision.HIGH
-ROUNDS = (0.48,)
+ROUNDS = (0.2,0.38,)
+STEPS = "P0 P1 F0 P2 G0 F1 O0 F2 G1 M0 O1 G2 T0 M1 O2 T1 M2 T2".split()
 BF16, F32 = jnp.bfloat16, jnp.float32
 NT = (((1,), (1,)), ((), ()))
 NN = (((1,), (0,)), ((), ()))
@@ -49,7 +50,7 @@
     return mul(a[0], b[0], dims) + (mul(a[0], b[1], dims) + mul(a[1], b[0], dims))
 
 
-def call(body, outs, args, flops=0, scratch=(), aliases=None):
+def call(body, outs, args, scratch=()):
     vmem = pl.BlockSpec(memory_space=pltpu.VMEM)
     return pl.pallas_call(
         body,
@@ -57,8 +58,7 @@
         in_specs=[vmem] * len(args),
         out_specs=[vmem] * len(outs),
         scratch_shapes=list(scratch),
-        input_output_aliases=aliases or {},
-        cost_estimate=pl.CostEstimate(flops=flops // 2**20, bytes_accessed=0, transcendentals=0),
+        cost_estimate=pl.CostEstimate(flops=0, bytes_accessed=0, transcendentals=0),
         compiler_params=pltpu.CompilerParams(vmem_limit_bytes=40 * 2**20),
     )(*args)
 
@@ -125,7 +125,6 @@
         own_body,
         [shaped((rows, wide), BF16)] * 2,
         (own, *cent),
-        flops=8 * rows * wide * width,
         scratch=row_scratch(rows, width),
     )
 
@@ -151,7 +150,6 @@
         near_body,
         [shaped((3 * rows, wide), BF16)] * 2,
         (x, y, *cent, *own),
-        flops=16 * rows * wide * width,
         scratch=row_scratch(2 * rows, width),
     )
 
@@ -174,66 +172,61 @@
     return pl.ds(0, 2 * rows), pl.ds(rows, 2 * rows)
 
 
-def keep_body(edges, rows, w0, w1, running, targets, near_high, near_low, *kept):
+def keep_body(edges, rows, w0, w1, running, targets, near_high, near_low, *outs):
+    kept, going = outs[: len(edges)], outs[len(edges) :]
+    left, middle, right = pl.ds(0, rows), pl.ds(rows, rows), pl.ds(2 * rows, rows)
     for i, (a, b) in enumerate(edges):
         cols = pl.ds(a, b - a)
-        value = share((w0, w1), cols, (near_high, near_low), stays(rows)[i % 2])
-        own = slice(0, rows) if i % 2 == 0 else slice(rows, 2 * rows)
-        other = slice(rows, 2 * rows) if i % 2 == 0 else slice(0, rows)
-        kept[i][:, own] = value[:, own] + (running[cols] - targets[cols])
-        kept[i][:, other] = value[:, other]
+        value = share((w0, w1), cols, (near_high, near_low), pl.ds(0, 3 * rows))
+        own = value[:, rows : 2 * rows] + (running[cols] - targets[cols])
+        x, y = value[:, :rows], value[:, 2 * rows :]
+        if i % 2 == 0:
+            kept[i][:, left], kept[i][:, middle], going[i][...] = own, y, x
+        else:
+            kept[i][:, left], kept[i][:, middle], going[i][...] = x, own, y
 
 
 def keep_shares(edges, w0, w1, running, targets, near):
     rows = running.shape[1]
-    outs = [shaped((b - a, 2 * rows)) for a, b in edges]
-    flops = 12 * rows * near[0].shape[1] * w0.shape[0]
-    return call(
-        functools.partial(keep_body, edges, rows), outs, (w0, w1, running, targets, *near), flops
+    outs = [shaped((b - a, n * rows)) for n in (2, 1) for a, b in edges]
+    out = call(
+        functools.partial(keep_body, edges, rows), outs, (w0, w1, running, targets, *near)
     )
+    return out[: len(edges)], out[len(edges) :]
 
 
 def far_body(edges, low_rows, high_rows, c_high, c_low, c_sq, near_high, near_low, w0, w1, *rest):
-    outs, (high, low, row_sq) = rest[:-3], rest[-3:]
+    count = len(edges)
+    going, outs, (high, low, row_sq) = rest[:count], rest[count:-3], rest[-3:]
     far_high, far_low, sent = outs[0], outs[1], outs[2:]
-    rows = low.shape[0]
+    rows = high.shape[0]
+    left, middle, right = pl.ds(0, rows), pl.ds(rows, rows), pl.ds(2 * rows, rows)
     fill((low_rows, high_rows), high, low, row_sq)
     for far, near in ((far_high, near_high), (far_low, near_low)):
-        far[pl.ds(0, rows)] = near[pl.ds(0, rows)]
-        far[pl.ds(2 * rows, rows)] = near[pl.ds(2 * rows, rows)]
+        far[left] = near[left]
+        far[right] = near[right]
 
     def put(to, pair):
-        far_high[pl.ds(rows, rows), to], far_low[pl.ds(rows, rows), to] = pair
+        far_high[middle, to], far_low[middle, to] = pair
 
     kernel_rows(high[...], low[...], row_sq[:, 0:1], (c_high, c_low, c_sq), put)
     for i, (a, b) in enumerate(edges):
-        sent[i][...] = share((w0, w1), pl.ds(a, b - a), (far_high, far_low), goes(rows)[i % 2])
-
-
-def far_kernels(edges, low, high, cent, near, w0, w1):
+        value = share((w0, w1), pl.ds(a, b - a), (far_high, far_low), middle)
+        sent[i][:, left], sent[i][:, middle] = (
+            (going[i][...], value) if i % 2 == 0 else (value, going[i][...])
+        )
+
+
+def far_kernels(edges, low, high, cent, near, w0, w1, going):
     rows, width = 2 * low.shape[0], low.shape[1]
-    wide = cent[0].shape[0]
     outs = [shaped(near[0].shape, BF16)] * 2 + [shaped((b - a, 2 * rows)) for a, b in edges]
     out = call(
         functools.partial(far_body, edges),
         outs,
-        (low, high, *cent, *near, w0, w1),
-        flops=8 * rows * wide * width,
+        (low, high, *cent, *near, w0, w1, *going),
         scratch=row_scratch(rows, width),
     )
     return out[:2], out[2:]
-
-
-def send_body(edges, rows, w0, w1, far_high, far_low, *sent):
-    for i, (a, b) in enumerate(edges):
-        sent[i][...] = share((w0, w1), pl.ds(a, b - a), (far_high, far_low), goes(rows)[i % 2])
-
-
-def send_shares(edges, w0, w1, far):
-    rows = far[0].shape[0] // 3
-    outs = [shaped((b - a, 2 * rows)) for a, b in edges]
-    flops = sum(12 * rows * far[0].shape[1] * (b - a) for a, b in edges)
-    return call(functools.partial(send_body, edges, rows), outs, (w0, w1, *far), flops)
 
 
 PARTS = 3
@@ -269,9 +262,8 @@
 
 def grad_parts(factor, full, other, near, far):
     cols, half = full[0].shape[0] + full[1].shape[0], near[0].shape[1] // 2
-    flops = 12 * cols * full[0].shape[1] * 2 * half
     outs = [shaped((cols, half))] + [shaped((b - a, half)) for a, b in part_rows(cols)]
-    out = call(functools.partial(grad_body, factor), outs, (*full, *other, *near, *far), flops)
+    out = call(functools.partial(grad_body, factor), outs, (*full, *other, *near, *far))
     return out[1:], out[0]
 
 
@@ -353,7 +345,8 @@
     low = swap(block_x[:mid], "chip", 2)
     high = swap(block_y[mid:], "chip", 1)
     near = line(near_kernels, block_x, block_y, cent, own)
-    far, sent = line(lambda *a: far_kernels(edges[:4], *a), low, high, cent, near, w0, w1)
+    kept, going = line(lambda *a: keep_shares(edges, *a), w0, w1, running_t, targets_t, near)
+    far, sent = line(lambda *a: far_kernels(edges, *a), low, high, cent, near, w0, w1, going)
 
     axes = ((1, 2), (2, 1))
     place = lax.axis_index("col")
@@ -389,21 +382,10 @@
         (total[r],) = line(add, [mine[r]], [across[r]])
         back[r] = pass_line(total[r], BESIDE)
 
-    coming[0] = both(sent[0:2], 0)
-    coming[1] = both(line.hold(tuple(sent[2:4])), 0)
-    kept = line(lambda *a: keep_shares(edges, *a), w0, w1, running_t, targets_t, near)
-    do_partial(0)
-    do_partial(1)
-    do_full(0)
-    do_full(1)
-    do_grad(0)
-    do_owned(0)
-    do_grad(1)
-    do_mine(0)
-    do_owned(1)
-    do_mine(1)
-    do_total(0)
-    do_total(1)
+    for r in range(rounds):
+        coming[r] = both(sent[2 * r : 2 * r + 2], 0)
+    for step in STEPS:
+        dict(P=do_partial, F=do_full, G=do_grad, O=do_owned, M=do_mine, T=do_total)[step[0]](int(step[1]))
 
     first = [jnp.where(ends, t, b) for t, b in zip(total, back)]
     second = [jnp.where(ends, b, t) for t, b in zip(total, back)]

time: 106 us -> 109 us (1.028)
  starting transfers between devices: 40.1 us -> 42.9 us
  Pallas kernels: 9.82 us -> 12.2 us
  waiting for transfers between devices: 52.8 us -> 51.7 us
    ppermute x24 -> x33, starting transfers between devices: 20.6 us -> 27.6 us  [swap(): return lax.ppermute(value, axis, [(i, i ^ flip) for i in range(size)])]
    ppermute x24 -> x33, waiting for transfers between devices: 33.9 us -> 27.9 us  [swap(): return lax.ppermute(value, axis, [(i, i ^ flip) for i in range(size)])]
    ppermute x6 -> x9, waiting for transfers between devices: 18.9 us -> 23.9 us  [pass_line(): return lax.ppermute(value, 'col', pairs)]
    ppermute x6 -> x9, starting transfers between devices: 19.5 us -> 15.3 us  [pass_line(): return lax.ppermute(value, 'col', pairs)]
    pallas_call x17 -> x23, Pallas kernels: 9.82 us -> 12.2 us  [call(): pl.pallas_call(body, out_shape=outs, in_specs=[vmem] * len(args), out_spe...]
  transfers between devices with their start and end apart: 30 -> 42, of which waited for: 18 -> 17; matrix products, arithmetic and copies ran while one was open for 1% -> 0% of each run, Pallas kernels for 7% -> 8%
where the time goes in v7:
time: 109 us
  waiting for transfers between devices  51.7 us (47%)
  starting transfers between devices  42.9 us (39%)
  Pallas kernels  12.2 us (11%)
  other arithmetic  1.1 us (1%)
    ppermute x33, waiting for transfers between devices, swap(): return lax.ppermute(value, axis, [(i, i ^ flip) for i in range(size)])  27.9 us
    ppermute x33, starting transfers between devices, swap(): return lax.ppermute(value, axis, [(i, i ^ flip) for i in range(size)])  27.6 us
    ppermute x9, waiting for transfers between devices, pass_line(): return lax.ppermute(value, 'col', pairs)  23.9 us
    ppermute x9, starting transfers between devices, pass_line(): return lax.ppermute(value, 'col', pairs)  15.3 us
    pallas_call x23, Pallas kernels, call(): pl.pallas_call(body, out_shape=outs, in_specs=[vmem] * len(args), out_spe...  12.2 us
  transfers between devices with their start and end apart: 42, of which 17 were waited for; matrix products, arithmetic and copies ran while one was open for 0% of the time, Pallas kernels for 8%

profile of v7, /device:TPU:0, one launch (start us, length us, event | category | flops | bytes accessed | tf_op | source)
XLA Modules:
  0.0 109.1 jit_solution(14797047037546502658)
XLA Ops:
  1.2 2.9 %collective-permute-start.1 = (f32[128,1024]{1,0:T(8,128)}, f32[128,1024]{1,0:T(8,128)S(1)}, u32[]{:S(2)}, u32[]{:S(2)}) collective-permute-start(f32[128,1024]{1,0:T(8,128)} %own), channel_id=1, source_target_pairs={{0,8},{8,0},{16,24},{24,16},{1,9},{9,1},{17,25},{25,17},{2,10},{10... | collective-permute-start | bytes 1572872 | tf_op jit(solution)/shard_map/ppermute | solution.py:22
  5.7 10.9 %collective-permute-done.1.x = f32[128,1024]{1,0:T(8,128)S(1)} collective-permute-done((f32[128,1024]{1,0:T(8,128)}, f32[128,1024]{1,0:T(8,128)S(1)}, u32[]{:S(2)}, u32[]{:S(2)}) %collective-permute-start.1) | collective-permute-done | bytes 524320 | tf_op jit(solution)/shard_map/ppermute | solution.py:22
  16.6 1.8 %collective-permute-start.4 = (f32[64,1024]{1,0:T(8,128)S(1)}, f32[64,1024]{1,0:T(8,128)S(1)}, u32[]{:S(2)}, u32[]{:S(2)}) collective-permute-start(f32[64,1024]{1,0:T(8,128)S(1)} %slice.32), channel_id=1, source_target_pairs={{0,16},{8,24},{16,0},{24,8},{1,17},{9,25},{17,1},{25,9},{2,18},{10... | collective-permute-start | bytes 786440 | tf_op jit(solution)/shard_map/ppermute | solution.py:22
  18.4 1.6 %collective-permute-start.5 = (f32[64,1024]{1,0:T(8,128)S(1)}, f32[64,1024]{1,0:T(8,128)S(1)}, u32[]{:S(2)}, u32[]{:S(2)}) collective-permute-start(f32[64,1024]{1,0:T(8,128)S(1)} %slice.33), channel_id=1, source_target_pairs={{0,8},{8,0},{16,24},{24,16},{1,9},{9,1},{17,25},{25,17},{2,10},{10... | collective-permute-start | bytes 786440 | tf_op jit(solution)/shard_map/ppermute | solution.py:22
  20.5 1.7 %shard_map.69 = (bf16[128,512]{1,0:T(8,128)(2,1)S(1)}, bf16[128,512]{1,0:T(8,128)(2,1)S(1)}) custom-call(f32[128,1024]{1,0:T(8,128)S(1)} %copy-done.2, bf16[512,1024]{1,0:T(8,128)(2,1)S(1)} %get-tuple-element.197.c_high, bf16[512,1024]{1,0:T(8,128)(2,1)S(1)} %get-tuple-element.198.c_low, f32[8,512]{1,0:T(8,128)S(1)} %get-tuple-element.199.c_sq), custom_call_target="tpu_custom_call" | custom-call | tf_op jit(solution)/shard_map/pallas_call | solution.py:55
  22.2 1.6 %shard_map.70 = (bf16[384,512]{1,0:T(8,128)(2,1)S(1)}, bf16[384,512]{1,0:T(8,128)(2,1)S(1)}) custom-call(f32[128,1024]{1,0:T(8,128)S(1)} %collective-permute-done.1.x, f32[128,1024]{1,0:T(8,128)S(1)} %collective-permute-done.2.y, bf16[512,1024]{1,0:T(8,128)(2,1)S(1)} %get-tuple-element.197.c_high, bf16[512,1024]{1,0:T(8,128)(2,1)S(1)} %get-tuple-element.198.c_low, ...), custom_call_target="tpu_custom_call" | custom-call | tf_op jit(solution)/shard_map/pallas_call | solution.py:55
  23.8 2.4 %shard_map.71 = (f32[96,256]{1,0:T(8,128)S(1)}, f32[96,256]{1,0:T(8,128)S(1)}, f32[192,256]{1,0:T(8,128)S(1)}, f32[192,256]{1,0:T(8,128)S(1)}, f32[216,256]{1,0:...) custom-call(f32[1000,256]{1,0:T(8,128)S(1)} %bitcast.7, ...), custom_call_target="tpu_custom_call" | custom-call | tf_op jit(solution)/shard_map/pallas_call | solution.py:55
  26.2 3.3 %shard_map.72 = (bf16[384,512]{1,0:T(8,128)(2,1)S(1)}, bf16[384,512]{1,0:T(8,128)(2,1)S(1)}, f32[96,256]{1,0:T(8,128)S(1)}, f32[96,256]{1,0:T(8,128)S(1)}, f32[1...) custom-call(f32[64,1024]{1,0:T(8,128)S(1)} %collective-permute-done.4.low_rows, ...), custom_call_target="tpu_custom_call" | custom-call | tf_op jit(solution)/shard_map/pallas_call | solution.py:55
  35.0 1.8 %collective-permute-done.7.refs_3_ = f32[96,256]{1,0:T(8,128)S(1)} collective-permute-done((f32[96,256]{1,0:T(8,128)S(1)}, f32[96,256]{1,0:T(8,128)S(1)}, u32[]{:S(2)}, u32[]{:S(2)}) %collective-permute-start.7) | collective-permute-done | bytes 98336 | tf_op jit(solution)/shard_map/ppermute | solution.py:22
  44.9 3.5 %collective-permute-done.15.refs_3_ = f32[208,256]{1,0:T(8,128)S(1)} collective-permute-done((f32[208,256]{1,0:T(8,128)}, f32[208,256]{1,0:T(8,128)S(1)}, u32[]{:S(2)}, u32[]{:S(2)}) %collective-permute-start.15) | collective-permute-done | bytes 213024 | tf_op jit(solution)/shard_map/ppermute | solution.py:22
  49.1 2.5 %collective-permute-done.13.other_b = f32[96,256]{1,0:T(8,128)S(1)} collective-permute-done((f32[96,256]{1,0:T(8,128)S(1)}, f32[96,256]{1,0:T(8,128)S(1)}, u32[]{:S(2)}, u32[]{:S(2)}) %collective-permute-start.13) | collective-permute-done | bytes 98336 | tf_op jit(solution)/shard_map/ppermute | solution.py:22
  57.2 1.6 %collective-permute-start.21 = (f32[192,128]{1,0:T(8,128)S(1)}, f32[192,128]{1,0:T(8,128)S(1)}, u32[]{:S(2)}, u32[]{:S(2)}) collective-permute-start(f32[192,128]{1,0:T(8,128)S(1)} %get-tuple-element.267), channel_id=1, source_target_pairs={{0,1},{1,0},{2,3},{3,2},{4,5},{5,4},{6,7},{7,6},{8,9},{9,8},{10,11... | collective-permute-start | bytes 294920 | tf_op jit(solution)/shard_map/ppermute | solution.py:271
  58.9 3.3 %collective-permute-done.25.refs_3_ = f32[208,256]{1,0:T(8,128)S(1)} collective-permute-done((f32[208,256]{1,0:T(8,128)S(1)}, f32[208,256]{1,0:T(8,128)S(1)}, u32[]{:S(2)}, u32[]{:S(2)}) %collective-permute-start.25) | collective-permute-done | bytes 213024 | tf_op jit(solution)/shard_map/ppermute | solution.py:22
  63.9 2.4 %collective-permute-done.22.other_a = f32[192,256]{1,0:T(8,128)S(1)} collective-permute-done((f32[192,256]{1,0:T(8,128)S(1)}, f32[192,256]{1,0:T(8,128)S(1)}, u32[]{:S(2)}, u32[]{:S(2)}) %collective-permute-start.22) | collective-permute-done | bytes 196640 | tf_op jit(solution)/shard_map/ppermute | solution.py:22
  68.5 3.6 %collective-permute-start.26 = (f32[192,128]{1,0:T(8,128)S(1)}, f32[192,128]{1,0:T(8,128)S(1)}, u32[]{:S(2)}, u32[]{:S(2)}) collective-permute-start(f32[192,128]{1,0:T(8,128)S(1)} %shard_map.82.refs_0_), channel_id=1, source_target_pairs={{0,3},{3,0},{1,2},{2,1},{4,7},{7,4},{5,6},{6,5},{8,11},{11,8},{9,1... | collective-permute-start | bytes 294920 | tf_op jit(solution)/shard_map/ppermute | solution.py:271
  73.8 2.2 %collective-permute-done.26.refs_1_ = f32[192,128]{1,0:T(8,128)S(1)} collective-permute-done((f32[192,128]{1,0:T(8,128)S(1)}, f32[192,128]{1,0:T(8,128)S(1)}, u32[]{:S(2)}, u32[]{:S(2)}) %collective-permute-start.26) | collective-permute-done | bytes 98336 | tf_op jit(solution)/shard_map/ppermute | solution.py:271
  77.2 3.0 %collective-permute-done.33.refs_1_ = f32[384,128]{1,0:T(8,128)S(1)} collective-permute-done((f32[384,128]{1,0:T(8,128)S(1)}, f32[384,128]{1,0:T(8,128)S(1)}, u32[]{:S(2)}, u32[]{:S(2)}) %collective-permute-start.33) | collective-permute-done | bytes 196640 | tf_op jit(solution)/shard_map/ppermute | solution.py:271
  80.2 2.5 %collective-permute-start.34 = (f32[384,128]{1,0:T(8,128)S(1)}, f32[384,128]{1,0:T(8,128)S(1)}, u32[]{:S(2)}, u32[]{:S(2)}) collective-permute-start(f32[384,128]{1,0:T(8,128)S(1)} %shard_map.86.refs_0_), channel_id=1, source_target_pairs={{0,3},{3,0},{1,2},{2,1},{4,7},{7,4},{5,6},{6,5},{8,11},{11,8},{9,1... | collective-permute-start | bytes 589832 | tf_op jit(solution)/shard_map/ppermute | solution.py:271
  82.9 6.9 %collective-permute-done.34.refs_1_ = f32[384,128]{1,0:T(8,128)S(1)} collective-permute-done((f32[384,128]{1,0:T(8,128)S(1)}, f32[384,128]{1,0:T(8,128)S(1)}, u32[]{:S(2)}, u32[]{:S(2)}) %collective-permute-start.34) | collective-permute-done | bytes 196640 | tf_op jit(solution)/shard_map/ppermute | solution.py:271
  89.9 1.9 %collective-permute-start.38 = (f32[384,128]{1,0:T(8,128)S(1)}, f32[384,128]{1,0:T(8,128)S(1)}, u32[]{:S(2)}, u32[]{:S(2)}) collective-permute-start(f32[384,128]{1,0:T(8,128)S(1)} %shard_map.88), channel_id=1, source_target_pairs={{0,1},{1,0},{2,3},{3,2},{4,5},{5,4},{6,7},{7,6},{8,9},{9,8},{10,11... | collective-permute-start | bytes 589832 | tf_op jit(solution)/shard_map/ppermute | solution.py:271
  92.9 2.0 %collective-permute-start.40 = (f32[424,128]{1,0:T(8,128)S(1)}, f32[424,128]{1,0:T(8,128)S(1)}, u32[]{:S(2)}, u32[]{:S(2)}) collective-permute-start(f32[424,128]{1,0:T(8,128)S(1)} %shard_map.89.refs_0_), channel_id=1, source_target_pairs={{0,3},{3,0},{1,2},{2,1},{4,7},{7,4},{5,6},{6,5},{8,11},{11,8},{9,1... | collective-permute-start | bytes 651272 | tf_op jit(solution)/shard_map/ppermute | solution.py:271
  94.9 6.9 %collective-permute-done.40.refs_1_ = f32[424,128]{1,0:T(8,128)S(1)} collective-permute-done((f32[424,128]{1,0:T(8,128)S(1)}, f32[424,128]{1,0:T(8,128)S(1)}, u32[]{:S(2)}, u32[]{:S(2)}) %collective-permute-start.40) | collective-permute-done | bytes 217120 | tf_op jit(solution)/shard_map/ppermute | solution.py:271
  101.8 2.4 %collective-permute-start.41 = (f32[424,128]{1,0:T(8,128)S(1)}, f32[424,128]{1,0:T(8,128)S(1)}, u32[]{:S(2)}, u32[]{:S(2)}) collective-permute-start(f32[424,128]{1,0:T(8,128)S(1)} %shard_map.90), channel_id=1, source_target_pairs={{0,1},{1,0},{2,3},{3,2},{4,5},{5,4},{6,7},{7,6},{8,9},{9,8},{10,11... | collective-permute-start | bytes 651272 | tf_op jit(solution)/shard_map/ppermute | solution.py:271
  104.2 3.8 %collective-permute-done.41 = f32[424,128]{1,0:T(8,128)S(1)} collective-permute-done((f32[424,128]{1,0:T(8,128)S(1)}, f32[424,128]{1,0:T(8,128)S(1)}, u32[]{:S(2)}, u32[]{:S(2)}) %collective-permute-start.41) | collective-permute-done | bytes 217120 | tf_op jit(solution)/shard_map/ppermute | solution.py:271
  (109 shorter events, 31.7 us)
Async XLA Ops:
  0.6 19.3 %collective-permute-start.3 = (f32[256,1024]{1,0:T(8,128)}, f32[256,1024]{1,0:T(8,128)S(1)}, u32[]{:S(2)}, u32[]{:S(2)}) collective-permute-start(f32[256,1024]{1,0:T(8,128)} %mine_ref.1), channel_id=1, source_target_pairs={{0,4},{4,0},{1,5},{5,1},{2,6},{6,2},{3,7},{7,3},{8,12},{12,8},{9,1... | collective-permute-start | bytes 3145736 | tf_op jit(solution)/shard_map/ppermute | solution.py:22
  1.2 22.7 %collective-permute-start = (f32[1000,256]{1,0:T(8,128)}, f32[1000,256]{1,0:T(8,128)S(1)}, u32[]{:S(2)}, u32[]{:S(2)}) collective-permute-start(f32[1000,256]{1,0:T(8,128)} %bitcast.6), channel_id=1, source_target_pairs={{0,4},{4,0},{1,5},{5,1},{2,6},{6,2},{3,7},{7,3},{8,12},{12,8},{9,1... | collective-permute-start | bytes 3072008 | tf_op jit(solution)/shard_map/ppermute | solution.py:22
  1.2 15.3 %collective-permute-start.1 = (f32[128,1024]{1,0:T(8,128)}, f32[128,1024]{1,0:T(8,128)S(1)}, u32[]{:S(2)}, u32[]{:S(2)}) collective-permute-start(f32[128,1024]{1,0:T(8,128)} %own), channel_id=1, source_target_pairs={{0,8},{8,0},{16,24},{24,16},{1,9},{9,1},{17,25},{25,17},{2,10},{10... | collective-permute-start | bytes 1572872 | tf_op jit(solution)/shard_map/ppermute | solution.py:22
  4.2 14.2 %collective-permute-start.2 = (f32[128,1024]{1,0:T(8,128)}, f32[128,1024]{1,0:T(8,128)S(1)}, u32[]{:S(2)}, u32[]{:S(2)}) collective-permute-start(f32[128,1024]{1,0:T(8,128)} %own), channel_id=1, source_target_pairs={{0,16},{8,24},{16,0},{24,8},{1,17},{9,25},{17,1},{25,9},{2,18},{10... | collective-permute-start | bytes 1572872 | tf_op jit(solution)/shard_map/ppermute | solution.py:22
  16.6 9.7 %collective-permute-start.4 = (f32[64,1024]{1,0:T(8,128)S(1)}, f32[64,1024]{1,0:T(8,128)S(1)}, u32[]{:S(2)}, u32[]{:S(2)}) collective-permute-start(f32[64,1024]{1,0:T(8,128)S(1)} %slice.32), channel_id=1, source_target_pairs={{0,16},{8,24},{16,0},{24,8},{1,17},{9,25},{17,1},{25,9},{2,18},{10... | collective-permute-start | bytes 786440 | tf_op jit(solution)/shard_map/ppermute | solution.py:22
  30.5 9.5 %collective-permute-start.10 = (f32[192,256]{1,0:T(8,128)}, f32[192,256]{1,0:T(8,128)S(1)}, u32[]{:S(2)}, u32[]{:S(2)}) collective-permute-start(f32[192,256]{1,0:T(8,128)} %get-tuple-element.221), channel_id=1, source_target_pairs={{0,8},{8,0},{16,24},{24,16},{1,9},{9,1},{17,25},{25,17},{2,10},{10... | collective-permute-start | bytes 589832 | tf_op jit(solution)/shard_map/ppermute | solution.py:22
  32.1 9.0 %collective-permute-start.11 = (f32[192,256]{1,0:T(8,128)}, f32[192,256]{1,0:T(8,128)S(1)}, u32[]{:S(2)}, u32[]{:S(2)}) collective-permute-start(f32[192,256]{1,0:T(8,128)} %get-tuple-element.222), channel_id=1, source_target_pairs={{0,16},{8,24},{16,0},{24,8},{1,17},{9,25},{17,1},{25,9},{2,18},{10... | collective-permute-start | bytes 589832 | tf_op jit(solution)/shard_map/ppermute | solution.py:22
  38.6 10.4 %collective-permute-start.14 = (f32[216,256]{1,0:T(8,128)S(1)}, f32[216,256]{1,0:T(8,128)S(1)}, u32[]{:S(2)}, u32[]{:S(2)}) collective-permute-start(f32[216,256]{1,0:T(8,128)S(1)} %get-tuple-element.237), channel_id=1, source_target_pairs={{0,8},{8,0},{16,24},{24,16},{1,9},{9,1},{17,25},{25,17},{2,10},{10... | collective-permute-start | bytes 663560 | tf_op jit(solution)/shard_map/ppermute | solution.py:22
  39.9 8.4 %collective-permute-start.15 = (f32[208,256]{1,0:T(8,128)}, f32[208,256]{1,0:T(8,128)S(1)}, u32[]{:S(2)}, u32[]{:S(2)}) collective-permute-start(f32[208,256]{1,0:T(8,128)} %copy-done.5), channel_id=1, source_target_pairs={{0,16},{8,24},{16,0},{24,8},{1,17},{9,25},{17,1},{25,9},{2,18},{10... | collective-permute-start | bytes 638984 | tf_op jit(solution)/shard_map/ppermute | solution.py:22
  41.1 11.8 %collective-permute-start.19 = (f32[192,256]{1,0:T(8,128)S(1)}, f32[192,256]{1,0:T(8,128)S(1)}, u32[]{:S(2)}, u32[]{:S(2)}) collective-permute-start(f32[192,256]{1,0:T(8,128)S(1)} %get-tuple-element.257.refs_0_), channel_id=1, source_target_pairs={{0,16},{8,24},{16,0},{24,8},{1,17},{9,25},{17,1},{25,9},{2,18},{10... | collective-permute-start | bytes 589832 | tf_op jit(solution)/shard_map/ppermute | solution.py:22
  52.9 9.2 %collective-permute-start.24 = (f32[216,256]{1,0:T(8,128)S(1)}, f32[216,256]{1,0:T(8,128)S(1)}, u32[]{:S(2)}, u32[]{:S(2)}) collective-permute-start(f32[216,256]{1,0:T(8,128)S(1)} %get-tuple-element.270.refs_0_), channel_id=1, source_target_pairs={{0,16},{8,24},{16,0},{24,8},{1,17},{9,25},{17,1},{25,9},{2,18},{10... | collective-permute-start | bytes 663560 | tf_op jit(solution)/shard_map/ppermute | solution.py:22
  54.7 11.6 %collective-permute-start.22 = (f32[192,256]{1,0:T(8,128)S(1)}, f32[192,256]{1,0:T(8,128)S(1)}, u32[]{:S(2)}, u32[]{:S(2)}) collective-permute-start(f32[192,256]{1,0:T(8,128)S(1)} %get-tuple-element.275.full_a), channel_id=1, source_target_pairs={{0,8},{8,0},{16,24},{24,16},{1,9},{9,1},{17,25},{25,17},{2,10},{10... | collective-permute-start | bytes 589832 | tf_op jit(solution)/shard_map/ppermute | solution.py:22
  56.2 10.2 %collective-permute-start.23 = (f32[192,256]{1,0:T(8,128)S(1)}, f32[192,256]{1,0:T(8,128)S(1)}, u32[]{:S(2)}, u32[]{:S(2)}) collective-permute-start(f32[192,256]{1,0:T(8,128)S(1)} %get-tuple-element.276.full_b), channel_id=1, source_target_pairs={{0,16},{8,24},{16,0},{24,8},{1,17},{9,25},{17,1},{25,9},{2,18},{10... | collective-permute-start | bytes 589832 | tf_op jit(solution)/shard_map/ppermute | solution.py:22
  57.2 10.5 %collective-permute-start.21 = (f32[192,128]{1,0:T(8,128)S(1)}, f32[192,128]{1,0:T(8,128)S(1)}, u32[]{:S(2)}, u32[]{:S(2)}) collective-permute-start(f32[192,128]{1,0:T(8,128)S(1)} %get-tuple-element.267), channel_id=1, source_target_pairs={{0,1},{1,0},{2,3},{3,2},{4,5},{5,4},{6,7},{7,6},{8,9},{9,8},{10,11... | collective-permute-start | bytes 294920 | tf_op jit(solution)/shard_map/ppermute | solution.py:271
  62.2 10.1 %collective-permute-start.27 = (f32[216,256]{1,0:T(8,128)S(1)}, f32[216,256]{1,0:T(8,128)S(1)}, u32[]{:S(2)}, u32[]{:S(2)}) collective-permute-start(f32[216,256]{1,0:T(8,128)S(1)} %get-tuple-element.295.full_a), channel_id=1, source_target_pairs={{0,8},{8,0},{16,24},{24,16},{1,9},{9,1},{17,25},{25,17},{2,10},{10... | collective-permute-start | bytes 663560 | tf_op jit(solution)/shard_map/ppermute | solution.py:22
  62.9 9.4 %collective-permute-start.28 = (f32[208,256]{1,0:T(8,128)S(1)}, f32[208,256]{1,0:T(8,128)S(1)}, u32[]{:S(2)}, u32[]{:S(2)}) collective-permute-start(f32[208,256]{1,0:T(8,128)S(1)} %get-tuple-element.296.full_b), channel_id=1, source_target_pairs={{0,16},{8,24},{16,0},{24,8},{1,17},{9,25},{17,1},{25,9},{2,18},{10... | collective-permute-start | bytes 638984 | tf_op jit(solution)/shard_map/ppermute | solution.py:22
  73.2 9.6 %collective-permute-start.35 = (f32[144,256]{1,0:T(8,128)S(1)}, f32[144,256]{1,0:T(8,128)S(1)}, u32[]{:S(2)}, u32[]{:S(2)}) collective-permute-start(f32[144,256]{1,0:T(8,128)S(1)} %get-tuple-element.303), channel_id=1, source_target_pairs={{0,4},{4,0},{1,5},{5,1},{2,6},{6,2},{3,7},{7,3},{8,12},{12,8},{9,1... | collective-permute-start | bytes 442376 | tf_op jit(solution)/shard_map/ppermute | solution.py:22
  73.3 9.5 %collective-permute-start.36 = (f32[144,256]{1,0:T(8,128)S(1)}, f32[144,256]{1,0:T(8,128)S(1)}, u32[]{:S(2)}, u32[]{:S(2)}) collective-permute-start(f32[144,256]{1,0:T(8,128)S(1)} %get-tuple-element.310), channel_id=1, source_target_pairs={{0,4},{4,0},{1,5},{5,1},{2,6},{6,2},{3,7},{7,3},{8,12},{12,8},{9,1... | collective-permute-start | bytes 442376 | tf_op jit(solution)/shard_map/ppermute | solution.py:22
  73.7 9.0 %collective-permute-start.37 = (f32[136,256]{1,0:T(8,128)S(1)}, f32[136,256]{1,0:T(8,128)S(1)}, u32[]{:S(2)}, u32[]{:S(2)}) collective-permute-start(f32[136,256]{1,0:T(8,128)S(1)} %get-tuple-element.311), channel_id=1, source_target_pairs={{0,4},{4,0},{1,5},{5,1},{2,6},{6,2},{3,7},{7,3},{8,12},{12,8},{9,1... | collective-permute-start | bytes 417800 | tf_op jit(solution)/shard_map/ppermute | solution.py:22
  76.0 18.8 %collective-permute-start.32 = (f32[192,128]{1,0:T(8,128)S(1)}, f32[192,128]{1,0:T(8,128)S(1)}, u32[]{:S(2)}, u32[]{:S(2)}) collective-permute-start(f32[192,128]{1,0:T(8,128)S(1)} %shard_map.85), channel_id=1, source_target_pairs={{0,1},{1,0},{2,3},{3,2},{4,5},{5,4},{6,7},{7,6},{8,9},{9,8},{10,11... | collective-permute-start | bytes 294920 | tf_op jit(solution)/shard_map/ppermute | solution.py:271
  80.2 9.7 %collective-permute-start.34 = (f32[384,128]{1,0:T(8,128)S(1)}, f32[384,128]{1,0:T(8,128)S(1)}, u32[]{:S(2)}, u32[]{:S(2)}) collective-permute-start(f32[384,128]{1,0:T(8,128)S(1)} %shard_map.86.refs_0_), channel_id=1, source_target_pairs={{0,3},{3,0},{1,2},{2,1},{4,7},{7,4},{5,6},{6,5},{8,11},{11,8},{9,1... | collective-permute-start | bytes 589832 | tf_op jit(solution)/shard_map/ppermute | solution.py:271
  82.8 10.0 %collective-permute-start.39 = (f32[424,128]{1,0:T(8,128)S(1)}, f32[424,128]{1,0:T(8,128)S(1)}, u32[]{:S(2)}, u32[]{:S(2)}) collective-permute-start(f32[424,128]{1,0:T(8,128)S(1)} %get-tuple-element.316), channel_id=1, source_target_pairs={{0,1},{1,0},{2,3},{3,2},{4,5},{5,4},{6,7},{7,6},{8,9},{9,8},{10,11... | collective-permute-start | bytes 651272 | tf_op jit(solution)/shard_map/ppermute | solution.py:271
  89.9 14.2 %collective-permute-start.38 = (f32[384,128]{1,0:T(8,128)S(1)}, f32[384,128]{1,0:T(8,128)S(1)}, u32[]{:S(2)}, u32[]{:S(2)}) collective-permute-start(f32[384,128]{1,0:T(8,128)S(1)} %shard_map.88), channel_id=1, source_target_pairs={{0,1},{1,0},{2,3},{3,2},{4,5},{5,4},{6,7},{7,6},{8,9},{9,8},{10,11... | collective-permute-start | bytes 589832 | tf_op jit(solution)/shard_map/ppermute | solution.py:271
  92.9 8.9 %collective-permute-start.40 = (f32[424,128]{1,0:T(8,128)S(1)}, f32[424,128]{1,0:T(8,128)S(1)}, u32[]{:S(2)}, u32[]{:S(2)}) collective-permute-start(f32[424,128]{1,0:T(8,128)S(1)} %shard_map.89.refs_0_), channel_id=1, source_target_pairs={{0,3},{3,0},{1,2},{2,1},{4,7},{7,4},{5,6},{6,5},{8,11},{11,8},{9,1... | collective-permute-start | bytes 651272 | tf_op jit(solution)/shard_map/ppermute | solution.py:271
  (25 other events, 144.1 us)

commit v8 on v7

v8 whole, which is shorter than its diff:
```python
import functools
import math

import jax
import jax.numpy as jnp
from jax import lax
from jax.experimental import pallas as pl
from jax.experimental.pallas import tpu as pltpu
from jax.sharding import Mesh, PartitionSpec as P

HIGHEST = lax.Precision.HIGHEST
HIGH = lax.Precision.HIGH
ROUNDS = (0.48,)
STEPS = ("P0 P1 F0 F1", "G0 O0 G1 M0", "O1 M1 T0 T1")
BF16, F32 = jnp.bfloat16, jnp.float32
NT = (((1,), (1,)), ((), ()))
NN = (((1,), (0,)), ((), ()))


def swap(value, axis, flip=1):
    size = lax.axis_size(axis)
    return lax.ppermute(value, axis, [(i, i ^ flip) for i in range(size)])


class Line:
    def __init__(self):
        self.last = None

    def hold(self, args):
        if self.last is None:
            return args
        return lax.optimization_barrier((args, self.last))[0]

    def __call__(self, step, *args):
        out = step(*self.hold(args))
        self.last = jax.tree.leaves(out)[0]
        return out


def halves(value):
    high = value.astype(BF16)
    return high, (value - high.astype(F32)).astype(BF16)


def mul(a, b, dims):
    return lax.dot_general(a, b, dims, preferred_element_type=F32)


def mul3(a, b, dims):
    return mul(a[0], b[0], dims) + (mul(a[0], b[1], dims) + mul(a[1], b[0], dims))


def call(body, outs, args, scratch=()):
    vmem = pl.BlockSpec(memory_space=pltpu.VMEM)
    return pl.pallas_call(
        body,
        out_shape=outs,
        in_specs=[vmem] * len(args),
        out_specs=[vmem] * len(outs),
        scratch_shapes=list(scratch),
        cost_estimate=pl.CostEstimate(flops=0, bytes_accessed=0, transcendentals=0),
        compiler_params=pltpu.CompilerParams(vmem_limit_bytes=40 * 2**20),
    )(*args)


def shaped(shape, dtype=F32):
    return jax.ShapeDtypeStruct(shape, dtype)


def cent_body(mine_ref, theirs_ref, high_ref, low_ref, sq_ref):
    half = mine_ref.shape[0]
    for i, ref in enumerate((mine_ref, theirs_ref)):
        for at in range(0, half, 128):
            to = pl.ds(i * half + at, 128)
            value = ref[pl.ds(at, 128)]
            high_ref[to], low_ref[to] = halves(value)
            total = jnp.sum(value * value, axis=1, keepdims=True)
            sq_ref[:, to] = jnp.broadcast_to(total, (128, 128)).T[:8]


def split_cent(mine, theirs):
    half, width = mine.shape
    pair = [shaped((2 * half, width), BF16)] * 2
    return call(cent_body, pair + [shaped((8, 2 * half))], (mine, theirs))


def kernel_rows(high, low, row_sq, cent_refs, put):
    cent_high, cent_low, cent_sq = cent_refs
    scale = -4.0 / math.sqrt(cent_high.shape[1])
    for at in range(0, cent_high.shape[0], 256):
        to = pl.ds(at, 256)
        ch, cl = cent_high[to], cent_low[to]
        crossed = mul(high, ch, NT) + (mul(high, cl, NT) + mul(low, ch, NT) + mul(low, cl, NT))
        dist_sq = row_sq + cent_sq[0:1, to] - 2.0 * crossed
        put(to, halves(jnp.exp(jnp.sqrt(dist_sq + 1.0) * scale)))


def fill(refs, high_ref, low_ref, sq_ref):
    at = 0
    for ref in refs:
        to = pl.ds(at, ref.shape[0])
        value = ref[...]
        high_ref[to], low_ref[to] = halves(value)
        sq_ref[to] = jnp.broadcast_to(jnp.sum(value * value, axis=1, keepdims=True), (ref.shape[0], 128))
        at += ref.shape[0]


def own_body(own, c_high, c_low, c_sq, own_high, own_low, high, low, row_sq):
    fill((own,), high, low, row_sq)

    def put(to, pair):
        own_high[:, to], own_low[:, to] = pair

    kernel_rows(high[...], low[...], row_sq[:, 0:1], (c_high, c_low, c_sq), put)


def row_scratch(rows, width):
    return [pltpu.VMEM((rows, width), BF16)] * 2 + [pltpu.VMEM((rows, 128), F32)]


def own_kernels(own, cent):
    rows, width = own.shape
    wide = cent[0].shape[0]
    return call(
        own_body,
        [shaped((rows, wide), BF16)] * 2,
        (own, *cent),
        scratch=row_scratch(rows, width),
    )


def near_body(first, second, c_high, c_low, c_sq, own_high, own_low, *rest):
    stay_high, stay_low, first_high, first_low, high, low, row_sq = rest
    rows = first.shape[0]
    fill((first, second), high, low, row_sq)
    stay_high[pl.ds(0, rows)] = own_high[...]
    stay_low[pl.ds(0, rows)] = own_low[...]

    def put(to, pair):
        for stay, ref, value in zip((stay_high, stay_low), (first_high, first_low), pair):
            ref[:, to] = value[:rows]
            stay[pl.ds(rows, rows), to] = value[rows:]

    kernel_rows(high[...], low[...], row_sq[:, 0:1], (c_high, c_low, c_sq), put)


def near_kernels(first, second, cent, own):
    rows, width = first.shape
    wide = cent[0].shape[0]
    outs = [shaped((n * rows, wide), BF16) for n in (2, 2, 1, 1)]
    out = call(
        near_body, outs, (first, second, *cent, *own), scratch=row_scratch(2 * rows, width)
    )
    return out[:2], out[2:]


def share(w_refs, cols, k_refs):
    half = w_refs[0].shape[1]
    total = None
    for i, ref in enumerate(w_refs):
        kept = pl.ds(i * half, half)
        part = mul3(halves(ref[cols]), (k_refs[0][:, kept], k_refs[1][:, kept]), NT)
        total = part if total is None else total + part
    return total


def keep_body(edges, w0, w1, running, targets, stay_high, stay_low, *kept):
    rows = running.shape[1]
    left, right = pl.ds(0, rows), pl.ds(rows, rows)
    for ref, (a, b) in zip(kept, edges):
        cols = pl.ds(a, b - a)
        value = share((w0, w1), cols, (stay_high, stay_low))
        ref[:, left] = value[:, :rows] + (running[cols] - targets[cols])
        ref[:, right] = value[:, rows:]


def keep_shares(edges, w0, w1, running, targets, stay):
    outs = [shaped((b - a, 2 * running.shape[1])) for a, b in edges]
    return call(functools.partial(keep_body, edges), outs, (w0, w1, running, targets, *stay))


def far_body(edges, far, c_high, c_low, c_sq, first_high, first_low, w0, w1, *rest):
    go_high, go_low, *sent = rest[:-3]
    high, low, row_sq = rest[-3:]
    rows = far.shape[0]
    fill((far,), high, low, row_sq)
    go_high[pl.ds(0, rows)] = first_high[...]
    go_low[pl.ds(0, rows)] = first_low[...]

    def put(to, pair):
        go_high[pl.ds(rows, rows), to], go_low[pl.ds(rows, rows), to] = pair

    kernel_rows(high[...], low[...], row_sq[:, 0:1], (c_high, c_low, c_sq), put)
    for ref, (a, b) in zip(sent, edges):
        ref[...] = share((w0, w1), pl.ds(a, b - a), (go_high, go_low))


def far_kernels(edges, far, cent, first, w0, w1):
    rows, width = far.shape
    outs = [shaped((2 * rows, cent[0].shape[0]), BF16)] * 2
    outs += [shaped((b - a, 2 * rows)) for a, b in edges]
    out = call(
        functools.partial(far_body, edges),
        outs,
        (far, *cent, *first, w0, w1),
        scratch=row_scratch(rows, width),
    )
    return out[:2], out[2:]


def send_body(edges, w0, w1, go_high, go_low, *sent):
    for ref, (a, b) in zip(sent, edges):
        ref[...] = share((w0, w1), pl.ds(a, b - a), (go_high, go_low))


def send_shares(edges, w0, w1, go):
    outs = [shaped((b - a, go[0].shape[0])) for a, b in edges]
    return call(functools.partial(send_body, edges), outs, (w0, w1, *go))


PARTS = 3


def part_rows(size):
    step = -(-size // PARTS // 8) * 8
    return [(at, min(size, at + step)) for at in range(0, size, step)]


def grad_body(factor, full, other, stay_high, stay_low, go_high, go_low, here, *gone):
    half = here.shape[1]
    full_pair, other_pair = halves(full[...]), halves(other[...])

    def part(cols):
        return factor * (
            mul3(full_pair, (stay_high[:, cols], stay_low[:, cols]), NN)
            + mul3(other_pair, (go_high[:, cols], go_low[:, cols]), NN)
        )

    away = part(pl.ds(half, half))
    for ref, (a, b) in zip(gone, part_rows(here.shape[0])):
        ref[...] = away[a:b]
    here[...] = part(pl.ds(0, half))


def grad_parts(factor, full, other, stay, go):
    cols, half = full.shape[0], stay[0].shape[1] // 2
    outs = [shaped((cols, half))] + [shaped((b - a, half)) for a, b in part_rows(cols)]
    out = call(functools.partial(grad_body, factor), outs, (full, other, *stay, *go))
    return out[1:], out[0]


def pass_line(value, pairs):
    return lax.ppermute(value, "col", pairs)


BESIDE = [(0, 1), (1, 0), (2, 3), (3, 2)]
ACROSS = [(0, 3), (3, 0), (1, 2), (2, 1)]


def add_body(a, b, out):
    out[...] = a[...] + b[...]


def add(a, b):
    return call(add_body, [shaped(a.shape)], (a, b))[0]


def turn_body(a, b, out):
    rows = a.shape[1] // 2
    left, right = pl.ds(0, rows), pl.ds(rows, rows)
    out[:, left] = a[:, left] + b[:, right]
    out[:, right] = a[:, right] + b[:, left]


def turn(a, b):
    return call(turn_body, [shaped(a.shape)], (a, b))[0]


def split_body(here, *refs):
    gone, sends, mine = refs[:-2], refs[-2], refs[-1]
    place = lax.axis_index("col")
    ends = (place == 0) | (place == 3)
    quarter = mine.shape[1]
    left, right = pl.ds(0, quarter), pl.ds(quarter, quarter)

    def put(kept, sent):
        for ref, (a, b) in zip(gone, part_rows(here.shape[0])):
            to = pl.ds(a, b - a)
            mine[to] = here[to, kept] + ref[:, kept]
            sends[to] = here[to, sent] + ref[:, sent]

    pl.when(ends)(lambda: put(left, right))
    pl.when(~ends)(lambda: put(right, left))


def split(here, gone):
    outs = [shaped((here.shape[0], here.shape[1] // 2))] * 2
    return call(split_body, outs, (here, *gone))


def cut(out):
    edges, at = [], 0
    for part in ROUNDS + (1.0,):
        to = out if part == 1.0 else min(out, at + round(out * part / 8) * 8)
        edges.append((at, to))
        at = to
    return edges


def hop(value, second):
    pairs = []
    for chip in range(4):
        for core in range(2):
            flip = 1 if core == second else 2
            pairs.append((chip * 2 + core, (chip ^ flip) * 2 + core))
    return lax.ppermute(value, ("chip", "core"), pairs)


def square(batch, running_t, targets_t, centers, weights_t, factor):
    rows, out = batch.shape[0], weights_t.shape[0]
    edges = cut(out)
    rounds = len(edges)
    line = Line()
    first = hop(batch, 0)
    second = hop(batch, 1)
    cent_theirs = swap(centers, "core")
    w0, w1 = weights_t, swap(weights_t, "core")
    cent = line(split_cent, centers, cent_theirs)
    own = line(own_kernels, batch, cent)
    far = hop(first, 1)
    stay, go_first = line(near_kernels, first, second, cent, own)
    go, sent = line(lambda *a: far_kernels(edges[:1], *a), far, cent, go_first, w0, w1)

    coming, crossing, beside, across, back = ([None] * rounds for _ in range(5))
    partial, full, other, gone, here, mine, total = ([None] * rounds for _ in range(7))

    def do_partial(r):
        partial[r] = line(add, kept[r], coming[r])
        crossing[r] = hop(partial[r], 1)

    def do_full(r):
        full[r] = line(turn, partial[r], crossing[r])
        other[r] = hop(full[r], 0)

    def do_grad(r):
        gone[r], here[r] = line(lambda *a: grad_parts(factor, *a), full[r], other[r], stay, go)
        gone[r] = [swap(part, "core") for part in gone[r]]

    def do_owned(r):
        sends, mine[r] = line(split, here[r], gone[r])
        beside[r] = pass_line(sends, BESIDE)

    def do_mine(r):
        mine[r] = line(add, mine[r], beside[r])
        across[r] = pass_line(mine[r], ACROSS)

    def do_total(r):
        total[r] = line(add, mine[r], across[r])
        back[r] = pass_line(total[r], BESIDE)

    sent = list(sent) + list(line(lambda *a: send_shares(edges[1:], *a), w0, w1, go))
    coming = [hop(value, 0) for value in sent]
    kept = line(lambda *a: keep_shares(edges, *a), w0, w1, running_t, targets_t, stay)
    steps = dict(P=do_partial, F=do_full, G=do_grad, O=do_owned, M=do_mine, T=do_total)
    for step in " ".join(STEPS).split():
        steps[step[0]](int(step[1]))

    place = lax.axis_index("col")
    ends = (place == 0) | (place == 3)
    left = [jnp.where(ends, t, b) for t, b in zip(total, back)]
    right = [jnp.where(ends, b, t) for t, b in zip(total, back)]
    gradient = jnp.concatenate([jnp.concatenate(left), jnp.concatenate(right)], axis=1)
    residual = jnp.concatenate([f[:, :rows] for f in full])
    return gradient, residual


def any_plane(batch, running_t, targets_t, centers, weights_t, factor):
    def dot(a, b, dims, precision):
        return lax.dot_general(a, b, dims, precision=precision, preferred_element_type=F32)

    rows_here, chips = batch.shape[0], lax.axis_size("chip")
    half, out = centers.shape[0], weights_t.shape[0]
    cent = jnp.concatenate([centers, swap(centers, "core")], axis=0)
    weight = jnp.concatenate([weights_t, swap(weights_t, "core")], axis=1)
    rows = lax.all_gather(batch, "chip", axis=0, tiled=True)
    row_sq = jnp.sum(rows * rows, axis=1, keepdims=True)
    dist_sq = row_sq + jnp.sum(cent * cent, axis=1)[None, :] - 2.0 * dot(rows, cent, NT, HIGHEST)
    kernel = jnp.exp(-jnp.sqrt(dist_sq + 1.0) / (math.sqrt(rows.shape[1]) / 4.0))
    shares = dot(weight, kernel, NT, HIGH).reshape(out, chips, rows_here).transpose(1, 0, 2)
    residual = running_t - targets_t + lax.psum_scatter(shares, "chip", scatter_dimension=0, tiled=False)
    moved = lax.all_gather(residual, "chip", axis=0, tiled=False)
    moved = moved.transpose(1, 0, 2).reshape(out, chips * rows_here)
    gradient = dot(moved, kernel, NN, HIGH) * factor
    owned = gradient[:, :half] + swap(gradient[:, half:], "core")
    return lax.psum(owned, "col"), residual


def per_device(batch, running, targets, centers, weights):
    chips, depth = lax.axis_size("chip"), lax.axis_size("col")
    factor = 1.0 / math.sqrt(batch.shape[0] * chips * 2 * depth)
    plane = square if (chips, depth) == (4, 4) else any_plane
    gradient, residual = plane(batch, running.T, targets.T, centers, weights.T, factor)
    return gradient.T, residual.T


def solution(mesh):
    owners, depth = mesh.shape["row"], mesh.shape["col"]
    split = Mesh(mesh.devices.reshape(owners // 2, 2, depth), ("chip", "core", "col"))
    everywhere = P(("chip", "core", "col"), None)
    owned = P(("chip", "core"), None)
    return jax.shard_map(
        per_device,
        mesh=split,
        in_specs=(everywhere, everywhere, everywhere, owned, owned),
        out_specs=(owned, everywhere),
        check_vma=False,
    )
```

time: 109 us -> 112 us (1.028)
  waiting for transfers between devices: 51.7 us -> 56.5 us
  starting transfers between devices: 42.9 us -> 39.4 us
  Pallas kernels: 12.2 us -> 10 us
  local copies, waits for them, and re-layouts: 0.12 us -> 2.26 us
    ppermute x0 -> x9, waiting for transfers between devices: none -> 38.9 us  [hop(): return lax.ppermute(value, ('chip', 'core'), pairs)]
    ppermute x33 -> x8, waiting for transfers between devices: 27.9 us -> 1.33 us  [swap(): return lax.ppermute(value, axis, [(i, i ^ flip) for i in range(size)])]
    ppermute x33 -> x8, starting transfers between devices: 27.6 us -> 1.99 us  [swap(): return lax.ppermute(value, axis, [(i, i ^ flip) for i in range(size)])]
    ppermute x0 -> x9, starting transfers between devices: none -> 18 us  [hop(): return lax.ppermute(value, ('chip', 'core'), pairs)]
    ppermute x9 -> x6, waiting for transfers between devices: 23.9 us -> 16.3 us  [pass_line(): return lax.ppermute(value, 'col', pairs)]
    ppermute x9 -> x6, starting transfers between devices: 15.3 us -> 19.5 us  [pass_line(): return lax.ppermute(value, 'col', pairs)]
    pallas_call x23 -> x18, Pallas kernels: 12.2 us -> 10 us  [call(): pl.pallas_call(body, out_shape=outs, in_specs=[vmem] * len(args), out_spe...]
    unnamed x19 -> x10, local copies, waits for them, and re-layouts: 0.07 us -> 2.22 us
  transfers between devices with their start and end apart: 42 -> 23, of which waited for: 17 -> 13; matrix products, arithmetic and copies ran while one was open for 0% -> 1% of each run, Pallas kernels for 8% -> 7%
where the time goes in v8:
time: 112 us; the launch traced here: 111 us
  waiting for transfers between devices  56.5 us (50%)
  starting transfers between devices  39.4 us (35%)
  Pallas kernels  10 us (9%)
  local copies, waits for them, and re-layouts  2.26 us (2%)
  other arithmetic  1.98 us (2%)
    ppermute x9, waiting for transfers between devices, hop(): return lax.ppermute(value, ('chip', 'core'), pairs)  38.9 us
    ppermute x6, starting transfers between devices, pass_line(): return lax.ppermute(value, 'col', pairs)  19.5 us
    ppermute x9, starting transfers between devices, hop(): return lax.ppermute(value, ('chip', 'core'), pairs)  18 us
    ppermute x6, waiting for transfers between devices, pass_line(): return lax.ppermute(value, 'col', pairs)  16.3 us
    pallas_call x18, Pallas kernels, call(): pl.pallas_call(body, out_shape=outs, in_specs=[vmem] * len(args), out_spe...  10 us
  transfers between devices with their start and end apart: 23, of which 13 were waited for; matrix products, arithmetic and copies ran while one was open for 1% of the time, Pallas kernels for 7%

profile of v8, /device:TPU:0, one launch (start us, length us, event | category | flops | bytes accessed | tf_op | source)
XLA Modules:
  0.0 111.0 jit_solution(2087187781646161256)
XLA Ops:
  1.1 2.6 %collective-permute-start.1 = (f32[128,1024]{1,0:T(8,128)}, f32[128,1024]{1,0:T(8,128)S(1)}, u32[]{:S(2)}, u32[]{:S(2)}) collective-permute-start(f32[128,1024]{1,0:T(8,128)} %own), channel_id=1, source_target_pairs={{0,8},{4,20},{8,0},{12,28},{16,24},{20,4},{24,16},{28,12},{1,9},{5... | collective-permute-start | bytes 1572872 | tf_op jit(solution)/shard_map/ppermute | solution.py:316
  5.2 10.4 %collective-permute-done.1.first = f32[128,1024]{1,0:T(8,128)S(1)} collective-permute-done((f32[128,1024]{1,0:T(8,128)}, f32[128,1024]{1,0:T(8,128)S(1)}, u32[]{:S(2)}, u32[]{:S(2)}) %collective-permute-start.1) | collective-permute-done | bytes 524320 | tf_op jit(solution)/shard_map/ppermute | solution.py:316
  15.7 2.1 %collective-permute-start.4 = (f32[128,1024]{1,0:T(8,128)S(1)}, f32[128,1024]{1,0:T(8,128)S(1)}, u32[]{:S(2)}, u32[]{:S(2)}) collective-permute-start(f32[128,1024]{1,0:T(8,128)S(1)} %collective-permute-done.1.first), channel_id=1, source_target_pairs={{0,16},{4,12},{8,24},{12,4},{16,0},{20,28},{24,8},{28,20},{1,17},{... | collective-permute-start | bytes 1572872 | tf_op jit(solution)/shard_map/ppermute | solution.py:316
  20.1 1.6 %shard_map.69 = (bf16[128,512]{1,0:T(8,128)(2,1)S(1)}, bf16[128,512]{1,0:T(8,128)(2,1)S(1)}) custom-call(f32[128,1024]{1,0:T(8,128)S(1)} %copy-done.2, bf16[512,1024]{1,0:T(8,128)(2,1)S(1)} %get-tuple-element.114.c_high, bf16[512,1024]{1,0:T(8,128)(2,1)S(1)} %get-tuple-element.115.c_low, f32[8,512]{1,0:T(8,128)S(1)} %get-tuple-element.116.c_sq), custom_call_target="tpu_custom_call" | custom-call | tf_op jit(solution)/shard_map/pallas_call | solution.py:55
  23.3 1.6 %collective-permute-done.4.far = f32[128,1024]{1,0:T(8,128)S(1)} collective-permute-done((f32[128,1024]{1,0:T(8,128)S(1)}, f32[128,1024]{1,0:T(8,128)S(1)}, u32[]{:S(2)}, u32[]{:S(2)}) %collective-permute-start.4) | collective-permute-done | bytes 524320 | tf_op jit(solution)/shard_map/ppermute | solution.py:316
  24.9 2.2 %shard_map.71 = (bf16[256,512]{1,0:T(8,128)(2,1)S(1)}, bf16[256,512]{1,0:T(8,128)(2,1)S(1)}, f32[480,256]{1,0:T(8,128)S(1)}) custom-call(f32[128,1024]{1,0:T(8,128)S(1)} %collective-permute-done.4.far, bf16[512,1024]{1,0:T(8,128)(2,1)S(1)} %get-tuple-element.114.c_high, bf16[512,1024]{1,0:T(8,128)(2,1)S(1)} %get-tuple-element.115.c_low, ...), custom_call_target="tpu_custom_call" | custom-call | tf_op jit(solution)/shard_map/pallas_call | solution.py:55
  27.1 2.4 %collective-permute-start.5 = (f32[480,256]{1,0:T(8,128)S(1)}, f32[480,256]{1,0:T(8,128)S(1)}, u32[]{:S(2)}, u32[]{:S(2)}) collective-permute-start(f32[480,256]{1,0:T(8,128)S(1)} %get-tuple-element.134), channel_id=1, source_target_pairs={{0,8},{4,20},{8,0},{12,28},{16,24},{20,4},{24,16},{28,12},{1,9},{5... | collective-permute-start | bytes 1474568 | tf_op jit(solution)/shard_map/ppermute | solution.py:316
  31.8 4.6 %collective-permute-done.5.b = f32[480,256]{1,0:T(8,128)S(1)} collective-permute-done((f32[480,256]{1,0:T(8,128)S(1)}, f32[480,256]{1,0:T(8,128)S(1)}, u32[]{:S(2)}, u32[]{:S(2)}) %collective-permute-start.5) | collective-permute-done | bytes 491552 | tf_op jit(solution)/shard_map/ppermute | solution.py:316
  36.4 2.3 %collective-permute-start.6 = (f32[480,256]{1,0:T(8,128)S(1)}, f32[480,256]{1,0:T(8,128)S(1)}, u32[]{:S(2)}, u32[]{:S(2)}) collective-permute-start(f32[480,256]{1,0:T(8,128)S(1)} %shard_map.74.a), channel_id=1, source_target_pairs={{0,16},{4,12},{8,24},{12,4},{16,0},{20,28},{24,8},{28,20},{1,17},{... | collective-permute-start | bytes 1474568 | tf_op jit(solution)/shard_map/ppermute | solution.py:316
  38.7 9.0 %collective-permute-done.7.b = f32[520,256]{1,0:T(8,128)S(1)} collective-permute-done((f32[520,256]{1,0:T(8,128)S(1)}, f32[520,256]{1,0:T(8,128)S(1)}, u32[]{:S(2)}, u32[]{:S(2)}) %collective-permute-start.7) | collective-permute-done | bytes 532512 | tf_op jit(solution)/shard_map/ppermute | solution.py:316
  47.8 2.4 %collective-permute-start.9 = (f32[520,256]{1,0:T(8,128)S(1)}, f32[520,256]{1,0:T(8,128)S(1)}, u32[]{:S(2)}, u32[]{:S(2)}) collective-permute-start(f32[520,256]{1,0:T(8,128)S(1)} %shard_map.75.a), channel_id=1, source_target_pairs={{0,16},{4,12},{8,24},{12,4},{16,0},{20,28},{24,8},{28,20},{1,17},{... | collective-permute-start | bytes 1597448 | tf_op jit(solution)/shard_map/ppermute | solution.py:316
  50.2 2.4 %collective-permute-start.8 = (f32[480,256]{1,0:T(8,128)S(1)}, f32[480,256]{1,0:T(8,128)S(1)}, u32[]{:S(2)}, u32[]{:S(2)}) collective-permute-start(f32[480,256]{1,0:T(8,128)S(1)} %shard_map.76.full), channel_id=1, source_target_pairs={{0,8},{4,20},{8,0},{12,28},{16,24},{20,4},{24,16},{28,12},{1,9},{5... | collective-permute-start | bytes 1474568 | tf_op jit(solution)/shard_map/ppermute | solution.py:316
  52.6 10.6 %collective-permute-done.9.b = f32[520,256]{1,0:T(8,128)S(1)} collective-permute-done((f32[520,256]{1,0:T(8,128)S(1)}, f32[520,256]{1,0:T(8,128)S(1)}, u32[]{:S(2)}, u32[]{:S(2)}) %collective-permute-start.9) | collective-permute-done | bytes 532512 | tf_op jit(solution)/shard_map/ppermute | solution.py:316
  63.3 2.4 %collective-permute-start.14 = (f32[520,256]{1,0:T(8,128)S(1)}, f32[520,256]{1,0:T(8,128)S(1)}, u32[]{:S(2)}, u32[]{:S(2)}) collective-permute-start(f32[520,256]{1,0:T(8,128)S(1)} %shard_map.77.full), channel_id=1, source_target_pairs={{0,8},{4,20},{8,0},{12,28},{16,24},{20,4},{24,16},{28,12},{1,9},{5... | collective-permute-start | bytes 1597448 | tf_op jit(solution)/shard_map/ppermute | solution.py:316
  68.6 1.6 %collective-permute-start.13 = (f32[480,128]{1,0:T(8,128)S(1)}, f32[480,128]{1,0:T(8,128)S(1)}, u32[]{:S(2)}, u32[]{:S(2)}) collective-permute-start(f32[480,128]{1,0:T(8,128)S(1)} %get-tuple-element.159), channel_id=1, source_target_pairs={{0,1},{1,0},{2,3},{3,2},{4,5},{5,4},{6,7},{7,6},{8,9},{9,8},{10,11... | collective-permute-start | bytes 737288 | tf_op jit(solution)/shard_map/ppermute | solution.py:253
  70.2 2.6 %collective-permute-done.14.other = f32[520,256]{1,0:T(8,128)S(1)} collective-permute-done((f32[520,256]{1,0:T(8,128)S(1)}, f32[520,256]{1,0:T(8,128)S(1)}, u32[]{:S(2)}, u32[]{:S(2)}) %collective-permute-start.14) | collective-permute-done | bytes 532512 | tf_op jit(solution)/shard_map/ppermute | solution.py:316
  74.5 2.2 %collective-permute-done.13.b = f32[480,128]{1,0:T(8,128)S(1)} collective-permute-done((f32[480,128]{1,0:T(8,128)S(1)}, f32[480,128]{1,0:T(8,128)S(1)}, u32[]{:S(2)}, u32[]{:S(2)}) %collective-permute-start.13) | collective-permute-done | bytes 245792 | tf_op jit(solution)/shard_map/ppermute | solution.py:253
  76.9 1.6 %collective-permute-start.19 = (f32[520,128]{1,0:T(8,128)S(1)}, f32[520,128]{1,0:T(8,128)S(1)}, u32[]{:S(2)}, u32[]{:S(2)}) collective-permute-start(f32[520,128]{1,0:T(8,128)S(1)} %get-tuple-element.177), channel_id=1, source_target_pairs={{0,1},{1,0},{2,3},{3,2},{4,5},{5,4},{6,7},{7,6},{8,9},{9,8},{10,11... | collective-permute-start | bytes 798728 | tf_op jit(solution)/shard_map/ppermute | solution.py:253
  78.5 2.5 %collective-permute-start.15 = (f32[480,128]{1,0:T(8,128)S(1)}, f32[480,128]{1,0:T(8,128)S(1)}, u32[]{:S(2)}, u32[]{:S(2)}) collective-permute-start(f32[480,128]{1,0:T(8,128)S(1)} %shard_map.81.a), channel_id=1, source_target_pairs={{0,3},{3,0},{1,2},{2,1},{4,7},{7,4},{5,6},{6,5},{8,11},{11,8},{9,1... | collective-permute-start | bytes 737288 | tf_op jit(solution)/shard_map/ppermute | solution.py:253
  81.0 4.4 %collective-permute-done.19.b = f32[520,128]{1,0:T(8,128)S(1)} collective-permute-done((f32[520,128]{1,0:T(8,128)S(1)}, f32[520,128]{1,0:T(8,128)S(1)}, u32[]{:S(2)}, u32[]{:S(2)}) %collective-permute-start.19) | collective-permute-done | bytes 266272 | tf_op jit(solution)/shard_map/ppermute | solution.py:253
  85.4 11.1 %collective-permute-start.21 = (f32[520,128]{1,0:T(8,128)S(1)}, f32[520,128]{1,0:T(8,128)S(1)}, u32[]{:S(2)}, u32[]{:S(2)}) collective-permute-start(f32[520,128]{1,0:T(8,128)S(1)} %shard_map.83.a), channel_id=1, source_target_pairs={{0,3},{3,0},{1,2},{2,1},{4,7},{7,4},{5,6},{6,5},{8,11},{11,8},{9,1... | collective-permute-start | bytes 798728 | tf_op jit(solution)/shard_map/ppermute | solution.py:253
  96.7 4.4 %collective-permute-done.21.b = f32[520,128]{1,0:T(8,128)S(1)} collective-permute-done((f32[520,128]{1,0:T(8,128)S(1)}, f32[520,128]{1,0:T(8,128)S(1)}, u32[]{:S(2)}, u32[]{:S(2)}) %collective-permute-start.21) | collective-permute-done | bytes 266272 | tf_op jit(solution)/shard_map/ppermute | solution.py:253
  101.2 2.6 %collective-permute-start.22 = (f32[520,128]{1,0:T(8,128)S(1)}, f32[520,128]{1,0:T(8,128)S(1)}, u32[]{:S(2)}, u32[]{:S(2)}) collective-permute-start(f32[520,128]{1,0:T(8,128)S(1)} %shard_map.85), channel_id=1, source_target_pairs={{0,1},{1,0},{2,3},{3,2},{4,5},{5,4},{6,7},{7,6},{8,9},{9,8},{10,11... | collective-permute-start | bytes 798728 | tf_op jit(solution)/shard_map/ppermute | solution.py:253
  104.6 5.3 %collective-permute-done.22 = f32[520,128]{1,0:T(8,128)S(1)} collective-permute-done((f32[520,128]{1,0:T(8,128)S(1)}, f32[520,128]{1,0:T(8,128)S(1)}, u32[]{:S(2)}, u32[]{:S(2)}) %collective-permute-start.22) | collective-permute-done | bytes 266272 | tf_op jit(solution)/shard_map/ppermute | solution.py:253
  (56 shorter events, 15.3 us)
Async XLA Ops:
  0.6 17.2 %collective-permute-start.3 = (f32[256,1024]{1,0:T(8,128)}, f32[256,1024]{1,0:T(8,128)S(1)}, u32[]{:S(2)}, u32[]{:S(2)}) collective-permute-start(f32[256,1024]{1,0:T(8,128)} %mine_ref.1), channel_id=1, source_target_pairs={{0,4},{4,0},{1,5},{5,1},{2,6},{6,2},{3,7},{7,3},{8,12},{12,8},{9,1... | collective-permute-start | bytes 3145736 | tf_op jit(solution)/shard_map/ppermute | solution.py:22
  1.1 14.5 %collective-permute-start.1 = (f32[128,1024]{1,0:T(8,128)}, f32[128,1024]{1,0:T(8,128)S(1)}, u32[]{:S(2)}, u32[]{:S(2)}) collective-permute-start(f32[128,1024]{1,0:T(8,128)} %own), channel_id=1, source_target_pairs={{0,8},{4,20},{8,0},{12,28},{16,24},{20,4},{24,16},{28,12},{1,9},{5... | collective-permute-start | bytes 1572872 | tf_op jit(solution)/shard_map/ppermute | solution.py:316
  3.7 19.6 %collective-permute-start = (f32[1000,256]{1,0:T(8,128)}, f32[1000,256]{1,0:T(8,128)S(1)}, u32[]{:S(2)}, u32[]{:S(2)}) collective-permute-start(f32[1000,256]{1,0:T(8,128)} %bitcast.7), channel_id=1, source_target_pairs={{0,4},{4,0},{1,5},{5,1},{2,6},{6,2},{3,7},{7,3},{8,12},{12,8},{9,1... | collective-permute-start | bytes 3072008 | tf_op jit(solution)/shard_map/ppermute | solution.py:22
  3.9 17.8 %collective-permute-start.2 = (f32[128,1024]{1,0:T(8,128)}, f32[128,1024]{1,0:T(8,128)S(1)}, u32[]{:S(2)}, u32[]{:S(2)}) collective-permute-start(f32[128,1024]{1,0:T(8,128)} %own), channel_id=1, source_target_pairs={{0,16},{4,12},{8,24},{12,4},{16,0},{20,28},{24,8},{28,20},{1,17},{... | collective-permute-start | bytes 1572872 | tf_op jit(solution)/shard_map/ppermute | solution.py:316
  15.7 9.3 %collective-permute-start.4 = (f32[128,1024]{1,0:T(8,128)S(1)}, f32[128,1024]{1,0:T(8,128)S(1)}, u32[]{:S(2)}, u32[]{:S(2)}) collective-permute-start(f32[128,1024]{1,0:T(8,128)S(1)} %collective-permute-done.1.first), channel_id=1, source_target_pairs={{0,16},{4,12},{8,24},{12,4},{16,0},{20,28},{24,8},{28,20},{1,17},{... | collective-permute-start | bytes 1572872 | tf_op jit(solution)/shard_map/ppermute | solution.py:316
  21.7 3.3 %copy-start = (f32[256,1000]{0,1:T(8,128)S(1)}, f32[256,1000]{0,1:T(8,128)}, u32[]{:S(2)}) copy-start(f32[256,1000]{0,1:T(8,128)} %param.9) | copy-start | bytes 3072004
  27.1 9.2 %collective-permute-start.5 = (f32[480,256]{1,0:T(8,128)S(1)}, f32[480,256]{1,0:T(8,128)S(1)}, u32[]{:S(2)}, u32[]{:S(2)}) collective-permute-start(f32[480,256]{1,0:T(8,128)S(1)} %get-tuple-element.134), channel_id=1, source_target_pairs={{0,8},{4,20},{8,0},{12,28},{16,24},{20,4},{24,16},{28,12},{1,9},{5... | collective-permute-start | bytes 1474568 | tf_op jit(solution)/shard_map/ppermute | solution.py:316
  30.2 17.5 %collective-permute-start.7 = (f32[520,256]{1,0:T(8,128)S(1)}, f32[520,256]{1,0:T(8,128)S(1)}, u32[]{:S(2)}, u32[]{:S(2)}) collective-permute-start(f32[520,256]{1,0:T(8,128)S(1)} %shard_map.72), channel_id=1, source_target_pairs={{0,8},{4,20},{8,0},{12,28},{16,24},{20,4},{24,16},{28,12},{1,9},{5... | collective-permute-start | bytes 1597448 | tf_op jit(solution)/shard_map/ppermute | solution.py:316
  36.4 13.7 %collective-permute-start.6 = (f32[480,256]{1,0:T(8,128)S(1)}, f32[480,256]{1,0:T(8,128)S(1)}, u32[]{:S(2)}, u32[]{:S(2)}) collective-permute-start(f32[480,256]{1,0:T(8,128)S(1)} %shard_map.74.a), channel_id=1, source_target_pairs={{0,16},{4,12},{8,24},{12,4},{16,0},{20,28},{24,8},{28,20},{1,17},{... | collective-permute-start | bytes 1474568 | tf_op jit(solution)/shard_map/ppermute | solution.py:316
  47.8 15.4 %collective-permute-start.9 = (f32[520,256]{1,0:T(8,128)S(1)}, f32[520,256]{1,0:T(8,128)S(1)}, u32[]{:S(2)}, u32[]{:S(2)}) collective-permute-start(f32[520,256]{1,0:T(8,128)S(1)} %shard_map.75.a), channel_id=1, source_target_pairs={{0,16},{4,12},{8,24},{12,4},{16,0},{20,28},{24,8},{28,20},{1,17},{... | collective-permute-start | bytes 1597448 | tf_op jit(solution)/shard_map/ppermute | solution.py:316
  50.2 15.4 %collective-permute-start.8 = (f32[480,256]{1,0:T(8,128)S(1)}, f32[480,256]{1,0:T(8,128)S(1)}, u32[]{:S(2)}, u32[]{:S(2)}) collective-permute-start(f32[480,256]{1,0:T(8,128)S(1)} %shard_map.76.full), channel_id=1, source_target_pairs={{0,8},{4,20},{8,0},{12,28},{16,24},{20,4},{24,16},{28,12},{1,9},{5... | collective-permute-start | bytes 1474568 | tf_op jit(solution)/shard_map/ppermute | solution.py:316
  63.3 9.6 %collective-permute-start.14 = (f32[520,256]{1,0:T(8,128)S(1)}, f32[520,256]{1,0:T(8,128)S(1)}, u32[]{:S(2)}, u32[]{:S(2)}) collective-permute-start(f32[520,256]{1,0:T(8,128)S(1)} %shard_map.77.full), channel_id=1, source_target_pairs={{0,8},{4,20},{8,0},{12,28},{16,24},{20,4},{24,16},{28,12},{1,9},{5... | collective-permute-start | bytes 1597448 | tf_op jit(solution)/shard_map/ppermute | solution.py:316
  66.6 1.5 %collective-permute-start.10 = (f32[160,256]{1,0:T(8,128)S(1)}, f32[160,256]{1,0:T(8,128)S(1)}, u32[]{:S(2)}, u32[]{:S(2)}) collective-permute-start(f32[160,256]{1,0:T(8,128)S(1)} %get-tuple-element.151), channel_id=1, source_target_pairs={{0,4},{4,0},{1,5},{5,1},{2,6},{6,2},{3,7},{7,3},{8,12},{12,8},{9,1... | collective-permute-start | bytes 491528 | tf_op jit(solution)/shard_map/ppermute | solution.py:22
  66.7 1.6 %collective-permute-start.11 = (f32[160,256]{1,0:T(8,128)S(1)}, f32[160,256]{1,0:T(8,128)S(1)}, u32[]{:S(2)}, u32[]{:S(2)}) collective-permute-start(f32[160,256]{1,0:T(8,128)S(1)} %get-tuple-element.152), channel_id=1, source_target_pairs={{0,4},{4,0},{1,5},{5,1},{2,6},{6,2},{3,7},{7,3},{8,12},{12,8},{9,1... | collective-permute-start | bytes 491528 | tf_op jit(solution)/shard_map/ppermute | solution.py:22
  67.2 1.4 %collective-permute-start.12 = (f32[160,256]{1,0:T(8,128)S(1)}, f32[160,256]{1,0:T(8,128)S(1)}, u32[]{:S(2)}, u32[]{:S(2)}) collective-permute-start(f32[160,256]{1,0:T(8,128)S(1)} %get-tuple-element.153), channel_id=1, source_target_pairs={{0,4},{4,0},{1,5},{5,1},{2,6},{6,2},{3,7},{7,3},{8,12},{12,8},{9,1... | collective-permute-start | bytes 491528 | tf_op jit(solution)/shard_map/ppermute | solution.py:22
  68.6 8.2 %collective-permute-start.13 = (f32[480,128]{1,0:T(8,128)S(1)}, f32[480,128]{1,0:T(8,128)S(1)}, u32[]{:S(2)}, u32[]{:S(2)}) collective-permute-start(f32[480,128]{1,0:T(8,128)S(1)} %get-tuple-element.159), channel_id=1, source_target_pairs={{0,1},{1,0},{2,3},{3,2},{4,5},{5,4},{6,7},{7,6},{8,9},{9,8},{10,11... | collective-permute-start | bytes 737288 | tf_op jit(solution)/shard_map/ppermute | solution.py:253
  73.9 2.9 %collective-permute-start.16 = (f32[176,256]{1,0:T(8,128)S(1)}, f32[176,256]{1,0:T(8,128)S(1)}, u32[]{:S(2)}, u32[]{:S(2)}) collective-permute-start(f32[176,256]{1,0:T(8,128)S(1)} %get-tuple-element.166), channel_id=1, source_target_pairs={{0,4},{4,0},{1,5},{5,1},{2,6},{6,2},{3,7},{7,3},{8,12},{12,8},{9,1... | collective-permute-start | bytes 540680 | tf_op jit(solution)/shard_map/ppermute | solution.py:22
  74.0 2.9 %collective-permute-start.17 = (f32[176,256]{1,0:T(8,128)S(1)}, f32[176,256]{1,0:T(8,128)S(1)}, u32[]{:S(2)}, u32[]{:S(2)}) collective-permute-start(f32[176,256]{1,0:T(8,128)S(1)} %get-tuple-element.170), channel_id=1, source_target_pairs={{0,4},{4,0},{1,5},{5,1},{2,6},{6,2},{3,7},{7,3},{8,12},{12,8},{9,1... | collective-permute-start | bytes 540680 | tf_op jit(solution)/shard_map/ppermute | solution.py:22
  74.5 2.4 %collective-permute-start.18 = (f32[168,256]{1,0:T(8,128)S(1)}, f32[168,256]{1,0:T(8,128)S(1)}, u32[]{:S(2)}, u32[]{:S(2)}) collective-permute-start(f32[168,256]{1,0:T(8,128)S(1)} %get-tuple-element.171), channel_id=1, source_target_pairs={{0,4},{4,0},{1,5},{5,1},{2,6},{6,2},{3,7},{7,3},{8,12},{12,8},{9,1... | collective-permute-start | bytes 516104 | tf_op jit(solution)/shard_map/ppermute | solution.py:22
  76.9 8.5 %collective-permute-start.19 = (f32[520,128]{1,0:T(8,128)S(1)}, f32[520,128]{1,0:T(8,128)S(1)}, u32[]{:S(2)}, u32[]{:S(2)}) collective-permute-start(f32[520,128]{1,0:T(8,128)S(1)} %get-tuple-element.177), channel_id=1, source_target_pairs={{0,1},{1,0},{2,3},{3,2},{4,5},{5,4},{6,7},{7,6},{8,9},{9,8},{10,11... | collective-permute-start | bytes 798728 | tf_op jit(solution)/shard_map/ppermute | solution.py:253
  78.5 18.0 %collective-permute-start.15 = (f32[480,128]{1,0:T(8,128)S(1)}, f32[480,128]{1,0:T(8,128)S(1)}, u32[]{:S(2)}, u32[]{:S(2)}) collective-permute-start(f32[480,128]{1,0:T(8,128)S(1)} %shard_map.81.a), channel_id=1, source_target_pairs={{0,3},{3,0},{1,2},{2,1},{4,7},{7,4},{5,6},{6,5},{8,11},{11,8},{9,1... | collective-permute-start | bytes 737288 | tf_op jit(solution)/shard_map/ppermute | solution.py:253
  85.4 15.7 %collective-permute-start.21 = (f32[520,128]{1,0:T(8,128)S(1)}, f32[520,128]{1,0:T(8,128)S(1)}, u32[]{:S(2)}, u32[]{:S(2)}) collective-permute-start(f32[520,128]{1,0:T(8,128)S(1)} %shard_map.83.a), channel_id=1, source_target_pairs={{0,3},{3,0},{1,2},{2,1},{4,7},{7,4},{5,6},{6,5},{8,11},{11,8},{9,1... | collective-permute-start | bytes 798728 | tf_op jit(solution)/shard_map/ppermute | solution.py:253
  96.6 8.0 %collective-permute-start.20 = (f32[480,128]{1,0:T(8,128)S(1)}, f32[480,128]{1,0:T(8,128)S(1)}, u32[]{:S(2)}, u32[]{:S(2)}) collective-permute-start(f32[480,128]{1,0:T(8,128)S(1)} %shard_map.84), channel_id=1, source_target_pairs={{0,1},{1,0},{2,3},{3,2},{4,5},{5,4},{6,7},{7,6},{8,9},{9,8},{10,11... | collective-permute-start | bytes 737288 | tf_op jit(solution)/shard_map/ppermute | solution.py:253
  101.2 8.8 %collective-permute-start.22 = (f32[520,128]{1,0:T(8,128)S(1)}, f32[520,128]{1,0:T(8,128)S(1)}, u32[]{:S(2)}, u32[]{:S(2)}) collective-permute-start(f32[520,128]{1,0:T(8,128)S(1)} %shard_map.85), channel_id=1, source_target_pairs={{0,1},{1,0},{2,3},{3,2},{4,5},{5,4},{6,7},{7,6},{8,9},{9,8},{10,11... | collective-permute-start | bytes 798728 | tf_op jit(solution)/shard_map/ppermute | solution.py:253
  (4 other events, 4.5 us)

commit v9 on v6

--- a/solution.py
+++ b/solution.py
@@ -11,6 +11,8 @@
 HIGHEST = lax.Precision.HIGHEST
 HIGH = lax.Precision.HIGH
 ROUNDS = (0.48,)
+STEPS = ("P0 P1 F0 F1", "G0 O0 G1 O1", "M0 T0 M1 M2", "T1 T2")
+LINE_PIECES = (1,2,)
 BF16, F32 = jnp.bfloat16, jnp.float32
 NT = (((1,), (1,)), ((), ()))
 NN = (((1,), (0,)), ((), ()))
@@ -49,7 +51,7 @@
     return mul(a[0], b[0], dims) + (mul(a[0], b[1], dims) + mul(a[1], b[0], dims))
 
 
-def call(body, outs, args, flops=0, scratch=(), aliases=None):
+def call(body, outs, args, scratch=()):
     vmem = pl.BlockSpec(memory_space=pltpu.VMEM)
     return pl.pallas_call(
         body,
@@ -57,8 +59,7 @@
         in_specs=[vmem] * len(args),
         out_specs=[vmem] * len(outs),
         scratch_shapes=list(scratch),
-        input_output_aliases=aliases or {},
-        cost_estimate=pl.CostEstimate(flops=flops // 2**20, bytes_accessed=0, transcendentals=0),
+        cost_estimate=pl.CostEstimate(flops=0, bytes_accessed=0, transcendentals=0),
         compiler_params=pltpu.CompilerParams(vmem_limit_bytes=40 * 2**20),
     )(*args)
 
@@ -125,7 +126,6 @@
         own_body,
         [shaped((rows, wide), BF16)] * 2,
         (own, *cent),
-        flops=8 * rows * wide * width,
         scratch=row_scratch(rows, width),
     )
 
@@ -151,7 +151,6 @@
         near_body,
         [shaped((3 * rows, wide), BF16)] * 2,
         (x, y, *cent, *own),
-        flops=16 * rows * wide * width,
         scratch=row_scratch(2 * rows, width),
     )
 
@@ -187,17 +186,16 @@
 def keep_shares(edges, w0, w1, running, targets, near):
     rows = running.shape[1]
     outs = [shaped((b - a, 2 * rows)) for a, b in edges]
-    flops = 12 * rows * near[0].shape[1] * w0.shape[0]
     return call(
-        functools.partial(keep_body, edges, rows), outs, (w0, w1, running, targets, *near), flops
+        functools.partial(keep_body, edges, rows), outs, (w0, w1, running, targets, *near)
     )
 
 
-def far_body(edges, low_rows, high_rows, c_high, c_low, c_sq, near_high, near_low, w0, w1, *rest):
+def far_body(edges, block, c_high, c_low, c_sq, near_high, near_low, w0, w1, *rest):
     outs, (high, low, row_sq) = rest[:-3], rest[-3:]
     far_high, far_low, sent = outs[0], outs[1], outs[2:]
     rows = low.shape[0]
-    fill((low_rows, high_rows), high, low, row_sq)
+    fill((block,), high, low, row_sq)
     for far, near in ((far_high, near_high), (far_low, near_low)):
         far[pl.ds(0, rows)] = near[pl.ds(0, rows)]
         far[pl.ds(2 * rows, rows)] = near[pl.ds(2 * rows, rows)]
@@ -210,15 +208,14 @@
         sent[i][...] = share((w0, w1), pl.ds(a, b - a), (far_high, far_low), goes(rows)[i % 2])
 
 
-def far_kernels(edges, low, high, cent, near, w0, w1):
-    rows, width = 2 * low.shape[0], low.shape[1]
+def far_kernels(edges, block, cent, near, w0, w1):
+    rows, width = block.shape
     wide = cent[0].shape[0]
     outs = [shaped(near[0].shape, BF16)] * 2 + [shaped((b - a, 2 * rows)) for a, b in edges]
     out = call(
         functools.partial(far_body, edges),
         outs,
-        (low, high, *cent, *near, w0, w1),
-        flops=8 * rows * wide * width,
+        (block, *cent, *near, w0, w1),
         scratch=row_scratch(rows, width),
     )
     return out[:2], out[2:]
@@ -232,15 +229,14 @@
 def send_shares(edges, w0, w1, far):
     rows = far[0].shape[0] // 3
     outs = [shaped((b - a, 2 * rows)) for a, b in edges]
-    flops = sum(12 * rows * far[0].shape[1] * (b - a) for a, b in edges)
-    return call(functools.partial(send_body, edges, rows), outs, (w0, w1, *far), flops)
+    return call(functools.partial(send_body, edges, rows), outs, (w0, w1, *far))
 
 
 PARTS = 3
 
 
-def part_rows(size):
-    step = -(-size // PARTS // 8) * 8
+def blocks(size, count):
+    step = -(-size // count // 8) * 8
     return [(at, min(size, at + step)) for at in range(0, size, step)]
 
 
@@ -261,7 +257,7 @@
                 here[to] = value
                 continue
             start, end = at - full.shape[0], at
-            for ref, (low, high) in zip(gone, part_rows(here.shape[0])):
+            for ref, (low, high) in zip(gone, blocks(here.shape[0], PARTS)):
                 low_at, high_at = max(low, start), min(high, end)
                 if low_at < high_at:
                     ref[pl.ds(low_at - low, high_at - low_at)] = value[low_at - start : high_at - start]
@@ -269,9 +265,8 @@
 
 def grad_parts(factor, full, other, near, far):
     cols, half = full[0].shape[0] + full[1].shape[0], near[0].shape[1] // 2
-    flops = 12 * cols * full[0].shape[1] * 2 * half
-    outs = [shaped((cols, half))] + [shaped((b - a, half)) for a, b in part_rows(cols)]
-    out = call(functools.partial(grad_body, factor), outs, (*full, *other, *near, *far), flops)
+    outs = [shaped((cols, half))] + [shaped((b - a, half)) for a, b in blocks(cols, PARTS)]
+    out = call(functools.partial(grad_body, factor), outs, (*full, *other, *near, *far))
     return out[1:], out[0]
 
 
@@ -306,25 +301,33 @@
 
 
 def split_body(here, *refs):
-    gone, sends, mine = refs[:-2], refs[-2], refs[-1]
+    parts = blocks(here.shape[0], PARTS)
+    gone, outs = refs[: len(parts)], refs[len(parts) :]
+    count = len(outs) // 2
+    pieces = blocks(here.shape[0], count)
     place = lax.axis_index("col")
     ends = (place == 0) | (place == 3)
-    quarter = mine.shape[1]
+    quarter = here.shape[1] // 2
     left, right = pl.ds(0, quarter), pl.ds(quarter, quarter)
 
     def put(kept, sent):
-        for ref, (a, b) in zip(gone, part_rows(here.shape[0])):
-            to = pl.ds(a, b - a)
-            mine[to] = here[to, kept] + ref[:, kept]
-            sends[to] = here[to, sent] + ref[:, sent]
+        for ref, (a, b) in zip(gone, parts):
+            for i, (low, high) in enumerate(pieces):
+                at, end = max(a, low), min(b, high)
+                if at < end:
+                    of, part, to = (pl.ds(at - n, end - at) for n in (0, a, low))
+                    outs[i][to] = here[of, sent] + ref[part, sent]
+                    outs[count + i][to] = here[of, kept] + ref[part, kept]
 
     pl.when(ends)(lambda: put(left, right))
     pl.when(~ends)(lambda: put(right, left))
 
 
-def split(here, gone):
-    outs = [shaped((here.shape[0], here.shape[1] // 2))] * 2
-    return call(split_body, outs, (here, *gone))
+def split(count, here, gone):
+    rows, half = here.shape
+    outs = [shaped((b - a, half // 2)) for a, b in blocks(rows, count)] * 2
+    out = call(split_body, outs, (here, *gone))
+    return out[: len(out) // 2], out[len(out) // 2 :]
 
 
 def cut(out):
@@ -338,32 +341,39 @@
     return edges
 
 
+def hop(value, second):
+    pairs = []
+    for chip in range(4):
+        for core in range(2):
+            flip = 1 if core == second else 2
+            pairs.append((chip * 2 + core, (chip ^ flip) * 2 + core))
+    return lax.ppermute(value, ("chip", "core"), pairs)
+
+
 def square(batch, running_t, targets_t, centers, weights_t, factor):
     rows, out = batch.shape[0], weights_t.shape[0]
-    mid = rows // 2
     edges = cut(out)
     rounds = len(edges) // 2
     line = Line()
-    block_x = swap(batch, "chip", 1)
-    block_y = swap(batch, "chip", 2)
+    block_x = hop(batch, 0)
+    block_y = hop(batch, 1)
     cent_theirs = swap(centers, "core")
     w0, w1 = weights_t, swap(weights_t, "core")
     cent = line(split_cent, centers, cent_theirs)
     own = line(own_kernels, batch, cent)
-    low = swap(block_x[:mid], "chip", 2)
-    high = swap(block_y[mid:], "chip", 1)
+    block = hop(block_x, 1)
     near = line(near_kernels, block_x, block_y, cent, own)
-    far, sent = line(lambda *a: far_kernels(edges[:4], *a), low, high, cent, near, w0, w1)
-
-    axes = ((1, 2), (2, 1))
+    far, sent = line(lambda *a: far_kernels(edges[:2], *a), block, cent, near, w0, w1)
+
     place = lax.axis_index("col")
     ends = (place == 0) | (place == 3)
 
     def both(pair, step):
-        return [swap(pair[i], "chip", axes[i][step]) for i in (0, 1)]
-
-    coming, crossing, beside, across, back = ([None] * rounds for _ in range(5))
-    partial, full, other, gone, here, mine, total = ([None] * rounds for _ in range(7))
+        return [hop(pair[i], (i + step) % 2) for i in (0, 1)]
+
+    coming, crossing = [None] * rounds, [None] * rounds
+    partial, full, other, gone, here = ([None] * rounds for _ in range(5))
+    beside, mine, across, total, back = [], [], [], [], []
 
     def do_partial(r):
         partial[r] = line(add, kept[2 * r : 2 * r + 2], coming[r])
@@ -378,32 +388,25 @@
         gone[r] = [swap(part, "core") for part in gone[r]]
 
     def do_owned(r):
-        sends, mine[r] = line(split, here[r], gone[r])
-        beside[r] = pass_line(sends, BESIDE)
-
-    def do_mine(r):
-        (mine[r],) = line(add, [mine[r]], [beside[r]])
-        across[r] = pass_line(mine[r], ACROSS)
-
-    def do_total(r):
-        (total[r],) = line(add, [mine[r]], [across[r]])
-        back[r] = pass_line(total[r], BESIDE)
-
-    coming[0] = both(sent[0:2], 0)
-    coming[1] = both(line.hold(tuple(sent[2:4])), 0)
+        sends, keeps = line(lambda *a: split(LINE_PIECES[r], *a), here[r], gone[r])
+        mine.extend(keeps)
+        beside.extend(pass_line(value, BESIDE) for value in sends)
+
+    def do_mine(i):
+        (mine[i],) = line(add, [mine[i]], [beside[i]])
+        across.append(pass_line(mine[i], ACROSS))
+
+    def do_total(i):
+        (value,) = line(add, [mine[i]], [across[i]])
+        total.append(value)
+        back.append(pass_line(value, BESIDE))
+
+    sent = list(sent) + list(line(lambda *a: send_shares(edges[2:], *a), w0, w1, far))
+    coming = [both(sent[2 * r : 2 * r + 2], 0) for r in range(rounds)]
     kept = line(lambda *a: keep_shares(edges, *a), w0, w1, running_t, targets_t, near)
-    do_partial(0)
-    do_partial(1)
-    do_full(0)
-    do_full(1)
-    do_grad(0)
-    do_owned(0)
-    do_grad(1)
-    do_mine(0)
-    do_owned(1)
-    do_mine(1)
-    do_total(0)
-    do_total(1)
+    steps = dict(P=do_partial, F=do_full, G=do_grad, O=do_owned, M=do_mine, T=do_total)
+    for step in " ".join(STEPS).split():
+        steps[step[0]](int(step[1]))
 
     first = [jnp.where(ends, t, b) for t, b in zip(total, back)]
     second = [jnp.where(ends, b, t) for t, b in zip(total, back)]

time: 106 us -> 104 us (0.981)
  waiting for transfers between devices: 52.8 us -> 46.4 us
  starting transfers between devices: 40.1 us -> 42.4 us
  local copies, waits for them, and re-layouts: 0.1 us -> 2.19 us
    ppermute x24 -> x8, waiting for transfers between devices: 33.9 us -> 2.66 us  [swap(): return lax.ppermute(value, axis, [(i, i ^ flip) for i in range(size)])]
    ppermute x0 -> x15, starting transfers between devices: none -> 24.8 us  [hop(): return lax.ppermute(value, ('chip', 'core'), pairs)]
    ppermute x0 -> x15, waiting for transfers between devices: none -> 22.8 us  [hop(): return lax.ppermute(value, ('chip', 'core'), pairs)]
    ppermute x24 -> x8, starting transfers between devices: 20.6 us -> 1.99 us  [swap(): return lax.ppermute(value, axis, [(i, i ^ flip) for i in range(size)])]
    ppermute x6 -> x9, starting transfers between devices: 19.5 us -> 15.7 us  [pass_line(): return lax.ppermute(value, 'col', pairs)]
    unnamed x10, local copies, waits for them, and re-layouts: 0.03 us -> 2.15 us
    ppermute x6 -> x9, waiting for transfers between devices: 18.9 us -> 20.9 us  [pass_line(): return lax.ppermute(value, 'col', pairs)]
    pallas_call x17 -> x20, Pallas kernels: 9.82 us -> 10 us  [call(): pl.pallas_call(body, out_shape=outs, in_specs=[vmem] * len(args), out_spe...]
  transfers between devices with their start and end apart: 30 -> 32, of which waited for: 18 -> 17; matrix products, arithmetic and copies ran while one was open for 1% -> 1% of each run, Pallas kernels for 7% -> 7%
where the time goes in v9:
time: 104 us
  waiting for transfers between devices  46.4 us (45%)
  starting transfers between devices  42.4 us (41%)
  Pallas kernels  10 us (10%)
  local copies, waits for them, and re-layouts  2.19 us (2%)
  other arithmetic  1.97 us (2%)
    ppermute x15, starting transfers between devices, hop(): return lax.ppermute(value, ('chip', 'core'), pairs)  24.8 us
    ppermute x15, waiting for transfers between devices, hop(): return lax.ppermute(value, ('chip', 'core'), pairs)  22.8 us
    ppermute x9, waiting for transfers between devices, pass_line(): return lax.ppermute(value, 'col', pairs)  20.9 us
    ppermute x9, starting transfers between devices, pass_line(): return lax.ppermute(value, 'col', pairs)  15.7 us
    pallas_call x20, Pallas kernels, call(): pl.pallas_call(body, out_shape=outs, in_specs=[vmem] * len(args), out_spe...  10 us
    ppermute x8, waiting for transfers between devices, swap(): return lax.ppermute(value, axis, [(i, i ^ flip) for i in range(size)])  2.66 us
    unnamed x10, local copies, waits for them, and re-layouts  2.15 us
  transfers between devices with their start and end apart: 32, of which 17 were waited for; matrix products, arithmetic and copies ran while one was open for 1% of the time, Pallas kernels for 7%

profile of v9, /device:TPU:0, one launch (start us, length us, event | category | flops | bytes accessed | tf_op | source)
XLA Modules:
  0.0 103.8 jit_solution(1741536204256082657)
XLA Ops:
  1.1 2.6 %collective-permute-start.1 = (f32[128,1024]{1,0:T(8,128)}, f32[128,1024]{1,0:T(8,128)S(1)}, u32[]{:S(2)}, u32[]{:S(2)}) collective-permute-start(f32[128,1024]{1,0:T(8,128)} %own), channel_id=1, source_target_pairs={{0,8},{4,20},{8,0},{12,28},{16,24},{20,4},{24,16},{28,12},{1,9},{5... | collective-permute-start | bytes 1572872 | tf_op jit(solution)/shard_map/ppermute | solution.py:350
  5.2 10.4 %collective-permute-done.1.x = f32[128,1024]{1,0:T(8,128)S(1)} collective-permute-done((f32[128,1024]{1,0:T(8,128)}, f32[128,1024]{1,0:T(8,128)S(1)}, u32[]{:S(2)}, u32[]{:S(2)}) %collective-permute-start.1) | collective-permute-done | bytes 524320 | tf_op jit(solution)/shard_map/ppermute | solution.py:350
  15.7 2.1 %collective-permute-start.4 = (f32[128,1024]{1,0:T(8,128)S(1)}, f32[128,1024]{1,0:T(8,128)S(1)}, u32[]{:S(2)}, u32[]{:S(2)}) collective-permute-start(f32[128,1024]{1,0:T(8,128)S(1)} %collective-permute-done.1.x), channel_id=1, source_target_pairs={{0,16},{4,12},{8,24},{12,4},{16,0},{20,28},{24,8},{28,20},{1,17},{... | collective-permute-start | bytes 1572872 | tf_op jit(solution)/shard_map/ppermute | solution.py:350
  23.3 1.6 %collective-permute-done.4.block = f32[128,1024]{1,0:T(8,128)S(1)} collective-permute-done((f32[128,1024]{1,0:T(8,128)S(1)}, f32[128,1024]{1,0:T(8,128)S(1)}, u32[]{:S(2)}, u32[]{:S(2)}) %collective-permute-start.4) | collective-permute-done | bytes 524320 | tf_op jit(solution)/shard_map/ppermute | solution.py:350
  24.9 2.2 %shard_map.71 = (bf16[384,512]{1,0:T(8,128)(2,1)S(1)}, bf16[384,512]{1,0:T(8,128)(2,1)S(1)}, f32[240,256]{1,0:T(8,128)S(1)}, f32[240,256]{1,0:T(8,128)S(1)}) custom-call(f32[128,1024]{1,0:T(8,128)S(1)} %collective-permute-done.4.block, bf16[512,1024]{1,0:T(8,128)(2,1)S(1)} %get-tuple-element.141.c_high, bf16[512,1024]{1,0:T(8,128)(2,1)S(1)} %get-tuple-element.142.c_low, ...), custom_call_target="tpu_custom_call" | custom-call | tf_op jit(solution)/shard_map/pallas_call | solution.py:56
  27.2 2.4 %collective-permute-start.5 = (f32[240,256]{1,0:T(8,128)S(1)}, f32[240,256]{1,0:T(8,128)S(1)}, u32[]{:S(2)}, u32[]{:S(2)}) collective-permute-start(f32[240,256]{1,0:T(8,128)S(1)} %get-tuple-element.163), channel_id=1, source_target_pairs={{0,8},{4,20},{8,0},{12,28},{16,24},{20,4},{24,16},{28,12},{1,9},{5... | collective-permute-start | bytes 737288 | tf_op jit(solution)/shard_map/ppermute | solution.py:350
  29.6 2.0 %collective-permute-start.6 = (f32[240,256]{1,0:T(8,128)S(1)}, f32[240,256]{1,0:T(8,128)S(1)}, u32[]{:S(2)}, u32[]{:S(2)}) collective-permute-start(f32[240,256]{1,0:T(8,128)S(1)} %get-tuple-element.164), channel_id=1, source_target_pairs={{0,16},{4,12},{8,24},{12,4},{16,0},{20,28},{24,8},{28,20},{1,17},{... | collective-permute-start | bytes 737288 | tf_op jit(solution)/shard_map/ppermute | solution.py:350
  33.9 2.6 %collective-permute-done.5.refs_2_ = f32[240,256]{1,0:T(8,128)S(1)} collective-permute-done((f32[240,256]{1,0:T(8,128)S(1)}, f32[240,256]{1,0:T(8,128)S(1)}, u32[]{:S(2)}, u32[]{:S(2)}) %collective-permute-start.5) | collective-permute-done | bytes 245792 | tf_op jit(solution)/shard_map/ppermute | solution.py:350
  38.6 2.1 %collective-permute-start.8 = (f32[240,256]{1,0:T(8,128)S(1)}, f32[240,256]{1,0:T(8,128)S(1)}, u32[]{:S(2)}, u32[]{:S(2)}) collective-permute-start(f32[240,256]{1,0:T(8,128)S(1)} %get-tuple-element.180.refs_1_), channel_id=1, source_target_pairs={{0,8},{4,20},{8,0},{12,28},{16,24},{20,4},{24,16},{28,12},{1,9},{5... | collective-permute-start | bytes 737288 | tf_op jit(solution)/shard_map/ppermute | solution.py:350
  40.7 2.1 %collective-permute-done.10.refs_3_ = f32[256,256]{1,0:T(8,128)S(1)} collective-permute-done((f32[256,256]{1,0:T(8,128)S(1)}, f32[256,256]{1,0:T(8,128)S(1)}, u32[]{:S(2)}, u32[]{:S(2)}) %collective-permute-start.10) | collective-permute-done | bytes 262176 | tf_op jit(solution)/shard_map/ppermute | solution.py:350
  43.9 2.5 %collective-permute-start.14 = (f32[256,256]{1,0:T(8,128)S(1)}, f32[256,256]{1,0:T(8,128)S(1)}, u32[]{:S(2)}, u32[]{:S(2)}) collective-permute-start(f32[256,256]{1,0:T(8,128)S(1)} %get-tuple-element.187.refs_1_), channel_id=1, source_target_pairs={{0,8},{4,20},{8,0},{12,28},{16,24},{20,4},{24,16},{28,12},{1,9},{5... | collective-permute-start | bytes 786440 | tf_op jit(solution)/shard_map/ppermute | solution.py:350
  47.8 1.8 %collective-permute-start.11 = (f32[240,256]{1,0:T(8,128)S(1)}, f32[240,256]{1,0:T(8,128)S(1)}, u32[]{:S(2)}, u32[]{:S(2)}) collective-permute-start(f32[240,256]{1,0:T(8,128)S(1)} %get-tuple-element.191.full_a), channel_id=1, source_target_pairs={{0,8},{4,20},{8,0},{12,28},{16,24},{20,4},{24,16},{28,12},{1,9},{5... | collective-permute-start | bytes 737288 | tf_op jit(solution)/shard_map/ppermute | solution.py:350
  49.7 1.9 %collective-permute-start.12 = (f32[240,256]{1,0:T(8,128)S(1)}, f32[240,256]{1,0:T(8,128)S(1)}, u32[]{:S(2)}, u32[]{:S(2)}) collective-permute-start(f32[240,256]{1,0:T(8,128)S(1)} %get-tuple-element.192.full_b), channel_id=1, source_target_pairs={{0,16},{4,12},{8,24},{12,4},{16,0},{20,28},{24,8},{28,20},{1,17},{... | collective-permute-start | bytes 737288 | tf_op jit(solution)/shard_map/ppermute | solution.py:350
  51.6 2.1 %collective-permute-done.14.refs_3_ = f32[256,256]{1,0:T(8,128)S(1)} collective-permute-done((f32[256,256]{1,0:T(8,128)S(1)}, f32[256,256]{1,0:T(8,128)S(1)}, u32[]{:S(2)}, u32[]{:S(2)}) %collective-permute-start.14) | collective-permute-done | bytes 262176 | tf_op jit(solution)/shard_map/ppermute | solution.py:350
  53.7 2.1 %collective-permute-start.19 = (f32[264,256]{1,0:T(8,128)S(1)}, f32[264,256]{1,0:T(8,128)S(1)}, u32[]{:S(2)}, u32[]{:S(2)}) collective-permute-start(f32[264,256]{1,0:T(8,128)S(1)} %get-tuple-element.210.full_a), channel_id=1, source_target_pairs={{0,8},{4,20},{8,0},{12,28},{16,24},{20,4},{24,16},{28,12},{1,9},{5... | collective-permute-start | bytes 811016 | tf_op jit(solution)/shard_map/ppermute | solution.py:350
  61.9 1.6 %collective-permute-start.18 = (f32[480,128]{1,0:T(8,128)S(1)}, f32[480,128]{1,0:T(8,128)S(1)}, u32[]{:S(2)}, u32[]{:S(2)}) collective-permute-start(f32[480,128]{1,0:T(8,128)S(1)} %get-tuple-element.208), channel_id=1, source_target_pairs={{0,1},{1,0},{2,3},{3,2},{4,5},{5,4},{6,7},{7,6},{8,9},{9,8},{10,11... | collective-permute-start | bytes 737288 | tf_op jit(solution)/shard_map/ppermute | solution.py:274
  66.6 3.4 %collective-permute-done.18.refs_1_ = f32[480,128]{1,0:T(8,128)S(1)} collective-permute-done((f32[480,128]{1,0:T(8,128)S(1)}, f32[480,128]{1,0:T(8,128)S(1)}, u32[]{:S(2)}, u32[]{:S(2)}) %collective-permute-start.18) | collective-permute-done | bytes 245792 | tf_op jit(solution)/shard_map/ppermute | solution.py:274
  70.1 3.7 %collective-permute-start.24 = (f32[480,128]{1,0:T(8,128)S(1)}, f32[480,128]{1,0:T(8,128)S(1)}, u32[]{:S(2)}, u32[]{:S(2)}) collective-permute-start(f32[480,128]{1,0:T(8,128)S(1)} %shard_map.82.refs_0_), channel_id=1, source_target_pairs={{0,3},{3,0},{1,2},{2,1},{4,7},{7,4},{5,6},{6,5},{8,11},{11,8},{9,1... | collective-permute-start | bytes 737288 | tf_op jit(solution)/shard_map/ppermute | solution.py:274
  73.8 2.0 %collective-permute-start.28 = (f32[256,128]{1,0:T(8,128)S(1)}, f32[256,128]{1,0:T(8,128)S(1)}, u32[]{:S(2)}, u32[]{:S(2)}) collective-permute-start(f32[256,128]{1,0:T(8,128)S(1)} %get-tuple-element.235), channel_id=1, source_target_pairs={{0,1},{1,0},{2,3},{3,2},{4,5},{5,4},{6,7},{7,6},{8,9},{9,8},{10,11... | collective-permute-start | bytes 393224 | tf_op jit(solution)/shard_map/ppermute | solution.py:274
  75.8 5.1 %collective-permute-done.24.refs_1_ = f32[480,128]{1,0:T(8,128)S(1)} collective-permute-done((f32[480,128]{1,0:T(8,128)S(1)}, f32[480,128]{1,0:T(8,128)S(1)}, u32[]{:S(2)}, u32[]{:S(2)}) %collective-permute-start.24) | collective-permute-done | bytes 245792 | tf_op jit(solution)/shard_map/ppermute | solution.py:274
  80.9 3.5 %collective-permute-start.25 = (f32[480,128]{1,0:T(8,128)S(1)}, f32[480,128]{1,0:T(8,128)S(1)}, u32[]{:S(2)}, u32[]{:S(2)}) collective-permute-start(f32[480,128]{1,0:T(8,128)S(1)} %shard_map.83), channel_id=1, source_target_pairs={{0,1},{1,0},{2,3},{3,2},{4,5},{5,4},{6,7},{7,6},{8,9},{9,8},{10,11... | collective-permute-start | bytes 737288 | tf_op jit(solution)/shard_map/ppermute | solution.py:274
  84.4 2.5 %collective-permute-start.27 = (f32[264,128]{1,0:T(8,128)S(1)}, f32[264,128]{1,0:T(8,128)S(1)}, u32[]{:S(2)}, u32[]{:S(2)}) collective-permute-start(f32[264,128]{1,0:T(8,128)S(1)} %shard_map.84.refs_0_), channel_id=1, source_target_pairs={{0,3},{3,0},{1,2},{2,1},{4,7},{7,4},{5,6},{6,5},{8,11},{11,8},{9,1... | collective-permute-start | bytes 405512 | tf_op jit(solution)/shard_map/ppermute | solution.py:274
  89.2 6.4 %collective-permute-done.27.refs_1_ = f32[264,128]{1,0:T(8,128)S(1)} collective-permute-done((f32[264,128]{1,0:T(8,128)S(1)}, f32[264,128]{1,0:T(8,128)S(1)}, u32[]{:S(2)}, u32[]{:S(2)}) %collective-permute-start.27) | collective-permute-done | bytes 135200 | tf_op jit(solution)/shard_map/ppermute | solution.py:274
  98.1 4.6 %collective-permute-done.31 = f32[256,128]{1,0:T(8,128)S(1)} collective-permute-done((f32[256,128]{1,0:T(8,128)S(1)}, f32[256,128]{1,0:T(8,128)S(1)}, u32[]{:S(2)}, u32[]{:S(2)}) %collective-permute-start.31) | collective-permute-done | bytes 131104 | tf_op jit(solution)/shard_map/ppermute | solution.py:274
  (79 shorter events, 29.5 us)
Async XLA Ops:
  0.6 17.2 %collective-permute-start.3 = (f32[256,1024]{1,0:T(8,128)}, f32[256,1024]{1,0:T(8,128)S(1)}, u32[]{:S(2)}, u32[]{:S(2)}) collective-permute-start(f32[256,1024]{1,0:T(8,128)} %mine_ref.1), channel_id=1, source_target_pairs={{0,4},{4,0},{1,5},{5,1},{2,6},{6,2},{3,7},{7,3},{8,12},{12,8},{9,1... | collective-permute-start | bytes 3145736 | tf_op jit(solution)/shard_map/ppermute | solution.py:23
  1.1 14.5 %collective-permute-start.1 = (f32[128,1024]{1,0:T(8,128)}, f32[128,1024]{1,0:T(8,128)S(1)}, u32[]{:S(2)}, u32[]{:S(2)}) collective-permute-start(f32[128,1024]{1,0:T(8,128)} %own), channel_id=1, source_target_pairs={{0,8},{4,20},{8,0},{12,28},{16,24},{20,4},{24,16},{28,12},{1,9},{5... | collective-permute-start | bytes 1572872 | tf_op jit(solution)/shard_map/ppermute | solution.py:350
  3.7 19.6 %collective-permute-start = (f32[1000,256]{1,0:T(8,128)}, f32[1000,256]{1,0:T(8,128)S(1)}, u32[]{:S(2)}, u32[]{:S(2)}) collective-permute-start(f32[1000,256]{1,0:T(8,128)} %bitcast.7), channel_id=1, source_target_pairs={{0,4},{4,0},{1,5},{5,1},{2,6},{6,2},{3,7},{7,3},{8,12},{12,8},{9,1... | collective-permute-start | bytes 3072008 | tf_op jit(solution)/shard_map/ppermute | solution.py:23
  3.9 17.8 %collective-permute-start.2 = (f32[128,1024]{1,0:T(8,128)}, f32[128,1024]{1,0:T(8,128)S(1)}, u32[]{:S(2)}, u32[]{:S(2)}) collective-permute-start(f32[128,1024]{1,0:T(8,128)} %own), channel_id=1, source_target_pairs={{0,16},{4,12},{8,24},{12,4},{16,0},{20,28},{24,8},{28,20},{1,17},{... | collective-permute-start | bytes 1572872 | tf_op jit(solution)/shard_map/ppermute | solution.py:350
  15.7 9.3 %collective-permute-start.4 = (f32[128,1024]{1,0:T(8,128)S(1)}, f32[128,1024]{1,0:T(8,128)S(1)}, u32[]{:S(2)}, u32[]{:S(2)}) collective-permute-start(f32[128,1024]{1,0:T(8,128)S(1)} %collective-permute-done.1.x), channel_id=1, source_target_pairs={{0,16},{4,12},{8,24},{12,4},{16,0},{20,28},{24,8},{28,20},{1,17},{... | collective-permute-start | bytes 1572872 | tf_op jit(solution)/shard_map/ppermute | solution.py:350
  27.2 9.3 %collective-permute-start.5 = (f32[240,256]{1,0:T(8,128)S(1)}, f32[240,256]{1,0:T(8,128)S(1)}, u32[]{:S(2)}, u32[]{:S(2)}) collective-permute-start(f32[240,256]{1,0:T(8,128)S(1)} %get-tuple-element.163), channel_id=1, source_target_pairs={{0,8},{4,20},{8,0},{12,28},{16,24},{20,4},{24,16},{28,12},{1,9},{5... | collective-permute-start | bytes 737288 | tf_op jit(solution)/shard_map/ppermute | solution.py:350
  29.6 7.9 %collective-permute-start.6 = (f32[240,256]{1,0:T(8,128)S(1)}, f32[240,256]{1,0:T(8,128)S(1)}, u32[]{:S(2)}, u32[]{:S(2)}) collective-permute-start(f32[240,256]{1,0:T(8,128)S(1)} %get-tuple-element.164), channel_id=1, source_target_pairs={{0,16},{4,12},{8,24},{12,4},{16,0},{20,28},{24,8},{28,20},{1,17},{... | collective-permute-start | bytes 737288 | tf_op jit(solution)/shard_map/ppermute | solution.py:350
  32.3 10.6 %collective-permute-start.9 = (f32[264,256]{1,0:T(8,128)S(1)}, f32[264,256]{1,0:T(8,128)S(1)}, u32[]{:S(2)}, u32[]{:S(2)}) collective-permute-start(f32[264,256]{1,0:T(8,128)S(1)} %get-tuple-element.154), channel_id=1, source_target_pairs={{0,8},{4,20},{8,0},{12,28},{16,24},{20,4},{24,16},{28,12},{1,9},{5... | collective-permute-start | bytes 811016 | tf_op jit(solution)/shard_map/ppermute | solution.py:350
  32.4 10.5 %collective-permute-start.10 = (f32[256,256]{1,0:T(8,128)S(1)}, f32[256,256]{1,0:T(8,128)S(1)}, u32[]{:S(2)}, u32[]{:S(2)}) collective-permute-start(f32[256,256]{1,0:T(8,128)S(1)} %get-tuple-element.173), channel_id=1, source_target_pairs={{0,16},{4,12},{8,24},{12,4},{16,0},{20,28},{24,8},{28,20},{1,17},{... | collective-permute-start | bytes 786440 | tf_op jit(solution)/shard_map/ppermute | solution.py:350
  37.5 10.3 %collective-permute-start.7 = (f32[240,256]{1,0:T(8,128)S(1)}, f32[240,256]{1,0:T(8,128)S(1)}, u32[]{:S(2)}, u32[]{:S(2)}) collective-permute-start(f32[240,256]{1,0:T(8,128)S(1)} %get-tuple-element.179.refs_0_), channel_id=1, source_target_pairs={{0,16},{4,12},{8,24},{12,4},{16,0},{20,28},{24,8},{28,20},{1,17},{... | collective-permute-start | bytes 737288 | tf_op jit(solution)/shard_map/ppermute | solution.py:350
  38.6 9.2 %collective-permute-start.8 = (f32[240,256]{1,0:T(8,128)S(1)}, f32[240,256]{1,0:T(8,128)S(1)}, u32[]{:S(2)}, u32[]{:S(2)}) collective-permute-start(f32[240,256]{1,0:T(8,128)S(1)} %get-tuple-element.180.refs_1_), channel_id=1, source_target_pairs={{0,8},{4,20},{8,0},{12,28},{16,24},{20,4},{24,16},{28,12},{1,9},{5... | collective-permute-start | bytes 737288 | tf_op jit(solution)/shard_map/ppermute | solution.py:350
  42.9 10.7 %collective-permute-start.13 = (f32[264,256]{1,0:T(8,128)S(1)}, f32[264,256]{1,0:T(8,128)S(1)}, u32[]{:S(2)}, u32[]{:S(2)}) collective-permute-start(f32[264,256]{1,0:T(8,128)S(1)} %get-tuple-element.186.refs_0_), channel_id=1, source_target_pairs={{0,16},{4,12},{8,24},{12,4},{16,0},{20,28},{24,8},{28,20},{1,17},{... | collective-permute-start | bytes 811016 | tf_op jit(solution)/shard_map/ppermute | solution.py:350
  43.9 9.7 %collective-permute-start.14 = (f32[256,256]{1,0:T(8,128)S(1)}, f32[256,256]{1,0:T(8,128)S(1)}, u32[]{:S(2)}, u32[]{:S(2)}) collective-permute-start(f32[256,256]{1,0:T(8,128)S(1)} %get-tuple-element.187.refs_1_), channel_id=1, source_target_pairs={{0,8},{4,20},{8,0},{12,28},{16,24},{20,4},{24,16},{28,12},{1,9},{5... | collective-permute-start | bytes 786440 | tf_op jit(solution)/shard_map/ppermute | solution.py:350
  47.8 11.1 %collective-permute-start.11 = (f32[240,256]{1,0:T(8,128)S(1)}, f32[240,256]{1,0:T(8,128)S(1)}, u32[]{:S(2)}, u32[]{:S(2)}) collective-permute-start(f32[240,256]{1,0:T(8,128)S(1)} %get-tuple-element.191.full_a), channel_id=1, source_target_pairs={{0,8},{4,20},{8,0},{12,28},{16,24},{20,4},{24,16},{28,12},{1,9},{5... | collective-permute-start | bytes 737288 | tf_op jit(solution)/shard_map/ppermute | solution.py:350
  49.7 9.3 %collective-permute-start.12 = (f32[240,256]{1,0:T(8,128)S(1)}, f32[240,256]{1,0:T(8,128)S(1)}, u32[]{:S(2)}, u32[]{:S(2)}) collective-permute-start(f32[240,256]{1,0:T(8,128)S(1)} %get-tuple-element.192.full_b), channel_id=1, source_target_pairs={{0,16},{4,12},{8,24},{12,4},{16,0},{20,28},{24,8},{28,20},{1,17},{... | collective-permute-start | bytes 737288 | tf_op jit(solution)/shard_map/ppermute | solution.py:350
  53.7 9.8 %collective-permute-start.19 = (f32[264,256]{1,0:T(8,128)S(1)}, f32[264,256]{1,0:T(8,128)S(1)}, u32[]{:S(2)}, u32[]{:S(2)}) collective-permute-start(f32[264,256]{1,0:T(8,128)S(1)} %get-tuple-element.210.full_a), channel_id=1, source_target_pairs={{0,8},{4,20},{8,0},{12,28},{16,24},{20,4},{24,16},{28,12},{1,9},{5... | collective-permute-start | bytes 811016 | tf_op jit(solution)/shard_map/ppermute | solution.py:350
  55.8 7.7 %collective-permute-start.20 = (f32[256,256]{1,0:T(8,128)S(1)}, f32[256,256]{1,0:T(8,128)S(1)}, u32[]{:S(2)}, u32[]{:S(2)}) collective-permute-start(f32[256,256]{1,0:T(8,128)S(1)} %get-tuple-element.211.full_b), channel_id=1, source_target_pairs={{0,16},{4,12},{8,24},{12,4},{16,0},{20,28},{24,8},{28,20},{1,17},{... | collective-permute-start | bytes 786440 | tf_op jit(solution)/shard_map/ppermute | solution.py:350
  61.9 8.2 %collective-permute-start.18 = (f32[480,128]{1,0:T(8,128)S(1)}, f32[480,128]{1,0:T(8,128)S(1)}, u32[]{:S(2)}, u32[]{:S(2)}) collective-permute-start(f32[480,128]{1,0:T(8,128)S(1)} %get-tuple-element.208), channel_id=1, source_target_pairs={{0,1},{1,0},{2,3},{3,2},{4,5},{5,4},{6,7},{7,6},{8,9},{9,8},{10,11... | collective-permute-start | bytes 737288 | tf_op jit(solution)/shard_map/ppermute | solution.py:274
  70.1 10.8 %collective-permute-start.24 = (f32[480,128]{1,0:T(8,128)S(1)}, f32[480,128]{1,0:T(8,128)S(1)}, u32[]{:S(2)}, u32[]{:S(2)}) collective-permute-start(f32[480,128]{1,0:T(8,128)S(1)} %shard_map.82.refs_0_), channel_id=1, source_target_pairs={{0,3},{3,0},{1,2},{2,1},{4,7},{7,4},{5,6},{6,5},{8,11},{11,8},{9,1... | collective-permute-start | bytes 737288 | tf_op jit(solution)/shard_map/ppermute | solution.py:274
  73.7 10.6 %collective-permute-start.26 = (f32[264,128]{1,0:T(8,128)S(1)}, f32[264,128]{1,0:T(8,128)S(1)}, u32[]{:S(2)}, u32[]{:S(2)}) collective-permute-start(f32[264,128]{1,0:T(8,128)S(1)} %get-tuple-element.226), channel_id=1, source_target_pairs={{0,1},{1,0},{2,3},{3,2},{4,5},{5,4},{6,7},{7,6},{8,9},{9,8},{10,11... | collective-permute-start | bytes 405512 | tf_op jit(solution)/shard_map/ppermute | solution.py:274
  73.8 13.2 %collective-permute-start.28 = (f32[256,128]{1,0:T(8,128)S(1)}, f32[256,128]{1,0:T(8,128)S(1)}, u32[]{:S(2)}, u32[]{:S(2)}) collective-permute-start(f32[256,128]{1,0:T(8,128)S(1)} %get-tuple-element.235), channel_id=1, source_target_pairs={{0,1},{1,0},{2,3},{3,2},{4,5},{5,4},{6,7},{7,6},{8,9},{9,8},{10,11... | collective-permute-start | bytes 393224 | tf_op jit(solution)/shard_map/ppermute | solution.py:274
  80.9 17.2 %collective-permute-start.25 = (f32[480,128]{1,0:T(8,128)S(1)}, f32[480,128]{1,0:T(8,128)S(1)}, u32[]{:S(2)}, u32[]{:S(2)}) collective-permute-start(f32[480,128]{1,0:T(8,128)S(1)} %shard_map.83), channel_id=1, source_target_pairs={{0,1},{1,0},{2,3},{3,2},{4,5},{5,4},{6,7},{7,6},{8,9},{9,8},{10,11... | collective-permute-start | bytes 737288 | tf_op jit(solution)/shard_map/ppermute | solution.py:274
  84.4 11.3 %collective-permute-start.27 = (f32[264,128]{1,0:T(8,128)S(1)}, f32[264,128]{1,0:T(8,128)S(1)}, u32[]{:S(2)}, u32[]{:S(2)}) collective-permute-start(f32[264,128]{1,0:T(8,128)S(1)} %shard_map.84.refs_0_), channel_id=1, source_target_pairs={{0,3},{3,0},{1,2},{2,1},{4,7},{7,4},{5,6},{6,5},{8,11},{11,8},{9,1... | collective-permute-start | bytes 405512 | tf_op jit(solution)/shard_map/ppermute | solution.py:274
  86.9 10.3 %collective-permute-start.30 = (f32[256,128]{1,0:T(8,128)S(1)}, f32[256,128]{1,0:T(8,128)S(1)}, u32[]{:S(2)}, u32[]{:S(2)}) collective-permute-start(f32[256,128]{1,0:T(8,128)S(1)} %shard_map.85.refs_0_), channel_id=1, source_target_pairs={{0,3},{3,0},{1,2},{2,1},{4,7},{7,4},{5,6},{6,5},{8,11},{11,8},{9,1... | collective-permute-start | bytes 393224 | tf_op jit(solution)/shard_map/ppermute | solution.py:274
  (13 other events, 30.0 us)

commit v10 on v9

--- a/solution.py
+++ b/solution.py
@@ -10,8 +10,8 @@
 
 HIGHEST = lax.Precision.HIGHEST
 HIGH = lax.Precision.HIGH
-ROUNDS = (0.48,)
-STEPS = ("P0 P1 F0 F1", "G0 O0 G1 O1", "M0 T0 M1 M2", "T1 T2")
+ROUNDS = (0.36,)
+STEPS = ("P0 F0 P1 G0", "O0 M0 F1 T0", "G1 O1 M1 M2", "T1 D0 T2 D1", "D2")
 LINE_PIECES = (1,2,)
 BF16, F32 = jnp.bfloat16, jnp.float32
 NT = (((1,), (1,)), ((), ()))
@@ -330,6 +330,24 @@
     return out[: len(out) // 2], out[len(out) // 2 :]
 
 
+def join_body(a, b, out):
+    place = lax.axis_index("col")
+    ends = (place == 0) | (place == 3)
+    quarter = a.shape[1]
+    left, right = pl.ds(0, quarter), pl.ds(quarter, quarter)
+
+    def put(mine, other):
+        out[:, mine] = a[...]
+        out[:, other] = b[...]
+
+    pl.when(ends)(lambda: put(left, right))
+    pl.when(~ends)(lambda: put(right, left))
+
+
+def join(a, b):
+    return call(join_body, [shaped((a.shape[0], 2 * a.shape[1]))], (a, b))[0]
+
+
 def cut(out):
     edges, at = [], 0
     for part in ROUNDS + (1.0,):
@@ -365,15 +383,12 @@
     near = line(near_kernels, block_x, block_y, cent, own)
     far, sent = line(lambda *a: far_kernels(edges[:2], *a), block, cent, near, w0, w1)
 
-    place = lax.axis_index("col")
-    ends = (place == 0) | (place == 3)
-
     def both(pair, step):
         return [hop(pair[i], (i + step) % 2) for i in (0, 1)]
 
     coming, crossing = [None] * rounds, [None] * rounds
     partial, full, other, gone, here = ([None] * rounds for _ in range(5))
-    beside, mine, across, total, back = [], [], [], [], []
+    beside, mine, across, total, back, whole = [], [], [], [], [], []
 
     def do_partial(r):
         partial[r] = line(add, kept[2 * r : 2 * r + 2], coming[r])
@@ -401,16 +416,17 @@
         total.append(value)
         back.append(pass_line(value, BESIDE))
 
+    def do_whole(i):
+        whole.append(line(join, total[i], back[i]))
+
     sent = list(sent) + list(line(lambda *a: send_shares(edges[2:], *a), w0, w1, far))
     coming = [both(sent[2 * r : 2 * r + 2], 0) for r in range(rounds)]
     kept = line(lambda *a: keep_shares(edges, *a), w0, w1, running_t, targets_t, near)
-    steps = dict(P=do_partial, F=do_full, G=do_grad, O=do_owned, M=do_mine, T=do_total)
+    steps = dict(P=do_partial, F=do_full, G=do_grad, O=do_owned, M=do_mine, T=do_total, D=do_whole)
     for step in " ".join(STEPS).split():
         steps[step[0]](int(step[1]))
 
-    first = [jnp.where(ends, t, b) for t, b in zip(total, back)]
-    second = [jnp.where(ends, b, t) for t, b in zip(total, back)]
-    gradient = jnp.concatenate([jnp.concatenate(first), jnp.concatenate(second)], axis=1)
+    gradient = jnp.concatenate(whole)
     mine_rows = (slice(0, rows), slice(rows, None))
     residual = jnp.concatenate([f[i][:, mine_rows[i]] for f in full for i in (0, 1)])
     return gradient, residual

time: 104 us -> 109 us (1.048)
  waiting for transfers between devices: 46.4 us -> 56.5 us
  starting transfers between devices: 42.4 us -> 37.5 us
    ppermute x15, starting transfers between devices: 24.8 us -> 18.3 us  [hop(): return lax.ppermute(value, ('chip', 'core'), pairs)]
    ppermute x9, waiting for transfers between devices: 20.9 us -> 27.1 us  [pass_line(): return lax.ppermute(value, 'col', pairs)]
    ppermute x15, waiting for transfers between devices: 22.8 us -> 26.6 us  [hop(): return lax.ppermute(value, ('chip', 'core'), pairs)]
    ppermute x9, starting transfers between devices: 15.7 us -> 17.2 us  [pass_line(): return lax.ppermute(value, 'col', pairs)]
    pallas_call x20 -> x23, Pallas kernels: 10 us -> 10.4 us  [call(): pl.pallas_call(body, out_shape=outs, in_specs=[vmem] * len(args), out_spe...]
  transfers between devices with their start and end apart: 32 -> 32, of which waited for: 17 -> 20; matrix products, arithmetic and copies ran while one was open for 1% -> 1% of each run, Pallas kernels for 7% -> 6%
where the time goes in v10:
time: 109 us
  waiting for transfers between devices  56.5 us (52%)
  starting transfers between devices  37.5 us (34%)
  Pallas kernels  10.4 us (10%)
  local copies, waits for them, and re-layouts  2.12 us (2%)
  other arithmetic  1.85 us (2%)
    ppermute x9, waiting for transfers between devices, pass_line(): return lax.ppermute(value, 'col', pairs)  27.1 us
    ppermute x15, waiting for transfers between devices, hop(): return lax.ppermute(value, ('chip', 'core'), pairs)  26.6 us
    ppermute x15, starting transfers between devices, hop(): return lax.ppermute(value, ('chip', 'core'), pairs)  18.3 us
    ppermute x9, starting transfers between devices, pass_line(): return lax.ppermute(value, 'col', pairs)  17.2 us
    pallas_call x23, Pallas kernels, call(): pl.pallas_call(body, out_shape=outs, in_specs=[vmem] * len(args), out_spe...  10.4 us
    ppermute x8, waiting for transfers between devices, swap(): return lax.ppermute(value, axis, [(i, i ^ flip) for i in range(size)])  2.78 us
  transfers between devices with their start and end apart: 32, of which 20 were waited for; matrix products, arithmetic and copies ran while one was open for 1% of the time, Pallas kernels for 6%

profile of v10, /device:TPU:0, one launch (start us, length us, event | category | flops | bytes accessed | tf_op | source)
XLA Modules:
  0.0 109.2 jit_solution(10349601901532578640)
XLA Ops:
  1.1 2.6 %collective-permute-start.1 = (f32[128,1024]{1,0:T(8,128)}, f32[128,1024]{1,0:T(8,128)S(1)}, u32[]{:S(2)}, u32[]{:S(2)}) collective-permute-start(f32[128,1024]{1,0:T(8,128)} %own), channel_id=1, source_target_pairs={{0,8},{4,20},{8,0},{12,28},{16,24},{20,4},{24,16},{28,12},{1,9},{5... | collective-permute-start | bytes 1572872 | tf_op jit(solution)/shard_map/ppermute | solution.py:368
  5.2 10.4 %collective-permute-done.1.x = f32[128,1024]{1,0:T(8,128)S(1)} collective-permute-done((f32[128,1024]{1,0:T(8,128)}, f32[128,1024]{1,0:T(8,128)S(1)}, u32[]{:S(2)}, u32[]{:S(2)}) %collective-permute-start.1) | collective-permute-done | bytes 524320 | tf_op jit(solution)/shard_map/ppermute | solution.py:368
  15.7 2.1 %collective-permute-start.4 = (f32[128,1024]{1,0:T(8,128)S(1)}, f32[128,1024]{1,0:T(8,128)S(1)}, u32[]{:S(2)}, u32[]{:S(2)}) collective-permute-start(f32[128,1024]{1,0:T(8,128)S(1)} %collective-permute-done.1.x), channel_id=1, source_target_pairs={{0,16},{4,12},{8,24},{12,4},{16,0},{20,28},{24,8},{28,20},{1,17},{... | collective-permute-start | bytes 1572872 | tf_op jit(solution)/shard_map/ppermute | solution.py:368
  24.9 2.2 %shard_map.71 = (bf16[384,512]{1,0:T(8,128)(2,1)S(1)}, bf16[384,512]{1,0:T(8,128)(2,1)S(1)}, f32[176,256]{1,0:T(8,128)S(1)}, f32[176,256]{1,0:T(8,128)S(1)}) custom-call(f32[128,1024]{1,0:T(8,128)S(1)} %collective-permute-done.4.block, bf16[512,1024]{1,0:T(8,128)(2,1)S(1)} %get-tuple-element.147.c_high, bf16[512,1024]{1,0:T(8,128)(2,1)S(1)} %get-tuple-element.148.c_low, ...), custom_call_target="tpu_custom_call" | custom-call | tf_op jit(solution)/shard_map/pallas_call | solution.py:56
  27.1 2.4 %collective-permute-start.5 = (f32[176,256]{1,0:T(8,128)S(1)}, f32[176,256]{1,0:T(8,128)S(1)}, u32[]{:S(2)}, u32[]{:S(2)}) collective-permute-start(f32[176,256]{1,0:T(8,128)S(1)} %get-tuple-element.169), channel_id=1, source_target_pairs={{0,8},{4,20},{8,0},{12,28},{16,24},{20,4},{24,16},{28,12},{1,9},{5... | collective-permute-start | bytes 540680 | tf_op jit(solution)/shard_map/ppermute | solution.py:368
  29.6 2.0 %collective-permute-start.6 = (f32[176,256]{1,0:T(8,128)S(1)}, f32[176,256]{1,0:T(8,128)S(1)}, u32[]{:S(2)}, u32[]{:S(2)}) collective-permute-start(f32[176,256]{1,0:T(8,128)S(1)} %get-tuple-element.170), channel_id=1, source_target_pairs={{0,16},{4,12},{8,24},{12,4},{16,0},{20,28},{24,8},{28,20},{1,17},{... | collective-permute-start | bytes 540680 | tf_op jit(solution)/shard_map/ppermute | solution.py:368
  34.1 3.0 %collective-permute-done.6.refs_3_ = f32[176,256]{1,0:T(8,128)S(1)} collective-permute-done((f32[176,256]{1,0:T(8,128)S(1)}, f32[176,256]{1,0:T(8,128)S(1)}, u32[]{:S(2)}, u32[]{:S(2)}) %collective-permute-start.6) | collective-permute-done | bytes 180256 | tf_op jit(solution)/shard_map/ppermute | solution.py:368
  37.1 2.1 %collective-permute-start.7 = (f32[176,256]{1,0:T(8,128)S(1)}, f32[176,256]{1,0:T(8,128)S(1)}, u32[]{:S(2)}, u32[]{:S(2)}) collective-permute-start(f32[176,256]{1,0:T(8,128)S(1)} %get-tuple-element.177.refs_0_), channel_id=1, source_target_pairs={{0,16},{4,12},{8,24},{12,4},{16,0},{20,28},{24,8},{28,20},{1,17},{... | collective-permute-start | bytes 540680 | tf_op jit(solution)/shard_map/ppermute | solution.py:368
  39.4 3.9 %collective-permute-done.7.refs_2_ = f32[176,256]{1,0:T(8,128)S(1)} collective-permute-done((f32[176,256]{1,0:T(8,128)S(1)}, f32[176,256]{1,0:T(8,128)S(1)}, u32[]{:S(2)}, u32[]{:S(2)}) %collective-permute-start.7) | collective-permute-done | bytes 180256 | tf_op jit(solution)/shard_map/ppermute | solution.py:368
  43.2 3.8 %collective-permute-done.8.refs_3_ = f32[176,256]{1,0:T(8,128)S(1)} collective-permute-done((f32[176,256]{1,0:T(8,128)S(1)}, f32[176,256]{1,0:T(8,128)S(1)}, u32[]{:S(2)}, u32[]{:S(2)}) %collective-permute-start.8) | collective-permute-done | bytes 180256 | tf_op jit(solution)/shard_map/ppermute | solution.py:368
  47.1 1.9 %collective-permute-start.9 = (f32[176,256]{1,0:T(8,128)S(1)}, f32[176,256]{1,0:T(8,128)S(1)}, u32[]{:S(2)}, u32[]{:S(2)}) collective-permute-start(f32[176,256]{1,0:T(8,128)S(1)} %get-tuple-element.191.full_a), channel_id=1, source_target_pairs={{0,8},{4,20},{8,0},{12,28},{16,24},{20,4},{24,16},{28,12},{1,9},{5... | collective-permute-start | bytes 540680 | tf_op jit(solution)/shard_map/ppermute | solution.py:368
  51.3 3.2 %collective-permute-done.10.other_b = f32[176,256]{1,0:T(8,128)S(1)} collective-permute-done((f32[176,256]{1,0:T(8,128)S(1)}, f32[176,256]{1,0:T(8,128)S(1)}, u32[]{:S(2)}, u32[]{:S(2)}) %collective-permute-start.10) | collective-permute-done | bytes 180256 | tf_op jit(solution)/shard_map/ppermute | solution.py:368
  58.9 5.0 %collective-permute-done.16.refs_1_ = f32[352,128]{1,0:T(8,128)S(1)} collective-permute-done((f32[352,128]{1,0:T(8,128)S(1)}, f32[352,128]{1,0:T(8,128)S(1)}, u32[]{:S(2)}, u32[]{:S(2)}) %collective-permute-start.16) | collective-permute-done | bytes 180256 | tf_op jit(solution)/shard_map/ppermute | solution.py:274
  65.3 3.6 %collective-permute-start.17 = (f32[352,128]{1,0:T(8,128)S(1)}, f32[352,128]{1,0:T(8,128)S(1)}, u32[]{:S(2)}, u32[]{:S(2)}) collective-permute-start(f32[352,128]{1,0:T(8,128)S(1)} %shard_map.79.refs_0_), channel_id=1, source_target_pairs={{0,3},{3,0},{1,2},{2,1},{4,7},{7,4},{5,6},{6,5},{8,11},{11,8},{9,1... | collective-permute-start | bytes 540680 | tf_op jit(solution)/shard_map/ppermute | solution.py:274
  68.9 3.8 %collective-permute-done.17.refs_1_ = f32[352,128]{1,0:T(8,128)S(1)} collective-permute-done((f32[352,128]{1,0:T(8,128)S(1)}, f32[352,128]{1,0:T(8,128)S(1)}, u32[]{:S(2)}, u32[]{:S(2)}) %collective-permute-start.17) | collective-permute-done | bytes 180256 | tf_op jit(solution)/shard_map/ppermute | solution.py:274
  76.8 2.9 %collective-permute-start.26 = (f32[328,128]{1,0:T(8,128)S(1)}, f32[328,128]{1,0:T(8,128)S(1)}, u32[]{:S(2)}, u32[]{:S(2)}) collective-permute-start(f32[328,128]{1,0:T(8,128)S(1)} %get-tuple-element.237), channel_id=1, source_target_pairs={{0,1},{1,0},{2,3},{3,2},{4,5},{5,4},{6,7},{7,6},{8,9},{9,8},{10,11... | collective-permute-start | bytes 503816 | tf_op jit(solution)/shard_map/ppermute | solution.py:274
  79.7 1.9 %collective-permute-start.20 = (f32[352,128]{1,0:T(8,128)S(1)}, f32[352,128]{1,0:T(8,128)S(1)}, u32[]{:S(2)}, u32[]{:S(2)}) collective-permute-start(f32[352,128]{1,0:T(8,128)S(1)} %shard_map.81.a), channel_id=1, source_target_pairs={{0,1},{1,0},{2,3},{3,2},{4,5},{5,4},{6,7},{7,6},{8,9},{9,8},{10,11... | collective-permute-start | bytes 540680 | tf_op jit(solution)/shard_map/ppermute | solution.py:274
  81.6 3.0 %collective-permute-done.26.refs_1_ = f32[328,128]{1,0:T(8,128)S(1)} collective-permute-done((f32[328,128]{1,0:T(8,128)S(1)}, f32[328,128]{1,0:T(8,128)S(1)}, u32[]{:S(2)}, u32[]{:S(2)}) %collective-permute-start.26) | collective-permute-done | bytes 167968 | tf_op jit(solution)/shard_map/ppermute | solution.py:274
  84.7 2.9 %collective-permute-start.27 = (f32[328,128]{1,0:T(8,128)S(1)}, f32[328,128]{1,0:T(8,128)S(1)}, u32[]{:S(2)}, u32[]{:S(2)}) collective-permute-start(f32[328,128]{1,0:T(8,128)S(1)} %shard_map.84.refs_0_), channel_id=1, source_target_pairs={{0,3},{3,0},{1,2},{2,1},{4,7},{7,4},{5,6},{6,5},{8,11},{11,8},{9,1... | collective-permute-start | bytes 503816 | tf_op jit(solution)/shard_map/ppermute | solution.py:274
  88.2 2.9 %collective-permute-start.30 = (f32[320,128]{1,0:T(8,128)S(1)}, f32[320,128]{1,0:T(8,128)S(1)}, u32[]{:S(2)}, u32[]{:S(2)}) collective-permute-start(f32[320,128]{1,0:T(8,128)S(1)} %shard_map.85.refs_0_), channel_id=1, source_target_pairs={{0,3},{3,0},{1,2},{2,1},{4,7},{7,4},{5,6},{6,5},{8,11},{11,8},{9,1... | collective-permute-start | bytes 491528 | tf_op jit(solution)/shard_map/ppermute | solution.py:274
  91.2 7.1 %collective-permute-done.27.refs_1_ = f32[328,128]{1,0:T(8,128)S(1)} collective-permute-done((f32[328,128]{1,0:T(8,128)S(1)}, f32[328,128]{1,0:T(8,128)S(1)}, u32[]{:S(2)}, u32[]{:S(2)}) %collective-permute-start.27) | collective-permute-done | bytes 167968 | tf_op jit(solution)/shard_map/ppermute | solution.py:274
  98.4 3.3 %collective-permute-done.30.refs_1_ = f32[320,128]{1,0:T(8,128)S(1)} collective-permute-done((f32[320,128]{1,0:T(8,128)S(1)}, f32[320,128]{1,0:T(8,128)S(1)}, u32[]{:S(2)}, u32[]{:S(2)}) %collective-permute-start.30) | collective-permute-done | bytes 163872 | tf_op jit(solution)/shard_map/ppermute | solution.py:274
  103.8 1.8 %collective-permute-done.29.b = f32[328,128]{1,0:T(8,128)S(1)} collective-permute-done((f32[328,128]{1,0:T(8,128)S(1)}, f32[328,128]{1,0:T(8,128)S(1)}, u32[]{:S(2)}, u32[]{:S(2)}) %collective-permute-start.29) | collective-permute-done | bytes 167968 | tf_op jit(solution)/shard_map/ppermute | solution.py:274
  105.6 2.5 %collective-permute-done.31.b = f32[320,128]{1,0:T(8,128)S(1)} collective-permute-done((f32[320,128]{1,0:T(8,128)S(1)}, f32[320,128]{1,0:T(8,128)S(1)}, u32[]{:S(2)}, u32[]{:S(2)}) %collective-permute-start.31) | collective-permute-done | bytes 163872 | tf_op jit(solution)/shard_map/ppermute | solution.py:274
  (79 shorter events, 27.8 us)
Async XLA Ops:
  0.6 17.2 %collective-permute-start.3 = (f32[256,1024]{1,0:T(8,128)}, f32[256,1024]{1,0:T(8,128)S(1)}, u32[]{:S(2)}, u32[]{:S(2)}) collective-permute-start(f32[256,1024]{1,0:T(8,128)} %mine_ref.1), channel_id=1, source_target_pairs={{0,4},{4,0},{1,5},{5,1},{2,6},{6,2},{3,7},{7,3},{8,12},{12,8},{9,1... | collective-permute-start | bytes 3145736 | tf_op jit(solution)/shard_map/ppermute | solution.py:23
  1.1 14.5 %collective-permute-start.1 = (f32[128,1024]{1,0:T(8,128)}, f32[128,1024]{1,0:T(8,128)S(1)}, u32[]{:S(2)}, u32[]{:S(2)}) collective-permute-start(f32[128,1024]{1,0:T(8,128)} %own), channel_id=1, source_target_pairs={{0,8},{4,20},{8,0},{12,28},{16,24},{20,4},{24,16},{28,12},{1,9},{5... | collective-permute-start | bytes 1572872 | tf_op jit(solution)/shard_map/ppermute | solution.py:368
  3.7 19.6 %collective-permute-start = (f32[1000,256]{1,0:T(8,128)}, f32[1000,256]{1,0:T(8,128)S(1)}, u32[]{:S(2)}, u32[]{:S(2)}) collective-permute-start(f32[1000,256]{1,0:T(8,128)} %bitcast.7), channel_id=1, source_target_pairs={{0,4},{4,0},{1,5},{5,1},{2,6},{6,2},{3,7},{7,3},{8,12},{12,8},{9,1... | collective-permute-start | bytes 3072008 | tf_op jit(solution)/shard_map/ppermute | solution.py:23
  3.9 17.8 %collective-permute-start.2 = (f32[128,1024]{1,0:T(8,128)}, f32[128,1024]{1,0:T(8,128)S(1)}, u32[]{:S(2)}, u32[]{:S(2)}) collective-permute-start(f32[128,1024]{1,0:T(8,128)} %own), channel_id=1, source_target_pairs={{0,16},{4,12},{8,24},{12,4},{16,0},{20,28},{24,8},{28,20},{1,17},{... | collective-permute-start | bytes 1572872 | tf_op jit(solution)/shard_map/ppermute | solution.py:368
  15.7 9.3 %collective-permute-start.4 = (f32[128,1024]{1,0:T(8,128)S(1)}, f32[128,1024]{1,0:T(8,128)S(1)}, u32[]{:S(2)}, u32[]{:S(2)}) collective-permute-start(f32[128,1024]{1,0:T(8,128)S(1)} %collective-permute-done.1.x), channel_id=1, source_target_pairs={{0,16},{4,12},{8,24},{12,4},{16,0},{20,28},{24,8},{28,20},{1,17},{... | collective-permute-start | bytes 1572872 | tf_op jit(solution)/shard_map/ppermute | solution.py:368
  27.1 6.9 %collective-permute-start.5 = (f32[176,256]{1,0:T(8,128)S(1)}, f32[176,256]{1,0:T(8,128)S(1)}, u32[]{:S(2)}, u32[]{:S(2)}) collective-permute-start(f32[176,256]{1,0:T(8,128)S(1)} %get-tuple-element.169), channel_id=1, source_target_pairs={{0,8},{4,20},{8,0},{12,28},{16,24},{20,4},{24,16},{28,12},{1,9},{5... | collective-permute-start | bytes 540680 | tf_op jit(solution)/shard_map/ppermute | solution.py:368
  29.6 7.4 %collective-permute-start.6 = (f32[176,256]{1,0:T(8,128)S(1)}, f32[176,256]{1,0:T(8,128)S(1)}, u32[]{:S(2)}, u32[]{:S(2)}) collective-permute-start(f32[176,256]{1,0:T(8,128)S(1)} %get-tuple-element.170), channel_id=1, source_target_pairs={{0,16},{4,12},{8,24},{12,4},{16,0},{20,28},{24,8},{28,20},{1,17},{... | collective-permute-start | bytes 540680 | tf_op jit(solution)/shard_map/ppermute | solution.py:368
  32.3 16.7 %collective-permute-start.11 = (f32[328,256]{1,0:T(8,128)S(1)}, f32[328,256]{1,0:T(8,128)S(1)}, u32[]{:S(2)}, u32[]{:S(2)}) collective-permute-start(f32[328,256]{1,0:T(8,128)S(1)} %get-tuple-element.160), channel_id=1, source_target_pairs={{0,8},{4,20},{8,0},{12,28},{16,24},{20,4},{24,16},{28,12},{1,9},{5... | collective-permute-start | bytes 1007624 | tf_op jit(solution)/shard_map/ppermute | solution.py:368
  39.2 7.8 %collective-permute-start.8 = (f32[176,256]{1,0:T(8,128)S(1)}, f32[176,256]{1,0:T(8,128)S(1)}, u32[]{:S(2)}, u32[]{:S(2)}) collective-permute-start(f32[176,256]{1,0:T(8,128)S(1)} %get-tuple-element.178.refs_1_), channel_id=1, source_target_pairs={{0,8},{4,20},{8,0},{12,28},{16,24},{20,4},{24,16},{28,12},{1,9},{5... | collective-permute-start | bytes 540680 | tf_op jit(solution)/shard_map/ppermute | solution.py:368
  39.3 9.8 %collective-permute-start.12 = (f32[320,256]{1,0:T(8,128)S(1)}, f32[320,256]{1,0:T(8,128)S(1)}, u32[]{:S(2)}, u32[]{:S(2)}) collective-permute-start(f32[320,256]{1,0:T(8,128)S(1)} %get-tuple-element.185), channel_id=1, source_target_pairs={{0,16},{4,12},{8,24},{12,4},{16,0},{20,28},{24,8},{28,20},{1,17},{... | collective-permute-start | bytes 983048 | tf_op jit(solution)/shard_map/ppermute | solution.py:368
  47.1 7.5 %collective-permute-start.10 = (f32[176,256]{1,0:T(8,128)S(1)}, f32[176,256]{1,0:T(8,128)S(1)}, u32[]{:S(2)}, u32[]{:S(2)}) collective-permute-start(f32[176,256]{1,0:T(8,128)S(1)} %get-tuple-element.192.full_b), channel_id=1, source_target_pairs={{0,16},{4,12},{8,24},{12,4},{16,0},{20,28},{24,8},{28,20},{1,17},{... | collective-permute-start | bytes 540680 | tf_op jit(solution)/shard_map/ppermute | solution.py:368
  47.1 7.4 %collective-permute-start.9 = (f32[176,256]{1,0:T(8,128)S(1)}, f32[176,256]{1,0:T(8,128)S(1)}, u32[]{:S(2)}, u32[]{:S(2)}) collective-permute-start(f32[176,256]{1,0:T(8,128)S(1)} %get-tuple-element.191.full_a), channel_id=1, source_target_pairs={{0,8},{4,20},{8,0},{12,28},{16,24},{20,4},{24,16},{28,12},{1,9},{5... | collective-permute-start | bytes 540680 | tf_op jit(solution)/shard_map/ppermute | solution.py:368
  49.1 14.9 %collective-permute-start.18 = (f32[328,256]{1,0:T(8,128)S(1)}, f32[328,256]{1,0:T(8,128)S(1)}, u32[]{:S(2)}, u32[]{:S(2)}) collective-permute-start(f32[328,256]{1,0:T(8,128)S(1)} %get-tuple-element.212.refs_0_), channel_id=1, source_target_pairs={{0,16},{4,12},{8,24},{12,4},{16,0},{20,28},{24,8},{28,20},{1,17},{... | collective-permute-start | bytes 1007624 | tf_op jit(solution)/shard_map/ppermute | solution.py:368
  50.5 13.5 %collective-permute-start.19 = (f32[320,256]{1,0:T(8,128)S(1)}, f32[320,256]{1,0:T(8,128)S(1)}, u32[]{:S(2)}, u32[]{:S(2)}) collective-permute-start(f32[320,256]{1,0:T(8,128)S(1)} %get-tuple-element.213.refs_1_), channel_id=1, source_target_pairs={{0,8},{4,20},{8,0},{12,28},{16,24},{20,4},{24,16},{28,12},{1,9},{5... | collective-permute-start | bytes 983048 | tf_op jit(solution)/shard_map/ppermute | solution.py:368
  57.3 6.7 %collective-permute-start.16 = (f32[352,128]{1,0:T(8,128)S(1)}, f32[352,128]{1,0:T(8,128)S(1)}, u32[]{:S(2)}, u32[]{:S(2)}) collective-permute-start(f32[352,128]{1,0:T(8,128)S(1)} %get-tuple-element.208), channel_id=1, source_target_pairs={{0,1},{1,0},{2,3},{3,2},{4,5},{5,4},{6,7},{7,6},{8,9},{9,8},{10,11... | collective-permute-start | bytes 540680 | tf_op jit(solution)/shard_map/ppermute | solution.py:274
  64.1 9.2 %collective-permute-start.21 = (f32[328,256]{1,0:T(8,128)S(1)}, f32[328,256]{1,0:T(8,128)S(1)}, u32[]{:S(2)}, u32[]{:S(2)}) collective-permute-start(f32[328,256]{1,0:T(8,128)S(1)} %get-tuple-element.220.full_a), channel_id=1, source_target_pairs={{0,8},{4,20},{8,0},{12,28},{16,24},{20,4},{24,16},{28,12},{1,9},{5... | collective-permute-start | bytes 1007624 | tf_op jit(solution)/shard_map/ppermute | solution.py:368
  65.0 8.2 %collective-permute-start.22 = (f32[320,256]{1,0:T(8,128)S(1)}, f32[320,256]{1,0:T(8,128)S(1)}, u32[]{:S(2)}, u32[]{:S(2)}) collective-permute-start(f32[320,256]{1,0:T(8,128)S(1)} %get-tuple-element.221.full_b), channel_id=1, source_target_pairs={{0,16},{4,12},{8,24},{12,4},{16,0},{20,28},{24,8},{28,20},{1,17},{... | collective-permute-start | bytes 983048 | tf_op jit(solution)/shard_map/ppermute | solution.py:368
  65.3 7.3 %collective-permute-start.17 = (f32[352,128]{1,0:T(8,128)S(1)}, f32[352,128]{1,0:T(8,128)S(1)}, u32[]{:S(2)}, u32[]{:S(2)}) collective-permute-start(f32[352,128]{1,0:T(8,128)S(1)} %shard_map.79.refs_0_), channel_id=1, source_target_pairs={{0,3},{3,0},{1,2},{2,1},{4,7},{7,4},{5,6},{6,5},{8,11},{11,8},{9,1... | collective-permute-start | bytes 540680 | tf_op jit(solution)/shard_map/ppermute | solution.py:274
  76.8 7.9 %collective-permute-start.26 = (f32[328,128]{1,0:T(8,128)S(1)}, f32[328,128]{1,0:T(8,128)S(1)}, u32[]{:S(2)}, u32[]{:S(2)}) collective-permute-start(f32[328,128]{1,0:T(8,128)S(1)} %get-tuple-element.237), channel_id=1, source_target_pairs={{0,1},{1,0},{2,3},{3,2},{4,5},{5,4},{6,7},{7,6},{8,9},{9,8},{10,11... | collective-permute-start | bytes 503816 | tf_op jit(solution)/shard_map/ppermute | solution.py:274
  79.6 8.6 %collective-permute-start.28 = (f32[320,128]{1,0:T(8,128)S(1)}, f32[320,128]{1,0:T(8,128)S(1)}, u32[]{:S(2)}, u32[]{:S(2)}) collective-permute-start(f32[320,128]{1,0:T(8,128)S(1)} %get-tuple-element.241), channel_id=1, source_target_pairs={{0,1},{1,0},{2,3},{3,2},{4,5},{5,4},{6,7},{7,6},{8,9},{9,8},{10,11... | collective-permute-start | bytes 491528 | tf_op jit(solution)/shard_map/ppermute | solution.py:274
  79.7 18.7 %collective-permute-start.20 = (f32[352,128]{1,0:T(8,128)S(1)}, f32[352,128]{1,0:T(8,128)S(1)}, u32[]{:S(2)}, u32[]{:S(2)}) collective-permute-start(f32[352,128]{1,0:T(8,128)S(1)} %shard_map.81.a), channel_id=1, source_target_pairs={{0,1},{1,0},{2,3},{3,2},{4,5},{5,4},{6,7},{7,6},{8,9},{9,8},{10,11... | collective-permute-start | bytes 540680 | tf_op jit(solution)/shard_map/ppermute | solution.py:274
  84.7 13.6 %collective-permute-start.27 = (f32[328,128]{1,0:T(8,128)S(1)}, f32[328,128]{1,0:T(8,128)S(1)}, u32[]{:S(2)}, u32[]{:S(2)}) collective-permute-start(f32[328,128]{1,0:T(8,128)S(1)} %shard_map.84.refs_0_), channel_id=1, source_target_pairs={{0,3},{3,0},{1,2},{2,1},{4,7},{7,4},{5,6},{6,5},{8,11},{11,8},{9,1... | collective-permute-start | bytes 503816 | tf_op jit(solution)/shard_map/ppermute | solution.py:274
  88.2 13.5 %collective-permute-start.30 = (f32[320,128]{1,0:T(8,128)S(1)}, f32[320,128]{1,0:T(8,128)S(1)}, u32[]{:S(2)}, u32[]{:S(2)}) collective-permute-start(f32[320,128]{1,0:T(8,128)S(1)} %shard_map.85.refs_0_), channel_id=1, source_target_pairs={{0,3},{3,0},{1,2},{2,1},{4,7},{7,4},{5,6},{6,5},{8,11},{11,8},{9,1... | collective-permute-start | bytes 491528 | tf_op jit(solution)/shard_map/ppermute | solution.py:274
  98.3 7.3 %collective-permute-start.29 = (f32[328,128]{1,0:T(8,128)S(1)}, f32[328,128]{1,0:T(8,128)S(1)}, u32[]{:S(2)}, u32[]{:S(2)}) collective-permute-start(f32[328,128]{1,0:T(8,128)S(1)} %shard_map.86.a), channel_id=1, source_target_pairs={{0,1},{1,0},{2,3},{3,2},{4,5},{5,4},{6,7},{7,6},{8,9},{9,8},{10,11... | collective-permute-start | bytes 503816 | tf_op jit(solution)/shard_map/ppermute | solution.py:274
  (13 other events, 30.3 us)

commit v11 on v10

--- a/solution.py
+++ b/solution.py
@@ -10,8 +10,8 @@
 
 HIGHEST = lax.Precision.HIGHEST
 HIGH = lax.Precision.HIGH
-ROUNDS = (0.36,)
-STEPS = ("P0 F0 P1 G0", "O0 M0 F1 T0", "G1 O1 M1 M2", "T1 D0 T2 D1", "D2")
+ROUNDS = (0.48,)
+STEPS = ("P0 P1 F0 F1", "G0 O0 G1 O1", "M0 T0 M1 M2", "T1 D0 T2 D1", "D2")
 LINE_PIECES = (1,2,)
 BF16, F32 = jnp.bfloat16, jnp.float32
 NT = (((1,), (1,)), ((), ()))
@@ -130,31 +130,6 @@
     )
 
 
-def near_body(x, y, c_high, c_low, c_sq, own_high, own_low, near_high, near_low, high, low, row_sq):
-    rows = x.shape[0]
-    fill((x, y), high, low, row_sq)
-    near_high[pl.ds(rows, rows)] = own_high[...]
-    near_low[pl.ds(rows, rows)] = own_low[...]
-
-    def put(to, pair):
-        for ref, value in zip((near_high, near_low), pair):
-            ref[pl.ds(0, rows), to] = value[:rows]
-            ref[pl.ds(2 * rows, rows), to] = value[rows:]
-
-    kernel_rows(high[...], low[...], row_sq[:, 0:1], (c_high, c_low, c_sq), put)
-
-
-def near_kernels(x, y, cent, own):
-    rows, width = x.shape
-    wide = cent[0].shape[0]
-    return call(
-        near_body,
-        [shaped((3 * rows, wide), BF16)] * 2,
-        (x, y, *cent, *own),
-        scratch=row_scratch(2 * rows, width),
-    )
-
-
 def share(w_refs, cols, k_refs, rows):
     half = w_refs[0].shape[1]
     total = None
@@ -191,34 +166,40 @@
     )
 
 
-def far_body(edges, block, c_high, c_low, c_sq, near_high, near_low, w0, w1, *rest):
-    outs, (high, low, row_sq) = rest[:-3], rest[-3:]
-    far_high, far_low, sent = outs[0], outs[1], outs[2:]
-    rows = low.shape[0]
-    fill((block,), high, low, row_sq)
-    for far, near in ((far_high, near_high), (far_low, near_low)):
-        far[pl.ds(0, rows)] = near[pl.ds(0, rows)]
-        far[pl.ds(2 * rows, rows)] = near[pl.ds(2 * rows, rows)]
+def far_body(edges, block_y, block_far, c_high, c_low, c_sq, *rest):
+    pairs, (w0, w1), rest = rest[:4], rest[4:6], rest[6:]
+    near_high, near_low, far_high, far_low, *sent = rest[:-3]
+    high, low, row_sq = rest[-3:]
+    rows = block_y.shape[0]
+    left, middle, right = pl.ds(0, rows), pl.ds(rows, rows), pl.ds(2 * rows, rows)
+    fill((block_y, block_far), high, low, row_sq)
+    for near, far, own, x in zip((near_high, near_low), (far_high, far_low), pairs[:2], pairs[2:]):
+        near[left] = x[...]
+        near[middle] = own[...]
+        far[left] = x[...]
 
     def put(to, pair):
-        far_high[pl.ds(rows, rows), to], far_low[pl.ds(rows, rows), to] = pair
+        for near, far, value in zip((near_high, near_low), (far_high, far_low), pair):
+            near[right, to] = value[:rows]
+            far[right, to] = value[:rows]
+            far[middle, to] = value[rows:]
 
     kernel_rows(high[...], low[...], row_sq[:, 0:1], (c_high, c_low, c_sq), put)
     for i, (a, b) in enumerate(edges):
         sent[i][...] = share((w0, w1), pl.ds(a, b - a), (far_high, far_low), goes(rows)[i % 2])
 
 
-def far_kernels(edges, block, cent, near, w0, w1):
-    rows, width = block.shape
-    wide = cent[0].shape[0]
-    outs = [shaped(near[0].shape, BF16)] * 2 + [shaped((b - a, 2 * rows)) for a, b in edges]
+def far_kernels(edges, block_y, block_far, cent, own, x, w0, w1):
+    rows, width = block_y.shape
+    outs = [shaped((3 * rows, cent[0].shape[0]), BF16)] * 4
+    outs += [shaped((b - a, 2 * rows)) for a, b in edges]
     out = call(
         functools.partial(far_body, edges),
         outs,
-        (block, *cent, *near, w0, w1),
-        scratch=row_scratch(rows, width),
+        (block_y, block_far, *cent, *own, *x, w0, w1),
+        scratch=row_scratch(2 * rows, width),
     )
-    return out[:2], out[2:]
+    return out[:2], out[2:4], out[4:]
 
 
 def send_body(edges, rows, w0, w1, far_high, far_low, *sent):
@@ -374,14 +355,16 @@
     rounds = len(edges) // 2
     line = Line()
     block_x = hop(batch, 0)
-    block_y = hop(batch, 1)
     cent_theirs = swap(centers, "core")
     w0, w1 = weights_t, swap(weights_t, "core")
     cent = line(split_cent, centers, cent_theirs)
     own = line(own_kernels, batch, cent)
-    block = hop(block_x, 1)
-    near = line(near_kernels, block_x, block_y, cent, own)
-    far, sent = line(lambda *a: far_kernels(edges[:2], *a), block, cent, near, w0, w1)
+    block_far = hop(block_x, 1)
+    block_y = hop(lax.optimization_barrier((batch, block_x))[0], 1)
+    x = line(own_kernels, block_x, cent)
+    near, far, sent = line(
+        lambda *a: far_kernels(edges[:2], *a), block_y, block_far, cent, own, x, w0, w1
+    )
 
     def both(pair, step):
         return [hop(pair[i], (i + step) % 2) for i in (0, 1)]

time: 109 us -> 105 us (0.963)
  waiting for transfers between devices: 56.5 us -> 51.6 us
  starting transfers between devices: 37.5 us -> 38.6 us
    ppermute x9, waiting for transfers between devices: 27.1 us -> 20.9 us  [pass_line(): return lax.ppermute(value, 'col', pairs)]
    ppermute x15, starting transfers between devices: 18.3 us -> 21 us  [hop(): return lax.ppermute(value, ('chip', 'core'), pairs)]
    ppermute x9, starting transfers between devices: 17.2 us -> 15.6 us  [pass_line(): return lax.ppermute(value, 'col', pairs)]
    ppermute x15, waiting for transfers between devices: 26.6 us -> 28 us  [hop(): return lax.ppermute(value, ('chip', 'core'), pairs)]
  transfers between devices with their start and end apart: 32 -> 32, of which waited for: 20 -> 21; matrix products, arithmetic and copies ran while one was open for 1% -> 1% of each run, Pallas kernels for 6% -> 8%
where the time goes in v11:
time: 105 us
  waiting for transfers between devices  51.6 us (49%)
  starting transfers between devices  38.6 us (37%)
  Pallas kernels  10.1 us (10%)
  other arithmetic  1.85 us (2%)
  local copies, waits for them, and re-layouts  1.82 us (2%)
    ppermute x15, waiting for transfers between devices, hop(): return lax.ppermute(value, ('chip', 'core'), pairs)  28 us
    ppermute x15, starting transfers between devices, hop(): return lax.ppermute(value, ('chip', 'core'), pairs)  21 us
    ppermute x9, waiting for transfers between devices, pass_line(): return lax.ppermute(value, 'col', pairs)  20.9 us
    ppermute x9, starting transfers between devices, pass_line(): return lax.ppermute(value, 'col', pairs)  15.6 us
    pallas_call x23, Pallas kernels, call(): pl.pallas_call(body, out_shape=outs, in_specs=[vmem] * len(args), out_spe...  10.1 us
    ppermute x8, waiting for transfers between devices, swap(): return lax.ppermute(value, axis, [(i, i ^ flip) for i in range(size)])  2.66 us
  transfers between devices with their start and end apart: 32, of which 21 were waited for; matrix products, arithmetic and copies ran while one was open for 1% of the time, Pallas kernels for 8%

profile of v11, /device:TPU:0, one launch (start us, length us, event | category | flops | bytes accessed | tf_op | source)
XLA Modules:
  0.0 104.8 jit_solution(7385047259155984802)
XLA Ops:
  1.1 2.6 %collective-permute-start.1 = (f32[128,1024]{1,0:T(8,128)}, f32[128,1024]{1,0:T(8,128)S(1)}, u32[]{:S(2)}, u32[]{:S(2)}) collective-permute-start(f32[128,1024]{1,0:T(8,128)} %own), channel_id=1, source_target_pairs={{0,8},{4,20},{8,0},{12,28},{16,24},{20,4},{24,16},{28,12},{1,9},{5... | collective-permute-start | bytes 1572872 | tf_op jit(solution)/shard_map/ppermute | solution.py:349
  3.9 7.2 %collective-permute-done.1.own = f32[128,1024]{1,0:T(8,128)S(1)} collective-permute-done((f32[128,1024]{1,0:T(8,128)}, f32[128,1024]{1,0:T(8,128)S(1)}, u32[]{:S(2)}, u32[]{:S(2)}) %collective-permute-start.1) | collective-permute-done | bytes 524320 | tf_op jit(solution)/shard_map/ppermute | solution.py:349
  11.1 2.0 %collective-permute-start.2 = (f32[128,1024]{1,0:T(8,128)}, f32[128,1024]{1,0:T(8,128)S(1)}, u32[]{:S(2)}, u32[]{:S(2)}) collective-permute-start(f32[128,1024]{1,0:T(8,128)} %own), channel_id=1, source_target_pairs={{0,16},{4,12},{8,24},{12,4},{16,0},{20,28},{24,8},{28,20},{1,17},{... | collective-permute-start | bytes 1572872 | tf_op jit(solution)/shard_map/ppermute | solution.py:349
  18.7 1.8 %collective-permute-done.2.block_y = f32[128,1024]{1,0:T(8,128)S(1)} collective-permute-done((f32[128,1024]{1,0:T(8,128)}, f32[128,1024]{1,0:T(8,128)S(1)}, u32[]{:S(2)}, u32[]{:S(2)}) %collective-permute-start.2) | collective-permute-done | bytes 524320 | tf_op jit(solution)/shard_map/ppermute | solution.py:349
  20.5 5.6 %collective-permute-done.3.block_far = f32[128,1024]{1,0:T(8,128)S(1)} collective-permute-done((f32[128,1024]{1,0:T(8,128)S(1)}, f32[128,1024]{1,0:T(8,128)S(1)}, u32[]{:S(2)}, u32[]{:S(2)}) %collective-permute-start.3) | collective-permute-done | bytes 524320 | tf_op jit(solution)/shard_map/ppermute | solution.py:349
  26.1 2.2 %shard_map.71 = (bf16[384,512]{1,0:T(8,128)(2,1)S(1)}, bf16[384,512]{1,0:T(8,128)(2,1)S(1)}, bf16[384,512]{1,0:T(8,128)(2,1)S(1)}, bf16[384,512]{1,0:T(8,128)(2,...) custom-call(f32[128,1024]{1,0:T(8,128)S(1)} %collective-permute-done.2.block_y, ...), custom_call_target="tpu_custom_call" | custom-call | tf_op jit(solution)/shard_map/pallas_call | solution.py:56
  28.3 2.1 %collective-permute-start.5 = (f32[240,256]{1,0:T(8,128)S(1)}, f32[240,256]{1,0:T(8,128)S(1)}, u32[]{:S(2)}, u32[]{:S(2)}) collective-permute-start(f32[240,256]{1,0:T(8,128)S(1)} %get-tuple-element.175), channel_id=1, source_target_pairs={{0,8},{4,20},{8,0},{12,28},{16,24},{20,4},{24,16},{28,12},{1,9},{5... | collective-permute-start | bytes 737288 | tf_op jit(solution)/shard_map/ppermute | solution.py:349
  34.3 2.9 %collective-permute-done.5.refs_2_ = f32[240,256]{1,0:T(8,128)S(1)} collective-permute-done((f32[240,256]{1,0:T(8,128)S(1)}, f32[240,256]{1,0:T(8,128)S(1)}, u32[]{:S(2)}, u32[]{:S(2)}) %collective-permute-start.5) | collective-permute-done | bytes 245792 | tf_op jit(solution)/shard_map/ppermute | solution.py:349
  37.1 1.8 %collective-permute-done.6.refs_3_ = f32[240,256]{1,0:T(8,128)S(1)} collective-permute-done((f32[240,256]{1,0:T(8,128)S(1)}, f32[240,256]{1,0:T(8,128)S(1)}, u32[]{:S(2)}, u32[]{:S(2)}) %collective-permute-start.6) | collective-permute-done | bytes 245792 | tf_op jit(solution)/shard_map/ppermute | solution.py:349
  39.5 2.0 %collective-permute-start.7 = (f32[240,256]{1,0:T(8,128)S(1)}, f32[240,256]{1,0:T(8,128)S(1)}, u32[]{:S(2)}, u32[]{:S(2)}) collective-permute-start(f32[240,256]{1,0:T(8,128)S(1)} %get-tuple-element.191.refs_0_), channel_id=1, source_target_pairs={{0,16},{4,12},{8,24},{12,4},{16,0},{20,28},{24,8},{28,20},{1,17},{... | collective-permute-start | bytes 737288 | tf_op jit(solution)/shard_map/ppermute | solution.py:349
  41.5 2.8 %collective-permute-done.10.refs_3_ = f32[256,256]{1,0:T(8,128)S(1)} collective-permute-done((f32[256,256]{1,0:T(8,128)S(1)}, f32[256,256]{1,0:T(8,128)S(1)}, u32[]{:S(2)}, u32[]{:S(2)}) %collective-permute-start.10) | collective-permute-done | bytes 262176 | tf_op jit(solution)/shard_map/ppermute | solution.py:349
  48.5 1.8 %collective-permute-start.12 = (f32[240,256]{1,0:T(8,128)S(1)}, f32[240,256]{1,0:T(8,128)S(1)}, u32[]{:S(2)}, u32[]{:S(2)}) collective-permute-start(f32[240,256]{1,0:T(8,128)S(1)} %get-tuple-element.204.full_b), channel_id=1, source_target_pairs={{0,16},{4,12},{8,24},{12,4},{16,0},{20,28},{24,8},{28,20},{1,17},{... | collective-permute-start | bytes 737288 | tf_op jit(solution)/shard_map/ppermute | solution.py:349
  50.3 1.9 %collective-permute-start.11 = (f32[240,256]{1,0:T(8,128)S(1)}, f32[240,256]{1,0:T(8,128)S(1)}, u32[]{:S(2)}, u32[]{:S(2)}) collective-permute-start(f32[240,256]{1,0:T(8,128)S(1)} %get-tuple-element.203.full_a), channel_id=1, source_target_pairs={{0,8},{4,20},{8,0},{12,28},{16,24},{20,4},{24,16},{28,12},{1,9},{5... | collective-permute-start | bytes 737288 | tf_op jit(solution)/shard_map/ppermute | solution.py:349
  52.2 2.5 %collective-permute-done.14.refs_3_ = f32[256,256]{1,0:T(8,128)S(1)} collective-permute-done((f32[256,256]{1,0:T(8,128)S(1)}, f32[256,256]{1,0:T(8,128)S(1)}, u32[]{:S(2)}, u32[]{:S(2)}) %collective-permute-start.14) | collective-permute-done | bytes 262176 | tf_op jit(solution)/shard_map/ppermute | solution.py:349
  56.3 1.7 %collective-permute-start.20 = (f32[256,256]{1,0:T(8,128)S(1)}, f32[256,256]{1,0:T(8,128)S(1)}, u32[]{:S(2)}, u32[]{:S(2)}) collective-permute-start(f32[256,256]{1,0:T(8,128)S(1)} %get-tuple-element.223.full_b), channel_id=1, source_target_pairs={{0,16},{4,12},{8,24},{12,4},{16,0},{20,28},{24,8},{28,20},{1,17},{... | collective-permute-start | bytes 786440 | tf_op jit(solution)/shard_map/ppermute | solution.py:349
  62.9 1.6 %collective-permute-start.18 = (f32[480,128]{1,0:T(8,128)S(1)}, f32[480,128]{1,0:T(8,128)S(1)}, u32[]{:S(2)}, u32[]{:S(2)}) collective-permute-start(f32[480,128]{1,0:T(8,128)S(1)} %get-tuple-element.220), channel_id=1, source_target_pairs={{0,1},{1,0},{2,3},{3,2},{4,5},{5,4},{6,7},{7,6},{8,9},{9,8},{10,11... | collective-permute-start | bytes 737288 | tf_op jit(solution)/shard_map/ppermute | solution.py:255
  67.7 3.4 %collective-permute-done.18.refs_1_ = f32[480,128]{1,0:T(8,128)S(1)} collective-permute-done((f32[480,128]{1,0:T(8,128)S(1)}, f32[480,128]{1,0:T(8,128)S(1)}, u32[]{:S(2)}, u32[]{:S(2)}) %collective-permute-start.18) | collective-permute-done | bytes 245792 | tf_op jit(solution)/shard_map/ppermute | solution.py:255
  71.1 3.7 %collective-permute-start.24 = (f32[480,128]{1,0:T(8,128)S(1)}, f32[480,128]{1,0:T(8,128)S(1)}, u32[]{:S(2)}, u32[]{:S(2)}) collective-permute-start(f32[480,128]{1,0:T(8,128)S(1)} %shard_map.82.refs_0_), channel_id=1, source_target_pairs={{0,3},{3,0},{1,2},{2,1},{4,7},{7,4},{5,6},{6,5},{8,11},{11,8},{9,1... | collective-permute-start | bytes 737288 | tf_op jit(solution)/shard_map/ppermute | solution.py:255
  74.8 2.0 %collective-permute-start.28 = (f32[256,128]{1,0:T(8,128)S(1)}, f32[256,128]{1,0:T(8,128)S(1)}, u32[]{:S(2)}, u32[]{:S(2)}) collective-permute-start(f32[256,128]{1,0:T(8,128)S(1)} %get-tuple-element.247), channel_id=1, source_target_pairs={{0,1},{1,0},{2,3},{3,2},{4,5},{5,4},{6,7},{7,6},{8,9},{9,8},{10,11... | collective-permute-start | bytes 393224 | tf_op jit(solution)/shard_map/ppermute | solution.py:255
  76.8 5.1 %collective-permute-done.24.refs_1_ = f32[480,128]{1,0:T(8,128)S(1)} collective-permute-done((f32[480,128]{1,0:T(8,128)S(1)}, f32[480,128]{1,0:T(8,128)S(1)}, u32[]{:S(2)}, u32[]{:S(2)}) %collective-permute-start.24) | collective-permute-done | bytes 245792 | tf_op jit(solution)/shard_map/ppermute | solution.py:255
  81.9 3.5 %collective-permute-start.25 = (f32[480,128]{1,0:T(8,128)S(1)}, f32[480,128]{1,0:T(8,128)S(1)}, u32[]{:S(2)}, u32[]{:S(2)}) collective-permute-start(f32[480,128]{1,0:T(8,128)S(1)} %shard_map.83.a), channel_id=1, source_target_pairs={{0,1},{1,0},{2,3},{3,2},{4,5},{5,4},{6,7},{7,6},{8,9},{9,8},{10,11... | collective-permute-start | bytes 737288 | tf_op jit(solution)/shard_map/ppermute | solution.py:255
  85.4 2.5 %collective-permute-start.27 = (f32[264,128]{1,0:T(8,128)S(1)}, f32[264,128]{1,0:T(8,128)S(1)}, u32[]{:S(2)}, u32[]{:S(2)}) collective-permute-start(f32[264,128]{1,0:T(8,128)S(1)} %shard_map.84.refs_0_), channel_id=1, source_target_pairs={{0,3},{3,0},{1,2},{2,1},{4,7},{7,4},{5,6},{6,5},{8,11},{11,8},{9,1... | collective-permute-start | bytes 405512 | tf_op jit(solution)/shard_map/ppermute | solution.py:255
  89.4 7.3 %collective-permute-done.27.refs_1_ = f32[264,128]{1,0:T(8,128)S(1)} collective-permute-done((f32[264,128]{1,0:T(8,128)S(1)}, f32[264,128]{1,0:T(8,128)S(1)}, u32[]{:S(2)}, u32[]{:S(2)}) %collective-permute-start.27) | collective-permute-done | bytes 135200 | tf_op jit(solution)/shard_map/ppermute | solution.py:255
  100.0 2.3 %collective-permute-done.29.b = f32[264,128]{1,0:T(8,128)S(1)} collective-permute-done((f32[264,128]{1,0:T(8,128)S(1)}, f32[264,128]{1,0:T(8,128)S(1)}, u32[]{:S(2)}, u32[]{:S(2)}) %collective-permute-start.29) | collective-permute-done | bytes 135200 | tf_op jit(solution)/shard_map/ppermute | solution.py:255
  (79 shorter events, 31.8 us)
Async XLA Ops:
  0.6 12.5 %collective-permute-start.4 = (f32[256,1024]{1,0:T(8,128)}, f32[256,1024]{1,0:T(8,128)S(1)}, u32[]{:S(2)}, u32[]{:S(2)}) collective-permute-start(f32[256,1024]{1,0:T(8,128)} %mine_ref.1), channel_id=1, source_target_pairs={{0,4},{4,0},{1,5},{5,1},{2,6},{6,2},{3,7},{7,3},{8,12},{12,8},{9,1... | collective-permute-start | bytes 3145736 | tf_op jit(solution)/shard_map/ppermute | solution.py:23
  1.1 9.9 %collective-permute-start.1 = (f32[128,1024]{1,0:T(8,128)}, f32[128,1024]{1,0:T(8,128)S(1)}, u32[]{:S(2)}, u32[]{:S(2)}) collective-permute-start(f32[128,1024]{1,0:T(8,128)} %own), channel_id=1, source_target_pairs={{0,8},{4,20},{8,0},{12,28},{16,24},{20,4},{24,16},{28,12},{1,9},{5... | collective-permute-start | bytes 1572872 | tf_op jit(solution)/shard_map/ppermute | solution.py:349
  3.7 15.0 %collective-permute-start = (f32[1000,256]{1,0:T(8,128)}, f32[1000,256]{1,0:T(8,128)S(1)}, u32[]{:S(2)}, u32[]{:S(2)}) collective-permute-start(f32[1000,256]{1,0:T(8,128)} %bitcast.7), channel_id=1, source_target_pairs={{0,4},{4,0},{1,5},{5,1},{2,6},{6,2},{3,7},{7,3},{8,12},{12,8},{9,1... | collective-permute-start | bytes 3072008 | tf_op jit(solution)/shard_map/ppermute | solution.py:23
  11.1 9.4 %collective-permute-start.2 = (f32[128,1024]{1,0:T(8,128)}, f32[128,1024]{1,0:T(8,128)S(1)}, u32[]{:S(2)}, u32[]{:S(2)}) collective-permute-start(f32[128,1024]{1,0:T(8,128)} %own), channel_id=1, source_target_pairs={{0,16},{4,12},{8,24},{12,4},{16,0},{20,28},{24,8},{28,20},{1,17},{... | collective-permute-start | bytes 1572872 | tf_op jit(solution)/shard_map/ppermute | solution.py:349
  13.1 13.0 %collective-permute-start.3 = (f32[128,1024]{1,0:T(8,128)S(1)}, f32[128,1024]{1,0:T(8,128)S(1)}, u32[]{:S(2)}, u32[]{:S(2)}) collective-permute-start(f32[128,1024]{1,0:T(8,128)S(1)} %collective-permute-done.1.own), channel_id=1, source_target_pairs={{0,16},{4,12},{8,24},{12,4},{16,0},{20,28},{24,8},{28,20},{1,17},{... | collective-permute-start | bytes 1572872 | tf_op jit(solution)/shard_map/ppermute | solution.py:349
  28.3 8.8 %collective-permute-start.5 = (f32[240,256]{1,0:T(8,128)S(1)}, f32[240,256]{1,0:T(8,128)S(1)}, u32[]{:S(2)}, u32[]{:S(2)}) collective-permute-start(f32[240,256]{1,0:T(8,128)S(1)} %get-tuple-element.175), channel_id=1, source_target_pairs={{0,8},{4,20},{8,0},{12,28},{16,24},{20,4},{24,16},{28,12},{1,9},{5... | collective-permute-start | bytes 737288 | tf_op jit(solution)/shard_map/ppermute | solution.py:349
  30.4 8.5 %collective-permute-start.6 = (f32[240,256]{1,0:T(8,128)S(1)}, f32[240,256]{1,0:T(8,128)S(1)}, u32[]{:S(2)}, u32[]{:S(2)}) collective-permute-start(f32[240,256]{1,0:T(8,128)S(1)} %get-tuple-element.176), channel_id=1, source_target_pairs={{0,16},{4,12},{8,24},{12,4},{16,0},{20,28},{24,8},{28,20},{1,17},{... | collective-permute-start | bytes 737288 | tf_op jit(solution)/shard_map/ppermute | solution.py:349
  32.5 11.7 %collective-permute-start.9 = (f32[264,256]{1,0:T(8,128)S(1)}, f32[264,256]{1,0:T(8,128)S(1)}, u32[]{:S(2)}, u32[]{:S(2)}) collective-permute-start(f32[264,256]{1,0:T(8,128)S(1)} %get-tuple-element.166), channel_id=1, source_target_pairs={{0,8},{4,20},{8,0},{12,28},{16,24},{20,4},{24,16},{28,12},{1,9},{5... | collective-permute-start | bytes 811016 | tf_op jit(solution)/shard_map/ppermute | solution.py:349
  33.1 11.1 %collective-permute-start.10 = (f32[256,256]{1,0:T(8,128)S(1)}, f32[256,256]{1,0:T(8,128)S(1)}, u32[]{:S(2)}, u32[]{:S(2)}) collective-permute-start(f32[256,256]{1,0:T(8,128)S(1)} %get-tuple-element.185), channel_id=1, source_target_pairs={{0,16},{4,12},{8,24},{12,4},{16,0},{20,28},{24,8},{28,20},{1,17},{... | collective-permute-start | bytes 786440 | tf_op jit(solution)/shard_map/ppermute | solution.py:349
  38.9 9.3 %collective-permute-start.8 = (f32[240,256]{1,0:T(8,128)S(1)}, f32[240,256]{1,0:T(8,128)S(1)}, u32[]{:S(2)}, u32[]{:S(2)}) collective-permute-start(f32[240,256]{1,0:T(8,128)S(1)} %get-tuple-element.192.refs_1_), channel_id=1, source_target_pairs={{0,8},{4,20},{8,0},{12,28},{16,24},{20,4},{24,16},{28,12},{1,9},{5... | collective-permute-start | bytes 737288 | tf_op jit(solution)/shard_map/ppermute | solution.py:349
  39.5 9.0 %collective-permute-start.7 = (f32[240,256]{1,0:T(8,128)S(1)}, f32[240,256]{1,0:T(8,128)S(1)}, u32[]{:S(2)}, u32[]{:S(2)}) collective-permute-start(f32[240,256]{1,0:T(8,128)S(1)} %get-tuple-element.191.refs_0_), channel_id=1, source_target_pairs={{0,16},{4,12},{8,24},{12,4},{16,0},{20,28},{24,8},{28,20},{1,17},{... | collective-permute-start | bytes 737288 | tf_op jit(solution)/shard_map/ppermute | solution.py:349
  44.3 10.4 %collective-permute-start.13 = (f32[264,256]{1,0:T(8,128)S(1)}, f32[264,256]{1,0:T(8,128)S(1)}, u32[]{:S(2)}, u32[]{:S(2)}) collective-permute-start(f32[264,256]{1,0:T(8,128)S(1)} %get-tuple-element.198.refs_0_), channel_id=1, source_target_pairs={{0,16},{4,12},{8,24},{12,4},{16,0},{20,28},{24,8},{28,20},{1,17},{... | collective-permute-start | bytes 811016 | tf_op jit(solution)/shard_map/ppermute | solution.py:349
  45.5 9.2 %collective-permute-start.14 = (f32[256,256]{1,0:T(8,128)S(1)}, f32[256,256]{1,0:T(8,128)S(1)}, u32[]{:S(2)}, u32[]{:S(2)}) collective-permute-start(f32[256,256]{1,0:T(8,128)S(1)} %get-tuple-element.199.refs_1_), channel_id=1, source_target_pairs={{0,8},{4,20},{8,0},{12,28},{16,24},{20,4},{24,16},{28,12},{1,9},{5... | collective-permute-start | bytes 786440 | tf_op jit(solution)/shard_map/ppermute | solution.py:349
  48.5 11.0 %collective-permute-start.12 = (f32[240,256]{1,0:T(8,128)S(1)}, f32[240,256]{1,0:T(8,128)S(1)}, u32[]{:S(2)}, u32[]{:S(2)}) collective-permute-start(f32[240,256]{1,0:T(8,128)S(1)} %get-tuple-element.204.full_b), channel_id=1, source_target_pairs={{0,16},{4,12},{8,24},{12,4},{16,0},{20,28},{24,8},{28,20},{1,17},{... | collective-permute-start | bytes 737288 | tf_op jit(solution)/shard_map/ppermute | solution.py:349
  50.3 9.7 %collective-permute-start.11 = (f32[240,256]{1,0:T(8,128)S(1)}, f32[240,256]{1,0:T(8,128)S(1)}, u32[]{:S(2)}, u32[]{:S(2)}) collective-permute-start(f32[240,256]{1,0:T(8,128)S(1)} %get-tuple-element.203.full_a), channel_id=1, source_target_pairs={{0,8},{4,20},{8,0},{12,28},{16,24},{20,4},{24,16},{28,12},{1,9},{5... | collective-permute-start | bytes 737288 | tf_op jit(solution)/shard_map/ppermute | solution.py:349
  54.8 9.8 %collective-permute-start.19 = (f32[264,256]{1,0:T(8,128)S(1)}, f32[264,256]{1,0:T(8,128)S(1)}, u32[]{:S(2)}, u32[]{:S(2)}) collective-permute-start(f32[264,256]{1,0:T(8,128)S(1)} %get-tuple-element.222.full_a), channel_id=1, source_target_pairs={{0,8},{4,20},{8,0},{12,28},{16,24},{20,4},{24,16},{28,12},{1,9},{5... | collective-permute-start | bytes 811016 | tf_op jit(solution)/shard_map/ppermute | solution.py:349
  56.3 8.3 %collective-permute-start.20 = (f32[256,256]{1,0:T(8,128)S(1)}, f32[256,256]{1,0:T(8,128)S(1)}, u32[]{:S(2)}, u32[]{:S(2)}) collective-permute-start(f32[256,256]{1,0:T(8,128)S(1)} %get-tuple-element.223.full_b), channel_id=1, source_target_pairs={{0,16},{4,12},{8,24},{12,4},{16,0},{20,28},{24,8},{28,20},{1,17},{... | collective-permute-start | bytes 786440 | tf_op jit(solution)/shard_map/ppermute | solution.py:349
  62.9 8.2 %collective-permute-start.18 = (f32[480,128]{1,0:T(8,128)S(1)}, f32[480,128]{1,0:T(8,128)S(1)}, u32[]{:S(2)}, u32[]{:S(2)}) collective-permute-start(f32[480,128]{1,0:T(8,128)S(1)} %get-tuple-element.220), channel_id=1, source_target_pairs={{0,1},{1,0},{2,3},{3,2},{4,5},{5,4},{6,7},{7,6},{8,9},{9,8},{10,11... | collective-permute-start | bytes 737288 | tf_op jit(solution)/shard_map/ppermute | solution.py:255
  71.1 10.8 %collective-permute-start.24 = (f32[480,128]{1,0:T(8,128)S(1)}, f32[480,128]{1,0:T(8,128)S(1)}, u32[]{:S(2)}, u32[]{:S(2)}) collective-permute-start(f32[480,128]{1,0:T(8,128)S(1)} %shard_map.82.refs_0_), channel_id=1, source_target_pairs={{0,3},{3,0},{1,2},{2,1},{4,7},{7,4},{5,6},{6,5},{8,11},{11,8},{9,1... | collective-permute-start | bytes 737288 | tf_op jit(solution)/shard_map/ppermute | solution.py:255
  74.8 10.6 %collective-permute-start.26 = (f32[264,128]{1,0:T(8,128)S(1)}, f32[264,128]{1,0:T(8,128)S(1)}, u32[]{:S(2)}, u32[]{:S(2)}) collective-permute-start(f32[264,128]{1,0:T(8,128)S(1)} %get-tuple-element.238), channel_id=1, source_target_pairs={{0,1},{1,0},{2,3},{3,2},{4,5},{5,4},{6,7},{7,6},{8,9},{9,8},{10,11... | collective-permute-start | bytes 405512 | tf_op jit(solution)/shard_map/ppermute | solution.py:255
  74.8 13.2 %collective-permute-start.28 = (f32[256,128]{1,0:T(8,128)S(1)}, f32[256,128]{1,0:T(8,128)S(1)}, u32[]{:S(2)}, u32[]{:S(2)}) collective-permute-start(f32[256,128]{1,0:T(8,128)S(1)} %get-tuple-element.247), channel_id=1, source_target_pairs={{0,1},{1,0},{2,3},{3,2},{4,5},{5,4},{6,7},{7,6},{8,9},{9,8},{10,11... | collective-permute-start | bytes 393224 | tf_op jit(solution)/shard_map/ppermute | solution.py:255
  81.9 14.9 %collective-permute-start.25 = (f32[480,128]{1,0:T(8,128)S(1)}, f32[480,128]{1,0:T(8,128)S(1)}, u32[]{:S(2)}, u32[]{:S(2)}) collective-permute-start(f32[480,128]{1,0:T(8,128)S(1)} %shard_map.83.a), channel_id=1, source_target_pairs={{0,1},{1,0},{2,3},{3,2},{4,5},{5,4},{6,7},{7,6},{8,9},{9,8},{10,11... | collective-permute-start | bytes 737288 | tf_op jit(solution)/shard_map/ppermute | solution.py:255
  85.4 11.3 %collective-permute-start.27 = (f32[264,128]{1,0:T(8,128)S(1)}, f32[264,128]{1,0:T(8,128)S(1)}, u32[]{:S(2)}, u32[]{:S(2)}) collective-permute-start(f32[264,128]{1,0:T(8,128)S(1)} %shard_map.84.refs_0_), channel_id=1, source_target_pairs={{0,3},{3,0},{1,2},{2,1},{4,7},{7,4},{5,6},{6,5},{8,11},{11,8},{9,1... | collective-permute-start | bytes 405512 | tf_op jit(solution)/shard_map/ppermute | solution.py:255
  88.0 10.3 %collective-permute-start.30 = (f32[256,128]{1,0:T(8,128)S(1)}, f32[256,128]{1,0:T(8,128)S(1)}, u32[]{:S(2)}, u32[]{:S(2)}) collective-permute-start(f32[256,128]{1,0:T(8,128)S(1)} %shard_map.85.refs_0_), channel_id=1, source_target_pairs={{0,3},{3,0},{1,2},{2,1},{4,7},{7,4},{5,6},{6,5},{8,11},{11,8},{9,1... | collective-permute-start | bytes 393224 | tf_op jit(solution)/shard_map/ppermute | solution.py:255
  (13 other events, 34.8 us)

commit v12 on v10

--- a/solution.py
+++ b/solution.py
@@ -10,9 +10,9 @@
 
 HIGHEST = lax.Precision.HIGHEST
 HIGH = lax.Precision.HIGH
-ROUNDS = (0.36,)
-STEPS = ("P0 F0 P1 G0", "O0 M0 F1 T0", "G1 O1 M1 M2", "T1 D0 T2 D1", "D2")
-LINE_PIECES = (1,2,)
+ROUNDS = (0.32,0.336,)
+STEPS = ("P0 P1 F0 P2", "F1 G0 O0 F2", "G1 M0 O1 G2", "T0 M1 O2 T1", "M2 D0 T2 D1", "D2")
+LINE_PIECES = (1,1,1,)
 BF16, F32 = jnp.bfloat16, jnp.float32
 NT = (((1,), (1,)), ((), ()))
 NN = (((1,), (0,)), ((), ()))
@@ -232,7 +232,7 @@
     return call(functools.partial(send_body, edges, rows), outs, (w0, w1, *far))
 
 
-PARTS = 3
+PARTS = 1
 
 
 def blocks(size, count):

time: 109 us -> 115 us (1.055)
  waiting for transfers between devices: 56.5 us -> 63.8 us
  starting transfers between devices: 37.5 us -> 35.3 us
    ppermute x9, starting transfers between devices: 17.2 us -> 10.7 us  [pass_line(): return lax.ppermute(value, 'col', pairs)]
    ppermute x15 -> x21, starting transfers between devices: 18.3 us -> 23.8 us  [hop(): return lax.ppermute(value, ('chip', 'core'), pairs)]
    ppermute x9, waiting for transfers between devices: 27.1 us -> 32.5 us  [pass_line(): return lax.ppermute(value, 'col', pairs)]
    ppermute x15 -> x21, waiting for transfers between devices: 26.6 us -> 31.3 us  [hop(): return lax.ppermute(value, ('chip', 'core'), pairs)]
    ppermute x8 -> x5, waiting for transfers between devices: 2.78 us -> 0.01 us  [swap(): return lax.ppermute(value, axis, [(i, i ^ flip) for i in range(size)])]
    pallas_call x23 -> x27, Pallas kernels: 10.4 us -> 11.5 us  [call(): pl.pallas_call(body, out_shape=outs, in_specs=[vmem] * len(args), out_spe...]
  transfers between devices with their start and end apart: 32 -> 35, of which waited for: 20 -> 24; matrix products, arithmetic and copies ran while one was open for 1% -> 0% of each run, Pallas kernels for 6% -> 6%
where the time goes in v12:
time: 115 us; the launch traced here: 114 us
  waiting for transfers between devices  63.8 us (55%)
  starting transfers between devices  35.3 us (31%)
  Pallas kernels  11.5 us (10%)
  local copies, waits for them, and re-layouts  1.83 us (2%)
    ppermute x9, waiting for transfers between devices, pass_line(): return lax.ppermute(value, 'col', pairs)  32.5 us
    ppermute x21, waiting for transfers between devices, hop(): return lax.ppermute(value, ('chip', 'core'), pairs)  31.3 us
    ppermute x21, starting transfers between devices, hop(): return lax.ppermute(value, ('chip', 'core'), pairs)  23.8 us
    pallas_call x27, Pallas kernels, call(): pl.pallas_call(body, out_shape=outs, in_specs=[vmem] * len(args), out_spe...  11.5 us
    ppermute x9, starting transfers between devices, pass_line(): return lax.ppermute(value, 'col', pairs)  10.7 us
  transfers between devices with their start and end apart: 35, of which 24 were waited for; matrix products, arithmetic and copies ran while one was open for 0% of the time, Pallas kernels for 6%

profile of v12, /device:TPU:0, one launch (start us, length us, event | category | flops | bytes accessed | tf_op | source)
XLA Modules:
  0.0 114.3 jit_solution(7105006830289192744)
XLA Ops:
  1.1 2.6 %collective-permute-start.1 = (f32[128,1024]{1,0:T(8,128)}, f32[128,1024]{1,0:T(8,128)S(1)}, u32[]{:S(2)}, u32[]{:S(2)}) collective-permute-start(f32[128,1024]{1,0:T(8,128)} %own), channel_id=1, source_target_pairs={{0,8},{4,20},{8,0},{12,28},{16,24},{20,4},{24,16},{28,12},{1,9},{5... | collective-permute-start | bytes 1572872 | tf_op jit(solution)/shard_map/ppermute | solution.py:368
  5.2 10.4 %collective-permute-done.1.x = f32[128,1024]{1,0:T(8,128)S(1)} collective-permute-done((f32[128,1024]{1,0:T(8,128)}, f32[128,1024]{1,0:T(8,128)S(1)}, u32[]{:S(2)}, u32[]{:S(2)}) %collective-permute-start.1) | collective-permute-done | bytes 524320 | tf_op jit(solution)/shard_map/ppermute | solution.py:368
  15.7 2.1 %collective-permute-start.4 = (f32[128,1024]{1,0:T(8,128)S(1)}, f32[128,1024]{1,0:T(8,128)S(1)}, u32[]{:S(2)}, u32[]{:S(2)}) collective-permute-start(f32[128,1024]{1,0:T(8,128)S(1)} %collective-permute-done.1.x), channel_id=1, source_target_pairs={{0,16},{4,12},{8,24},{12,4},{16,0},{20,28},{24,8},{28,20},{1,17},{... | collective-permute-start | bytes 1572872 | tf_op jit(solution)/shard_map/ppermute | solution.py:368
  23.3 1.6 %collective-permute-done.4.block = f32[128,1024]{1,0:T(8,128)S(1)} collective-permute-done((f32[128,1024]{1,0:T(8,128)S(1)}, f32[128,1024]{1,0:T(8,128)S(1)}, u32[]{:S(2)}, u32[]{:S(2)}) %collective-permute-start.4) | collective-permute-done | bytes 524320 | tf_op jit(solution)/shard_map/ppermute | solution.py:368
  24.9 2.2 %shard_map.71 = (bf16[384,512]{1,0:T(8,128)(2,1)S(1)}, bf16[384,512]{1,0:T(8,128)(2,1)S(1)}, f32[160,256]{1,0:T(8,128)S(1)}, f32[160,256]{1,0:T(8,128)S(1)}) custom-call(f32[128,1024]{1,0:T(8,128)S(1)} %collective-permute-done.4.block, bf16[512,1024]{1,0:T(8,128)(2,1)S(1)} %get-tuple-element.167.c_high, bf16[512,1024]{1,0:T(8,128)(2,1)S(1)} %get-tuple-element.168.c_low, ...), custom_call_target="tpu_custom_call" | custom-call | tf_op jit(solution)/shard_map/pallas_call | solution.py:56
  27.1 2.4 %collective-permute-start.5 = (f32[160,256]{1,0:T(8,128)S(1)}, f32[160,256]{1,0:T(8,128)S(1)}, u32[]{:S(2)}, u32[]{:S(2)}) collective-permute-start(f32[160,256]{1,0:T(8,128)S(1)} %get-tuple-element.189), channel_id=1, source_target_pairs={{0,8},{4,20},{8,0},{12,28},{16,24},{20,4},{24,16},{28,12},{1,9},{5... | collective-permute-start | bytes 491528 | tf_op jit(solution)/shard_map/ppermute | solution.py:368
  29.6 2.0 %collective-permute-start.6 = (f32[160,256]{1,0:T(8,128)S(1)}, f32[160,256]{1,0:T(8,128)S(1)}, u32[]{:S(2)}, u32[]{:S(2)}) collective-permute-start(f32[160,256]{1,0:T(8,128)S(1)} %get-tuple-element.190), channel_id=1, source_target_pairs={{0,16},{4,12},{8,24},{12,4},{16,0},{20,28},{24,8},{28,20},{1,17},{... | collective-permute-start | bytes 491528 | tf_op jit(solution)/shard_map/ppermute | solution.py:368
  33.0 1.7 %shard_map.73 = (f32[160,256]{1,0:T(8,128)S(1)}, f32[160,256]{1,0:T(8,128)S(1)}, f32[168,256]{1,0:T(8,128)S(1)}, f32[168,256]{1,0:T(8,128)S(1)}, f32[176,256]{1,0:T(8,128)S(1)}, /*index=5*/f32[168,256]{1,0:T(8,128)S(1)}) custom-call(f32[1000,256]{1,0:T(8,128)S(1)} %bitcast.9, f32[1000,256]{1,0:T(8,128)S(1)} %collective-permute-done.w1, ...), custom_call_target="tpu_custom_call" | custom-call | tf_op jit(solution)/shard_map/pallas_call | solution.py:56
  40.3 1.9 %collective-permute-start.13 = (f32[168,256]{1,0:T(8,128)S(1)}, f32[168,256]{1,0:T(8,128)S(1)}, u32[]{:S(2)}, u32[]{:S(2)}) collective-permute-start(f32[168,256]{1,0:T(8,128)S(1)} %get-tuple-element.221.refs_0_), channel_id=1, source_target_pairs={{0,16},{4,12},{8,24},{12,4},{16,0},{20,28},{24,8},{28,20},{1,17},{... | collective-permute-start | bytes 516104 | tf_op jit(solution)/shard_map/ppermute | solution.py:368
  47.9 2.8 %collective-permute-done.13.refs_2_ = f32[168,256]{1,0:T(8,128)S(1)} collective-permute-done((f32[168,256]{1,0:T(8,128)S(1)}, f32[168,256]{1,0:T(8,128)S(1)}, u32[]{:S(2)}, u32[]{:S(2)}) %collective-permute-start.13) | collective-permute-done | bytes 172064 | tf_op jit(solution)/shard_map/ppermute | solution.py:368
  57.5 3.8 %collective-permute-done.22.refs_3_ = f32[168,256]{1,0:T(8,128)S(1)} collective-permute-done((f32[168,256]{1,0:T(8,128)S(1)}, f32[168,256]{1,0:T(8,128)S(1)}, u32[]{:S(2)}, u32[]{:S(2)}) %collective-permute-start.22) | collective-permute-done | bytes 172064 | tf_op jit(solution)/shard_map/ppermute | solution.py:368
  61.4 2.5 %collective-permute-done.19.other_a = f32[168,256]{1,0:T(8,128)S(1)} collective-permute-done((f32[168,256]{1,0:T(8,128)S(1)}, f32[168,256]{1,0:T(8,128)S(1)}, u32[]{:S(2)}, u32[]{:S(2)}) %collective-permute-start.19) | collective-permute-done | bytes 172064 | tf_op jit(solution)/shard_map/ppermute | solution.py:368
  65.0 1.7 %collective-permute-start.18 = (f32[320,128]{1,0:T(8,128)S(1)}, f32[320,128]{1,0:T(8,128)S(1)}, u32[]{:S(2)}, u32[]{:S(2)}) collective-permute-start(f32[320,128]{1,0:T(8,128)S(1)} %get-tuple-element.239), channel_id=1, source_target_pairs={{0,1},{1,0},{2,3},{3,2},{4,5},{5,4},{6,7},{7,6},{8,9},{9,8},{10,11... | collective-permute-start | bytes 491528 | tf_op jit(solution)/shard_map/ppermute | solution.py:274
  68.8 2.9 %collective-permute-done.18.refs_1_ = f32[320,128]{1,0:T(8,128)S(1)} collective-permute-done((f32[320,128]{1,0:T(8,128)S(1)}, f32[320,128]{1,0:T(8,128)S(1)}, u32[]{:S(2)}, u32[]{:S(2)}) %collective-permute-start.18) | collective-permute-done | bytes 163872 | tf_op jit(solution)/shard_map/ppermute | solution.py:274
  74.3 2.5 %collective-permute-start.23 = (f32[320,128]{1,0:T(8,128)S(1)}, f32[320,128]{1,0:T(8,128)S(1)}, u32[]{:S(2)}, u32[]{:S(2)}) collective-permute-start(f32[320,128]{1,0:T(8,128)S(1)} %shard_map.83.refs_0_), channel_id=1, source_target_pairs={{0,3},{3,0},{1,2},{2,1},{4,7},{7,4},{5,6},{6,5},{8,11},{11,8},{9,1... | collective-permute-start | bytes 491528 | tf_op jit(solution)/shard_map/ppermute | solution.py:274
  77.5 5.7 %collective-permute-done.23.refs_1_ = f32[320,128]{1,0:T(8,128)S(1)} collective-permute-done((f32[320,128]{1,0:T(8,128)S(1)}, f32[320,128]{1,0:T(8,128)S(1)}, u32[]{:S(2)}, u32[]{:S(2)}) %collective-permute-start.23) | collective-permute-done | bytes 163872 | tf_op jit(solution)/shard_map/ppermute | solution.py:274
  83.3 3.2 %collective-permute-done.29.refs_1_ = f32[336,128]{1,0:T(8,128)S(1)} collective-permute-done((f32[336,128]{1,0:T(8,128)S(1)}, f32[336,128]{1,0:T(8,128)S(1)}, u32[]{:S(2)}, u32[]{:S(2)}) %collective-permute-start.29) | collective-permute-done | bytes 172064 | tf_op jit(solution)/shard_map/ppermute | solution.py:274
  86.5 1.7 %collective-permute-start.31 = (f32[336,128]{1,0:T(8,128)S(1)}, f32[336,128]{1,0:T(8,128)S(1)}, u32[]{:S(2)}, u32[]{:S(2)}) collective-permute-start(f32[336,128]{1,0:T(8,128)S(1)} %shard_map.87.refs_0_), channel_id=1, source_target_pairs={{0,3},{3,0},{1,2},{2,1},{4,7},{7,4},{5,6},{6,5},{8,11},{11,8},{9,1... | collective-permute-start | bytes 516104 | tf_op jit(solution)/shard_map/ppermute | solution.py:274
  88.4 2.0 %collective-permute-start.27 = (f32[320,128]{1,0:T(8,128)S(1)}, f32[320,128]{1,0:T(8,128)S(1)}, u32[]{:S(2)}, u32[]{:S(2)}) collective-permute-start(f32[320,128]{1,0:T(8,128)S(1)} %shard_map.86.a), channel_id=1, source_target_pairs={{0,1},{1,0},{2,3},{3,2},{4,5},{5,4},{6,7},{7,6},{8,9},{9,8},{10,11... | collective-permute-start | bytes 491528 | tf_op jit(solution)/shard_map/ppermute | solution.py:274
  90.4 5.3 %collective-permute-done.31.refs_1_ = f32[336,128]{1,0:T(8,128)S(1)} collective-permute-done((f32[336,128]{1,0:T(8,128)S(1)}, f32[336,128]{1,0:T(8,128)S(1)}, u32[]{:S(2)}, u32[]{:S(2)}) %collective-permute-start.31) | collective-permute-done | bytes 172064 | tf_op jit(solution)/shard_map/ppermute | solution.py:274
  95.7 3.0 %collective-permute-done.30.refs_1_ = f32[344,128]{1,0:T(8,128)S(1)} collective-permute-done((f32[344,128]{1,0:T(8,128)S(1)}, f32[344,128]{1,0:T(8,128)S(1)}, u32[]{:S(2)}, u32[]{:S(2)}) %collective-permute-start.30) | collective-permute-done | bytes 176160 | tf_op jit(solution)/shard_map/ppermute | solution.py:274
  101.0 6.7 %collective-permute-done.33.refs_1_ = f32[344,128]{1,0:T(8,128)S(1)} collective-permute-done((f32[344,128]{1,0:T(8,128)S(1)}, f32[344,128]{1,0:T(8,128)S(1)}, u32[]{:S(2)}, u32[]{:S(2)}) %collective-permute-start.33) | collective-permute-done | bytes 176160 | tf_op jit(solution)/shard_map/ppermute | solution.py:274
  107.9 1.8 %collective-permute-done.32.b = f32[336,128]{1,0:T(8,128)S(1)} collective-permute-done((f32[336,128]{1,0:T(8,128)S(1)}, f32[336,128]{1,0:T(8,128)S(1)}, u32[]{:S(2)}, u32[]{:S(2)}) %collective-permute-start.32) | collective-permute-done | bytes 172064 | tf_op jit(solution)/shard_map/ppermute | solution.py:274
  109.7 3.6 %collective-permute-done.34.b = f32[344,128]{1,0:T(8,128)S(1)} collective-permute-done((f32[344,128]{1,0:T(8,128)S(1)}, f32[344,128]{1,0:T(8,128)S(1)}, u32[]{:S(2)}, u32[]{:S(2)}) %collective-permute-start.34) | collective-permute-done | bytes 176160 | tf_op jit(solution)/shard_map/ppermute | solution.py:274
  (92 shorter events, 37.2 us)
Async XLA Ops:
  0.6 17.2 %collective-permute-start.3 = (f32[256,1024]{1,0:T(8,128)}, f32[256,1024]{1,0:T(8,128)S(1)}, u32[]{:S(2)}, u32[]{:S(2)}) collective-permute-start(f32[256,1024]{1,0:T(8,128)} %mine_ref.1), channel_id=1, source_target_pairs={{0,4},{4,0},{1,5},{5,1},{2,6},{6,2},{3,7},{7,3},{8,12},{12,8},{9,1... | collective-permute-start | bytes 3145736 | tf_op jit(solution)/shard_map/ppermute | solution.py:23
  1.1 14.5 %collective-permute-start.1 = (f32[128,1024]{1,0:T(8,128)}, f32[128,1024]{1,0:T(8,128)S(1)}, u32[]{:S(2)}, u32[]{:S(2)}) collective-permute-start(f32[128,1024]{1,0:T(8,128)} %own), channel_id=1, source_target_pairs={{0,8},{4,20},{8,0},{12,28},{16,24},{20,4},{24,16},{28,12},{1,9},{5... | collective-permute-start | bytes 1572872 | tf_op jit(solution)/shard_map/ppermute | solution.py:368
  3.7 19.6 %collective-permute-start = (f32[1000,256]{1,0:T(8,128)}, f32[1000,256]{1,0:T(8,128)S(1)}, u32[]{:S(2)}, u32[]{:S(2)}) collective-permute-start(f32[1000,256]{1,0:T(8,128)} %bitcast.6), channel_id=1, source_target_pairs={{0,4},{4,0},{1,5},{5,1},{2,6},{6,2},{3,7},{7,3},{8,12},{12,8},{9,1... | collective-permute-start | bytes 3072008 | tf_op jit(solution)/shard_map/ppermute | solution.py:23
  3.9 17.8 %collective-permute-start.2 = (f32[128,1024]{1,0:T(8,128)}, f32[128,1024]{1,0:T(8,128)S(1)}, u32[]{:S(2)}, u32[]{:S(2)}) collective-permute-start(f32[128,1024]{1,0:T(8,128)} %own), channel_id=1, source_target_pairs={{0,16},{4,12},{8,24},{12,4},{16,0},{20,28},{24,8},{28,20},{1,17},{... | collective-permute-start | bytes 1572872 | tf_op jit(solution)/shard_map/ppermute | solution.py:368
  15.7 9.3 %collective-permute-start.4 = (f32[128,1024]{1,0:T(8,128)S(1)}, f32[128,1024]{1,0:T(8,128)S(1)}, u32[]{:S(2)}, u32[]{:S(2)}) collective-permute-start(f32[128,1024]{1,0:T(8,128)S(1)} %collective-permute-done.1.x), channel_id=1, source_target_pairs={{0,16},{4,12},{8,24},{12,4},{16,0},{20,28},{24,8},{28,20},{1,17},{... | collective-permute-start | bytes 1572872 | tf_op jit(solution)/shard_map/ppermute | solution.py:368
  27.1 7.6 %collective-permute-start.5 = (f32[160,256]{1,0:T(8,128)S(1)}, f32[160,256]{1,0:T(8,128)S(1)}, u32[]{:S(2)}, u32[]{:S(2)}) collective-permute-start(f32[160,256]{1,0:T(8,128)S(1)} %get-tuple-element.189), channel_id=1, source_target_pairs={{0,8},{4,20},{8,0},{12,28},{16,24},{20,4},{24,16},{28,12},{1,9},{5... | collective-permute-start | bytes 491528 | tf_op jit(solution)/shard_map/ppermute | solution.py:368
  32.8 7.3 %collective-permute-start.10 = (f32[168,256]{1,0:T(8,128)S(1)}, f32[168,256]{1,0:T(8,128)S(1)}, u32[]{:S(2)}, u32[]{:S(2)}) collective-permute-start(f32[168,256]{1,0:T(8,128)S(1)} %get-tuple-element.199), channel_id=1, source_target_pairs={{0,16},{4,12},{8,24},{12,4},{16,0},{20,28},{24,8},{28,20},{1,17},{... | collective-permute-start | bytes 516104 | tf_op jit(solution)/shard_map/ppermute | solution.py:368
  32.8 7.5 %collective-permute-start.9 = (f32[168,256]{1,0:T(8,128)S(1)}, f32[168,256]{1,0:T(8,128)S(1)}, u32[]{:S(2)}, u32[]{:S(2)}) collective-permute-start(f32[168,256]{1,0:T(8,128)S(1)} %get-tuple-element.180), channel_id=1, source_target_pairs={{0,8},{4,20},{8,0},{12,28},{16,24},{20,4},{24,16},{28,12},{1,9},{5... | collective-permute-start | bytes 516104 | tf_op jit(solution)/shard_map/ppermute | solution.py:368
  36.1 7.4 %collective-permute-start.7 = (f32[160,256]{1,0:T(8,128)S(1)}, f32[160,256]{1,0:T(8,128)S(1)}, u32[]{:S(2)}, u32[]{:S(2)}) collective-permute-start(f32[160,256]{1,0:T(8,128)S(1)} %get-tuple-element.205.refs_0_), channel_id=1, source_target_pairs={{0,16},{4,12},{8,24},{12,4},{16,0},{20,28},{24,8},{28,20},{1,17},{... | collective-permute-start | bytes 491528 | tf_op jit(solution)/shard_map/ppermute | solution.py:368
  37.0 10.3 %collective-permute-start.16 = (f32[168,256]{1,0:T(8,128)S(1)}, f32[168,256]{1,0:T(8,128)S(1)}, u32[]{:S(2)}, u32[]{:S(2)}) collective-permute-start(f32[168,256]{1,0:T(8,128)S(1)} %get-tuple-element.215), channel_id=1, source_target_pairs={{0,16},{4,12},{8,24},{12,4},{16,0},{20,28},{24,8},{28,20},{1,17},{... | collective-permute-start | bytes 516104 | tf_op jit(solution)/shard_map/ppermute | solution.py:368
  40.1 7.8 %collective-permute-start.15 = (f32[176,256]{1,0:T(8,128)S(1)}, f32[176,256]{1,0:T(8,128)S(1)}, u32[]{:S(2)}, u32[]{:S(2)}) collective-permute-start(f32[176,256]{1,0:T(8,128)S(1)} %get-tuple-element.214), channel_id=1, source_target_pairs={{0,8},{4,20},{8,0},{12,28},{16,24},{20,4},{24,16},{28,12},{1,9},{5... | collective-permute-start | bytes 540680 | tf_op jit(solution)/shard_map/ppermute | solution.py:368
  40.3 10.3 %collective-permute-start.13 = (f32[168,256]{1,0:T(8,128)S(1)}, f32[168,256]{1,0:T(8,128)S(1)}, u32[]{:S(2)}, u32[]{:S(2)}) collective-permute-start(f32[168,256]{1,0:T(8,128)S(1)} %get-tuple-element.221.refs_0_), channel_id=1, source_target_pairs={{0,16},{4,12},{8,24},{12,4},{16,0},{20,28},{24,8},{28,20},{1,17},{... | collective-permute-start | bytes 516104 | tf_op jit(solution)/shard_map/ppermute | solution.py:368
  53.4 8.0 %collective-permute-start.21 = (f32[176,256]{1,0:T(8,128)S(1)}, f32[176,256]{1,0:T(8,128)S(1)}, u32[]{:S(2)}, u32[]{:S(2)}) collective-permute-start(f32[176,256]{1,0:T(8,128)S(1)} %get-tuple-element.242.refs_0_), channel_id=1, source_target_pairs={{0,16},{4,12},{8,24},{12,4},{16,0},{20,28},{24,8},{28,20},{1,17},{... | collective-permute-start | bytes 540680 | tf_op jit(solution)/shard_map/ppermute | solution.py:368
  54.1 7.3 %collective-permute-start.22 = (f32[168,256]{1,0:T(8,128)S(1)}, f32[168,256]{1,0:T(8,128)S(1)}, u32[]{:S(2)}, u32[]{:S(2)}) collective-permute-start(f32[168,256]{1,0:T(8,128)S(1)} %get-tuple-element.243.refs_1_), channel_id=1, source_target_pairs={{0,8},{4,20},{8,0},{12,28},{16,24},{20,4},{24,16},{28,12},{1,9},{5... | collective-permute-start | bytes 516104 | tf_op jit(solution)/shard_map/ppermute | solution.py:368
  55.7 8.2 %collective-permute-start.19 = (f32[168,256]{1,0:T(8,128)S(1)}, f32[168,256]{1,0:T(8,128)S(1)}, u32[]{:S(2)}, u32[]{:S(2)}) collective-permute-start(f32[168,256]{1,0:T(8,128)S(1)} %get-tuple-element.247.full_a), channel_id=1, source_target_pairs={{0,8},{4,20},{8,0},{12,28},{16,24},{20,4},{24,16},{28,12},{1,9},{5... | collective-permute-start | bytes 516104 | tf_op jit(solution)/shard_map/ppermute | solution.py:368
  56.1 8.1 %collective-permute-start.20 = (f32[168,256]{1,0:T(8,128)S(1)}, f32[168,256]{1,0:T(8,128)S(1)}, u32[]{:S(2)}, u32[]{:S(2)}) collective-permute-start(f32[168,256]{1,0:T(8,128)S(1)} %get-tuple-element.248.full_b), channel_id=1, source_target_pairs={{0,16},{4,12},{8,24},{12,4},{16,0},{20,28},{24,8},{28,20},{1,17},{... | collective-permute-start | bytes 516104 | tf_op jit(solution)/shard_map/ppermute | solution.py:368
  74.2 14.0 %collective-permute-start.28 = (f32[344,256]{1,0:T(8,128)S(1)}, f32[344,256]{1,0:T(8,128)S(1)}, u32[]{:S(2)}, u32[]{:S(2)}) collective-permute-start(f32[344,256]{1,0:T(8,128)S(1)} %get-tuple-element.271), channel_id=1, source_target_pairs={{0,4},{4,0},{1,5},{5,1},{2,6},{6,2},{3,7},{7,3},{8,12},{12,8},{9,1... | collective-permute-start | bytes 1056776 | tf_op jit(solution)/shard_map/ppermute | solution.py:23
  74.3 8.9 %collective-permute-start.23 = (f32[320,128]{1,0:T(8,128)S(1)}, f32[320,128]{1,0:T(8,128)S(1)}, u32[]{:S(2)}, u32[]{:S(2)}) collective-permute-start(f32[320,128]{1,0:T(8,128)S(1)} %shard_map.83.refs_0_), channel_id=1, source_target_pairs={{0,3},{3,0},{1,2},{2,1},{4,7},{7,4},{5,6},{6,5},{8,11},{11,8},{9,1... | collective-permute-start | bytes 491528 | tf_op jit(solution)/shard_map/ppermute | solution.py:274
  76.9 9.6 %collective-permute-start.29 = (f32[336,128]{1,0:T(8,128)S(1)}, f32[336,128]{1,0:T(8,128)S(1)}, u32[]{:S(2)}, u32[]{:S(2)}) collective-permute-start(f32[336,128]{1,0:T(8,128)S(1)} %get-tuple-element.262), channel_id=1, source_target_pairs={{0,1},{1,0},{2,3},{3,2},{4,5},{5,4},{6,7},{7,6},{8,9},{9,8},{10,11... | collective-permute-start | bytes 516104 | tf_op jit(solution)/shard_map/ppermute | solution.py:274
  86.5 9.1 %collective-permute-start.31 = (f32[336,128]{1,0:T(8,128)S(1)}, f32[336,128]{1,0:T(8,128)S(1)}, u32[]{:S(2)}, u32[]{:S(2)}) collective-permute-start(f32[336,128]{1,0:T(8,128)S(1)} %shard_map.87.refs_0_), channel_id=1, source_target_pairs={{0,3},{3,0},{1,2},{2,1},{4,7},{7,4},{5,6},{6,5},{8,11},{11,8},{9,1... | collective-permute-start | bytes 516104 | tf_op jit(solution)/shard_map/ppermute | solution.py:274
  88.3 10.4 %collective-permute-start.30 = (f32[344,128]{1,0:T(8,128)S(1)}, f32[344,128]{1,0:T(8,128)S(1)}, u32[]{:S(2)}, u32[]{:S(2)}) collective-permute-start(f32[344,128]{1,0:T(8,128)S(1)} %get-tuple-element.281), channel_id=1, source_target_pairs={{0,1},{1,0},{2,3},{3,2},{4,5},{5,4},{6,7},{7,6},{8,9},{9,8},{10,11... | collective-permute-start | bytes 528392 | tf_op jit(solution)/shard_map/ppermute | solution.py:274
  88.4 12.6 %collective-permute-start.27 = (f32[320,128]{1,0:T(8,128)S(1)}, f32[320,128]{1,0:T(8,128)S(1)}, u32[]{:S(2)}, u32[]{:S(2)}) collective-permute-start(f32[320,128]{1,0:T(8,128)S(1)} %shard_map.86.a), channel_id=1, source_target_pairs={{0,1},{1,0},{2,3},{3,2},{4,5},{5,4},{6,7},{7,6},{8,9},{9,8},{10,11... | collective-permute-start | bytes 491528 | tf_op jit(solution)/shard_map/ppermute | solution.py:274
  98.7 9.0 %collective-permute-start.33 = (f32[344,128]{1,0:T(8,128)S(1)}, f32[344,128]{1,0:T(8,128)S(1)}, u32[]{:S(2)}, u32[]{:S(2)}) collective-permute-start(f32[344,128]{1,0:T(8,128)S(1)} %shard_map.90.refs_0_), channel_id=1, source_target_pairs={{0,3},{3,0},{1,2},{2,1},{4,7},{7,4},{5,6},{6,5},{8,11},{11,8},{9,1... | collective-permute-start | bytes 528392 | tf_op jit(solution)/shard_map/ppermute | solution.py:274
  99.7 9.9 %collective-permute-start.32 = (f32[336,128]{1,0:T(8,128)S(1)}, f32[336,128]{1,0:T(8,128)S(1)}, u32[]{:S(2)}, u32[]{:S(2)}) collective-permute-start(f32[336,128]{1,0:T(8,128)S(1)} %shard_map.89.a), channel_id=1, source_target_pairs={{0,1},{1,0},{2,3},{3,2},{4,5},{5,4},{6,7},{7,6},{8,9},{9,8},{10,11... | collective-permute-start | bytes 516104 | tf_op jit(solution)/shard_map/ppermute | solution.py:274
  (17 other events, 81.4 us)

commit v13 on v10

--- a/solution.py
+++ b/solution.py
@@ -10,9 +10,9 @@
 
 HIGHEST = lax.Precision.HIGHEST
 HIGH = lax.Precision.HIGH
-ROUNDS = (0.36,)
-STEPS = ("P0 F0 P1 G0", "O0 M0 F1 T0", "G1 O1 M1 M2", "T1 D0 T2 D1", "D2")
-LINE_PIECES = (1,2,)
+ROUNDS = (0.48,)
+STEPS = ("P0 P1 F0 F1", "G0 O0 G1 O1", "M0 M1 T0 D0", "T1 D1")
+LINE_PIECES = (1,1,)
 BF16, F32 = jnp.bfloat16, jnp.float32
 NT = (((1,), (1,)), ((), ()))
 NN = (((1,), (0,)), ((), ()))

time: 109 us -> 103 us (0.945)
  waiting for transfers between devices: 56.5 us -> 40.8 us
  starting transfers between devices: 37.5 us -> 47.2 us
    ppermute x9 -> x6, waiting for transfers between devices: 27.1 us -> 15.4 us  [pass_line(): return lax.ppermute(value, 'col', pairs)]
    ppermute x15, starting transfers between devices: 18.3 us -> 24.8 us  [hop(): return lax.ppermute(value, ('chip', 'core'), pairs)]
    ppermute x15, waiting for transfers between devices: 26.6 us -> 22.8 us  [hop(): return lax.ppermute(value, ('chip', 'core'), pairs)]
    ppermute x9 -> x6, starting transfers between devices: 17.2 us -> 20.5 us  [pass_line(): return lax.ppermute(value, 'col', pairs)]
    pallas_call x23 -> x20, Pallas kernels: 10.4 us -> 10.1 us  [call(): pl.pallas_call(body, out_shape=outs, in_specs=[vmem] * len(args), out_spe...]
  transfers between devices with their start and end apart: 32 -> 29, of which waited for: 20 -> 16; matrix products, arithmetic and copies ran while one was open for 1% -> 1% of each run, Pallas kernels for 6% -> 8%
where the time goes in v13:
time: 103 us
  starting transfers between devices  47.2 us (46%)
  waiting for transfers between devices  40.8 us (40%)
  Pallas kernels  10.1 us (10%)
  local copies, waits for them, and re-layouts  2.19 us (2%)
  other arithmetic  1.85 us (2%)
    ppermute x15, starting transfers between devices, hop(): return lax.ppermute(value, ('chip', 'core'), pairs)  24.8 us
    ppermute x15, waiting for transfers between devices, hop(): return lax.ppermute(value, ('chip', 'core'), pairs)  22.8 us
    ppermute x6, starting transfers between devices, pass_line(): return lax.ppermute(value, 'col', pairs)  20.5 us
    ppermute x6, waiting for transfers between devices, pass_line(): return lax.ppermute(value, 'col', pairs)  15.4 us
    pallas_call x20, Pallas kernels, call(): pl.pallas_call(body, out_shape=outs, in_specs=[vmem] * len(args), out_spe...  10.1 us
    ppermute x8, waiting for transfers between devices, swap(): return lax.ppermute(value, axis, [(i, i ^ flip) for i in range(size)])  2.66 us
    unnamed x10, local copies, waits for them, and re-layouts  2.15 us
  transfers between devices with their start and end apart: 29, of which 16 were waited for; matrix products, arithmetic and copies ran while one was open for 1% of the time, Pallas kernels for 8%

profile of v13, /device:TPU:0, one launch (start us, length us, event | category | flops | bytes accessed | tf_op | source)
XLA Modules:
  0.0 103.0 jit_solution(6632505786474005479)
XLA Ops:
  1.1 2.6 %collective-permute-start.1 = (f32[128,1024]{1,0:T(8,128)}, f32[128,1024]{1,0:T(8,128)S(1)}, u32[]{:S(2)}, u32[]{:S(2)}) collective-permute-start(f32[128,1024]{1,0:T(8,128)} %own), channel_id=1, source_target_pairs={{0,8},{4,20},{8,0},{12,28},{16,24},{20,4},{24,16},{28,12},{1,9},{5... | collective-permute-start | bytes 1572872 | tf_op jit(solution)/shard_map/ppermute | solution.py:368
  5.2 10.4 %collective-permute-done.1.x = f32[128,1024]{1,0:T(8,128)S(1)} collective-permute-done((f32[128,1024]{1,0:T(8,128)}, f32[128,1024]{1,0:T(8,128)S(1)}, u32[]{:S(2)}, u32[]{:S(2)}) %collective-permute-start.1) | collective-permute-done | bytes 524320 | tf_op jit(solution)/shard_map/ppermute | solution.py:368
  15.7 2.1 %collective-permute-start.4 = (f32[128,1024]{1,0:T(8,128)S(1)}, f32[128,1024]{1,0:T(8,128)S(1)}, u32[]{:S(2)}, u32[]{:S(2)}) collective-permute-start(f32[128,1024]{1,0:T(8,128)S(1)} %collective-permute-done.1.x), channel_id=1, source_target_pairs={{0,16},{4,12},{8,24},{12,4},{16,0},{20,28},{24,8},{28,20},{1,17},{... | collective-permute-start | bytes 1572872 | tf_op jit(solution)/shard_map/ppermute | solution.py:368
  20.1 1.6 %shard_map.69 = (bf16[128,512]{1,0:T(8,128)(2,1)S(1)}, bf16[128,512]{1,0:T(8,128)(2,1)S(1)}) custom-call(f32[128,1024]{1,0:T(8,128)S(1)} %copy-done.2, bf16[512,1024]{1,0:T(8,128)(2,1)S(1)} %get-tuple-element.139.c_high, bf16[512,1024]{1,0:T(8,128)(2,1)S(1)} %get-tuple-element.140.c_low, f32[8,512]{1,0:T(8,128)S(1)} %get-tuple-element.141.c_sq), custom_call_target="tpu_custom_call" | custom-call | tf_op jit(solution)/shard_map/pallas_call | solution.py:56
  21.7 1.6 %shard_map.70 = (bf16[384,512]{1,0:T(8,128)(2,1)S(1)}, bf16[384,512]{1,0:T(8,128)(2,1)S(1)}) custom-call(f32[128,1024]{1,0:T(8,128)S(1)} %collective-permute-done.1.x, f32[128,1024]{1,0:T(8,128)S(1)} %collective-permute-done.2.y, bf16[512,1024]{1,0:T(8,128)(2,1)S(1)} %get-tuple-element.139.c_high, bf16[512,1024]{1,0:T(8,128)(2,1)S(1)} %get-tuple-element.140.c_low, ...), custom_call_target="tpu_custom_call" | custom-call | tf_op jit(solution)/shard_map/pallas_call | solution.py:56
  23.3 1.6 %collective-permute-done.4.block = f32[128,1024]{1,0:T(8,128)S(1)} collective-permute-done((f32[128,1024]{1,0:T(8,128)S(1)}, f32[128,1024]{1,0:T(8,128)S(1)}, u32[]{:S(2)}, u32[]{:S(2)}) %collective-permute-start.4) | collective-permute-done | bytes 524320 | tf_op jit(solution)/shard_map/ppermute | solution.py:368
  24.9 2.2 %shard_map.71 = (bf16[384,512]{1,0:T(8,128)(2,1)S(1)}, bf16[384,512]{1,0:T(8,128)(2,1)S(1)}, f32[240,256]{1,0:T(8,128)S(1)}, f32[240,256]{1,0:T(8,128)S(1)}) custom-call(f32[128,1024]{1,0:T(8,128)S(1)} %collective-permute-done.4.block, bf16[512,1024]{1,0:T(8,128)(2,1)S(1)} %get-tuple-element.139.c_high, bf16[512,1024]{1,0:T(8,128)(2,1)S(1)} %get-tuple-element.140.c_low, ...), custom_call_target="tpu_custom_call" | custom-call | tf_op jit(solution)/shard_map/pallas_call | solution.py:56
  27.2 2.4 %collective-permute-start.5 = (f32[240,256]{1,0:T(8,128)S(1)}, f32[240,256]{1,0:T(8,128)S(1)}, u32[]{:S(2)}, u32[]{:S(2)}) collective-permute-start(f32[240,256]{1,0:T(8,128)S(1)} %get-tuple-element.161), channel_id=1, source_target_pairs={{0,8},{4,20},{8,0},{12,28},{16,24},{20,4},{24,16},{28,12},{1,9},{5... | collective-permute-start | bytes 737288 | tf_op jit(solution)/shard_map/ppermute | solution.py:368
  29.6 2.0 %collective-permute-start.6 = (f32[240,256]{1,0:T(8,128)S(1)}, f32[240,256]{1,0:T(8,128)S(1)}, u32[]{:S(2)}, u32[]{:S(2)}) collective-permute-start(f32[240,256]{1,0:T(8,128)S(1)} %get-tuple-element.162), channel_id=1, source_target_pairs={{0,16},{4,12},{8,24},{12,4},{16,0},{20,28},{24,8},{28,20},{1,17},{... | collective-permute-start | bytes 737288 | tf_op jit(solution)/shard_map/ppermute | solution.py:368
  33.9 2.6 %collective-permute-done.5.refs_2_ = f32[240,256]{1,0:T(8,128)S(1)} collective-permute-done((f32[240,256]{1,0:T(8,128)S(1)}, f32[240,256]{1,0:T(8,128)S(1)}, u32[]{:S(2)}, u32[]{:S(2)}) %collective-permute-start.5) | collective-permute-done | bytes 245792 | tf_op jit(solution)/shard_map/ppermute | solution.py:368
  38.6 2.1 %collective-permute-start.8 = (f32[240,256]{1,0:T(8,128)S(1)}, f32[240,256]{1,0:T(8,128)S(1)}, u32[]{:S(2)}, u32[]{:S(2)}) collective-permute-start(f32[240,256]{1,0:T(8,128)S(1)} %get-tuple-element.178.refs_1_), channel_id=1, source_target_pairs={{0,8},{4,20},{8,0},{12,28},{16,24},{20,4},{24,16},{28,12},{1,9},{5... | collective-permute-start | bytes 737288 | tf_op jit(solution)/shard_map/ppermute | solution.py:368
  40.7 2.1 %collective-permute-done.10.refs_3_ = f32[256,256]{1,0:T(8,128)S(1)} collective-permute-done((f32[256,256]{1,0:T(8,128)S(1)}, f32[256,256]{1,0:T(8,128)S(1)}, u32[]{:S(2)}, u32[]{:S(2)}) %collective-permute-start.10) | collective-permute-done | bytes 262176 | tf_op jit(solution)/shard_map/ppermute | solution.py:368
  43.9 2.5 %collective-permute-start.14 = (f32[256,256]{1,0:T(8,128)S(1)}, f32[256,256]{1,0:T(8,128)S(1)}, u32[]{:S(2)}, u32[]{:S(2)}) collective-permute-start(f32[256,256]{1,0:T(8,128)S(1)} %get-tuple-element.185.refs_1_), channel_id=1, source_target_pairs={{0,8},{4,20},{8,0},{12,28},{16,24},{20,4},{24,16},{28,12},{1,9},{5... | collective-permute-start | bytes 786440 | tf_op jit(solution)/shard_map/ppermute | solution.py:368
  47.8 1.8 %collective-permute-start.11 = (f32[240,256]{1,0:T(8,128)S(1)}, f32[240,256]{1,0:T(8,128)S(1)}, u32[]{:S(2)}, u32[]{:S(2)}) collective-permute-start(f32[240,256]{1,0:T(8,128)S(1)} %get-tuple-element.189.full_a), channel_id=1, source_target_pairs={{0,8},{4,20},{8,0},{12,28},{16,24},{20,4},{24,16},{28,12},{1,9},{5... | collective-permute-start | bytes 737288 | tf_op jit(solution)/shard_map/ppermute | solution.py:368
  49.7 1.9 %collective-permute-start.12 = (f32[240,256]{1,0:T(8,128)S(1)}, f32[240,256]{1,0:T(8,128)S(1)}, u32[]{:S(2)}, u32[]{:S(2)}) collective-permute-start(f32[240,256]{1,0:T(8,128)S(1)} %get-tuple-element.190.full_b), channel_id=1, source_target_pairs={{0,16},{4,12},{8,24},{12,4},{16,0},{20,28},{24,8},{28,20},{1,17},{... | collective-permute-start | bytes 737288 | tf_op jit(solution)/shard_map/ppermute | solution.py:368
  51.6 2.1 %collective-permute-done.14.refs_3_ = f32[256,256]{1,0:T(8,128)S(1)} collective-permute-done((f32[256,256]{1,0:T(8,128)S(1)}, f32[256,256]{1,0:T(8,128)S(1)}, u32[]{:S(2)}, u32[]{:S(2)}) %collective-permute-start.14) | collective-permute-done | bytes 262176 | tf_op jit(solution)/shard_map/ppermute | solution.py:368
  53.7 2.1 %collective-permute-start.19 = (f32[264,256]{1,0:T(8,128)S(1)}, f32[264,256]{1,0:T(8,128)S(1)}, u32[]{:S(2)}, u32[]{:S(2)}) collective-permute-start(f32[264,256]{1,0:T(8,128)S(1)} %get-tuple-element.208.full_a), channel_id=1, source_target_pairs={{0,8},{4,20},{8,0},{12,28},{16,24},{20,4},{24,16},{28,12},{1,9},{5... | collective-permute-start | bytes 811016 | tf_op jit(solution)/shard_map/ppermute | solution.py:368
  61.9 1.6 %collective-permute-start.18 = (f32[480,128]{1,0:T(8,128)S(1)}, f32[480,128]{1,0:T(8,128)S(1)}, u32[]{:S(2)}, u32[]{:S(2)}) collective-permute-start(f32[480,128]{1,0:T(8,128)S(1)} %get-tuple-element.206), channel_id=1, source_target_pairs={{0,1},{1,0},{2,3},{3,2},{4,5},{5,4},{6,7},{7,6},{8,9},{9,8},{10,11... | collective-permute-start | bytes 737288 | tf_op jit(solution)/shard_map/ppermute | solution.py:274
  67.4 3.1 %collective-permute-done.18.refs_1_ = f32[480,128]{1,0:T(8,128)S(1)} collective-permute-done((f32[480,128]{1,0:T(8,128)S(1)}, f32[480,128]{1,0:T(8,128)S(1)}, u32[]{:S(2)}, u32[]{:S(2)}) %collective-permute-start.18) | collective-permute-done | bytes 245792 | tf_op jit(solution)/shard_map/ppermute | solution.py:274
  70.5 3.9 %collective-permute-start.24 = (f32[480,128]{1,0:T(8,128)S(1)}, f32[480,128]{1,0:T(8,128)S(1)}, u32[]{:S(2)}, u32[]{:S(2)}) collective-permute-start(f32[480,128]{1,0:T(8,128)S(1)} %shard_map.82.refs_0_), channel_id=1, source_target_pairs={{0,3},{3,0},{1,2},{2,1},{4,7},{7,4},{5,6},{6,5},{8,11},{11,8},{9,1... | collective-permute-start | bytes 737288 | tf_op jit(solution)/shard_map/ppermute | solution.py:274
  75.8 11.8 %collective-permute-start.27 = (f32[520,128]{1,0:T(8,128)S(1)}, f32[520,128]{1,0:T(8,128)S(1)}, u32[]{:S(2)}, u32[]{:S(2)}) collective-permute-start(f32[520,128]{1,0:T(8,128)S(1)} %shard_map.83.refs_0_), channel_id=1, source_target_pairs={{0,3},{3,0},{1,2},{2,1},{4,7},{7,4},{5,6},{6,5},{8,11},{11,8},{9,1... | collective-permute-start | bytes 798728 | tf_op jit(solution)/shard_map/ppermute | solution.py:274
  87.9 6.8 %collective-permute-done.26.b = f32[480,128]{1,0:T(8,128)S(1)} collective-permute-done((f32[480,128]{1,0:T(8,128)S(1)}, f32[480,128]{1,0:T(8,128)S(1)}, u32[]{:S(2)}, u32[]{:S(2)}) %collective-permute-start.26) | collective-permute-done | bytes 245792 | tf_op jit(solution)/shard_map/ppermute | solution.py:274
  94.8 2.0 %collective-permute-start.28 = (f32[520,128]{1,0:T(8,128)S(1)}, f32[520,128]{1,0:T(8,128)S(1)}, u32[]{:S(2)}, u32[]{:S(2)}) collective-permute-start(f32[520,128]{1,0:T(8,128)S(1)} %shard_map.86.a), channel_id=1, source_target_pairs={{0,1},{1,0},{2,3},{3,2},{4,5},{5,4},{6,7},{7,6},{8,9},{9,8},{10,11... | collective-permute-start | bytes 798728 | tf_op jit(solution)/shard_map/ppermute | solution.py:274
  97.7 4.2 %collective-permute-done.28.b = f32[520,128]{1,0:T(8,128)S(1)} collective-permute-done((f32[520,128]{1,0:T(8,128)S(1)}, f32[520,128]{1,0:T(8,128)S(1)}, u32[]{:S(2)}, u32[]{:S(2)}) %collective-permute-start.28) | collective-permute-done | bytes 266272 | tf_op jit(solution)/shard_map/ppermute | solution.py:274
  (70 shorter events, 24.8 us)
Async XLA Ops:
  0.6 17.2 %collective-permute-start.3 = (f32[256,1024]{1,0:T(8,128)}, f32[256,1024]{1,0:T(8,128)S(1)}, u32[]{:S(2)}, u32[]{:S(2)}) collective-permute-start(f32[256,1024]{1,0:T(8,128)} %mine_ref.1), channel_id=1, source_target_pairs={{0,4},{4,0},{1,5},{5,1},{2,6},{6,2},{3,7},{7,3},{8,12},{12,8},{9,1... | collective-permute-start | bytes 3145736 | tf_op jit(solution)/shard_map/ppermute | solution.py:23
  1.1 14.5 %collective-permute-start.1 = (f32[128,1024]{1,0:T(8,128)}, f32[128,1024]{1,0:T(8,128)S(1)}, u32[]{:S(2)}, u32[]{:S(2)}) collective-permute-start(f32[128,1024]{1,0:T(8,128)} %own), channel_id=1, source_target_pairs={{0,8},{4,20},{8,0},{12,28},{16,24},{20,4},{24,16},{28,12},{1,9},{5... | collective-permute-start | bytes 1572872 | tf_op jit(solution)/shard_map/ppermute | solution.py:368
  3.7 19.6 %collective-permute-start = (f32[1000,256]{1,0:T(8,128)}, f32[1000,256]{1,0:T(8,128)S(1)}, u32[]{:S(2)}, u32[]{:S(2)}) collective-permute-start(f32[1000,256]{1,0:T(8,128)} %bitcast.7), channel_id=1, source_target_pairs={{0,4},{4,0},{1,5},{5,1},{2,6},{6,2},{3,7},{7,3},{8,12},{12,8},{9,1... | collective-permute-start | bytes 3072008 | tf_op jit(solution)/shard_map/ppermute | solution.py:23
  3.9 17.8 %collective-permute-start.2 = (f32[128,1024]{1,0:T(8,128)}, f32[128,1024]{1,0:T(8,128)S(1)}, u32[]{:S(2)}, u32[]{:S(2)}) collective-permute-start(f32[128,1024]{1,0:T(8,128)} %own), channel_id=1, source_target_pairs={{0,16},{4,12},{8,24},{12,4},{16,0},{20,28},{24,8},{28,20},{1,17},{... | collective-permute-start | bytes 1572872 | tf_op jit(solution)/shard_map/ppermute | solution.py:368
  15.7 9.3 %collective-permute-start.4 = (f32[128,1024]{1,0:T(8,128)S(1)}, f32[128,1024]{1,0:T(8,128)S(1)}, u32[]{:S(2)}, u32[]{:S(2)}) collective-permute-start(f32[128,1024]{1,0:T(8,128)S(1)} %collective-permute-done.1.x), channel_id=1, source_target_pairs={{0,16},{4,12},{8,24},{12,4},{16,0},{20,28},{24,8},{28,20},{1,17},{... | collective-permute-start | bytes 1572872 | tf_op jit(solution)/shard_map/ppermute | solution.py:368
  27.2 9.3 %collective-permute-start.5 = (f32[240,256]{1,0:T(8,128)S(1)}, f32[240,256]{1,0:T(8,128)S(1)}, u32[]{:S(2)}, u32[]{:S(2)}) collective-permute-start(f32[240,256]{1,0:T(8,128)S(1)} %get-tuple-element.161), channel_id=1, source_target_pairs={{0,8},{4,20},{8,0},{12,28},{16,24},{20,4},{24,16},{28,12},{1,9},{5... | collective-permute-start | bytes 737288 | tf_op jit(solution)/shard_map/ppermute | solution.py:368
  29.6 7.9 %collective-permute-start.6 = (f32[240,256]{1,0:T(8,128)S(1)}, f32[240,256]{1,0:T(8,128)S(1)}, u32[]{:S(2)}, u32[]{:S(2)}) collective-permute-start(f32[240,256]{1,0:T(8,128)S(1)} %get-tuple-element.162), channel_id=1, source_target_pairs={{0,16},{4,12},{8,24},{12,4},{16,0},{20,28},{24,8},{28,20},{1,17},{... | collective-permute-start | bytes 737288 | tf_op jit(solution)/shard_map/ppermute | solution.py:368
  32.3 10.6 %collective-permute-start.9 = (f32[264,256]{1,0:T(8,128)S(1)}, f32[264,256]{1,0:T(8,128)S(1)}, u32[]{:S(2)}, u32[]{:S(2)}) collective-permute-start(f32[264,256]{1,0:T(8,128)S(1)} %get-tuple-element.152), channel_id=1, source_target_pairs={{0,8},{4,20},{8,0},{12,28},{16,24},{20,4},{24,16},{28,12},{1,9},{5... | collective-permute-start | bytes 811016 | tf_op jit(solution)/shard_map/ppermute | solution.py:368
  32.4 10.5 %collective-permute-start.10 = (f32[256,256]{1,0:T(8,128)S(1)}, f32[256,256]{1,0:T(8,128)S(1)}, u32[]{:S(2)}, u32[]{:S(2)}) collective-permute-start(f32[256,256]{1,0:T(8,128)S(1)} %get-tuple-element.171), channel_id=1, source_target_pairs={{0,16},{4,12},{8,24},{12,4},{16,0},{20,28},{24,8},{28,20},{1,17},{... | collective-permute-start | bytes 786440 | tf_op jit(solution)/shard_map/ppermute | solution.py:368
  37.5 10.3 %collective-permute-start.7 = (f32[240,256]{1,0:T(8,128)S(1)}, f32[240,256]{1,0:T(8,128)S(1)}, u32[]{:S(2)}, u32[]{:S(2)}) collective-permute-start(f32[240,256]{1,0:T(8,128)S(1)} %get-tuple-element.177.refs_0_), channel_id=1, source_target_pairs={{0,16},{4,12},{8,24},{12,4},{16,0},{20,28},{24,8},{28,20},{1,17},{... | collective-permute-start | bytes 737288 | tf_op jit(solution)/shard_map/ppermute | solution.py:368
  38.6 9.2 %collective-permute-start.8 = (f32[240,256]{1,0:T(8,128)S(1)}, f32[240,256]{1,0:T(8,128)S(1)}, u32[]{:S(2)}, u32[]{:S(2)}) collective-permute-start(f32[240,256]{1,0:T(8,128)S(1)} %get-tuple-element.178.refs_1_), channel_id=1, source_target_pairs={{0,8},{4,20},{8,0},{12,28},{16,24},{20,4},{24,16},{28,12},{1,9},{5... | collective-permute-start | bytes 737288 | tf_op jit(solution)/shard_map/ppermute | solution.py:368
  42.9 10.7 %collective-permute-start.13 = (f32[264,256]{1,0:T(8,128)S(1)}, f32[264,256]{1,0:T(8,128)S(1)}, u32[]{:S(2)}, u32[]{:S(2)}) collective-permute-start(f32[264,256]{1,0:T(8,128)S(1)} %get-tuple-element.184.refs_0_), channel_id=1, source_target_pairs={{0,16},{4,12},{8,24},{12,4},{16,0},{20,28},{24,8},{28,20},{1,17},{... | collective-permute-start | bytes 811016 | tf_op jit(solution)/shard_map/ppermute | solution.py:368
  43.9 9.7 %collective-permute-start.14 = (f32[256,256]{1,0:T(8,128)S(1)}, f32[256,256]{1,0:T(8,128)S(1)}, u32[]{:S(2)}, u32[]{:S(2)}) collective-permute-start(f32[256,256]{1,0:T(8,128)S(1)} %get-tuple-element.185.refs_1_), channel_id=1, source_target_pairs={{0,8},{4,20},{8,0},{12,28},{16,24},{20,4},{24,16},{28,12},{1,9},{5... | collective-permute-start | bytes 786440 | tf_op jit(solution)/shard_map/ppermute | solution.py:368
  47.8 11.1 %collective-permute-start.11 = (f32[240,256]{1,0:T(8,128)S(1)}, f32[240,256]{1,0:T(8,128)S(1)}, u32[]{:S(2)}, u32[]{:S(2)}) collective-permute-start(f32[240,256]{1,0:T(8,128)S(1)} %get-tuple-element.189.full_a), channel_id=1, source_target_pairs={{0,8},{4,20},{8,0},{12,28},{16,24},{20,4},{24,16},{28,12},{1,9},{5... | collective-permute-start | bytes 737288 | tf_op jit(solution)/shard_map/ppermute | solution.py:368
  49.7 9.3 %collective-permute-start.12 = (f32[240,256]{1,0:T(8,128)S(1)}, f32[240,256]{1,0:T(8,128)S(1)}, u32[]{:S(2)}, u32[]{:S(2)}) collective-permute-start(f32[240,256]{1,0:T(8,128)S(1)} %get-tuple-element.190.full_b), channel_id=1, source_target_pairs={{0,16},{4,12},{8,24},{12,4},{16,0},{20,28},{24,8},{28,20},{1,17},{... | collective-permute-start | bytes 737288 | tf_op jit(solution)/shard_map/ppermute | solution.py:368
  53.7 9.8 %collective-permute-start.19 = (f32[264,256]{1,0:T(8,128)S(1)}, f32[264,256]{1,0:T(8,128)S(1)}, u32[]{:S(2)}, u32[]{:S(2)}) collective-permute-start(f32[264,256]{1,0:T(8,128)S(1)} %get-tuple-element.208.full_a), channel_id=1, source_target_pairs={{0,8},{4,20},{8,0},{12,28},{16,24},{20,4},{24,16},{28,12},{1,9},{5... | collective-permute-start | bytes 811016 | tf_op jit(solution)/shard_map/ppermute | solution.py:368
  55.8 7.7 %collective-permute-start.20 = (f32[256,256]{1,0:T(8,128)S(1)}, f32[256,256]{1,0:T(8,128)S(1)}, u32[]{:S(2)}, u32[]{:S(2)}) collective-permute-start(f32[256,256]{1,0:T(8,128)S(1)} %get-tuple-element.209.full_b), channel_id=1, source_target_pairs={{0,16},{4,12},{8,24},{12,4},{16,0},{20,28},{24,8},{28,20},{1,17},{... | collective-permute-start | bytes 786440 | tf_op jit(solution)/shard_map/ppermute | solution.py:368
  61.9 8.6 %collective-permute-start.18 = (f32[480,128]{1,0:T(8,128)S(1)}, f32[480,128]{1,0:T(8,128)S(1)}, u32[]{:S(2)}, u32[]{:S(2)}) collective-permute-start(f32[480,128]{1,0:T(8,128)S(1)} %get-tuple-element.206), channel_id=1, source_target_pairs={{0,1},{1,0},{2,3},{3,2},{4,5},{5,4},{6,7},{7,6},{8,9},{9,8},{10,11... | collective-permute-start | bytes 737288 | tf_op jit(solution)/shard_map/ppermute | solution.py:274
  64.5 2.0 %collective-permute-start.21 = (f32[176,256]{1,0:T(8,128)S(1)}, f32[176,256]{1,0:T(8,128)S(1)}, u32[]{:S(2)}, u32[]{:S(2)}) collective-permute-start(f32[176,256]{1,0:T(8,128)S(1)} %get-tuple-element.217), channel_id=1, source_target_pairs={{0,4},{4,0},{1,5},{5,1},{2,6},{6,2},{3,7},{7,3},{8,12},{12,8},{9,1... | collective-permute-start | bytes 540680 | tf_op jit(solution)/shard_map/ppermute | solution.py:23
  66.6 9.1 %collective-permute-start.25 = (f32[520,128]{1,0:T(8,128)S(1)}, f32[520,128]{1,0:T(8,128)S(1)}, u32[]{:S(2)}, u32[]{:S(2)}) collective-permute-start(f32[520,128]{1,0:T(8,128)S(1)} %get-tuple-element.224), channel_id=1, source_target_pairs={{0,1},{1,0},{2,3},{3,2},{4,5},{5,4},{6,7},{7,6},{8,9},{9,8},{10,11... | collective-permute-start | bytes 798728 | tf_op jit(solution)/shard_map/ppermute | solution.py:274
  70.5 17.1 %collective-permute-start.24 = (f32[480,128]{1,0:T(8,128)S(1)}, f32[480,128]{1,0:T(8,128)S(1)}, u32[]{:S(2)}, u32[]{:S(2)}) collective-permute-start(f32[480,128]{1,0:T(8,128)S(1)} %shard_map.82.refs_0_), channel_id=1, source_target_pairs={{0,3},{3,0},{1,2},{2,1},{4,7},{7,4},{5,6},{6,5},{8,11},{11,8},{9,1... | collective-permute-start | bytes 737288 | tf_op jit(solution)/shard_map/ppermute | solution.py:274
  75.8 19.0 %collective-permute-start.27 = (f32[520,128]{1,0:T(8,128)S(1)}, f32[520,128]{1,0:T(8,128)S(1)}, u32[]{:S(2)}, u32[]{:S(2)}) collective-permute-start(f32[520,128]{1,0:T(8,128)S(1)} %shard_map.83.refs_0_), channel_id=1, source_target_pairs={{0,3},{3,0},{1,2},{2,1},{4,7},{7,4},{5,6},{6,5},{8,11},{11,8},{9,1... | collective-permute-start | bytes 798728 | tf_op jit(solution)/shard_map/ppermute | solution.py:274
  87.6 7.1 %collective-permute-start.26 = (f32[480,128]{1,0:T(8,128)S(1)}, f32[480,128]{1,0:T(8,128)S(1)}, u32[]{:S(2)}, u32[]{:S(2)}) collective-permute-start(f32[480,128]{1,0:T(8,128)S(1)} %shard_map.84.a), channel_id=1, source_target_pairs={{0,1},{1,0},{2,3},{3,2},{4,5},{5,4},{6,7},{7,6},{8,9},{9,8},{10,11... | collective-permute-start | bytes 737288 | tf_op jit(solution)/shard_map/ppermute | solution.py:274
  94.8 7.1 %collective-permute-start.28 = (f32[520,128]{1,0:T(8,128)S(1)}, f32[520,128]{1,0:T(8,128)S(1)}, u32[]{:S(2)}, u32[]{:S(2)}) collective-permute-start(f32[520,128]{1,0:T(8,128)S(1)} %shard_map.86.a), channel_id=1, source_target_pairs={{0,1},{1,0},{2,3},{3,2},{4,5},{5,4},{6,7},{7,6},{8,9},{9,8},{10,11... | collective-permute-start | bytes 798728 | tf_op jit(solution)/shard_map/ppermute | solution.py:274
  (10 other events, 15.5 us)

commit v14 on v13

--- a/solution.py
+++ b/solution.py
@@ -240,34 +240,29 @@
     return [(at, min(size, at + step)) for at in range(0, size, step)]
 
 
-def grad_body(factor, full_a, full_b, other_a, other_b, near_high, near_low, far_high, far_low, here, *gone):
-    rows, half = full_a.shape[1] // 2, here.shape[1]
-    at = 0
+def grad_body(factor, away, full_a, full_b, other_a, other_b, near_high, near_low, far_high, far_low, *outs):
+    rows, half = full_a.shape[1] // 2, outs[0].shape[1]
+    cols = pl.ds(half if away else 0, half)
+    parts = blocks(full_a.shape[0] + full_b.shape[0], len(outs))
+    start = 0
     for i, (full, other) in enumerate(((full_a, other_a), (full_b, other_b))):
-        to = pl.ds(at, full.shape[0])
-        at += full.shape[0]
-        full_pair, other_pair = halves(full[...]), halves(other[...])
+        end = start + full.shape[0]
         stay, go = stays(rows)[i], goes(rows)[i]
-        for away, cols in ((True, pl.ds(half, half)), (False, pl.ds(0, half))):
-            value = factor * (
-                mul3(full_pair, (near_high[stay, cols], near_low[stay, cols]), NN)
-                + mul3(other_pair, (far_high[go, cols], far_low[go, cols]), NN)
-            )
-            if not away:
-                here[to] = value
-                continue
-            start, end = at - full.shape[0], at
-            for ref, (low, high) in zip(gone, blocks(here.shape[0], PARTS)):
-                low_at, high_at = max(low, start), min(high, end)
-                if low_at < high_at:
-                    ref[pl.ds(low_at - low, high_at - low_at)] = value[low_at - start : high_at - start]
-
-
-def grad_parts(factor, full, other, near, far):
+        value = factor * (
+            mul3(halves(full[...]), (near_high[stay, cols], near_low[stay, cols]), NN)
+            + mul3(halves(other[...]), (far_high[go, cols], far_low[go, cols]), NN)
+        )
+        for ref, (low, high) in zip(outs, parts):
+            at, to = max(low, start), min(high, end)
+            if at < to:
+                ref[pl.ds(at - low, to - at)] = value[at - start : to - start]
+        start = end
+
+
+def grad_parts(factor, away, full, other, near, far):
     cols, half = full[0].shape[0] + full[1].shape[0], near[0].shape[1] // 2
-    outs = [shaped((cols, half))] + [shaped((b - a, half)) for a, b in blocks(cols, PARTS)]
-    out = call(functools.partial(grad_body, factor), outs, (*full, *other, *near, *far))
-    return out[1:], out[0]
+    outs = [shaped((b - a, half)) for a, b in blocks(cols, PARTS if away else 1)]
+    return call(functools.partial(grad_body, factor, away), outs, (*full, *other, *near, *far))
 
 
 def pass_line(value, pairs):
@@ -399,8 +394,9 @@
         other[r] = both(full[r], 0)
 
     def do_grad(r):
-        gone[r], here[r] = line(lambda *a: grad_parts(factor, *a), full[r], other[r], near, far)
+        gone[r] = line(lambda *a: grad_parts(factor, True, *a), full[r], other[r], near, far)
         gone[r] = [swap(part, "core") for part in gone[r]]
+        (here[r],) = line(lambda *a: grad_parts(factor, False, *a), full[r], other[r], near, far)
 
     def do_owned(r):
         sends, keeps = line(lambda *a: split(LINE_PIECES[r], *a), here[r], gone[r])

time: 103 us -> 103 us (level)
    ppermute x8, waiting for transfers between devices: 2.66 us -> 1.49 us  [swap(): return lax.ppermute(value, axis, [(i, i ^ flip) for i in range(size)])]
    pallas_call x20 -> x22, Pallas kernels: 10.1 us -> 10.4 us  [call(): pl.pallas_call(body, out_shape=outs, in_specs=[vmem] * len(args), out_spe...]
where the time goes in v14:
time: 103 us
  starting transfers between devices  47.3 us (46%)
  waiting for transfers between devices  40 us (39%)
  Pallas kernels  10.4 us (10%)
  local copies, waits for them, and re-layouts  2.19 us (2%)
  other arithmetic  1.85 us (2%)
    ppermute x15, starting transfers between devices, hop(): return lax.ppermute(value, ('chip', 'core'), pairs)  24.8 us
    ppermute x15, waiting for transfers between devices, hop(): return lax.ppermute(value, ('chip', 'core'), pairs)  22.8 us
    ppermute x6, starting transfers between devices, pass_line(): return lax.ppermute(value, 'col', pairs)  20.6 us
    ppermute x6, waiting for transfers between devices, pass_line(): return lax.ppermute(value, 'col', pairs)  15.7 us
    pallas_call x22, Pallas kernels, call(): pl.pallas_call(body, out_shape=outs, in_specs=[vmem] * len(args), out_spe...  10.4 us
    unnamed x10, local copies, waits for them, and re-layouts  2.15 us
  transfers between devices with their start and end apart: 29, of which 16 were waited for; matrix products, arithmetic and copies ran while one was open for 1% of the time, Pallas kernels for 8%

profile of v14, /device:TPU:0, one launch (start us, length us, event | category | flops | bytes accessed | tf_op | source)
XLA Modules:
  0.0 102.7 jit_solution(6164638508818113474)
XLA Ops:
  1.1 2.6 %collective-permute-start.1 = (f32[128,1024]{1,0:T(8,128)}, f32[128,1024]{1,0:T(8,128)S(1)}, u32[]{:S(2)}, u32[]{:S(2)}) collective-permute-start(f32[128,1024]{1,0:T(8,128)} %own), channel_id=1, source_target_pairs={{0,8},{4,20},{8,0},{12,28},{16,24},{20,4},{24,16},{28,12},{1,9},{5... | collective-permute-start | bytes 1572872 | tf_op jit(solution)/shard_map/ppermute | solution.py:363
  5.2 10.4 %collective-permute-done.1.x = f32[128,1024]{1,0:T(8,128)S(1)} collective-permute-done((f32[128,1024]{1,0:T(8,128)}, f32[128,1024]{1,0:T(8,128)S(1)}, u32[]{:S(2)}, u32[]{:S(2)}) %collective-permute-start.1) | collective-permute-done | bytes 524320 | tf_op jit(solution)/shard_map/ppermute | solution.py:363
  15.7 2.1 %collective-permute-start.4 = (f32[128,1024]{1,0:T(8,128)S(1)}, f32[128,1024]{1,0:T(8,128)S(1)}, u32[]{:S(2)}, u32[]{:S(2)}) collective-permute-start(f32[128,1024]{1,0:T(8,128)S(1)} %collective-permute-done.1.x), channel_id=1, source_target_pairs={{0,16},{4,12},{8,24},{12,4},{16,0},{20,28},{24,8},{28,20},{1,17},{... | collective-permute-start | bytes 1572872 | tf_op jit(solution)/shard_map/ppermute | solution.py:363
  20.1 1.6 %shard_map.69 = (bf16[128,512]{1,0:T(8,128)(2,1)S(1)}, bf16[128,512]{1,0:T(8,128)(2,1)S(1)}) custom-call(f32[128,1024]{1,0:T(8,128)S(1)} %copy-done.2, bf16[512,1024]{1,0:T(8,128)(2,1)S(1)} %get-tuple-element.153.c_high, bf16[512,1024]{1,0:T(8,128)(2,1)S(1)} %get-tuple-element.154.c_low, f32[8,512]{1,0:T(8,128)S(1)} %get-tuple-element.155.c_sq), custom_call_target="tpu_custom_call" | custom-call | tf_op jit(solution)/shard_map/pallas_call | solution.py:56
  21.7 1.6 %shard_map.70 = (bf16[384,512]{1,0:T(8,128)(2,1)S(1)}, bf16[384,512]{1,0:T(8,128)(2,1)S(1)}) custom-call(f32[128,1024]{1,0:T(8,128)S(1)} %collective-permute-done.1.x, f32[128,1024]{1,0:T(8,128)S(1)} %collective-permute-done.2.y, bf16[512,1024]{1,0:T(8,128)(2,1)S(1)} %get-tuple-element.153.c_high, bf16[512,1024]{1,0:T(8,128)(2,1)S(1)} %get-tuple-element.154.c_low, ...), custom_call_target="tpu_custom_call" | custom-call | tf_op jit(solution)/shard_map/pallas_call | solution.py:56
  23.3 1.6 %collective-permute-done.4.block = f32[128,1024]{1,0:T(8,128)S(1)} collective-permute-done((f32[128,1024]{1,0:T(8,128)S(1)}, f32[128,1024]{1,0:T(8,128)S(1)}, u32[]{:S(2)}, u32[]{:S(2)}) %collective-permute-start.4) | collective-permute-done | bytes 524320 | tf_op jit(solution)/shard_map/ppermute | solution.py:363
  24.9 2.2 %shard_map.71 = (bf16[384,512]{1,0:T(8,128)(2,1)S(1)}, bf16[384,512]{1,0:T(8,128)(2,1)S(1)}, f32[240,256]{1,0:T(8,128)S(1)}, f32[240,256]{1,0:T(8,128)S(1)}) custom-call(f32[128,1024]{1,0:T(8,128)S(1)} %collective-permute-done.4.block, bf16[512,1024]{1,0:T(8,128)(2,1)S(1)} %get-tuple-element.153.c_high, bf16[512,1024]{1,0:T(8,128)(2,1)S(1)} %get-tuple-element.154.c_low, ...), custom_call_target="tpu_custom_call" | custom-call | tf_op jit(solution)/shard_map/pallas_call | solution.py:56
  27.2 2.4 %collective-permute-start.5 = (f32[240,256]{1,0:T(8,128)S(1)}, f32[240,256]{1,0:T(8,128)S(1)}, u32[]{:S(2)}, u32[]{:S(2)}) collective-permute-start(f32[240,256]{1,0:T(8,128)S(1)} %get-tuple-element.175), channel_id=1, source_target_pairs={{0,8},{4,20},{8,0},{12,28},{16,24},{20,4},{24,16},{28,12},{1,9},{5... | collective-permute-start | bytes 737288 | tf_op jit(solution)/shard_map/ppermute | solution.py:363
  29.6 2.0 %collective-permute-start.6 = (f32[240,256]{1,0:T(8,128)S(1)}, f32[240,256]{1,0:T(8,128)S(1)}, u32[]{:S(2)}, u32[]{:S(2)}) collective-permute-start(f32[240,256]{1,0:T(8,128)S(1)} %get-tuple-element.176), channel_id=1, source_target_pairs={{0,16},{4,12},{8,24},{12,4},{16,0},{20,28},{24,8},{28,20},{1,17},{... | collective-permute-start | bytes 737288 | tf_op jit(solution)/shard_map/ppermute | solution.py:363
  33.9 2.6 %collective-permute-done.5.refs_2_ = f32[240,256]{1,0:T(8,128)S(1)} collective-permute-done((f32[240,256]{1,0:T(8,128)S(1)}, f32[240,256]{1,0:T(8,128)S(1)}, u32[]{:S(2)}, u32[]{:S(2)}) %collective-permute-start.5) | collective-permute-done | bytes 245792 | tf_op jit(solution)/shard_map/ppermute | solution.py:363
  38.6 2.1 %collective-permute-start.8 = (f32[240,256]{1,0:T(8,128)S(1)}, f32[240,256]{1,0:T(8,128)S(1)}, u32[]{:S(2)}, u32[]{:S(2)}) collective-permute-start(f32[240,256]{1,0:T(8,128)S(1)} %get-tuple-element.192.refs_1_), channel_id=1, source_target_pairs={{0,8},{4,20},{8,0},{12,28},{16,24},{20,4},{24,16},{28,12},{1,9},{5... | collective-permute-start | bytes 737288 | tf_op jit(solution)/shard_map/ppermute | solution.py:363
  40.7 2.2 %collective-permute-done.10.refs_3_ = f32[256,256]{1,0:T(8,128)S(1)} collective-permute-done((f32[256,256]{1,0:T(8,128)S(1)}, f32[256,256]{1,0:T(8,128)S(1)}, u32[]{:S(2)}, u32[]{:S(2)}) %collective-permute-start.10) | collective-permute-done | bytes 262176 | tf_op jit(solution)/shard_map/ppermute | solution.py:363
  44.0 2.5 %collective-permute-start.14 = (f32[256,256]{1,0:T(8,128)S(1)}, f32[256,256]{1,0:T(8,128)S(1)}, u32[]{:S(2)}, u32[]{:S(2)}) collective-permute-start(f32[256,256]{1,0:T(8,128)S(1)} %get-tuple-element.199.refs_1_), channel_id=1, source_target_pairs={{0,8},{4,20},{8,0},{12,28},{16,24},{20,4},{24,16},{28,12},{1,9},{5... | collective-permute-start | bytes 786440 | tf_op jit(solution)/shard_map/ppermute | solution.py:363
  47.8 1.8 %collective-permute-start.11 = (f32[240,256]{1,0:T(8,128)S(1)}, f32[240,256]{1,0:T(8,128)S(1)}, u32[]{:S(2)}, u32[]{:S(2)}) collective-permute-start(f32[240,256]{1,0:T(8,128)S(1)} %get-tuple-element.212.full_a), channel_id=1, source_target_pairs={{0,8},{4,20},{8,0},{12,28},{16,24},{20,4},{24,16},{28,12},{1,9},{5... | collective-permute-start | bytes 737288 | tf_op jit(solution)/shard_map/ppermute | solution.py:363
  49.7 1.9 %collective-permute-start.12 = (f32[240,256]{1,0:T(8,128)S(1)}, f32[240,256]{1,0:T(8,128)S(1)}, u32[]{:S(2)}, u32[]{:S(2)}) collective-permute-start(f32[240,256]{1,0:T(8,128)S(1)} %get-tuple-element.213.full_b), channel_id=1, source_target_pairs={{0,16},{4,12},{8,24},{12,4},{16,0},{20,28},{24,8},{28,20},{1,17},{... | collective-permute-start | bytes 737288 | tf_op jit(solution)/shard_map/ppermute | solution.py:363
  51.6 2.1 %collective-permute-done.14.refs_3_ = f32[256,256]{1,0:T(8,128)S(1)} collective-permute-done((f32[256,256]{1,0:T(8,128)S(1)}, f32[256,256]{1,0:T(8,128)S(1)}, u32[]{:S(2)}, u32[]{:S(2)}) %collective-permute-start.14) | collective-permute-done | bytes 262176 | tf_op jit(solution)/shard_map/ppermute | solution.py:363
  53.7 2.1 %collective-permute-start.19 = (f32[264,256]{1,0:T(8,128)S(1)}, f32[264,256]{1,0:T(8,128)S(1)}, u32[]{:S(2)}, u32[]{:S(2)}) collective-permute-start(f32[264,256]{1,0:T(8,128)S(1)} %get-tuple-element.238.full_a), channel_id=1, source_target_pairs={{0,8},{4,20},{8,0},{12,28},{16,24},{20,4},{24,16},{28,12},{1,9},{5... | collective-permute-start | bytes 811016 | tf_op jit(solution)/shard_map/ppermute | solution.py:363
  61.5 1.6 %collective-permute-start.18 = (f32[480,128]{1,0:T(8,128)S(1)}, f32[480,128]{1,0:T(8,128)S(1)}, u32[]{:S(2)}, u32[]{:S(2)}) collective-permute-start(f32[480,128]{1,0:T(8,128)S(1)} %get-tuple-element.227), channel_id=1, source_target_pairs={{0,1},{1,0},{2,3},{3,2},{4,5},{5,4},{6,7},{7,6},{8,9},{9,8},{10,11... | collective-permute-start | bytes 737288 | tf_op jit(solution)/shard_map/ppermute | solution.py:269
  67.0 3.4 %collective-permute-done.18.refs_1_ = f32[480,128]{1,0:T(8,128)S(1)} collective-permute-done((f32[480,128]{1,0:T(8,128)S(1)}, f32[480,128]{1,0:T(8,128)S(1)}, u32[]{:S(2)}, u32[]{:S(2)}) %collective-permute-start.18) | collective-permute-done | bytes 245792 | tf_op jit(solution)/shard_map/ppermute | solution.py:269
  70.4 3.7 %collective-permute-start.24 = (f32[480,128]{1,0:T(8,128)S(1)}, f32[480,128]{1,0:T(8,128)S(1)}, u32[]{:S(2)}, u32[]{:S(2)}) collective-permute-start(f32[480,128]{1,0:T(8,128)S(1)} %shard_map.84.refs_0_), channel_id=1, source_target_pairs={{0,3},{3,0},{1,2},{2,1},{4,7},{7,4},{5,6},{6,5},{8,11},{11,8},{9,1... | collective-permute-start | bytes 737288 | tf_op jit(solution)/shard_map/ppermute | solution.py:269
  75.4 11.8 %collective-permute-start.27 = (f32[520,128]{1,0:T(8,128)S(1)}, f32[520,128]{1,0:T(8,128)S(1)}, u32[]{:S(2)}, u32[]{:S(2)}) collective-permute-start(f32[520,128]{1,0:T(8,128)S(1)} %shard_map.85.refs_0_), channel_id=1, source_target_pairs={{0,3},{3,0},{1,2},{2,1},{4,7},{7,4},{5,6},{6,5},{8,11},{11,8},{9,1... | collective-permute-start | bytes 798728 | tf_op jit(solution)/shard_map/ppermute | solution.py:269
  87.5 6.8 %collective-permute-done.26.b = f32[480,128]{1,0:T(8,128)S(1)} collective-permute-done((f32[480,128]{1,0:T(8,128)S(1)}, f32[480,128]{1,0:T(8,128)S(1)}, u32[]{:S(2)}, u32[]{:S(2)}) %collective-permute-start.26) | collective-permute-done | bytes 245792 | tf_op jit(solution)/shard_map/ppermute | solution.py:269
  94.4 2.0 %collective-permute-start.28 = (f32[520,128]{1,0:T(8,128)S(1)}, f32[520,128]{1,0:T(8,128)S(1)}, u32[]{:S(2)}, u32[]{:S(2)}) collective-permute-start(f32[520,128]{1,0:T(8,128)S(1)} %shard_map.88.a), channel_id=1, source_target_pairs={{0,1},{1,0},{2,3},{3,2},{4,5},{5,4},{6,7},{7,6},{8,9},{9,8},{10,11... | collective-permute-start | bytes 798728 | tf_op jit(solution)/shard_map/ppermute | solution.py:269
  97.4 4.2 %collective-permute-done.28.b = f32[520,128]{1,0:T(8,128)S(1)} collective-permute-done((f32[520,128]{1,0:T(8,128)S(1)}, f32[520,128]{1,0:T(8,128)S(1)}, u32[]{:S(2)}, u32[]{:S(2)}) %collective-permute-start.28) | collective-permute-done | bytes 266272 | tf_op jit(solution)/shard_map/ppermute | solution.py:269
  (72 shorter events, 24.4 us)
Async XLA Ops:
  0.6 17.2 %collective-permute-start.3 = (f32[256,1024]{1,0:T(8,128)}, f32[256,1024]{1,0:T(8,128)S(1)}, u32[]{:S(2)}, u32[]{:S(2)}) collective-permute-start(f32[256,1024]{1,0:T(8,128)} %mine_ref.1), channel_id=1, source_target_pairs={{0,4},{4,0},{1,5},{5,1},{2,6},{6,2},{3,7},{7,3},{8,12},{12,8},{9,1... | collective-permute-start | bytes 3145736 | tf_op jit(solution)/shard_map/ppermute | solution.py:23
  1.1 14.5 %collective-permute-start.1 = (f32[128,1024]{1,0:T(8,128)}, f32[128,1024]{1,0:T(8,128)S(1)}, u32[]{:S(2)}, u32[]{:S(2)}) collective-permute-start(f32[128,1024]{1,0:T(8,128)} %own), channel_id=1, source_target_pairs={{0,8},{4,20},{8,0},{12,28},{16,24},{20,4},{24,16},{28,12},{1,9},{5... | collective-permute-start | bytes 1572872 | tf_op jit(solution)/shard_map/ppermute | solution.py:363
  3.7 19.6 %collective-permute-start = (f32[1000,256]{1,0:T(8,128)}, f32[1000,256]{1,0:T(8,128)S(1)}, u32[]{:S(2)}, u32[]{:S(2)}) collective-permute-start(f32[1000,256]{1,0:T(8,128)} %bitcast.7), channel_id=1, source_target_pairs={{0,4},{4,0},{1,5},{5,1},{2,6},{6,2},{3,7},{7,3},{8,12},{12,8},{9,1... | collective-permute-start | bytes 3072008 | tf_op jit(solution)/shard_map/ppermute | solution.py:23
  3.9 17.8 %collective-permute-start.2 = (f32[128,1024]{1,0:T(8,128)}, f32[128,1024]{1,0:T(8,128)S(1)}, u32[]{:S(2)}, u32[]{:S(2)}) collective-permute-start(f32[128,1024]{1,0:T(8,128)} %own), channel_id=1, source_target_pairs={{0,16},{4,12},{8,24},{12,4},{16,0},{20,28},{24,8},{28,20},{1,17},{... | collective-permute-start | bytes 1572872 | tf_op jit(solution)/shard_map/ppermute | solution.py:363
  15.7 9.3 %collective-permute-start.4 = (f32[128,1024]{1,0:T(8,128)S(1)}, f32[128,1024]{1,0:T(8,128)S(1)}, u32[]{:S(2)}, u32[]{:S(2)}) collective-permute-start(f32[128,1024]{1,0:T(8,128)S(1)} %collective-permute-done.1.x), channel_id=1, source_target_pairs={{0,16},{4,12},{8,24},{12,4},{16,0},{20,28},{24,8},{28,20},{1,17},{... | collective-permute-start | bytes 1572872 | tf_op jit(solution)/shard_map/ppermute | solution.py:363
  27.2 9.3 %collective-permute-start.5 = (f32[240,256]{1,0:T(8,128)S(1)}, f32[240,256]{1,0:T(8,128)S(1)}, u32[]{:S(2)}, u32[]{:S(2)}) collective-permute-start(f32[240,256]{1,0:T(8,128)S(1)} %get-tuple-element.175), channel_id=1, source_target_pairs={{0,8},{4,20},{8,0},{12,28},{16,24},{20,4},{24,16},{28,12},{1,9},{5... | collective-permute-start | bytes 737288 | tf_op jit(solution)/shard_map/ppermute | solution.py:363
  29.6 7.9 %collective-permute-start.6 = (f32[240,256]{1,0:T(8,128)S(1)}, f32[240,256]{1,0:T(8,128)S(1)}, u32[]{:S(2)}, u32[]{:S(2)}) collective-permute-start(f32[240,256]{1,0:T(8,128)S(1)} %get-tuple-element.176), channel_id=1, source_target_pairs={{0,16},{4,12},{8,24},{12,4},{16,0},{20,28},{24,8},{28,20},{1,17},{... | collective-permute-start | bytes 737288 | tf_op jit(solution)/shard_map/ppermute | solution.py:363
  32.2 10.6 %collective-permute-start.9 = (f32[264,256]{1,0:T(8,128)S(1)}, f32[264,256]{1,0:T(8,128)S(1)}, u32[]{:S(2)}, u32[]{:S(2)}) collective-permute-start(f32[264,256]{1,0:T(8,128)S(1)} %get-tuple-element.166), channel_id=1, source_target_pairs={{0,8},{4,20},{8,0},{12,28},{16,24},{20,4},{24,16},{28,12},{1,9},{5... | collective-permute-start | bytes 811016 | tf_op jit(solution)/shard_map/ppermute | solution.py:363
  32.4 10.5 %collective-permute-start.10 = (f32[256,256]{1,0:T(8,128)S(1)}, f32[256,256]{1,0:T(8,128)S(1)}, u32[]{:S(2)}, u32[]{:S(2)}) collective-permute-start(f32[256,256]{1,0:T(8,128)S(1)} %get-tuple-element.185), channel_id=1, source_target_pairs={{0,16},{4,12},{8,24},{12,4},{16,0},{20,28},{24,8},{28,20},{1,17},{... | collective-permute-start | bytes 786440 | tf_op jit(solution)/shard_map/ppermute | solution.py:363
  37.5 10.3 %collective-permute-start.7 = (f32[240,256]{1,0:T(8,128)S(1)}, f32[240,256]{1,0:T(8,128)S(1)}, u32[]{:S(2)}, u32[]{:S(2)}) collective-permute-start(f32[240,256]{1,0:T(8,128)S(1)} %get-tuple-element.191.refs_0_), channel_id=1, source_target_pairs={{0,16},{4,12},{8,24},{12,4},{16,0},{20,28},{24,8},{28,20},{1,17},{... | collective-permute-start | bytes 737288 | tf_op jit(solution)/shard_map/ppermute | solution.py:363
  38.6 9.2 %collective-permute-start.8 = (f32[240,256]{1,0:T(8,128)S(1)}, f32[240,256]{1,0:T(8,128)S(1)}, u32[]{:S(2)}, u32[]{:S(2)}) collective-permute-start(f32[240,256]{1,0:T(8,128)S(1)} %get-tuple-element.192.refs_1_), channel_id=1, source_target_pairs={{0,8},{4,20},{8,0},{12,28},{16,24},{20,4},{24,16},{28,12},{1,9},{5... | collective-permute-start | bytes 737288 | tf_op jit(solution)/shard_map/ppermute | solution.py:363
  42.9 10.7 %collective-permute-start.13 = (f32[264,256]{1,0:T(8,128)S(1)}, f32[264,256]{1,0:T(8,128)S(1)}, u32[]{:S(2)}, u32[]{:S(2)}) collective-permute-start(f32[264,256]{1,0:T(8,128)S(1)} %get-tuple-element.198.refs_0_), channel_id=1, source_target_pairs={{0,16},{4,12},{8,24},{12,4},{16,0},{20,28},{24,8},{28,20},{1,17},{... | collective-permute-start | bytes 811016 | tf_op jit(solution)/shard_map/ppermute | solution.py:363
  44.0 9.7 %collective-permute-start.14 = (f32[256,256]{1,0:T(8,128)S(1)}, f32[256,256]{1,0:T(8,128)S(1)}, u32[]{:S(2)}, u32[]{:S(2)}) collective-permute-start(f32[256,256]{1,0:T(8,128)S(1)} %get-tuple-element.199.refs_1_), channel_id=1, source_target_pairs={{0,8},{4,20},{8,0},{12,28},{16,24},{20,4},{24,16},{28,12},{1,9},{5... | collective-permute-start | bytes 786440 | tf_op jit(solution)/shard_map/ppermute | solution.py:363
  47.8 11.1 %collective-permute-start.11 = (f32[240,256]{1,0:T(8,128)S(1)}, f32[240,256]{1,0:T(8,128)S(1)}, u32[]{:S(2)}, u32[]{:S(2)}) collective-permute-start(f32[240,256]{1,0:T(8,128)S(1)} %get-tuple-element.212.full_a), channel_id=1, source_target_pairs={{0,8},{4,20},{8,0},{12,28},{16,24},{20,4},{24,16},{28,12},{1,9},{5... | collective-permute-start | bytes 737288 | tf_op jit(solution)/shard_map/ppermute | solution.py:363
  49.7 9.3 %collective-permute-start.12 = (f32[240,256]{1,0:T(8,128)S(1)}, f32[240,256]{1,0:T(8,128)S(1)}, u32[]{:S(2)}, u32[]{:S(2)}) collective-permute-start(f32[240,256]{1,0:T(8,128)S(1)} %get-tuple-element.213.full_b), channel_id=1, source_target_pairs={{0,16},{4,12},{8,24},{12,4},{16,0},{20,28},{24,8},{28,20},{1,17},{... | collective-permute-start | bytes 737288 | tf_op jit(solution)/shard_map/ppermute | solution.py:363
  53.7 9.4 %collective-permute-start.19 = (f32[264,256]{1,0:T(8,128)S(1)}, f32[264,256]{1,0:T(8,128)S(1)}, u32[]{:S(2)}, u32[]{:S(2)}) collective-permute-start(f32[264,256]{1,0:T(8,128)S(1)} %get-tuple-element.238.full_a), channel_id=1, source_target_pairs={{0,8},{4,20},{8,0},{12,28},{16,24},{20,4},{24,16},{28,12},{1,9},{5... | collective-permute-start | bytes 811016 | tf_op jit(solution)/shard_map/ppermute | solution.py:363
  55.8 7.4 %collective-permute-start.20 = (f32[256,256]{1,0:T(8,128)S(1)}, f32[256,256]{1,0:T(8,128)S(1)}, u32[]{:S(2)}, u32[]{:S(2)}) collective-permute-start(f32[256,256]{1,0:T(8,128)S(1)} %get-tuple-element.239.full_b), channel_id=1, source_target_pairs={{0,16},{4,12},{8,24},{12,4},{16,0},{20,28},{24,8},{28,20},{1,17},{... | collective-permute-start | bytes 786440 | tf_op jit(solution)/shard_map/ppermute | solution.py:363
  61.5 8.9 %collective-permute-start.18 = (f32[480,128]{1,0:T(8,128)S(1)}, f32[480,128]{1,0:T(8,128)S(1)}, u32[]{:S(2)}, u32[]{:S(2)}) collective-permute-start(f32[480,128]{1,0:T(8,128)S(1)} %get-tuple-element.227), channel_id=1, source_target_pairs={{0,1},{1,0},{2,3},{3,2},{4,5},{5,4},{6,7},{7,6},{8,9},{9,8},{10,11... | collective-permute-start | bytes 737288 | tf_op jit(solution)/shard_map/ppermute | solution.py:269
  63.8 2.0 %collective-permute-start.21 = (f32[176,256]{1,0:T(8,128)S(1)}, f32[176,256]{1,0:T(8,128)S(1)}, u32[]{:S(2)}, u32[]{:S(2)}) collective-permute-start(f32[176,256]{1,0:T(8,128)S(1)} %get-tuple-element.237), channel_id=1, source_target_pairs={{0,4},{4,0},{1,5},{5,1},{2,6},{6,2},{3,7},{7,3},{8,12},{12,8},{9,1... | collective-permute-start | bytes 540680 | tf_op jit(solution)/shard_map/ppermute | solution.py:23
  65.9 9.5 %collective-permute-start.25 = (f32[520,128]{1,0:T(8,128)S(1)}, f32[520,128]{1,0:T(8,128)S(1)}, u32[]{:S(2)}, u32[]{:S(2)}) collective-permute-start(f32[520,128]{1,0:T(8,128)S(1)} %get-tuple-element.252), channel_id=1, source_target_pairs={{0,1},{1,0},{2,3},{3,2},{4,5},{5,4},{6,7},{7,6},{8,9},{9,8},{10,11... | collective-permute-start | bytes 798728 | tf_op jit(solution)/shard_map/ppermute | solution.py:269
  70.4 16.8 %collective-permute-start.24 = (f32[480,128]{1,0:T(8,128)S(1)}, f32[480,128]{1,0:T(8,128)S(1)}, u32[]{:S(2)}, u32[]{:S(2)}) collective-permute-start(f32[480,128]{1,0:T(8,128)S(1)} %shard_map.84.refs_0_), channel_id=1, source_target_pairs={{0,3},{3,0},{1,2},{2,1},{4,7},{7,4},{5,6},{6,5},{8,11},{11,8},{9,1... | collective-permute-start | bytes 737288 | tf_op jit(solution)/shard_map/ppermute | solution.py:269
  75.4 19.0 %collective-permute-start.27 = (f32[520,128]{1,0:T(8,128)S(1)}, f32[520,128]{1,0:T(8,128)S(1)}, u32[]{:S(2)}, u32[]{:S(2)}) collective-permute-start(f32[520,128]{1,0:T(8,128)S(1)} %shard_map.85.refs_0_), channel_id=1, source_target_pairs={{0,3},{3,0},{1,2},{2,1},{4,7},{7,4},{5,6},{6,5},{8,11},{11,8},{9,1... | collective-permute-start | bytes 798728 | tf_op jit(solution)/shard_map/ppermute | solution.py:269
  87.3 7.1 %collective-permute-start.26 = (f32[480,128]{1,0:T(8,128)S(1)}, f32[480,128]{1,0:T(8,128)S(1)}, u32[]{:S(2)}, u32[]{:S(2)}) collective-permute-start(f32[480,128]{1,0:T(8,128)S(1)} %shard_map.86.a), channel_id=1, source_target_pairs={{0,1},{1,0},{2,3},{3,2},{4,5},{5,4},{6,7},{7,6},{8,9},{9,8},{10,11... | collective-permute-start | bytes 737288 | tf_op jit(solution)/shard_map/ppermute | solution.py:269
  94.4 7.1 %collective-permute-start.28 = (f32[520,128]{1,0:T(8,128)S(1)}, f32[520,128]{1,0:T(8,128)S(1)}, u32[]{:S(2)}, u32[]{:S(2)}) collective-permute-start(f32[520,128]{1,0:T(8,128)S(1)} %shard_map.88.a), channel_id=1, source_target_pairs={{0,1},{1,0},{2,3},{3,2},{4,5},{5,4},{6,7},{7,6},{8,9},{9,8},{10,11... | collective-permute-start | bytes 798728 | tf_op jit(solution)/shard_map/ppermute | solution.py:269
  (10 other events, 15.5 us)
